TPU v7x, 32 devices: a whole 2x2x4 slice. The times are simulated.
32 devices in a mesh: sx: 16 (over z, x, core), sy: 2 (over y).
Axes of the slice: x: 2, y: 2, z: 4, core: 2. Of those that a mesh axis runs over, the one named last changes fastest.
Arguments:
- nodes: bfloat16 [16, 2, 1, 256, 256], P('sx', 'sy'), may hold values from -6 to 6
- grad_out: bfloat16 [16, 2, 1, 256, 256], P('sx', 'sy'), may hold values from -6 to 6
- w_query: bfloat16 [256, 256], replicated, as said below
- w_key: bfloat16 [256, 256], replicated, as said below
- w_value: bfloat16 [256, 256], replicated, may hold values from -0.375 to 0.375
- w_out: bfloat16 [256, 256], replicated, may hold values from -0.375 to 0.375
- w_up: bfloat16 [256, 512], replicated, may hold values from -0.375 to 0.375
- w_down: bfloat16 [512, 256], replicated, may hold values from -0.25 to 0.25
- counts: int32 [16, 2, 2], P('sx', 'sy'), may hold values from 64 to 128, as said below
- adjacency: int32 [16, 2, 2, 128, 128], P('sx', 'sy'), may hold values 0 or 1
- expander: int32 [16, 2, 3, 2, 128, 128], P('sx', 'sy'), may hold values 0 or 1
- pairing: int32 [16, 2, 3, 2], P('sx', 'sy'), may hold values from 0 to 1, each once within a row
- boundary: int32 [16, 2, 4, 128], P('sx', 'sy'), may hold values from 0 to 255, as said below
Outputs:
- layer_out: bfloat16 [16, 2, 1, 256, 256], P('sx', 'sy')
- grad_nodes: bfloat16 [16, 2, 1, 256, 256], P('sx', 'sy')
- grad_w_query: float32 [256, 256], replicated
- grad_w_key: float32 [256, 256], replicated
- grad_w_value: float32 [256, 256], replicated
- grad_w_out: float32 [256, 256], replicated
- grad_w_up: float32 [256, 512], replicated
- grad_w_down: float32 [512, 256], replicated
Inputs may be any that keep to these rules, and one draw needn't show every extreme that they name: `counts`: some block holds 128 real nodes. `boundary`: the 128 slots of one side are distinct and hold real nodes. `w_query`: a projection of the normalized features. `w_key`: a projection of the normalized features.
All inputs are finite; a program needn't handle non-finite values. No bound on the sum of `adjacency` or of `expander` on one device may be relied on, other than what follows from the above.
Results may differ from a plain program's by a relative error of at most 0.014.
The roundings to bfloat16 on the way count: a program that leaves them out, or rounds other values in their place, can miss the bound.
Values may be sent and summed in bfloat16 or wider, within the bound.
No kernel may reach another device: no remote copies, remote signals or barrier semaphores. Data moves between devices by JAX's collectives and lax.ppermute only.
A program may use at most 64 MiB of HBM per device.

v0:
```python
import jax
import jax.numpy as jnp
from jax import lax
from jax.sharding import PartitionSpec as P

HEADS = 8
HEAD_DIM = 32


EPSILON = 1e-06
NEG_FILL = -1e30


def from_behind(block, axis, distance):
    devices = range(lax.axis_size(axis))
    route = [(i - distance, i) for i in devices if i - distance in devices]
    return lax.ppermute(block, axis, route)


def swapped(value, axis, apart):
    mask = 2**apart
    pairs = [(source, source ^ mask) for source in range(lax.axis_size(axis))]
    return lax.ppermute(value, axis, pairs)


def rms_forward(inputs):
    factor = lax.rsqrt(jnp.mean(inputs * inputs, axis=-1, keepdims=True) + EPSILON)
    return inputs * factor


def rms_backward(inputs, cotangent):
    factor = lax.rsqrt(jnp.mean(inputs * inputs, axis=-1, keepdims=True) + EPSILON)
    normed = inputs * factor
    return factor * (cotangent - normed * jnp.mean(cotangent * normed, axis=-1, keepdims=True))


def gelu_tanh(inputs):
    return jax.nn.gelu(inputs, approximate=True)


def gelu_backward(inputs, cotangent):
    return jax.vjp(gelu_tanh, inputs)[1](cotangent)[0]


def split_heads(array):
    return array.reshape(array.shape[:-1] + (HEADS, HEAD_DIM))


def merge_heads(array):
    return array.reshape(array.shape[:-2] + (HEADS * HEAD_DIM,))


def mixed_dot(form, left, right):
    return jnp.einsum(form, left, right, preferred_element_type=jnp.float32)


def project(rows, weight):
    return jnp.dot(rows, weight, preferred_element_type=jnp.float32).astype(jnp.bfloat16)


def gram(left, right):
    return jnp.einsum("zni,znj->ij", left, right, preferred_element_type=jnp.float32)


def back_project(kv_rows, w_key, w_value):
    width = w_key.shape[0]
    first = mixed_dot("znj,ij->zni", kv_rows[..., :width], w_key)
    return first + mixed_dot("znj,ij->zni", kv_rows[..., width:], w_value)


def attention_weights(queries, key_rows, key_mask, rim_keys, rim_mask):
    score_scale = HEAD_DIM ** (-0.5)
    head_queries = split_heads(queries)
    main_scores = mixed_dot("bnqhe,bnkhe->bnhqk", head_queries, split_heads(key_rows)) * score_scale
    rim_scores = mixed_dot("bnqhe,bnqshe->bnhqs", head_queries, split_heads(rim_keys)) * score_scale
    main_scores = jnp.where(key_mask[None, :, None], main_scores, NEG_FILL)
    rim_scores = jnp.where(rim_mask[None, :, None], rim_scores, NEG_FILL)
    largest = jnp.maximum(
        jnp.max(main_scores, axis=-1, keepdims=True), jnp.max(rim_scores, axis=-1, keepdims=True)
    )
    main_exp = jnp.exp(main_scores - largest)
    rim_exp = jnp.exp(rim_scores - largest)
    totals = jnp.sum(main_exp, axis=-1, keepdims=True) + jnp.sum(rim_exp, axis=-1, keepdims=True)
    return (main_exp / totals, rim_exp / totals)


def attend(queries, key_rows, value_rows, key_mask, rim_keys, rim_values, rim_mask):
    main_prob, rim_prob = attention_weights(queries, key_rows, key_mask, rim_keys, rim_mask)
    mixed = mixed_dot("bnhqk,bnkhe->bnqhe", main_prob.astype(jnp.bfloat16), split_heads(value_rows))
    mixed = mixed + mixed_dot(
        "bnhqs,bnqshe->bnqhe", rim_prob.astype(jnp.bfloat16), split_heads(rim_values)
    )
    return merge_heads(mixed).astype(jnp.bfloat16)


def attend_back(queries, key_rows, value_rows, key_mask, rim_keys, rim_values, rim_mask, out_grad):
    main_prob, rim_prob = attention_weights(queries, key_rows, key_mask, rim_keys, rim_mask)
    score_scale = HEAD_DIM ** (-0.5)
    upstream = split_heads(out_grad)
    head_queries = split_heads(queries)
    main_dot = mixed_dot("bnqhe,bnkhe->bnhqk", upstream, split_heads(value_rows))
    rim_dot = mixed_dot("bnqhe,bnqshe->bnhqs", upstream, split_heads(rim_values))
    inner = jnp.sum(main_prob * main_dot, axis=-1, keepdims=True) + jnp.sum(
        rim_prob * rim_dot, axis=-1, keepdims=True
    )
    main_grad = (main_prob * (main_dot - inner) * score_scale).astype(jnp.bfloat16)
    rim_grad = (rim_prob * (rim_dot - inner) * score_scale).astype(jnp.bfloat16)
    main_bf = main_prob.astype(jnp.bfloat16)
    rim_bf = rim_prob.astype(jnp.bfloat16)
    query_grad = mixed_dot("bnhqk,bnkhe->bnqhe", main_grad, split_heads(key_rows))
    query_grad = query_grad + mixed_dot("bnhqs,bnqshe->bnqhe", rim_grad, split_heads(rim_keys))
    key_grad = mixed_dot("bnhqk,bnqhe->bnkhe", main_grad, head_queries)
    value_grad = mixed_dot("bnhqk,bnqhe->bnkhe", main_bf, upstream)
    rim_key_grad = mixed_dot("bnhqs,bnqhe->bnqshe", rim_grad, head_queries)
    rim_value_grad = mixed_dot("bnhqs,bnqhe->bnqshe", rim_bf, upstream)
    return (
        merge_heads(query_grad),
        merge_heads(key_grad),
        merge_heads(value_grad),
        merge_heads(rim_key_grad),
        merge_heads(rim_value_grad),
    )


def partner_bit(matching, sx_bits, sy_bits):
    if matching == 0:
        return sx_bits - 1 + sy_bits
    if matching == 1:
        return sy_bits - 1
    return sx_bits - 2 + sy_bits


def shift_x(rows, step):
    return from_behind(rows, "sx", step)


def shift_y(rows, step):
    return from_behind(rows, "sy", step)


def shards(
    nodes,
    grad_out,
    w_query,
    w_key,
    w_value,
    w_out,
    w_up,
    w_down,
    counts,
    adjacency,
    expander,
    pairing,
    boundary,
):
    features_in = nodes[0, 0]
    batch_size, node_count, width = features_in.shape
    block_count = counts.shape[2]
    block_size = node_count // block_count
    node_slot = jnp.arange(node_count) % block_size
    usable = node_slot < jnp.repeat(counts[0, 0], block_size)
    usable_flag = usable.astype(jnp.bfloat16)
    usable_rows = usable.astype(jnp.float32)[None, :, None]
    features = features_in.astype(jnp.float32)
    normed_in = rms_forward(features).astype(jnp.bfloat16)
    queries = project(normed_in, w_query)
    key_rows = project(normed_in, w_key)
    value_rows = project(normed_in, w_value)
    joined = jnp.concatenate([key_rows, value_rows], axis=-1)
    pair_shape = (batch_size, block_count, block_size, 2 * width)
    identity = jnp.eye(block_size, dtype=bool)
    local_mask = (adjacency[0, 0] == 1) & usable.reshape(block_count, block_size)[
        :, None, :
    ] | identity
    key_parts = [joined.reshape(pair_shape)]
    mask_parts = [local_mask]
    selections = []
    far_inputs = []
    sx_bits = lax.axis_size("sx").bit_length() - 1
    sy_bits = lax.axis_size("sy").bit_length() - 1
    for matching in range(3):
        bit_index = partner_bit(matching, sx_bits, sy_bits)
        far_rows, far_flag = swapped((normed_in, usable_flag), ("sx", "sy"), bit_index)
        far_joined = jnp.concatenate(
            [project(far_rows, w_key), project(far_rows, w_value)], axis=-1
        )
        far_inputs.append(far_rows)
        select_map = (pairing[0, 0, matching][:, None] == jnp.arange(block_count)[None, :]).astype(
            jnp.bfloat16
        )
        picked = mixed_dot("bc,zcqe->zbqe", select_map, far_joined.reshape(pair_shape)).astype(
            jnp.bfloat16
        )
        far_usable = (
            mixed_dot("bc,cq->bq", select_map, far_flag.reshape(block_count, block_size)) > 0.5
        )
        key_parts.append(picked)
        mask_parts.append((expander[0, 0, matching] == 1) & far_usable[:, None, :])
        selections.append(select_map)
    all_joined = jnp.concatenate(key_parts, axis=2)
    all_keys = all_joined[..., :width]
    all_values = all_joined[..., width:]
    key_mask = jnp.concatenate(mask_parts, axis=2)
    places = [
        (boundary[0, 0, side][None, :] == jnp.arange(node_count)[:, None]).astype(jnp.bfloat16)
        for side in range(4)
    ]
    outgoing = [jnp.take(normed_in, boundary[0, 0, side], axis=1) for side in range(4)]
    arrived = [
        shift_x(outgoing[1], 1),
        shift_x(outgoing[0], -1),
        shift_y(outgoing[3], 1),
        shift_y(outgoing[2], -1),
    ]
    rim_parts = []
    for side in range(4):
        came_rows = jnp.concatenate(
            [project(arrived[side], w_key), project(arrived[side], w_value)], axis=-1
        )
        rim_parts.append(mixed_dot("nr,zre->zne", places[side], came_rows).astype(jnp.bfloat16))
    rim_joined = jnp.stack(rim_parts, axis=2).reshape(
        batch_size, block_count, block_size, 4, 2 * width
    )
    rim_keys = rim_joined[..., :width]
    rim_values = rim_joined[..., width:]
    sx_index = lax.axis_index("sx")
    sy_index = lax.axis_index("sy")
    exists = jnp.stack(
        [
            sx_index > 0,
            sx_index < lax.axis_size("sx") - 1,
            sy_index > 0,
            sy_index < lax.axis_size("sy") - 1,
        ]
    )
    placed = jnp.stack(
        [jnp.sum(places[side], axis=1, dtype=jnp.float32) > 0.5 for side in range(4)], axis=-1
    )
    rim_mask = (placed & exists[None, :]).reshape(block_count, block_size, 4)
    query_blocks = queries.reshape(batch_size, block_count, block_size, width)
    attended = attend(query_blocks, all_keys, all_values, key_mask, rim_keys, rim_values, rim_mask)
    attended = attended.reshape(batch_size, node_count, width)
    hidden_in = features + jnp.dot(attended, w_out, preferred_element_type=jnp.float32)
    normed_mid = rms_forward(hidden_in).astype(jnp.bfloat16)
    pre_act = jnp.dot(normed_mid, w_up, preferred_element_type=jnp.float32)
    activ = gelu_tanh(pre_act).astype(jnp.bfloat16)
    ffn_out = jnp.dot(activ, w_down, preferred_element_type=jnp.float32)
    layer_out = ((hidden_in + ffn_out) * usable_rows).astype(jnp.bfloat16)
    upstream = grad_out[0, 0].astype(jnp.float32) * usable_rows
    upstream_bf = upstream.astype(jnp.bfloat16)
    grad_down = gram(activ, upstream_bf)
    grad_act = mixed_dot("znj,ij->zni", upstream_bf, w_down)
    grad_pre = gelu_backward(pre_act, grad_act).astype(jnp.bfloat16)
    grad_up = gram(normed_mid, grad_pre)
    grad_mid = mixed_dot("znj,ij->zni", grad_pre, w_up)
    grad_hidden = upstream + rms_backward(hidden_in, grad_mid)
    grad_hidden_bf = grad_hidden.astype(jnp.bfloat16)
    grad_outw = gram(attended, grad_hidden_bf)
    grad_attended = mixed_dot("znj,ij->zni", grad_hidden_bf, w_out).astype(jnp.bfloat16)
    grad_attended = grad_attended.reshape(batch_size, block_count, block_size, width)
    query_grad, key_grad, value_grad, rim_key_grad, rim_value_grad = attend_back(
        query_blocks, all_keys, all_values, key_mask, rim_keys, rim_values, rim_mask, grad_attended
    )
    joined_grad = jnp.concatenate([key_grad, value_grad], axis=-1).astype(jnp.bfloat16)
    own_grad = joined_grad[:, :, :block_size].reshape(batch_size, node_count, 2 * width)
    kv_total = own_grad.astype(jnp.float32)
    node_back = back_project(own_grad, w_key, w_value)
    extra_key = jnp.zeros((width, width), jnp.float32)
    extra_value = jnp.zeros((width, width), jnp.float32)
    for matching in range(3):
        piece = joined_grad[:, :, (matching + 1) * block_size : (matching + 2) * block_size]
        back = mixed_dot("bc,zbqe->zcqe", selections[matching], piece).astype(jnp.bfloat16)
        back = back.reshape(batch_size, node_count, 2 * width)
        bit_index = partner_bit(matching, sx_bits, sy_bits)
        extra_key = extra_key + gram(far_inputs[matching], back[..., :width])
        extra_value = extra_value + gram(far_inputs[matching], back[..., width:])
        sent_back = back_project(back, w_key, w_value).astype(jnp.bfloat16)
        came_normed = swapped(sent_back, ("sx", "sy"), bit_index)
        node_back = node_back + came_normed.astype(jnp.float32)
    rim_grad = jnp.concatenate([rim_key_grad, rim_value_grad], axis=-1).astype(jnp.bfloat16)
    rim_grad = rim_grad.reshape(batch_size, node_count, 4, 2 * width)
    outgoing_grads = [
        jnp.take(rim_grad[:, :, side], boundary[0, 0, side], axis=1) for side in range(4)
    ]
    sent_rim = []
    for side in range(4):
        extra_key = extra_key + gram(arrived[side], outgoing_grads[side][..., :width])
        extra_value = extra_value + gram(arrived[side], outgoing_grads[side][..., width:])
        sent_rim.append(back_project(outgoing_grads[side], w_key, w_value).astype(jnp.bfloat16))
    returned = [
        shift_x(sent_rim[1], 1),
        shift_x(sent_rim[0], -1),
        shift_y(sent_rim[3], 1),
        shift_y(sent_rim[2], -1),
    ]
    for side in range(4):
        node_back = node_back + mixed_dot("nr,zre->zne", places[side], returned[side])
    query_total = query_grad.reshape(batch_size, node_count, width).astype(jnp.bfloat16)
    grad_query = gram(normed_in, query_total)
    grad_key = gram(normed_in, kv_total[..., :width]) + extra_key
    grad_value = gram(normed_in, kv_total[..., width:]) + extra_value
    grad_normed = mixed_dot("znj,ij->zni", query_total, w_query) + node_back
    grad_nodes = (grad_hidden + rms_backward(features, grad_normed)).astype(jnp.bfloat16)
    summed_grads = lax.psum(
        (grad_query, grad_key, grad_value, grad_outw, grad_up, grad_down), ("sx", "sy")
    )
    return (
        layer_out[None, None],
        grad_nodes[None, None],
        summed_grads[0],
        summed_grads[1],
        summed_grads[2],
        summed_grads[3],
        summed_grads[4],
        summed_grads[5],
    )


def solution(mesh):
    return jax.shard_map(
        shards,
        mesh=mesh,
        in_specs=(
            P("sx", "sy", None, None, None),
            P("sx", "sy", None, None, None),
            P(),
            P(),
            P(),
            P(),
            P(),
            P(),
            P("sx", "sy", None),
            P("sx", "sy", None, None, None),
            P("sx", "sy", None, None, None, None),
            P("sx", "sy", None, None),
            P("sx", "sy", None, None),
        ),
        out_specs=(
            P("sx", "sy", None, None, None),
            P("sx", "sy", None, None, None),
            P(),
            P(),
            P(),
            P(),
            P(),
            P(),
        ),
        check_vma=False,
    )
```

profile of v0, /device:TPU:0, one launch (start us, length us, event | category | flops | bytes accessed | tf_op | source)
XLA Modules:
  0.0 289.6 jit_solution(1161696865381776014)
XLA Ops:
  7.3 1.1 copy.216
  9.2 3.0 %collective-permute-start.2 = (bf16[1,256,256]{1,2,0:T(8,128)(2,1)}, bf16[1,256,256]{1,2,0:T(8,128)(2,1)S(1)}, u32[]{:S(2)}, u32[]{:S(2)}) collective-permute-start(bf16[1,256,256]{1,2,0:T(8,128)(2,1)} %fusion.67), channel_id=1, source_target_pairs={{0,8},{1,9},{2,10},{3,11},{4,12},{5,13},{6,14},{7,15},{8,0},{9,1},... | collective-permute-start | bytes 393224 | tf_op jit(solution)/shard_map/ppermute | solution.py:23
  12.2 1.5 collective-permute-start.1
  13.7 2.6 collective-permute-start
  16.3 1.3 fusion.255
  20.9 1.1 convolution_convert_fusion.20
  22.1 1.1 convolution_convert_fusion.21
  27.8 0.9 fusion.260
  30.8 1.3 collective-permute-start.9
  32.3 1.6 collective-permute-done.4
  33.9 2.9 %collective-permute-start.8 = (bf16[1,128,256]{2,1,0:T(8,128)(2,1)S(1)}, bf16[1,128,256]{2,1,0:T(8,128)(2,1)S(1)}, u32[]{:S(2)}, u32[]{:S(2)}) collective-permute-start(bf16[1,128,256]{2,1,0:T(8,128)(2,1)S(1)} %bitcast_select_fusion.5), channel_id=1, source_target_pairs={{0,1},{2,3},{4,5},{6,7},{8,9},{10,11},{12,13},{14,15},{16,17},{18,... | collective-permute-start | bytes 196616 | tf_op jit(solution)/shard_map/ppermute | solution.py:17
  37.2 1.3 collective-permute-start.7
  39.1 3.0 %collective-permute-start.6 = (bf16[1,128,256]{2,1,0:T(8,128)(2,1)S(1)}, bf16[1,128,256]{2,1,0:T(8,128)(2,1)S(1)}, u32[]{:S(2)}, u32[]{:S(2)}) collective-permute-start(bf16[1,128,256]{2,1,0:T(8,128)(2,1)S(1)} %bitcast_select_fusion.7), channel_id=1, source_target_pairs={{0,2},{2,4},{4,6},{6,8},{8,10},{10,12},{12,14},{14,16},{16,18},{18... | collective-permute-start | bytes 196616 | tf_op jit(solution)/shard_map/ppermute | solution.py:17
  49.8 2.9 %pad_maximum_fusion = bf16[1,2,512,512]{3,1,2,0:T(2,128)(2,1)S(1)} fusion(bf16[1,2,128,512]{3,1,2,0:T(2,128)(2,1)S(1)} %fusion.5, bf16[1,2,128,512]{3,1,2,0:T(2,128)(2,1)S(1)} %fusion.4, bf16[1,2,128,512]{3,1,2,0:T(2,128)(2,1)S(1)} %fusion.3, bf16[1,2,128,256]{3,1,2,0:T(2,128)(2,1)S(1)} %copy.218, bf16[1,2,128,256]{3,1,2,0:T(2,128)(2,1)S(1)} %copy.217), kind=kLoop, calls=%fused_computation.121 | loop fusion | flops 5242880 | bytes 2097152 | tf_op jit(solution)/shard_map/concatenate | solution.py:200
  53.4 1.4 copy.228
  55.6 1.0 fusion
  56.6 1.4 fusion.2
  59.0 1.6 fusion.25
  61.9 1.1 fusion.34
  65.4 3.7 %multiply_reduce_fusion = (f32[2,8,128]{2,1,0:T(8,128)S(1)}, f32[2,8,128,512]{3,2,1,0:T(8,128)S(1)}) fusion(f32[2,8,128]{2,1,0:T(8,128)S(1)} %copy_add_fusion.1, f32[2,8,128]{2,1,0:T(8,128)S(1)} %copy_maximum_fusion, f32[2,8,128,512]{3,2,1,0:T(8,128)} %copy-done.1, pred[2,128,512]{2,1,0:T(8,128)(4,1)S(1)} %pad_add_fusion, ...), kind=kOutput, calls=%fused_computation.9 | convolution fusion | flops 73398272 | bytes 9199616 | tf_op jit(solution)/shard_map/bnqhe,bnkhe->bnhqk/dot_general | solution.py:54
  69.9 2.2 convolution_convert_fusion
  73.0 2.4 multiply_convert_fusion
  75.5 2.0 copy.255
  77.5 2.1 convolution_convert_fusion.1
  79.6 2.0 copy.254
  81.6 2.2 fusion.8
  83.8 2.2 fusion.7
  86.3 1.8 fusion.6
  88.1 0.9 fusion.146
  89.0 0.9 fusion.145
  89.9 0.9 fusion.147
  90.8 0.9 fusion.107
  91.7 1.0 fusion.212
  92.7 1.2 fusion.161
  93.9 1.7 copy.268
  95.6 1.4 convert_bitcast_fusion.4
  97.0 1.2 multiply_reduce_fusion.1
  99.2 1.5 fusion.61
  101.3 1.5 fusion.60
  103.5 1.1 gather_fusion.7
  105.7 1.4 collective-permute-start.16
  107.1 1.0 gather_fusion.6
  109.3 5.8 %collective-permute-start.15 = (bf16[1,128,256]{2,1,0:T(8,128)(2,1)}, bf16[1,128,256]{2,1,0:T(8,128)(2,1)}, u32[]{:S(2)}, u32[]{:S(2)}) collective-permute-start(bf16[1,128,256]{2,1,0:T(8,128)(2,1)} %fusion.48), channel_id=1, source_target_pairs={{0,1},{2,3},{4,5},{6,7},{8,9},{10,11},{12,13},{14,15},{16,17},{18,... | collective-permute-start | bytes 196616 | tf_op jit(solution)/shard_map/ppermute | solution.py:17
  115.0 1.1 gather_fusion.5
  117.2 1.3 collective-permute-start.14
  118.5 1.1 gather_fusion.4
  120.8 4.1 %collective-permute-start.13 = (bf16[1,128,256]{2,1,0:T(8,128)(2,1)}, bf16[1,128,256]{2,1,0:T(8,128)(2,1)}, u32[]{:S(2)}, u32[]{:S(2)}) collective-permute-start(bf16[1,128,256]{2,1,0:T(8,128)(2,1)} %fusion.50), channel_id=1, source_target_pairs={{0,2},{2,4},{4,6},{6,8},{8,10},{10,12},{12,14},{14,16},{16,18},{18... | collective-permute-start | bytes 196616 | tf_op jit(solution)/shard_map/ppermute | solution.py:17
  125.4 3.3 %collective-permute-start.12 = (bf16[1,256,256]{1,2,0:T(8,128)(2,1)S(1)}, bf16[1,256,256]{1,2,0:T(8,128)(2,1)S(1)}, u32[]{:S(2)}, u32[]{:S(2)}) collective-permute-start(bf16[1,256,256]{1,2,0:T(8,128)(2,1)S(1)} %fusion.31), channel_id=1, source_target_pairs={{0,8},{1,9},{2,10},{3,11},{4,12},{5,13},{6,14},{7,15},{8,0},{9,1},... | collective-permute-start | bytes 393224 | tf_op jit(solution)/shard_map/ppermute | solution.py:23
  130.0 0.9 fusion.104
  133.5 0.9 fusion.24
  134.4 0.9 fusion.21
  135.7 1.0 convolution_bitcast_fusion.4
  136.8 2.7 collective-permute-start.10
  139.4 1.0 convolution_bitcast_fusion.5
  140.5 1.0 convolution_bitcast_fusion.6
  141.6 6.0 %collective-permute-done.10 = bf16[1,256,256]{1,2,0:T(8,128)(2,1)S(1)} collective-permute-done((bf16[1,256,256]{1,2,0:T(8,128)(2,1)S(1)}, bf16[1,256,256]{1,2,0:T(8,128)(2,1)S(1)}, u32[]{:S(2)}, u32[]{:S(2)}) %collective-permute-start.10) | collective-permute-done | bytes 131104 | tf_op jit(solution)/shard_map/ppermute | solution.py:23
  147.6 1.1 fusion.71
  149.5 122.8 %all-reduce.3.cloned.1.call-done = (f32[256,256]{1,0:T(8,128)}, f32[256,256]{1,0:T(8,128)}, f32[256,256]{1,0:T(8,128)}, f32[256,256]{1,0:T(8,128)}, f32[256,512]{1,0:T(8,128)}, /*index=5*/f32[512,256]{1,0:T(8,128)}) async-done(((f32[256,256]{1,0:T(8,128)}, f32[256,256]{1,0:T(8,128)}, f32[256,256]{1,0:T(8,128)}, f32[256,256]{1,0:T(8,128)}, f32[256,512]{1,0:T(8,128)}, /*index=5*/f32[512,256]{1,0:T(8,128)}), ...) | async-done | bytes 2097168 | tf_op jit(solution)/shard_map/psum | solution.py:304
  272.4 1.7 copy.375
  274.0 1.7 copy.376
  275.7 1.7 copy.377
  277.4 1.7 copy.378
  279.0 1.9 copy.379
  280.9 1.9 copy.380
  (345 shorter events, 38.4 us)
Async XLA Ops:
  7.2 54.5 %copy-start = (bf16[256,512]{1,0:T(8,128)(2,1)S(1)}, bf16[256,512]{1,0:T(8,128)(2,1)}, u32[]{:S(2)}) copy-start(bf16[256,512]{1,0:T(8,128)(2,1)} %param.23) | copy-start | bytes 786436
  7.2 20.2 %copy-start.40 = (bf16[256,256]{1,0:T(8,128)(2,1)S(1)}, bf16[256,256]{1,0:T(8,128)(2,1)}, u32[]{:S(2)}) copy-start(bf16[256,256]{1,0:T(8,128)(2,1)} %param.19) | copy-start | bytes 393220
  7.2 22.2 %copy-start.50 = (s32[1,1,2,128,128]{4,3,2,1,0:T(8,128)S(1)}, s32[1,1,2,128,128]{4,3,2,1,0:T(8,128)}, u32[]{:S(2)}) copy-start(s32[1,1,2,128,128]{4,3,2,1,0:T(8,128)} %param.26) | copy-start | bytes 393220
  7.2 22.4 %copy-start.54 = (s32[1,1,3,2]{2,3,1,0:T(2,128)S(1)}, s32[1,1,3,2]{2,3,1,0:T(2,128)}, u32[]{:S(2)}) copy-start(s32[1,1,3,2]{2,3,1,0:T(2,128)} %param.28) | copy-start | bytes 76
  7.2 23.0 %copy-start.51 = (bf16[1,1,1,256,256]{4,3,2,1,0:T(8,128)(2,1)S(1)}, bf16[1,1,1,256,256]{4,3,2,1,0:T(8,128)(2,1)}, u32[]{:S(2)}) copy-start(bf16[1,1,1,256,256]{4,3,2,1,0:T(8,128)(2,1)} %param.18) | copy-start | bytes 393220
  7.2 29.8 %copy-start.45 = (s32[1,1,3,2,128,128]{5,4,3,2,1,0:T(8,128)S(1)}, s32[1,1,3,2,128,128]{5,4,3,2,1,0:T(8,128)}, u32[]{:S(2)}) copy-start(s32[1,1,3,2,128,128]{5,4,3,2,1,0:T(8,128)} %param.27) | copy-start | bytes 1179652
  7.2 265.1 %all-reduce.3.cloned.1.call-start = ((), (), s32[]{:S(2)}) async-start(), calls=%async_computation | async-start | bytes 4194304 | tf_op jit(solution)/shard_map/psum | solution.py:304
  8.5 30.0 %copy-start.3 = (bf16[256,256]{1,0:T(8,128)(2,1)S(1)}, bf16[256,256]{1,0:T(8,128)(2,1)}, u32[]{:S(2)}) copy-start(bf16[256,256]{1,0:T(8,128)(2,1)} %param.21) | copy-start | bytes 393220
  9.2 36.8 %collective-permute-start.2 = (bf16[1,256,256]{1,2,0:T(8,128)(2,1)}, bf16[1,256,256]{1,2,0:T(8,128)(2,1)S(1)}, u32[]{:S(2)}, u32[]{:S(2)}) collective-permute-start(bf16[1,256,256]{1,2,0:T(8,128)(2,1)} %fusion.67), channel_id=1, source_target_pairs={{0,8},{1,9},{2,10},{3,11},{4,12},{5,13},{6,14},{7,15},{8,0},{9,1},... | collective-permute-start | bytes 393224 | tf_op jit(solution)/shard_map/ppermute | solution.py:23
  12.2 34.5 %collective-permute-start.1 = (bf16[1,256,256]{1,2,0:T(8,128)(2,1)}, bf16[1,256,256]{1,2,0:T(8,128)(2,1)S(1)}, u32[]{:S(2)}, u32[]{:S(2)}) collective-permute-start(bf16[1,256,256]{1,2,0:T(8,128)(2,1)} %fusion.67), channel_id=1, source_target_pairs={{0,1},{1,0},{2,3},{3,2},{4,5},{5,4},{6,7},{7,6},{8,9},{9,8},{10,11... | collective-permute-start | bytes 393224 | tf_op jit(solution)/shard_map/ppermute | solution.py:23
  13.7 33.7 %collective-permute-start = (bf16[1,256,256]{1,2,0:T(8,128)(2,1)}, bf16[1,256,256]{1,2,0:T(8,128)(2,1)S(1)}, u32[]{:S(2)}, u32[]{:S(2)}) collective-permute-start(bf16[1,256,256]{1,2,0:T(8,128)(2,1)} %fusion.67), channel_id=1, source_target_pairs={{0,16},{1,17},{2,18},{3,19},{4,20},{5,21},{6,22},{7,23},{8,24},{9,... | collective-permute-start | bytes 393224 | tf_op jit(solution)/shard_map/ppermute | solution.py:23
  17.6 21.1 %copy-start.4 = (bf16[256,256]{1,0:T(8,128)(2,1)S(1)}, bf16[256,256]{1,0:T(8,128)(2,1)}, u32[]{:S(2)}) copy-start(bf16[256,256]{1,0:T(8,128)(2,1)} %param.20) | copy-start | bytes 393220
  17.6 12.7 %collective-permute-start.3 = (bf16[256]{0:T(256)(128)(2,1)S(1)}, bf16[256]{0:T(256)(128)(2,1)S(1)}, u32[]{:S(2)}, u32[]{:S(2)}) collective-permute-start(bf16[256]{0:T(256)(128)(2,1)S(1)} %convert_element_type.505), channel_id=1, source_target_pairs={{0,16},{1,17},{2,18},{3,19},{4,20},{5,21},{6,22},{7,23},{8,24},{9,... | collective-permute-start | bytes 1544 | tf_op jit(solution)/shard_map/ppermute | solution.py:23
  18.0 12.8 %collective-permute-start.5 = (bf16[256]{0:T(256)(128)(2,1)S(1)}, bf16[256]{0:T(256)(128)(2,1)S(1)}, u32[]{:S(2)}, u32[]{:S(2)}) collective-permute-start(bf16[256]{0:T(256)(128)(2,1)S(1)} %convert_element_type.505), channel_id=1, source_target_pairs={{0,8},{1,9},{2,10},{3,11},{4,12},{5,13},{6,14},{7,15},{8,0},{9,1},... | collective-permute-start | bytes 1544 | tf_op jit(solution)/shard_map/ppermute | solution.py:23
  19.3 9.9 %copy-start.71 = (pred[128]{0:T(512)(128)(4,1)}, pred[128]{0:T(512)(128)(4,1)S(1)}, u32[]{:S(2)}) copy-start(pred[128]{0:T(512)(128)(4,1)S(1)} %get-tuple-element.92) | copy-start | bytes 388
  19.3 10.8 %copy-start.67 = (pred[128]{0:T(512)(128)(4,1)}, pred[128]{0:T(512)(128)(4,1)S(1)}, u32[]{:S(2)}) copy-start(pred[128]{0:T(512)(128)(4,1)S(1)} %get-tuple-element.65) | copy-start | bytes 388
  19.3 10.8 %copy-start.69 = (pred[128]{0:T(512)(128)(4,1)}, pred[128]{0:T(512)(128)(4,1)S(1)}, u32[]{:S(2)}) copy-start(pred[128]{0:T(512)(128)(4,1)S(1)} %get-tuple-element.96) | copy-start | bytes 388
  19.3 10.8 %copy-start.73 = (pred[128]{0:T(512)(128)(4,1)}, pred[128]{0:T(512)(128)(4,1)S(1)}, u32[]{:S(2)}) copy-start(pred[128]{0:T(512)(128)(4,1)S(1)} %get-tuple-element.94) | copy-start | bytes 388
  20.2 18.7 %copy-start.61 = (s32[128]{0:T(128)}, s32[128]{0:T(128)S(1)}, u32[]{:S(2)}) copy-start(s32[128]{0:T(128)S(1)} %get-tuple-element.90) | copy-start | bytes 1540
  20.2 22.3 %copy-start.59 = (s32[128]{0:T(128)}, s32[128]{0:T(128)S(1)}, u32[]{:S(2)}) copy-start(s32[128]{0:T(128)S(1)} %get-tuple-element.91) | copy-start | bytes 1540
  20.2 22.9 %copy-start.57 = (s32[128]{0:T(128)}, s32[128]{0:T(128)S(1)}, u32[]{:S(2)}) copy-start(s32[128]{0:T(128)S(1)} %get-tuple-element.89) | copy-start | bytes 1540
  20.2 24.0 %copy-start.55 = (s32[128]{0:T(128)}, s32[128]{0:T(128)S(1)}, u32[]{:S(2)}) copy-start(s32[128]{0:T(128)S(1)} %get-tuple-element.88) | copy-start | bytes 1540
  27.8 27.8 %copy-start.20 = (bf16[2,128,8,32]{1,0,3,2:T(2,128)(2,1)}, bf16[2,128,8,32]{1,0,3,2:T(2,128)(2,1)S(1)}, u32[]{:S(2)}) copy-start(bf16[2,128,8,32]{1,0,3,2:T(2,128)(2,1)S(1)} %reshape.1139) | copy-start | bytes 393220
  29.8 7.0 %copy-start.80 = (s32[2]{0:T(128)}, s32[2]{0:T(128)S(1)}, u32[]{:S(2)}) copy-start(s32[2]{0:T(128)S(1)} %get-tuple-element.51) | copy-start | bytes 28
  29.8 18.9 %copy-start.78 = (s32[2]{0:T(128)}, s32[2]{0:T(128)S(1)}, u32[]{:S(2)}) copy-start(s32[2]{0:T(128)S(1)} %get-tuple-element.52) | copy-start | bytes 28
  29.8 19.4 %copy-start.77 = (s32[2]{0:T(128)}, s32[2]{0:T(128)S(1)}, u32[]{:S(2)}) copy-start(s32[2]{0:T(128)S(1)} %get-tuple-element.50) | copy-start | bytes 28
  30.3 33.9 %copy-start.43 = (bf16[1,1,1,256,256]{3,4,2,1,0:T(8,128)(2,1)}, bf16[1,1,1,256,256]{3,4,2,1,0:T(8,128)(2,1)S(1)}, u32[]{:S(2)}) copy-start(bf16[1,1,1,256,256]{3,4,2,1,0:T(8,128)(2,1)S(1)} %copy.246) | copy-start | bytes 393220
  30.3 3.6 %collective-permute-start.4 = (bf16[256]{0:T(256)(128)(2,1)S(1)}, bf16[256]{0:T(256)(128)(2,1)S(1)}, u32[]{:S(2)}, u32[]{:S(2)}) collective-permute-start(bf16[256]{0:T(256)(128)(2,1)S(1)} %convert_element_type.505), channel_id=1, source_target_pairs={{0,1},{1,0},{2,3},{3,2},{4,5},{5,4},{6,7},{7,6},{8,9},{9,8},{10,11... | collective-permute-start | bytes 1544 | tf_op jit(solution)/shard_map/ppermute | solution.py:23
  30.8 6.4 %collective-permute-start.9 = (bf16[1,128,256]{2,1,0:T(8,128)(2,1)S(1)}, bf16[1,128,256]{2,1,0:T(8,128)(2,1)S(1)}, u32[]{:S(2)}, u32[]{:S(2)}) collective-permute-start(bf16[1,128,256]{2,1,0:T(8,128)(2,1)S(1)} %bitcast_select_fusion.4), channel_id=1, source_target_pairs={{1,0},{3,2},{5,4},{7,6},{9,8},{11,10},{13,12},{15,14},{17,16},{19,... | collective-permute-start | bytes 196616 | tf_op jit(solution)/shard_map/ppermute | solution.py:17
  33.9 5.2 %collective-permute-start.8 = (bf16[1,128,256]{2,1,0:T(8,128)(2,1)S(1)}, bf16[1,128,256]{2,1,0:T(8,128)(2,1)S(1)}, u32[]{:S(2)}, u32[]{:S(2)}) collective-permute-start(bf16[1,128,256]{2,1,0:T(8,128)(2,1)S(1)} %bitcast_select_fusion.5), channel_id=1, source_target_pairs={{0,1},{2,3},{4,5},{6,7},{8,9},{10,11},{12,13},{14,15},{16,17},{18,... | collective-permute-start | bytes 196616 | tf_op jit(solution)/shard_map/ppermute | solution.py:17
  37.2 32.8 %copy-start.11 = (pred[2,128,512]{2,1,0:T(8,128)(4,1)}, pred[2,128,512]{2,1,0:T(8,128)(4,1)S(1)}, u32[]{:S(2)}) copy-start(pred[2,128,512]{2,1,0:T(8,128)(4,1)S(1)} %pad_add_fusion) | copy-start | bytes 393220
  37.2 5.5 %collective-permute-start.7 = (bf16[1,128,256]{2,1,0:T(8,128)(2,1)S(1)}, bf16[1,128,256]{2,1,0:T(8,128)(2,1)S(1)}, u32[]{:S(2)}, u32[]{:S(2)}) collective-permute-start(bf16[1,128,256]{2,1,0:T(8,128)(2,1)S(1)} %bitcast_select_fusion.6), channel_id=1, source_target_pairs={{2,0},{4,2},{6,4},{8,6},{10,8},{12,10},{14,12},{16,14},{18,16},{20... | collective-permute-start | bytes 196616 | tf_op jit(solution)/shard_map/ppermute | solution.py:17
  39.1 4.7 %collective-permute-start.6 = (bf16[1,128,256]{2,1,0:T(8,128)(2,1)S(1)}, bf16[1,128,256]{2,1,0:T(8,128)(2,1)S(1)}, u32[]{:S(2)}, u32[]{:S(2)}) collective-permute-start(bf16[1,128,256]{2,1,0:T(8,128)(2,1)S(1)} %bitcast_select_fusion.7), channel_id=1, source_target_pairs={{0,2},{2,4},{4,6},{6,8},{8,10},{10,12},{12,14},{14,16},{16,18},{18... | collective-permute-start | bytes 196616 | tf_op jit(solution)/shard_map/ppermute | solution.py:17
  58.1 11.8 %copy-start.52 = (f32[2,8,128]{2,1,0:T(8,128)}, f32[2,8,128]{2,1,0:T(8,128)S(1)}, u32[]{:S(2)}) copy-start(f32[2,8,128]{2,1,0:T(8,128)S(1)} %copy_add_fusion.1) | copy-start | bytes 24580
  58.8 13.6 %copy-start.42 = (f32[2,8,128,4]{2,0,1,3:T(2,128)}, f32[2,8,128,4]{2,0,1,3:T(2,128)S(1)}, u32[]{:S(2)}) copy-start(f32[2,8,128,4]{2,0,1,3:T(2,128)S(1)} %get-tuple-element.60) | copy-start | bytes 98308
  75.5 8.3 %copy-start.79 = (s32[2]{0:T(128)S(1)}, s32[2]{0:T(128)}, u32[]{:S(2)}) copy-start(s32[2]{0:T(128)} %copy-done.78) | copy-start | bytes 28
  83.8 7.0 %copy-start.7 = (f32[256,256]{0,1:T(8,128)S(1)}, f32[256,256]{0,1:T(8,128)}, u32[]{:S(2)}) copy-start(f32[256,256]{0,1:T(8,128)} %copy-done.6) | copy-start | bytes 786436
  83.8 7.0 %copy-start.22 = (bf16[1,2,128,8,32]{2,1,4,3,0:T(2,128)(2,1)S(1)}, bf16[1,2,128,8,32]{2,1,4,3,0:T(2,128)(2,1)}, u32[]{:S(2)}) copy-start(bf16[1,2,128,8,32]{2,1,4,3,0:T(2,128)(2,1)} %copy-done.21) | copy-start | bytes 393220
  83.8 7.9 %copy-start.27 = (bf16[256,512]{1,0:T(8,128)(2,1)S(1)}, bf16[256,512]{1,0:T(8,128)(2,1)}, u32[]{:S(2)}) copy-start(bf16[256,512]{1,0:T(8,128)(2,1)} %copy-done.26) | copy-start | bytes 786436
  86.2 9.3 %copy-start.53 = (f32[2,8,128]{2,0,1:T(2,128)S(1)}, f32[2,8,128]{2,0,1:T(2,128)}, u32[]{:S(2)}) copy-start(f32[2,8,128]{2,0,1:T(2,128)} %copy.250) | copy-start | bytes 24580
  101.3 6.8 %copy-start.72 = (pred[128]{0:T(512)(128)(4,1)S(1)}, pred[128]{0:T(512)(128)(4,1)}, u32[]{:S(2)}) copy-start(pred[128]{0:T(512)(128)(4,1)} %copy-done.71) | copy-start | bytes 388
  103.1 13.0 %copy-start.70 = (pred[128]{0:T(512)(128)(4,1)S(1)}, pred[128]{0:T(512)(128)(4,1)}, u32[]{:S(2)}) copy-start(pred[128]{0:T(512)(128)(4,1)} %copy-done.69) | copy-start | bytes 388
  103.4 16.2 %copy-start.68 = (pred[128]{0:T(512)(128)(4,1)S(1)}, pred[128]{0:T(512)(128)(4,1)}, u32[]{:S(2)}) copy-start(pred[128]{0:T(512)(128)(4,1)} %copy-done.67) | copy-start | bytes 388
  103.4 21.5 %copy-start.49 = (bf16[1,2,128,512]{3,1,2,0:T(2,128)(2,1)S(1)}, bf16[1,2,128,512]{3,1,2,0:T(2,128)(2,1)}, u32[]{:S(2)}) copy-start(bf16[1,2,128,512]{3,1,2,0:T(2,128)(2,1)} %fusion.8) | copy-start | bytes 786436
  105.7 23.0 %copy-start.48 = (bf16[1,2,128,512]{3,1,2,0:T(2,128)(2,1)S(1)}, bf16[1,2,128,512]{3,1,2,0:T(2,128)(2,1)}, u32[]{:S(2)}) copy-start(bf16[1,2,128,512]{3,1,2,0:T(2,128)(2,1)} %fusion.7) | copy-start | bytes 786436
  105.7 35.8 %collective-permute-start.16 = (bf16[1,128,256]{2,1,0:T(8,128)(2,1)}, bf16[1,128,256]{2,1,0:T(8,128)(2,1)}, u32[]{:S(2)}, u32[]{:S(2)}) collective-permute-start(bf16[1,128,256]{2,1,0:T(8,128)(2,1)} %fusion.47), channel_id=1, source_target_pairs={{1,0},{3,2},{5,4},{7,6},{9,8},{11,10},{13,12},{15,14},{17,16},{19,... | collective-permute-start | bytes 196616 | tf_op jit(solution)/shard_map/ppermute | solution.py:17
  108.2 21.0 %copy-start.10 = (bf16[1,2,128,512]{3,2,1,0:T(8,128)(2,1)S(1)}, bf16[1,2,128,512]{3,2,1,0:T(8,128)(2,1)}, u32[]{:S(2)}) copy-start(bf16[1,2,128,512]{3,2,1,0:T(8,128)(2,1)} %copy-done.9) | copy-start | bytes 786436
  108.2 21.0 %copy-start.25 = (f32[256,256]{0,1:T(8,128)S(1)}, f32[256,256]{0,1:T(8,128)}, u32[]{:S(2)}) copy-start(f32[256,256]{0,1:T(8,128)} %fusion.146) | copy-start | bytes 786436
  109.3 26.4 %collective-permute-start.15 = (bf16[1,128,256]{2,1,0:T(8,128)(2,1)}, bf16[1,128,256]{2,1,0:T(8,128)(2,1)}, u32[]{:S(2)}, u32[]{:S(2)}) collective-permute-start(bf16[1,128,256]{2,1,0:T(8,128)(2,1)} %fusion.48), channel_id=1, source_target_pairs={{0,1},{2,3},{4,5},{6,7},{8,9},{10,11},{12,13},{14,15},{16,17},{18,... | collective-permute-start | bytes 196616 | tf_op jit(solution)/shard_map/ppermute | solution.py:17
  115.0 14.5 %copy-start.47 = (bf16[1,2,128,512]{3,1,2,0:T(2,128)(2,1)S(1)}, bf16[1,2,128,512]{3,1,2,0:T(2,128)(2,1)}, u32[]{:S(2)}) copy-start(bf16[1,2,128,512]{3,1,2,0:T(2,128)(2,1)} %fusion.6) | copy-start | bytes 786436
  117.2 19.5 %collective-permute-start.14 = (bf16[1,128,256]{2,1,0:T(8,128)(2,1)}, bf16[1,128,256]{2,1,0:T(8,128)(2,1)}, u32[]{:S(2)}, u32[]{:S(2)}) collective-permute-start(bf16[1,128,256]{2,1,0:T(8,128)(2,1)} %fusion.49), channel_id=1, source_target_pairs={{2,0},{4,2},{6,4},{8,6},{10,8},{12,10},{14,12},{16,14},{18,16},{20... | collective-permute-start | bytes 196616 | tf_op jit(solution)/shard_map/ppermute | solution.py:17
  118.5 12.4 %copy-start.29 = (bf16[1,128,256]{2,1,0:T(8,128)(2,1)S(1)}, bf16[1,128,256]{2,1,0:T(8,128)(2,1)}, u32[]{:S(2)}) copy-start(bf16[1,128,256]{2,1,0:T(8,128)(2,1)} %copy-done.28) | copy-start | bytes 196612
  119.7 11.5 %copy-start.31 = (bf16[1,128,256]{2,1,0:T(8,128)(2,1)S(1)}, bf16[1,128,256]{2,1,0:T(8,128)(2,1)}, u32[]{:S(2)}) copy-start(bf16[1,128,256]{2,1,0:T(8,128)(2,1)} %copy-done.30) | copy-start | bytes 196612
  119.7 11.7 %copy-start.33 = (bf16[1,128,256]{2,1,0:T(8,128)(2,1)S(1)}, bf16[1,128,256]{2,1,0:T(8,128)(2,1)}, u32[]{:S(2)}) copy-start(bf16[1,128,256]{2,1,0:T(8,128)(2,1)} %copy-done.32) | copy-start | bytes 196612
  119.8 11.8 %copy-start.35 = (bf16[1,128,256]{2,1,0:T(8,128)(2,1)S(1)}, bf16[1,128,256]{2,1,0:T(8,128)(2,1)}, u32[]{:S(2)}) copy-start(bf16[1,128,256]{2,1,0:T(8,128)(2,1)} %copy-done.34) | copy-start | bytes 196612
  120.0 11.8 %copy-start.17 = (bf16[1,256,256]{1,2,0:T(8,128)(2,1)S(1)}, bf16[1,256,256]{1,2,0:T(8,128)(2,1)}, u32[]{:S(2)}) copy-start(bf16[1,256,256]{1,2,0:T(8,128)(2,1)} %copy-done.16) | copy-start | bytes 393220
  120.8 11.2 %copy-start.19 = (bf16[1,256,256]{1,2,0:T(8,128)(2,1)S(1)}, bf16[1,256,256]{1,2,0:T(8,128)(2,1)}, u32[]{:S(2)}) copy-start(bf16[1,256,256]{1,2,0:T(8,128)(2,1)} %copy-done.18) | copy-start | bytes 393220
  120.8 19.7 %collective-permute-start.13 = (bf16[1,128,256]{2,1,0:T(8,128)(2,1)}, bf16[1,128,256]{2,1,0:T(8,128)(2,1)}, u32[]{:S(2)}, u32[]{:S(2)}) collective-permute-start(bf16[1,128,256]{2,1,0:T(8,128)(2,1)} %fusion.50), channel_id=1, source_target_pairs={{0,2},{2,4},{4,6},{6,8},{8,10},{10,12},{12,14},{14,16},{16,18},{18... | collective-permute-start | bytes 196616 | tf_op jit(solution)/shard_map/ppermute | solution.py:17
  125.4 16.2 %collective-permute-start.12 = (bf16[1,256,256]{1,2,0:T(8,128)(2,1)S(1)}, bf16[1,256,256]{1,2,0:T(8,128)(2,1)S(1)}, u32[]{:S(2)}, u32[]{:S(2)}) collective-permute-start(bf16[1,256,256]{1,2,0:T(8,128)(2,1)S(1)} %fusion.31), channel_id=1, source_target_pairs={{0,8},{1,9},{2,10},{3,11},{4,12},{5,13},{6,14},{7,15},{8,0},{9,1},... | collective-permute-start | bytes 393224 | tf_op jit(solution)/shard_map/ppermute | solution.py:23
  133.3 7.2 %copy-start.56 = (s32[128]{0:T(128)S(1)}, s32[128]{0:T(128)}, u32[]{:S(2)}) copy-start(s32[128]{0:T(128)} %copy-done.55) | copy-start | bytes 1540
  134.4 13.1 %copy-start.62 = (s32[128]{0:T(128)S(1)}, s32[128]{0:T(128)}, u32[]{:S(2)}) copy-start(s32[128]{0:T(128)} %copy-done.61) | copy-start | bytes 1540
  134.4 14.3 %copy-start.8 = (f32[256,256]{0,1:T(8,128)S(1)}, f32[256,256]{0,1:T(8,128)}, u32[]{:S(2)}) copy-start(f32[256,256]{0,1:T(8,128)} %copy-done.6) | copy-start | bytes 786436
  135.6 6.0 %collective-permute-start.11 = (bf16[1,256,256]{1,2,0:T(8,128)(2,1)S(1)}, bf16[1,256,256]{1,2,0:T(8,128)(2,1)S(1)}, u32[]{:S(2)}, u32[]{:S(2)}) collective-permute-start(bf16[1,256,256]{1,2,0:T(8,128)(2,1)S(1)} %fusion.32), channel_id=1, source_target_pairs={{0,1},{1,0},{2,3},{3,2},{4,5},{5,4},{6,7},{7,6},{8,9},{9,8},{10,11... | collective-permute-start | bytes 393224 | tf_op jit(solution)/shard_map/ppermute | solution.py:23
  136.8 10.8 %collective-permute-start.10 = (bf16[1,256,256]{1,2,0:T(8,128)(2,1)S(1)}, bf16[1,256,256]{1,2,0:T(8,128)(2,1)S(1)}, u32[]{:S(2)}, u32[]{:S(2)}) collective-permute-start(bf16[1,256,256]{1,2,0:T(8,128)(2,1)S(1)} %fusion.33), channel_id=1, source_target_pairs={{0,16},{1,17},{2,18},{3,19},{4,20},{5,21},{6,22},{7,23},{8,24},{9,... | collective-permute-start | bytes 393224 | tf_op jit(solution)/shard_map/ppermute | solution.py:23
  (38 other events, 124.4 us)
Sparse Core Ops, SparseCore 0:
  135.5 136.8 all-reduce.2
where the time goes:
time: 291 us; the launch traced here: 290 us
  waiting for transfers between devices  131 us (45%)
  matrix products  49.1 us (17%)
  local copies, waits for them, and re-layouts  37.5 us (13%)
  starting transfers between devices  35.4 us (12%)
  other arithmetic  21 us (7%)
  between operations  16.2 us (6%)
    psum x1, waiting for transfers between devices, shards(): lax.psum((grad_query, grad_key, grad_value, grad_outw, grad_up, grad_down...  123 us
    dot_general x43, matrix products, mixed_dot(): return jnp.einsum(form, left, right, preferred_element_type=jnp.float32)  32.3 us
    ppermute x8, starting transfers between devices, from_behind(): return lax.ppermute(block, axis, route)  21.1 us
    unnamed x182, local copies, waits for them, and re-layouts  17.6 us
    ppermute x9, starting transfers between devices, swapped(): return lax.ppermute(value, axis, pairs)  14.3 us
    dot_general x20, matrix products, gram(): jnp.einsum('zni,znj->ij', left, right, preferred_element_type=jnp.float32)  10.1 us
    ppermute x9, waiting for transfers between devices, swapped(): return lax.ppermute(value, axis, pairs)  7.62 us
  transfers between devices with their start and end apart: 18, of which 3 were waited for; matrix products, arithmetic and copies ran while one was open for 12% of the time, Pallas kernels for 0%

commit v1 on v0

v1 whole, which is shorter than its diff:
```python
import math

import jax
import jax.numpy as jnp
from jax import lax
from jax.experimental import pallas as pl
from jax.experimental.pallas import tpu as pltpu
from jax.sharding import PartitionSpec as P

HEADS = 8
HEAD_DIM = 32
EPSILON = 1e-06
NEG_FILL = -1e30
AXES = ("sx", "sy")
EXTRA = 16
MATCHINGS = 3
SIDES = 4
F32 = jnp.float32
BF16 = jnp.bfloat16
GELU_C = math.sqrt(2.0 / math.pi)
GELU_A = 0.044715


def nn(a, b):
    return lax.dot_general(a, b, (((1,), (0,)), ((), ())), preferred_element_type=F32)


def nt(a, b):
    return lax.dot_general(a, b, (((1,), (1,)), ((), ())), preferred_element_type=F32)


def tn(a, b):
    return lax.dot_general(a, b, (((0,), (0,)), ((), ())), preferred_element_type=F32)


def iota(shape, dim):
    return lax.broadcasted_iota(jnp.int32, shape, dim)


def to_bf(mask):
    return jnp.where(mask, 1.0, 0.0).astype(BF16)


def flip(value):
    return jnp.transpose(value.astype(F32), (1, 0))


def from_behind(block, axis, distance):
    devices = range(lax.axis_size(axis))
    return lax.ppermute(block, axis, [(i - distance, i) for i in devices if i - distance in devices])


def xor_permute(value, mask):
    count = lax.axis_size("sx") * lax.axis_size("sy")
    return lax.ppermute(value, AXES, [(i, i ^ mask) for i in range(count)])


def call(kernel, outs, args, smem=0, scratch=(), limit=48, flops=0, nbytes=0):
    specs = [pl.BlockSpec(memory_space=pltpu.SMEM)] * smem
    specs += [pl.BlockSpec(memory_space=pltpu.VMEM)] * (len(args) - smem)
    return pl.pallas_call(
        kernel,
        out_shape=[jax.ShapeDtypeStruct(s, d) for s, d in outs],
        in_specs=specs,
        out_specs=[pl.BlockSpec(memory_space=pltpu.VMEM)] * len(outs),
        scratch_shapes=list(scratch),
        compiler_params=pltpu.CompilerParams(vmem_limit_bytes=limit * 2**20),
        cost_estimate=pl.CostEstimate(flops=flops, bytes_accessed=nbytes, transcendentals=0),
    )(*args)


def prepare_kernel(counts, nodes, boundary, pack, *rims):
    count, width = nodes.shape
    blocks = counts.shape[0]
    size = count // blocks
    feats = nodes[...].astype(F32)
    normed = (feats * lax.rsqrt(jnp.mean(feats * feats, axis=1, keepdims=True) + EPSILON)).astype(BF16)
    pack[0:count, :] = normed
    lane = iota((EXTRA, count), 1)
    row = iota((EXTRA, count), 0)
    limit = jnp.zeros((EXTRA, count), jnp.int32)
    for b in range(blocks):
        limit = jnp.where(lane // size == b, counts[b], limit)
    extra = jnp.where((row == 0) & (lane % size < limit), 1.0, 0.0)
    rim = boundary.shape[1]
    slots = boundary[...].astype(F32)
    for side in range(SIDES):
        line = slots[side : side + 1, :]
        if count > rim:
            line = jnp.concatenate([line, jnp.zeros((1, count - rim), F32)], axis=1)
        extra = jnp.where(row == side + 1, line, extra)
    pack[count : count + EXTRA, :] = extra.astype(BF16)
    for side, out in enumerate(rims):
        place = to_bf(iota((count, rim), 0) == boundary[side : side + 1, :])
        out[...] = tn(place, normed).astype(BF16)


def head_rows(width, shape, dim):
    return iota(shape, dim) // HEAD_DIM


def main_kernel(merge_y, info, counts, pairing, nodes, gout, wq, wk, wv, wo, wup, wdown, adjacency, expander, boundary, *refs):
    packs = refs[: MATCHINGS + 1]
    rims = refs[MATCHINGS + 1 : MATCHINGS + 1 + (2 if merge_y else 4)]
    refs = refs[MATCHINGS + 1 + len(rims) :]
    layer_out, grad_hidden_out, grad_normed_out = refs[:3]
    backs = refs[3 : 3 + MATCHINGS]
    rim_outs = refs[3 + MATCHINGS : 3 + MATCHINGS + len(rims)]
    refs = refs[3 + MATCHINGS + len(rims) :]
    keep, send = refs[:2]
    grads, xcat, kvg, probs, pbf, sgrad, qstack, gstack = refs[2:]

    count, width = nodes.shape
    hidden_units = wup.shape[1]
    blocks = counts.shape[0]
    size = count // blocks
    keys = (MATCHINGS + 1) * size
    rim = boundary.shape[1]
    scale = HEAD_DIM**-0.5
    log2e = math.log2(math.e)

    normed = packs[0][0:count, :]
    feats = nodes[...].astype(F32)
    for b in range(blocks):
        xcat[b * keys : b * keys + size, :] = packs[0][b * size : (b + 1) * size, :]
        for m in range(MATCHINGS):
            start = pl.multiple_of(pairing[m, b] * size, size)
            lo = b * keys + (m + 1) * size
            xcat[lo : lo + size, :] = packs[m + 1][pl.ds(start, size), :]
    base = blocks * keys
    places, moves = [], [None, None, None, None]
    for s in range(SIDES):
        here = (iota((count, rim), 0) == boundary[s : s + 1, :]) & (info[s] > 0)
        places.append(to_bf(here))
    for s in range(SIDES):
        if merge_y and s >= 2:
            other = 3 if s == 2 else 2
            far_slots = packs[2][count : count + EXTRA, :].astype(F32)[other + 1 : other + 2, 0:rim]
            spots = to_bf(iota((count, rim), 0).astype(F32) == far_slots)
            moves[s] = nt(places[s], spots).astype(BF16)
            rows = nn(moves[s], packs[2][0:count, :])
        else:
            rows = nn(places[s], rims[s][...])
        xcat[base + s * count : base + (s + 1) * count, :] = rows.astype(BF16)

    queries = nn(normed, wq[...]).astype(BF16)
    queries_t = flip(queries).astype(BF16)
    wk_t = flip(wk[...]).astype(BF16)
    wv_t = flip(wv[...]).astype(BF16)
    key_rows, key_cols, value_rows, value_cols = [], [], [], []
    for b in range(blocks):
        rows = xcat[b * keys : (b + 1) * keys, :]
        key_rows.append(nn(rows, wk[...]).astype(BF16))
        value_rows.append(nn(rows, wv[...]).astype(BF16))
        key_cols.append(nt(wk_t, rows).astype(BF16))
        value_cols.append(nt(wv_t, rows).astype(BF16))
    rim_keys, rim_values = [], []
    for s in range(SIDES):
        rows = xcat[base + s * count : base + (s + 1) * count, :]
        rim_keys.append(nn(rows, wk[...]).astype(BF16).astype(F32))
        rim_values.append(nn(rows, wv[...]).astype(BF16).astype(F32))

    bias = []
    eye = iota((size, size), 0) == iota((size, size), 1)
    for b in range(blocks):
        parts = []
        for g in range(MATCHINGS + 1):
            flags = packs[g][count : count + EXTRA, :].astype(F32)[0:1, :]
            if g == 0:
                real = flags[:, b * size : (b + 1) * size] > 0.5
                mask = ((adjacency[b] == 1) & real) | eye
            else:
                pick = flags[:, 0:size]
                for c in range(1, blocks):
                    pick = jnp.where(pairing[g - 1, b] == c, flags[:, c * size : (c + 1) * size], pick)
                mask = (expander[g - 1, b] == 1) & (pick > 0.5)
            parts.append(flip(jnp.where(mask, 0.0, NEG_FILL)))
        bias.append(jnp.concatenate(parts, axis=0))

    spread = to_bf(head_rows(width, (HEADS, width), 1) == iota((HEADS, width), 0))

    def head_sums(product):
        high = product.astype(BF16)
        low = (product - high.astype(F32)).astype(BF16)
        return nt(spread, high) + nt(spread, low)

    queries_f = queries.astype(F32)
    ones = jnp.ones((HEADS, rim), BF16)
    rim_scores = []
    for s in range(SIDES):
        there = nt(ones, places[s]) > 0.5
        score = head_sums(queries_f * rim_keys[s]) * (scale * log2e)
        rim_scores.append(jnp.where(there, score, NEG_FILL))
    rim_top = jnp.maximum(jnp.maximum(rim_scores[0], rim_scores[1]), jnp.maximum(rim_scores[2], rim_scores[3]))

    row_head = head_rows(width, (width, size), 0)
    tops, sums = [], []
    att_blocks = []
    for b in range(blocks):
        cols = slice(b * size, (b + 1) * size)
        top_rows, inv_rows, att_rows = [], [], []
        for h in range(HEADS):
            own = queries_t[:, cols]
            masked = jnp.where(row_head == h, own, jnp.zeros_like(own))
            score = nn(key_rows[b], masked) * (scale * log2e) + bias[b]
            top = jnp.maximum(jnp.max(score, axis=0, keepdims=True), rim_top[h : h + 1, cols])
            grown = jnp.exp2(score - top)
            total = jnp.sum(grown, axis=0, keepdims=True)
            for s in range(SIDES):
                total = total + jnp.exp2(rim_scores[s][h : h + 1, cols] - top)
            inverse = 1.0 / total
            prob = grown * inverse
            at = slice(h * size, (h + 1) * size)
            probs[b, :, at] = prob
            prob_bf = prob.astype(BF16)
            pbf[b, :, at] = prob_bf
            att_rows.append(nn(value_cols[b][h * HEAD_DIM : (h + 1) * HEAD_DIM, :], prob_bf))
            top_rows.append(top)
            inv_rows.append(inverse)
        tops.append(jnp.concatenate(top_rows, axis=0))
        sums.append(jnp.concatenate(inv_rows, axis=0))
        att_blocks.append(jnp.concatenate(att_rows, axis=0))
    top_all = jnp.concatenate(tops, axis=1)
    inv_all = jnp.concatenate(sums, axis=1)
    mixed = flip(jnp.concatenate(att_blocks, axis=1))
    rim_probs = [jnp.exp2(rim_scores[s] - top_all) * inv_all for s in range(SIDES)]
    rim_wide = [tn(rim_probs[s].astype(BF16), spread) for s in range(SIDES)]
    for s in range(SIDES):
        mixed = mixed + rim_wide[s] * rim_values[s]
    attended = mixed.astype(BF16)

    slot = iota((count, width), 0)
    limit = jnp.zeros((count, width), jnp.int32)
    for b in range(blocks):
        limit = jnp.where(slot // size == b, counts[b], limit)
    usable = jnp.where(slot % size < limit, 1.0, 0.0)
    hidden = feats + nn(attended, wo[...])
    factor = lax.rsqrt(jnp.mean(hidden * hidden, axis=1, keepdims=True) + EPSILON)
    mid = hidden * factor
    normed_mid = mid.astype(BF16)
    pre = nn(normed_mid, wup[...])
    square = pre * pre
    bent = jnp.tanh(GELU_C * pre * (1.0 + GELU_A * square))
    half = 0.5 * (1.0 + bent)
    activ = (pre * half).astype(BF16)
    layer_out[...] = ((hidden + nn(activ, wdown[...])) * usable).astype(BF16)
    upstream = gout[...].astype(F32) * usable
    upstream_bf = upstream.astype(BF16)
    grads[4 * width + hidden_units * 1 : 4 * width + 2 * hidden_units, :] = tn(activ, upstream_bf)
    slope = half + 0.5 * pre * (1.0 - bent * bent) * (GELU_C * (1.0 + 3.0 * GELU_A * square))
    grad_pre = (slope * nt(upstream_bf, wdown[...])).astype(BF16)
    grad_up = tn(normed_mid, grad_pre)
    for part in range(hidden_units // width):
        lo = 4 * width + part * width
        grads[lo : lo + width, :] = grad_up[:, part * width : (part + 1) * width]
    grad_mid = nt(grad_pre, wup[...])
    grad_hidden = upstream + factor * (grad_mid - mid * jnp.mean(grad_mid * mid, axis=1, keepdims=True))
    grad_hidden_out[...] = grad_hidden
    grad_hidden_bf = grad_hidden.astype(BF16)
    grads[3 * width : 4 * width, :] = tn(attended, grad_hidden_bf)
    grad_att = nt(grad_hidden_bf, wo[...]).astype(BF16)
    grad_att_f = grad_att.astype(F32)
    grad_att_t = flip(grad_att).astype(BF16)

    lane_head = head_rows(width, (size, width), 1)
    rim_dots = [head_sums(grad_att_f * rim_values[s]) for s in range(SIDES)]
    rim_inner = rim_probs[0] * rim_dots[0]
    for s in range(1, SIDES):
        rim_inner = rim_inner + rim_probs[s] * rim_dots[s]
    inner_blocks, query_blocks = [], []
    for b in range(blocks):
        cols = slice(b * size, (b + 1) * size)
        inner_rows, query_rows = [], []
        for h in range(HEADS):
            own = grad_att_t[:, cols]
            masked = jnp.where(row_head == h, own, jnp.zeros_like(own))
            dots = nn(value_rows[b], masked)
            at = slice(h * size, (h + 1) * size)
            prob = probs[b, :, at]
            inner = jnp.sum(prob * dots, axis=0, keepdims=True) + rim_inner[h : h + 1, cols]
            graded = (prob * (dots - inner) * scale).astype(BF16)
            sgrad[b, :, at] = graded
            query_rows.append(nn(key_cols[b][h * HEAD_DIM : (h + 1) * HEAD_DIM, :], graded))
            inner_rows.append(inner)
            mine = queries[cols, :]
            qstack[at, :] = jnp.where(lane_head == h, mine, jnp.zeros_like(mine))
            mine = grad_att[cols, :]
            gstack[at, :] = jnp.where(lane_head == h, mine, jnp.zeros_like(mine))
        inner_blocks.append(jnp.concatenate(inner_rows, axis=0))
        query_blocks.append(jnp.concatenate(query_rows, axis=0))
        span = slice(b * keys, (b + 1) * keys)
        kvg[span, 0:width] = nn(sgrad[b], qstack[...]).astype(BF16)
        kvg[span, width : 2 * width] = nn(pbf[b], gstack[...]).astype(BF16)
    inner_all = jnp.concatenate(inner_blocks, axis=1)
    query_grad = flip(jnp.concatenate(query_blocks, axis=1))
    for s in range(SIDES):
        graded = (rim_probs[s] * (rim_dots[s] - inner_all) * scale).astype(BF16)
        wide = tn(graded, spread)
        query_grad = query_grad + wide * rim_keys[s]
        span = slice(base + s * count, base + (s + 1) * count)
        kvg[span, 0:width] = (wide * queries_f).astype(BF16)
        kvg[span, width : 2 * width] = (rim_wide[s] * grad_att_f).astype(BF16)
    query_total = query_grad.astype(BF16)

    own_rows = []
    extra_back = None
    for s in range(SIDES):
        span = slice(base + s * count, base + (s + 1) * count)
        back = (nn(kvg[span, 0:width], wk_t) + nn(kvg[span, width : 2 * width], wv_t)).astype(BF16)
        if merge_y and s >= 2:
            moved = tn(moves[s], back)
            extra_back = moved if extra_back is None else extra_back + moved
        else:
            rim_outs[s][...] = tn(places[s], back).astype(BF16)
    if merge_y:
        grads[0:count, :] = extra_back
    for b in range(blocks):
        span = slice(b * keys, (b + 1) * keys)
        back = nn(kvg[span, 0:width], wk_t) + nn(kvg[span, width : 2 * width], wv_t)
        own_rows.append(back[0:size])
        for m in range(MATCHINGS):
            start = pl.multiple_of(pairing[m, b] * size, size)
            piece = back[(m + 1) * size : (m + 2) * size]
            if merge_y and m == 1:
                piece = piece + grads[pl.ds(start, size), :]
            backs[m][pl.ds(start, size), :] = piece.astype(BF16)
    grad_normed_out[...] = nt(query_total, wq[...]) + jnp.concatenate(own_rows, axis=0)

    grads[0:width, :] = tn(normed, query_total)
    both = tn(xcat[...], kvg[...])
    grads[width : 2 * width, :] = both[:, 0:width]
    grads[2 * width : 3 * width, :] = both[:, width : 2 * width]

    half_rows = grads.shape[0] // 2
    mine = info[SIDES]
    keep[...] = grads[pl.ds(pl.multiple_of(mine * half_rows, half_rows), half_rows), :]
    send[...] = grads[pl.ds(pl.multiple_of((1 - mine) * half_rows, half_rows), half_rows), :].astype(BF16)


def nodes_kernel(merge_y, nodes, grad_hidden, grad_normed, boundary, *refs):
    out = refs[-1]
    backs, rims = refs[:MATCHINGS], refs[MATCHINGS:-1]
    count = nodes.shape[0]
    rim = boundary.shape[1]
    cot = grad_normed[...]
    for back in backs:
        cot = cot + back[...].astype(F32)
    for s, rows in enumerate(rims):
        place = to_bf(iota((count, rim), 0) == boundary[s : s + 1, :])
        cot = cot + nn(place, rows[...])
    feats = nodes[...].astype(F32)
    factor = lax.rsqrt(jnp.mean(feats * feats, axis=1, keepdims=True) + EPSILON)
    normed = feats * factor
    out[...] = (grad_hidden[...] + factor * (cot - normed * jnp.mean(cot * normed, axis=1, keepdims=True))).astype(BF16)


def reduce_kernel(place, parts, kept_rows, *refs):
    info, kept = refs[0], refs[1]
    received = refs[2 : 2 + kept_rows]
    outs = refs[2 + kept_rows : -1]
    total_ref = refs[-1]
    total = kept[...].astype(F32)
    for piece in received:
        total = total + piece[...].astype(F32)
    if parts == 1:
        outs[0][...] = total.astype(BF16)
        return
    total_ref[...] = total
    rows = total.shape[0] // parts
    mine = info[place]
    outs[0][...] = total_ref[pl.ds(pl.multiple_of(mine * rows, rows), rows), :]
    for d in range(1, parts):
        outs[d][...] = total_ref[pl.ds(pl.multiple_of((mine ^ d) * rows, rows), rows), :].astype(BF16)


def gather_kernel(place, *refs):
    info, pieces, out = refs[0], refs[1:-1], refs[-1]
    mine = info[place]
    rows = pieces[0].shape[0]
    for d, piece in enumerate(pieces):
        out[pl.ds(pl.multiple_of((mine ^ d) * rows, rows), rows), :] = piece[...]


def final_kernel(place, info, own, other, *refs):
    outs, full = refs[:-1], refs[-1]
    rows = own.shape[0]
    mine = info[place]
    full[pl.ds(pl.multiple_of(mine * rows, rows), rows), :] = own[...]
    full[pl.ds(pl.multiple_of((1 - mine) * rows, rows), rows), :] = other[...]
    width = full.shape[1]
    row = 0
    for out in outs:
        for part in range(out.shape[1] // width):
            out[:, part * width : (part + 1) * width] = full[row : row + out.shape[0], :].astype(F32)
            row += out.shape[0]


def bit_of(mask_bits, index):
    value = jnp.int32(0)
    for k, bit in enumerate(mask_bits):
        value = value | (((index >> bit) & 1) << k)
    return value


def offset_mask(bits, d):
    return sum(1 << bit for k, bit in enumerate(bits) if d >> k & 1)


def all_sum(info, keep, arrived, groups, core_mask):
    width = keep.shape[1]
    kept, pieces = keep, [arrived]
    for level, bits in enumerate(groups):
        parts = 2 ** len(bits)
        rows = kept.shape[0] // parts
        outs = [((rows, width), F32)] + [((rows, width), BF16)] * (parts - 1)
        made = call(
            lambda *r, level=level, parts=parts, n=len(pieces): reduce_kernel(SIDES + 1 + level, parts, n, *r),
            outs,
            [info, kept, *pieces],
            smem=1,
            scratch=[pltpu.VMEM(kept.shape, F32)],
        )
        kept = made[0]
        pieces = [xor_permute(made[d], offset_mask(bits, d)) for d in range(1, parts)]
    whole = call(
        lambda *r, n=len(pieces): reduce_kernel(0, 1, n, *r),
        [(kept.shape, BF16)],
        [info, kept, *pieces],
        smem=1,
        scratch=[pltpu.VMEM((8, 128), F32)],
    )[0]
    for level in reversed(range(len(groups))):
        bits = groups[level]
        parts = 2 ** len(bits)
        pieces = [whole] + [xor_permute(whole, offset_mask(bits, d)) for d in range(1, parts)]
        whole = call(
            lambda *r, level=level: gather_kernel(SIDES + 1 + level, *r),
            [((whole.shape[0] * parts, width), BF16)],
            [info, *pieces],
            smem=1,
        )[0]
    return whole, xor_permute(whole, core_mask)


def shards(nodes, grad_out, w_query, w_key, w_value, w_out, w_up, w_down, counts, adjacency, expander, pairing, boundary):
    batch, count, width = nodes.shape[2:]
    feats, gout = nodes.reshape(count, width), grad_out.reshape(count, width)
    counts, boundary, pairing = counts[0, 0], boundary[0, 0], pairing[0, 0]
    adjacency, expander = adjacency[0, 0], expander[0, 0]
    rim = boundary.shape[1]
    size_x, size_y = lax.axis_size("sx"), lax.axis_size("sy")
    bits_x, bits_y = size_x.bit_length() - 1, size_y.bit_length() - 1
    merge_y = size_y == 2
    partner = [1 << (bits_x - 1 + bits_y), 1 << (bits_y - 1), 1 << (bits_x - 2 + bits_y)]
    core_bit = bits_y
    rest = [bit for bit in range(bits_x + bits_y) if bit != core_bit]
    groups = [rest[i : i + 2] for i in range(0, len(rest), 2)]
    ix, iy = lax.axis_index("sx"), lax.axis_index("sy")
    index = ix * size_y + iy
    info = jnp.stack(
        [ix > 0, ix < size_x - 1, iy > 0, iy < size_y - 1]
        + [bit_of([core_bit], index)]
        + [bit_of(bits, index) for bits in groups]
    ).astype(jnp.int32)

    rim_count = 2 if merge_y else 4
    prepared = call(
        prepare_kernel,
        [((count + EXTRA, width), BF16)] + [((rim, width), BF16)] * rim_count,
        [counts, feats, boundary],
        smem=1,
    )
    pack, sent = prepared[0], prepared[1:]
    far = [xor_permute(pack, mask) for mask in partner]
    arrived = [from_behind(sent[1], "sx", 1), from_behind(sent[0], "sx", -1)]
    if not merge_y:
        arrived += [from_behind(sent[3], "sy", 1), from_behind(sent[2], "sy", -1)]

    blocks = counts.shape[0]
    size = count // blocks
    keys = (MATCHINGS + 1) * size
    units = w_up.shape[1]
    total_rows = 4 * width + 2 * units
    all_rows = blocks * keys + SIDES * count
    square = (count, width)
    made = call(
        lambda *r: main_kernel(merge_y, *r),
        [(square, BF16), (square, F32), (square, F32)]
        + [(square, BF16)] * MATCHINGS
        + [((rim, width), BF16)] * rim_count
        + [((total_rows // 2, width), F32), ((total_rows // 2, width), BF16)],
        [info, counts, pairing, feats, gout, w_query, w_key, w_value, w_out, w_up, w_down, adjacency, expander, boundary, pack, *far, *arrived],
        smem=3,
        scratch=[
            pltpu.VMEM((total_rows, width), F32),
            pltpu.VMEM((all_rows, width), BF16),
            pltpu.VMEM((all_rows, 2 * width), BF16),
            pltpu.VMEM((blocks, keys, HEADS * size), F32),
            pltpu.VMEM((blocks, keys, HEADS * size), BF16),
            pltpu.VMEM((blocks, keys, HEADS * size), BF16),
            pltpu.VMEM((HEADS * size, width), BF16),
            pltpu.VMEM((HEADS * size, width), BF16),
        ],
        flops=10**10,
        nbytes=8 * 2**20,
    )
    layer_out, grad_hidden, grad_normed = made[:3]
    backs = made[3 : 3 + MATCHINGS]
    rim_back = made[3 + MATCHINGS : 3 + MATCHINGS + rim_count]
    keep, send = made[-2:]

    core_mask = 1 << core_bit
    own, other = all_sum(info, keep, xor_permute(send, core_mask), groups, core_mask)
    returned = [xor_permute(back, mask) for back, mask in zip(backs, partner)]
    rims = [from_behind(rim_back[1], "sx", 1), from_behind(rim_back[0], "sx", -1)]
    if not merge_y:
        rims += [from_behind(rim_back[3], "sy", 1), from_behind(rim_back[2], "sy", -1)]
    grad_nodes = call(
        lambda *r: nodes_kernel(merge_y, *r),
        [(square, BF16)],
        [feats, grad_hidden, grad_normed, boundary, *returned, *rims],
    )[0]
    weights = call(
        lambda *r: final_kernel(SIDES, *r),
        [((width, width), F32)] * 4 + [((width, units), F32), ((units, width), F32)],
        [info, own, other],
        smem=1,
        scratch=[pltpu.VMEM((total_rows, width), BF16)],
    )
    return (layer_out.reshape(nodes.shape), grad_nodes.reshape(nodes.shape), *weights)


def solution(mesh):
    grid = lambda n: P("sx", "sy", *([None] * n))
    return jax.shard_map(
        shards,
        mesh=mesh,
        in_specs=(grid(3), grid(3), P(), P(), P(), P(), P(), P(), grid(1), grid(3), grid(4), grid(2), grid(2)),
        out_specs=(grid(3), grid(3), P(), P(), P(), P(), P(), P()),
        check_vma=False,
    )
```

time: 291 us -> 103 us (0.35)
  waiting for transfers between devices: 131 us -> 27.6 us
  matrix products: 49.1 us -> 0 us
  Pallas kernels: 0 us -> 27.7 us
  local copies, waits for them, and re-layouts: 37.5 us -> 10.7 us
  other arithmetic: 21 us -> 0 us
  between operations: 16.2 us -> 0.82 us
    psum x1 -> x0, waiting for transfers between devices: 123 us -> none  [shards(): lax.psum((grad_query, grad_key, grad_value, grad_outw, grad_up, grad_down...]
    dot_general x83 -> x0, matrix products: 49.1 us -> none  [the longest x43 32.3 us: mixed_dot(): return jnp.einsum(form, left, right, preferred_element_type=jnp.float32)]
    pallas_call x0 -> x9, Pallas kernels: none -> 27.7 us  [call(): pl.pallas_call(kernel, out_shape=[jax.ShapeDtypeStruct(s, d) for s, d in...]
    ppermute x17 -> x24, waiting for transfers between devices: 7.65 us -> 27.6 us  [the longest x20 23.1 us: xor_permute(): return lax.ppermute(value, AXES, [(i, i ^ mask) for i in range(count)])]
    gather x8 -> x0, local copies, waits for them, and re-layouts: 7.66 us -> none  [the longest x4 4.27 us: shards(): jnp.take(rim_grad[:, :, side], boundary[0, 0, side], axis=1)]
    unnamed x182 -> x28, local copies, waits for them, and re-layouts: 17.6 us -> 10.6 us
    concatenate x14 -> x0, local copies, waits for them, and re-layouts: 6.16 us -> none  [the longest x2 3.99 us: shards(): jnp.concatenate([key_grad, value_grad], axis=-1).astype(jnp.bfloat16)]
    convert_element_type x4 -> x0, other arithmetic: 4.43 us -> none  [the longest x1 2.43 us: attend_back(): (main_prob * (main_dot - inner) * score_scale).astype(jnp.bfloat16)]
  transfers between devices with their start and end apart: 18 -> 24, of which waited for: 3 -> 15; matrix products, arithmetic and copies ran while one was open for 12% -> 0% of each run, Pallas kernels for 0% -> 1%
where the time goes in v1:
time: 103 us
  starting transfers between devices  35.8 us (35%)
  Pallas kernels  27.7 us (27%)
  waiting for transfers between devices  27.6 us (27%)
  local copies, waits for them, and re-layouts  10.7 us (10%)
    ppermute x20, starting transfers between devices, xor_permute(): return lax.ppermute(value, AXES, [(i, i ^ mask) for i in range(count)])  29.5 us
    pallas_call x9, Pallas kernels, call(): pl.pallas_call(kernel, out_shape=[jax.ShapeDtypeStruct(s, d) for s, d in...  27.7 us
    ppermute x20, waiting for transfers between devices, xor_permute(): return lax.ppermute(value, AXES, [(i, i ^ mask) for i in range(count)])  23.1 us
    unnamed x28, local copies, waits for them, and re-layouts  10.6 us
    ppermute x4, starting transfers between devices, from_behind(): lax.ppermute(block, axis, [(i - distance, i) for i in devices if i - dist...  6.25 us
    ppermute x4, waiting for transfers between devices, from_behind(): lax.ppermute(block, axis, [(i - distance, i) for i in devices if i - dist...  4.54 us
  transfers between devices with their start and end apart: 24, of which 15 were waited for; matrix products, arithmetic and copies ran while one was open for 0% of the time, Pallas kernels for 1%

profile of v1, /device:TPU:0, one launch (start us, length us, event | category | flops | bytes accessed | tf_op | source)
XLA Modules:
  0.0 102.6 jit_solution(118330109507940466)
XLA Ops:
  0.7 0.7 copy-done.2
  1.3 0.9 copy-done
  2.2 0.8 shard_map.188
  3.1 3.1 %collective-permute-start.2 = (bf16[272,256]{1,0:T(8,128)(2,1)S(1)}, bf16[272,256]{1,0:T(8,128)(2,1)S(1)}, u32[]{:S(2)}, u32[]{:S(2)}) collective-permute-start(bf16[272,256]{1,0:T(8,128)(2,1)S(1)} %get-tuple-element.35.r_14_), channel_id=1, source_target_pairs={{0,8},{1,9},{2,10},{3,11},{4,12},{5,13},{6,14},{7,15},{8,0},{9,1},... | collective-permute-start | bytes 417800 | tf_op jit(solution)/shard_map/ppermute | solution.py:55
  6.1 1.5 %collective-permute-start.1 = (bf16[272,256]{1,0:T(8,128)(2,1)S(1)}, bf16[272,256]{1,0:T(8,128)(2,1)S(1)}, u32[]{:S(2)}, u32[]{:S(2)}) collective-permute-start(bf16[272,256]{1,0:T(8,128)(2,1)S(1)} %get-tuple-element.35.r_14_), channel_id=1, source_target_pairs={{0,1},{1,0},{2,3},{3,2},{4,5},{5,4},{6,7},{7,6},{8,9},{9,8},{10,11... | collective-permute-start | bytes 417800 | tf_op jit(solution)/shard_map/ppermute | solution.py:55
  7.7 2.6 %collective-permute-start = (bf16[272,256]{1,0:T(8,128)(2,1)S(1)}, bf16[272,256]{1,0:T(8,128)(2,1)S(1)}, u32[]{:S(2)}, u32[]{:S(2)}) collective-permute-start(bf16[272,256]{1,0:T(8,128)(2,1)S(1)} %get-tuple-element.35.r_14_), channel_id=1, source_target_pairs={{0,16},{1,17},{2,18},{3,19},{4,20},{5,21},{6,22},{7,23},{8,24},{9,... | collective-permute-start | bytes 417800 | tf_op jit(solution)/shard_map/ppermute | solution.py:55
  10.3 1.3 %collective-permute-start.3 = (bf16[128,256]{1,0:T(8,128)(2,1)S(1)}, bf16[128,256]{1,0:T(8,128)(2,1)S(1)}, u32[]{:S(2)}, u32[]{:S(2)}) collective-permute-start(bf16[128,256]{1,0:T(8,128)(2,1)S(1)} %get-tuple-element.36), channel_id=1, source_target_pairs={{0,2},{2,4},{4,6},{6,8},{8,10},{10,12},{12,14},{14,16},{16,18},{18... | collective-permute-start | bytes 196616 | tf_op jit(solution)/shard_map/ppermute | solution.py:50
  11.5 1.3 %collective-permute-start.4 = (bf16[128,256]{1,0:T(8,128)(2,1)S(1)}, bf16[128,256]{1,0:T(8,128)(2,1)S(1)}, u32[]{:S(2)}, u32[]{:S(2)}) collective-permute-start(bf16[128,256]{1,0:T(8,128)(2,1)S(1)} %get-tuple-element.37), channel_id=1, source_target_pairs={{2,0},{4,2},{6,4},{8,6},{10,8},{12,10},{14,12},{16,14},{18,16},{20... | collective-permute-start | bytes 196616 | tf_op jit(solution)/shard_map/ppermute | solution.py:50
  12.9 0.0 copy-start.13
  12.9 0.7 copy-done.13
  13.6 0.1 copy.21.r_2_
  13.6 0.1 stack.47.r_0_
  13.7 0.0 collective-permute-done.3.r_18_
  13.7 2.7 %collective-permute-done.4.r_19_ = bf16[128,256]{1,0:T(8,128)(2,1)S(1)} collective-permute-done((bf16[128,256]{1,0:T(8,128)(2,1)S(1)}, bf16[128,256]{1,0:T(8,128)(2,1)S(1)}, u32[]{:S(2)}, u32[]{:S(2)}) %collective-permute-start.4) | collective-permute-done | bytes 65568 | tf_op jit(solution)/shard_map/ppermute | solution.py:50
  16.4 0.0 copy-start.4
  16.5 1.0 copy-done.4
  17.4 0.9 copy-done.5
  18.4 0.9 copy-done.6
  19.3 0.9 copy-done.7
  20.2 0.9 copy-done.8
  21.2 0.9 copy-done.9
  22.1 0.9 copy-done.10
  23.0 0.9 copy-done.11
  23.9 0.9 copy-done.12
  24.8 20.9 %shard_map.189 = (bf16[256,256]{1,0:T(8,128)(2,1)}, f32[256,256]{1,0:T(8,128)S(1)}, f32[256,256]{1,0:T(8,128)S(1)}, bf16[256,256]{1,0:T(8,128)(2,1)S(1)}, bf16[2...) custom-call(s32[7]{0:T(128)S(1)} %stack.47.r_0_, ...), custom_call_target="tpu_custom_call" | custom-call | flops 10000000000 | bytes 8388608 | tf_op jit(solution)/shard_map/pallas_call | solution.py:61
  45.7 2.9 %collective-permute-start.10 = (bf16[1024,256]{1,0:T(8,128)(2,1)S(1)}, bf16[1024,256]{1,0:T(8,128)(2,1)S(1)}, u32[]{:S(2)}, u32[]{:S(2)}) collective-permute-start(bf16[1024,256]{1,0:T(8,128)(2,1)S(1)} %get-tuple-element.47), channel_id=1, source_target_pairs={{0,2},{1,3},{2,0},{3,1},{4,6},{5,7},{6,4},{7,5},{8,10},{9,11},{10,... | collective-permute-start | bytes 1572872 | tf_op jit(solution)/shard_map/ppermute | solution.py:55
  48.6 1.5 %collective-permute-done.10.r_2_ = bf16[1024,256]{1,0:T(8,128)(2,1)S(1)} collective-permute-done((bf16[1024,256]{1,0:T(8,128)(2,1)S(1)}, bf16[1024,256]{1,0:T(8,128)(2,1)S(1)}, u32[]{:S(2)}, u32[]{:S(2)}) %collective-permute-start.10) | collective-permute-done | bytes 524320 | tf_op jit(solution)/shard_map/ppermute | solution.py:55
  50.2 0.7 shard_map.191
  50.9 0.6 collective-permute-start.11
  51.5 1.3 %collective-permute-start.12 = (bf16[256,256]{1,0:T(8,128)(2,1)S(1)}, bf16[256,256]{1,0:T(8,128)(2,1)S(1)}, u32[]{:S(2)}, u32[]{:S(2)}) collective-permute-start(bf16[256,256]{1,0:T(8,128)(2,1)S(1)} %get-tuple-element.50), channel_id=1, source_target_pairs={{0,4},{1,5},{2,6},{3,7},{4,0},{5,1},{6,2},{7,3},{8,12},{9,13},{10,... | collective-permute-start | bytes 393224 | tf_op jit(solution)/shard_map/ppermute | solution.py:55
  52.8 1.7 %collective-permute-start.13 = (bf16[256,256]{1,0:T(8,128)(2,1)S(1)}, bf16[256,256]{1,0:T(8,128)(2,1)S(1)}, u32[]{:S(2)}, u32[]{:S(2)}) collective-permute-start(bf16[256,256]{1,0:T(8,128)(2,1)S(1)} %get-tuple-element.51), channel_id=1, source_target_pairs={{0,5},{1,4},{2,7},{3,6},{4,1},{5,0},{6,3},{7,2},{8,13},{9,12},{10,... | collective-permute-start | bytes 393224 | tf_op jit(solution)/shard_map/ppermute | solution.py:55
  54.5 2.3 %collective-permute-done.11.r_2_ = bf16[256,256]{1,0:T(8,128)(2,1)S(1)} collective-permute-done((bf16[256,256]{1,0:T(8,128)(2,1)S(1)}, bf16[256,256]{1,0:T(8,128)(2,1)S(1)}, u32[]{:S(2)}, u32[]{:S(2)}) %collective-permute-start.11) | collective-permute-done | bytes 131104 | tf_op jit(solution)/shard_map/ppermute | solution.py:55
  56.7 1.0 %collective-permute-done.12.r_3_ = bf16[256,256]{1,0:T(8,128)(2,1)S(1)} collective-permute-done((bf16[256,256]{1,0:T(8,128)(2,1)S(1)}, bf16[256,256]{1,0:T(8,128)(2,1)S(1)}, u32[]{:S(2)}, u32[]{:S(2)}) %collective-permute-start.12) | collective-permute-done | bytes 131104 | tf_op jit(solution)/shard_map/ppermute | solution.py:55
  57.8 2.9 %collective-permute-done.13.r_4_ = bf16[256,256]{1,0:T(8,128)(2,1)S(1)} collective-permute-done((bf16[256,256]{1,0:T(8,128)(2,1)S(1)}, bf16[256,256]{1,0:T(8,128)(2,1)S(1)}, u32[]{:S(2)}, u32[]{:S(2)}) %collective-permute-start.13) | collective-permute-done | bytes 131104 | tf_op jit(solution)/shard_map/ppermute | solution.py:55
  60.7 0.6 shard_map.192
  61.4 0.5 collective-permute-start.14
  61.9 0.3 collective-permute-start.15
  62.2 3.6 %collective-permute-start.16 = (bf16[64,256]{1,0:T(8,128)(2,1)S(1)}, bf16[64,256]{1,0:T(8,128)(2,1)S(1)}, u32[]{:S(2)}, u32[]{:S(2)}) collective-permute-start(bf16[64,256]{1,0:T(8,128)(2,1)S(1)} %get-tuple-element.55), channel_id=1, source_target_pairs={{0,24},{1,25},{2,26},{3,27},{4,28},{5,29},{6,30},{7,31},{8,16},{9,... | collective-permute-start | bytes 98312 | tf_op jit(solution)/shard_map/ppermute | solution.py:55
  65.8 0.9 collective-permute-done.15.r_3_
  66.7 1.4 %collective-permute-done.16.r_4_ = bf16[64,256]{1,0:T(8,128)(2,1)S(1)} collective-permute-done((bf16[64,256]{1,0:T(8,128)(2,1)S(1)}, bf16[64,256]{1,0:T(8,128)(2,1)S(1)}, u32[]{:S(2)}, u32[]{:S(2)}) %collective-permute-start.16) | collective-permute-done | bytes 32800 | tf_op jit(solution)/shard_map/ppermute | solution.py:55
  68.1 0.6 shard_map.193.r_1_
  68.6 3.5 %collective-permute-start.19 = (bf16[64,256]{1,0:T(8,128)(2,1)S(1)}, bf16[64,256]{1,0:T(8,128)(2,1)S(1)}, u32[]{:S(2)}, u32[]{:S(2)}) collective-permute-start(bf16[64,256]{1,0:T(8,128)(2,1)S(1)} %shard_map.193.r_1_), channel_id=1, source_target_pairs={{0,24},{1,25},{2,26},{3,27},{4,28},{5,29},{6,30},{7,31},{8,16},{9,... | collective-permute-start | bytes 98312 | tf_op jit(solution)/shard_map/ppermute | solution.py:55
  72.2 0.9 collective-permute-start.17
  73.1 1.6 %collective-permute-done.19.r_4_ = bf16[64,256]{1,0:T(8,128)(2,1)S(1)} collective-permute-done((bf16[64,256]{1,0:T(8,128)(2,1)S(1)}, bf16[64,256]{1,0:T(8,128)(2,1)S(1)}, u32[]{:S(2)}, u32[]{:S(2)}) %collective-permute-start.19) | collective-permute-done | bytes 32800 | tf_op jit(solution)/shard_map/ppermute | solution.py:55
  74.7 2.3 %collective-permute-done.18.r_3_ = bf16[64,256]{1,0:T(8,128)(2,1)S(1)} collective-permute-done((bf16[64,256]{1,0:T(8,128)(2,1)S(1)}, bf16[64,256]{1,0:T(8,128)(2,1)S(1)}, u32[]{:S(2)}, u32[]{:S(2)}) %collective-permute-start.18) | collective-permute-done | bytes 32800 | tf_op jit(solution)/shard_map/ppermute | solution.py:55
  77.0 0.6 shard_map.194.r_1_
  77.5 1.3 %collective-permute-start.22 = (bf16[256,256]{1,0:T(8,128)(2,1)S(1)}, bf16[256,256]{1,0:T(8,128)(2,1)S(1)}, u32[]{:S(2)}, u32[]{:S(2)}) collective-permute-start(bf16[256,256]{1,0:T(8,128)(2,1)S(1)} %shard_map.194.r_1_), channel_id=1, source_target_pairs={{0,5},{1,4},{2,7},{3,6},{4,1},{5,0},{6,3},{7,2},{8,13},{9,12},{10,... | collective-permute-start | bytes 393224 | tf_op jit(solution)/shard_map/ppermute | solution.py:55
  78.9 0.7 collective-permute-start.21
  79.6 1.5 %collective-permute-start.20 = (bf16[256,256]{1,0:T(8,128)(2,1)S(1)}, bf16[256,256]{1,0:T(8,128)(2,1)S(1)}, u32[]{:S(2)}, u32[]{:S(2)}) collective-permute-start(bf16[256,256]{1,0:T(8,128)(2,1)S(1)} %shard_map.194.r_1_), channel_id=1, source_target_pairs={{0,1},{1,0},{2,3},{3,2},{4,5},{5,4},{6,7},{7,6},{8,9},{9,8},{10,11... | collective-permute-start | bytes 393224 | tf_op jit(solution)/shard_map/ppermute | solution.py:55
  81.1 2.4 %collective-permute-done.22.r_4_ = bf16[256,256]{1,0:T(8,128)(2,1)S(1)} collective-permute-done((bf16[256,256]{1,0:T(8,128)(2,1)S(1)}, bf16[256,256]{1,0:T(8,128)(2,1)S(1)}, u32[]{:S(2)}, u32[]{:S(2)}) %collective-permute-start.22) | collective-permute-done | bytes 131104 | tf_op jit(solution)/shard_map/ppermute | solution.py:55
  83.5 0.4 collective-permute-done.21.r_3_
  83.9 0.9 collective-permute-done.20.r_2_
  84.9 0.6 shard_map.195.r_1_
  85.5 0.1 collective-permute-start.23
  85.5 2.4 %collective-permute-start.8 = (bf16[128,256]{1,0:T(8,128)(2,1)S(1)}, bf16[128,256]{1,0:T(8,128)(2,1)S(1)}, u32[]{:S(2)}, u32[]{:S(2)}) collective-permute-start(bf16[128,256]{1,0:T(8,128)(2,1)S(1)} %get-tuple-element.44), channel_id=1, source_target_pairs={{0,2},{2,4},{4,6},{6,8},{8,10},{10,12},{12,14},{14,16},{16,18},{18... | collective-permute-start | bytes 196616 | tf_op jit(solution)/shard_map/ppermute | solution.py:50
  87.9 2.1 %collective-permute-start.5 = (bf16[256,256]{1,0:T(8,128)(2,1)S(1)}, bf16[256,256]{1,0:T(8,128)(2,1)S(1)}, u32[]{:S(2)}, u32[]{:S(2)}) collective-permute-start(bf16[256,256]{1,0:T(8,128)(2,1)S(1)} %get-tuple-element.41), channel_id=1, source_target_pairs={{0,16},{1,17},{2,18},{3,19},{4,20},{5,21},{6,22},{7,23},{8,24},{9,... | collective-permute-start | bytes 393224 | tf_op jit(solution)/shard_map/ppermute | solution.py:55
  90.0 1.2 %collective-permute-start.6 = (bf16[256,256]{1,0:T(8,128)(2,1)S(1)}, bf16[256,256]{1,0:T(8,128)(2,1)S(1)}, u32[]{:S(2)}, u32[]{:S(2)}) collective-permute-start(bf16[256,256]{1,0:T(8,128)(2,1)S(1)} %get-tuple-element.42), channel_id=1, source_target_pairs={{0,1},{1,0},{2,3},{3,2},{4,5},{5,4},{6,7},{7,6},{8,9},{9,8},{10,11... | collective-permute-start | bytes 393224 | tf_op jit(solution)/shard_map/ppermute | solution.py:55
  91.2 0.0 collective-permute-start.7
  91.3 1.3 %collective-permute-start.9 = (bf16[128,256]{1,0:T(8,128)(2,1)S(1)}, bf16[128,256]{1,0:T(8,128)(2,1)S(1)}, u32[]{:S(2)}, u32[]{:S(2)}) collective-permute-start(bf16[128,256]{1,0:T(8,128)(2,1)S(1)} %get-tuple-element.45), channel_id=1, source_target_pairs={{2,0},{4,2},{6,4},{8,6},{10,8},{12,10},{14,12},{16,14},{18,16},{20... | collective-permute-start | bytes 196616 | tf_op jit(solution)/shard_map/ppermute | solution.py:50
  92.5 1.8 %collective-permute-done.9.r_8_ = bf16[128,256]{1,0:T(8,128)(2,1)S(1)} collective-permute-done((bf16[128,256]{1,0:T(8,128)(2,1)S(1)}, bf16[128,256]{1,0:T(8,128)(2,1)S(1)}, u32[]{:S(2)}, u32[]{:S(2)}) %collective-permute-start.9) | collective-permute-done | bytes 65568 | tf_op jit(solution)/shard_map/ppermute | solution.py:50
  94.4 3.2 %collective-permute-done.5.r_4_ = bf16[256,256]{1,0:T(8,128)(2,1)S(1)} collective-permute-done((bf16[256,256]{1,0:T(8,128)(2,1)S(1)}, bf16[256,256]{1,0:T(8,128)(2,1)S(1)}, u32[]{:S(2)}, u32[]{:S(2)}) %collective-permute-start.5) | collective-permute-done | bytes 131104 | tf_op jit(solution)/shard_map/ppermute | solution.py:55
  97.6 2.1 %collective-permute-done.7.r_6_ = bf16[256,256]{1,0:T(8,128)(2,1)S(1)} collective-permute-done((bf16[256,256]{1,0:T(8,128)(2,1)S(1)}, bf16[256,256]{1,0:T(8,128)(2,1)S(1)}, u32[]{:S(2)}, u32[]{:S(2)}) %collective-permute-start.7) | collective-permute-done | bytes 131104 | tf_op jit(solution)/shard_map/ppermute | solution.py:55
  99.7 1.0 shard_map.190
  100.7 1.9 %shard_map.196 = (f32[256,256]{1,0:T(8,128)}, f32[256,256]{1,0:T(8,128)}, f32[256,256]{1,0:T(8,128)}, f32[256,256]{1,0:T(8,128)}, f32[256,512]{1,0:T(8,128)}, /*index=5*/f32[512,256]{1,0:T(8,128)}) custom-call(s32[7]{0:T(128)S(1)} %stack.47.r_0_, bf16[1024,256]{1,0:T(8,128)(2,1)S(1)} %shard_map.195.r_1_, bf16[1024,256]{1,0:T(8,128)(2,1)S(1)} %collective-permute-done.23.r_2_), custom_call_target="tpu_custom_call" | custom-call | tf_op jit(solution)/shard_map/pallas_call | solution.py:61
  (23 shorter events, 0.0 us)
Async XLA Ops:
  0.6 0.7 copy-start.2
  0.6 0.7 copy-start.3
  1.3 0.9 copy-start
  2.2 14.2 %copy-start.1 = (bf16[1,1,1,256,256]{4,3,2,1,0:T(8,128)(2,1)S(1)}, bf16[1,1,1,256,256]{4,3,2,1,0:T(8,128)(2,1)}, u32[]{:S(2)}) copy-start(bf16[1,1,1,256,256]{4,3,2,1,0:T(8,128)(2,1)} %param.13) | copy-start | bytes 393220
  3.1 13.4 %collective-permute-start.2 = (bf16[272,256]{1,0:T(8,128)(2,1)S(1)}, bf16[272,256]{1,0:T(8,128)(2,1)S(1)}, u32[]{:S(2)}, u32[]{:S(2)}) collective-permute-start(bf16[272,256]{1,0:T(8,128)(2,1)S(1)} %get-tuple-element.35.r_14_), channel_id=1, source_target_pairs={{0,8},{1,9},{2,10},{3,11},{4,12},{5,13},{6,14},{7,15},{8,0},{9,1},... | collective-permute-start | bytes 417800 | tf_op jit(solution)/shard_map/ppermute | solution.py:55
  6.1 10.3 %collective-permute-start.1 = (bf16[272,256]{1,0:T(8,128)(2,1)S(1)}, bf16[272,256]{1,0:T(8,128)(2,1)S(1)}, u32[]{:S(2)}, u32[]{:S(2)}) collective-permute-start(bf16[272,256]{1,0:T(8,128)(2,1)S(1)} %get-tuple-element.35.r_14_), channel_id=1, source_target_pairs={{0,1},{1,0},{2,3},{3,2},{4,5},{5,4},{6,7},{7,6},{8,9},{9,8},{10,11... | collective-permute-start | bytes 417800 | tf_op jit(solution)/shard_map/ppermute | solution.py:55
  7.7 8.8 %collective-permute-start = (bf16[272,256]{1,0:T(8,128)(2,1)S(1)}, bf16[272,256]{1,0:T(8,128)(2,1)S(1)}, u32[]{:S(2)}, u32[]{:S(2)}) collective-permute-start(bf16[272,256]{1,0:T(8,128)(2,1)S(1)} %get-tuple-element.35.r_14_), channel_id=1, source_target_pairs={{0,16},{1,17},{2,18},{3,19},{4,20},{5,21},{6,22},{7,23},{8,24},{9,... | collective-permute-start | bytes 417800 | tf_op jit(solution)/shard_map/ppermute | solution.py:55
  10.3 3.5 %collective-permute-start.3 = (bf16[128,256]{1,0:T(8,128)(2,1)S(1)}, bf16[128,256]{1,0:T(8,128)(2,1)S(1)}, u32[]{:S(2)}, u32[]{:S(2)}) collective-permute-start(bf16[128,256]{1,0:T(8,128)(2,1)S(1)} %get-tuple-element.36), channel_id=1, source_target_pairs={{0,2},{2,4},{4,6},{6,8},{8,10},{10,12},{12,14},{14,16},{16,18},{18... | collective-permute-start | bytes 196616 | tf_op jit(solution)/shard_map/ppermute | solution.py:50
  11.5 4.9 %collective-permute-start.4 = (bf16[128,256]{1,0:T(8,128)(2,1)S(1)}, bf16[128,256]{1,0:T(8,128)(2,1)S(1)}, u32[]{:S(2)}, u32[]{:S(2)}) collective-permute-start(bf16[128,256]{1,0:T(8,128)(2,1)S(1)} %get-tuple-element.37), channel_id=1, source_target_pairs={{2,0},{4,2},{6,4},{8,6},{10,8},{12,10},{14,12},{16,14},{18,16},{20... | collective-permute-start | bytes 196616 | tf_op jit(solution)/shard_map/ppermute | solution.py:50
  12.9 0.7 copy-start.13
  16.4 1.0 copy-start.4
  17.4 0.9 copy-start.5
  18.4 0.9 copy-start.6
  19.3 0.9 copy-start.7
  20.2 0.9 copy-start.8
  21.1 0.9 copy-start.9
  22.1 0.9 copy-start.10
  23.0 0.9 copy-start.11
  23.9 0.9 copy-start.12
  45.7 4.5 %collective-permute-start.10 = (bf16[1024,256]{1,0:T(8,128)(2,1)S(1)}, bf16[1024,256]{1,0:T(8,128)(2,1)S(1)}, u32[]{:S(2)}, u32[]{:S(2)}) collective-permute-start(bf16[1024,256]{1,0:T(8,128)(2,1)S(1)} %get-tuple-element.47), channel_id=1, source_target_pairs={{0,2},{1,3},{2,0},{3,1},{4,6},{5,7},{6,4},{7,5},{8,10},{9,11},{10,... | collective-permute-start | bytes 1572872 | tf_op jit(solution)/shard_map/ppermute | solution.py:55
  50.9 5.8 %collective-permute-start.11 = (bf16[256,256]{1,0:T(8,128)(2,1)S(1)}, bf16[256,256]{1,0:T(8,128)(2,1)S(1)}, u32[]{:S(2)}, u32[]{:S(2)}) collective-permute-start(bf16[256,256]{1,0:T(8,128)(2,1)S(1)} %get-tuple-element.49), channel_id=1, source_target_pairs={{0,1},{1,0},{2,3},{3,2},{4,5},{5,4},{6,7},{7,6},{8,9},{9,8},{10,11... | collective-permute-start | bytes 393224 | tf_op jit(solution)/shard_map/ppermute | solution.py:55
  51.5 6.3 %collective-permute-start.12 = (bf16[256,256]{1,0:T(8,128)(2,1)S(1)}, bf16[256,256]{1,0:T(8,128)(2,1)S(1)}, u32[]{:S(2)}, u32[]{:S(2)}) collective-permute-start(bf16[256,256]{1,0:T(8,128)(2,1)S(1)} %get-tuple-element.50), channel_id=1, source_target_pairs={{0,4},{1,5},{2,6},{3,7},{4,0},{5,1},{6,2},{7,3},{8,12},{9,13},{10,... | collective-permute-start | bytes 393224 | tf_op jit(solution)/shard_map/ppermute | solution.py:55
  52.8 7.9 %collective-permute-start.13 = (bf16[256,256]{1,0:T(8,128)(2,1)S(1)}, bf16[256,256]{1,0:T(8,128)(2,1)S(1)}, u32[]{:S(2)}, u32[]{:S(2)}) collective-permute-start(bf16[256,256]{1,0:T(8,128)(2,1)S(1)} %get-tuple-element.51), channel_id=1, source_target_pairs={{0,5},{1,4},{2,7},{3,6},{4,1},{5,0},{6,3},{7,2},{8,13},{9,12},{10,... | collective-permute-start | bytes 393224 | tf_op jit(solution)/shard_map/ppermute | solution.py:55
  61.4 4.5 %collective-permute-start.14 = (bf16[64,256]{1,0:T(8,128)(2,1)S(1)}, bf16[64,256]{1,0:T(8,128)(2,1)S(1)}, u32[]{:S(2)}, u32[]{:S(2)}) collective-permute-start(bf16[64,256]{1,0:T(8,128)(2,1)S(1)} %get-tuple-element.53), channel_id=1, source_target_pairs={{0,8},{1,9},{2,10},{3,11},{4,12},{5,13},{6,14},{7,15},{8,0},{9,1},... | collective-permute-start | bytes 98312 | tf_op jit(solution)/shard_map/ppermute | solution.py:55
  61.9 4.8 %collective-permute-start.15 = (bf16[64,256]{1,0:T(8,128)(2,1)S(1)}, bf16[64,256]{1,0:T(8,128)(2,1)S(1)}, u32[]{:S(2)}, u32[]{:S(2)}) collective-permute-start(bf16[64,256]{1,0:T(8,128)(2,1)S(1)} %get-tuple-element.54), channel_id=1, source_target_pairs={{0,16},{1,17},{2,18},{3,19},{4,20},{5,21},{6,22},{7,23},{8,24},{9,... | collective-permute-start | bytes 98312 | tf_op jit(solution)/shard_map/ppermute | solution.py:55
  62.2 5.8 %collective-permute-start.16 = (bf16[64,256]{1,0:T(8,128)(2,1)S(1)}, bf16[64,256]{1,0:T(8,128)(2,1)S(1)}, u32[]{:S(2)}, u32[]{:S(2)}) collective-permute-start(bf16[64,256]{1,0:T(8,128)(2,1)S(1)} %get-tuple-element.55), channel_id=1, source_target_pairs={{0,24},{1,25},{2,26},{3,27},{4,28},{5,29},{6,30},{7,31},{8,16},{9,... | collective-permute-start | bytes 98312 | tf_op jit(solution)/shard_map/ppermute | solution.py:55
  68.6 6.1 %collective-permute-start.19 = (bf16[64,256]{1,0:T(8,128)(2,1)S(1)}, bf16[64,256]{1,0:T(8,128)(2,1)S(1)}, u32[]{:S(2)}, u32[]{:S(2)}) collective-permute-start(bf16[64,256]{1,0:T(8,128)(2,1)S(1)} %shard_map.193.r_1_), channel_id=1, source_target_pairs={{0,24},{1,25},{2,26},{3,27},{4,28},{5,29},{6,30},{7,31},{8,16},{9,... | collective-permute-start | bytes 98312 | tf_op jit(solution)/shard_map/ppermute | solution.py:55
  72.2 4.8 %collective-permute-start.18 = (bf16[64,256]{1,0:T(8,128)(2,1)S(1)}, bf16[64,256]{1,0:T(8,128)(2,1)S(1)}, u32[]{:S(2)}, u32[]{:S(2)}) collective-permute-start(bf16[64,256]{1,0:T(8,128)(2,1)S(1)} %shard_map.193.r_1_), channel_id=1, source_target_pairs={{0,16},{1,17},{2,18},{3,19},{4,20},{5,21},{6,22},{7,23},{8,24},{9,... | collective-permute-start | bytes 98312 | tf_op jit(solution)/shard_map/ppermute | solution.py:55
  72.2 4.8 %collective-permute-start.17 = (bf16[64,256]{1,0:T(8,128)(2,1)S(1)}, bf16[64,256]{1,0:T(8,128)(2,1)S(1)}, u32[]{:S(2)}, u32[]{:S(2)}) collective-permute-start(bf16[64,256]{1,0:T(8,128)(2,1)S(1)} %shard_map.193.r_1_), channel_id=1, source_target_pairs={{0,8},{1,9},{2,10},{3,11},{4,12},{5,13},{6,14},{7,15},{8,0},{9,1},... | collective-permute-start | bytes 98312 | tf_op jit(solution)/shard_map/ppermute | solution.py:55
  77.5 6.0 %collective-permute-start.22 = (bf16[256,256]{1,0:T(8,128)(2,1)S(1)}, bf16[256,256]{1,0:T(8,128)(2,1)S(1)}, u32[]{:S(2)}, u32[]{:S(2)}) collective-permute-start(bf16[256,256]{1,0:T(8,128)(2,1)S(1)} %shard_map.194.r_1_), channel_id=1, source_target_pairs={{0,5},{1,4},{2,7},{3,6},{4,1},{5,0},{6,3},{7,2},{8,13},{9,12},{10,... | collective-permute-start | bytes 393224 | tf_op jit(solution)/shard_map/ppermute | solution.py:55
  78.9 5.1 %collective-permute-start.21 = (bf16[256,256]{1,0:T(8,128)(2,1)S(1)}, bf16[256,256]{1,0:T(8,128)(2,1)S(1)}, u32[]{:S(2)}, u32[]{:S(2)}) collective-permute-start(bf16[256,256]{1,0:T(8,128)(2,1)S(1)} %shard_map.194.r_1_), channel_id=1, source_target_pairs={{0,4},{1,5},{2,6},{3,7},{4,0},{5,1},{6,2},{7,3},{8,12},{9,13},{10,... | collective-permute-start | bytes 393224 | tf_op jit(solution)/shard_map/ppermute | solution.py:55
  79.6 5.3 %collective-permute-start.20 = (bf16[256,256]{1,0:T(8,128)(2,1)S(1)}, bf16[256,256]{1,0:T(8,128)(2,1)S(1)}, u32[]{:S(2)}, u32[]{:S(2)}) collective-permute-start(bf16[256,256]{1,0:T(8,128)(2,1)S(1)} %shard_map.194.r_1_), channel_id=1, source_target_pairs={{0,1},{1,0},{2,3},{3,2},{4,5},{5,4},{6,7},{7,6},{8,9},{9,8},{10,11... | collective-permute-start | bytes 393224 | tf_op jit(solution)/shard_map/ppermute | solution.py:55
  85.5 15.2 %collective-permute-start.23 = (bf16[1024,256]{1,0:T(8,128)(2,1)S(1)}, bf16[1024,256]{1,0:T(8,128)(2,1)S(1)}, u32[]{:S(2)}, u32[]{:S(2)}) collective-permute-start(bf16[1024,256]{1,0:T(8,128)(2,1)S(1)} %shard_map.195.r_1_), channel_id=1, source_target_pairs={{0,2},{1,3},{2,0},{3,1},{4,6},{5,7},{6,4},{7,5},{8,10},{9,11},{10,... | collective-permute-start | bytes 1572872 | tf_op jit(solution)/shard_map/ppermute | solution.py:55
  85.5 5.7 %collective-permute-start.8 = (bf16[128,256]{1,0:T(8,128)(2,1)S(1)}, bf16[128,256]{1,0:T(8,128)(2,1)S(1)}, u32[]{:S(2)}, u32[]{:S(2)}) collective-permute-start(bf16[128,256]{1,0:T(8,128)(2,1)S(1)} %get-tuple-element.44), channel_id=1, source_target_pairs={{0,2},{2,4},{4,6},{6,8},{8,10},{10,12},{12,14},{14,16},{16,18},{18... | collective-permute-start | bytes 196616 | tf_op jit(solution)/shard_map/ppermute | solution.py:50
  87.9 9.7 %collective-permute-start.5 = (bf16[256,256]{1,0:T(8,128)(2,1)S(1)}, bf16[256,256]{1,0:T(8,128)(2,1)S(1)}, u32[]{:S(2)}, u32[]{:S(2)}) collective-permute-start(bf16[256,256]{1,0:T(8,128)(2,1)S(1)} %get-tuple-element.41), channel_id=1, source_target_pairs={{0,16},{1,17},{2,18},{3,19},{4,20},{5,21},{6,22},{7,23},{8,24},{9,... | collective-permute-start | bytes 393224 | tf_op jit(solution)/shard_map/ppermute | solution.py:55
  90.0 7.6 %collective-permute-start.6 = (bf16[256,256]{1,0:T(8,128)(2,1)S(1)}, bf16[256,256]{1,0:T(8,128)(2,1)S(1)}, u32[]{:S(2)}, u32[]{:S(2)}) collective-permute-start(bf16[256,256]{1,0:T(8,128)(2,1)S(1)} %get-tuple-element.42), channel_id=1, source_target_pairs={{0,1},{1,0},{2,3},{3,2},{4,5},{5,4},{6,7},{7,6},{8,9},{9,8},{10,11... | collective-permute-start | bytes 393224 | tf_op jit(solution)/shard_map/ppermute | solution.py:55
  91.2 8.5 %collective-permute-start.7 = (bf16[256,256]{1,0:T(8,128)(2,1)S(1)}, bf16[256,256]{1,0:T(8,128)(2,1)S(1)}, u32[]{:S(2)}, u32[]{:S(2)}) collective-permute-start(bf16[256,256]{1,0:T(8,128)(2,1)S(1)} %get-tuple-element.43), channel_id=1, source_target_pairs={{0,8},{1,9},{2,10},{3,11},{4,12},{5,13},{6,14},{7,15},{8,0},{9,1},... | collective-permute-start | bytes 393224 | tf_op jit(solution)/shard_map/ppermute | solution.py:55
  91.3 3.1 %collective-permute-start.9 = (bf16[128,256]{1,0:T(8,128)(2,1)S(1)}, bf16[128,256]{1,0:T(8,128)(2,1)S(1)}, u32[]{:S(2)}, u32[]{:S(2)}) collective-permute-start(bf16[128,256]{1,0:T(8,128)(2,1)S(1)} %get-tuple-element.45), channel_id=1, source_target_pairs={{2,0},{4,2},{6,4},{8,6},{10,8},{12,10},{14,12},{16,14},{18,16},{20... | collective-permute-start | bytes 196616 | tf_op jit(solution)/shard_map/ppermute | solution.py:50

commit v2 on v1

--- a/solution.py
+++ b/solution.py
@@ -45,6 +45,12 @@
     return jnp.transpose(value.astype(F32), (1, 0))
 
 
+def pair_permute(value, odd_first):
+    count = lax.axis_size("sx")
+    pairs = [(i, i + 1) for i in range(1 if odd_first else 0, count - 1, 2)]
+    return lax.ppermute(value, "sx", pairs + [(b, a) for a, b in pairs])
+
+
 def from_behind(block, axis, distance):
     devices = range(lax.axis_size(axis))
     return lax.ppermute(block, axis, [(i - distance, i) for i in devices if i - distance in devices])
@@ -55,9 +61,14 @@
     return lax.ppermute(value, AXES, [(i, i ^ mask) for i in range(count)])
 
 
-def call(kernel, outs, args, smem=0, scratch=(), limit=48, flops=0, nbytes=0):
+def call(kernel, outs, args, smem=0, hbm=0, scratch=(), limit=48, flops=0, nbytes=0):
     specs = [pl.BlockSpec(memory_space=pltpu.SMEM)] * smem
-    specs += [pl.BlockSpec(memory_space=pltpu.VMEM)] * (len(args) - smem)
+    specs += [pl.BlockSpec(memory_space=pltpu.HBM)] * hbm
+    args = [pltpu.with_memory_space_constraint(a, pltpu.HBM) if smem <= i < smem + hbm else a for i, a in enumerate(args)]
+    specs += [pl.BlockSpec(memory_space=pltpu.VMEM)] * (len(args) - smem - hbm)
+    scratch = list(scratch)
+    if hbm:
+        scratch += [pltpu.VMEM(a.shape, a.dtype) for a in args[smem : smem + hbm]] + [pltpu.SemaphoreType.DMA((hbm,))]
     return pl.pallas_call(
         kernel,
         out_shape=[jax.ShapeDtypeStruct(s, d) for s, d in outs],
@@ -69,7 +80,27 @@
     )(*args)
 
 
-def prepare_kernel(counts, nodes, boundary, pack, *rims):
+def fetched(sources, buffers, semaphores):
+    copies = [pltpu.make_async_copy(a, b, semaphores.at[i]) for i, (a, b) in enumerate(zip(sources, buffers))]
+    for copy in copies:
+        copy.start()
+
+    def ready(i):
+        copies[i].wait()
+        return buffers[i]
+
+    return ready
+
+
+def side_lines(boundary, odd):
+    first, second = boundary[0:1, :], boundary[1:2, :]
+    return [jnp.where(odd, first, second), jnp.where(odd, second, first), boundary[2:3, :], boundary[3:4, :]]
+
+
+def prepare_kernel(info, counts, *refs):
+    pack, rims = refs[2], refs[3:-3]
+    ready = fetched(refs[:2], refs[-3:-1], refs[-1])
+    nodes = ready(0)
     count, width = nodes.shape
     blocks = counts.shape[0]
     size = count // blocks
@@ -82,6 +113,7 @@
     for b in range(blocks):
         limit = jnp.where(lane // size == b, counts[b], limit)
     extra = jnp.where((row == 0) & (lane % size < limit), 1.0, 0.0)
+    boundary = ready(1)
     rim = boundary.shape[1]
     slots = boundary[...].astype(F32)
     for side in range(SIDES):
@@ -90,8 +122,9 @@
             line = jnp.concatenate([line, jnp.zeros((1, count - rim), F32)], axis=1)
         extra = jnp.where(row == side + 1, line, extra)
     pack[count : count + EXTRA, :] = extra.astype(BF16)
+    lines = side_lines(boundary, info[SIDES] > 0)
     for side, out in enumerate(rims):
-        place = to_bf(iota((count, rim), 0) == boundary[side : side + 1, :])
+        place = to_bf(iota((count, rim), 0) == lines[side])
         out[...] = tn(place, normed).astype(BF16)
 
 
@@ -99,7 +132,11 @@
     return iota(shape, dim) // HEAD_DIM
 
 
-def main_kernel(merge_y, info, counts, pairing, nodes, gout, wq, wk, wv, wo, wup, wdown, adjacency, expander, boundary, *refs):
+def main_kernel(merge_y, info, counts, pairing, *refs):
+    copied = 11
+    ready = fetched(refs[:copied], refs[-copied - 1 : -1], refs[-1])
+    nodes, boundary, wq, wk, wv, adjacency, expander, wo, wup, wdown, gout = refs[-copied - 1 : -1]
+    refs = refs[copied : -copied - 1]
     packs = refs[: MATCHINGS + 1]
     rims = refs[MATCHINGS + 1 : MATCHINGS + 1 + (2 if merge_y else 4)]
     refs = refs[MATCHINGS + 1 + len(rims) :]
@@ -120,7 +157,8 @@
     log2e = math.log2(math.e)
 
     normed = packs[0][0:count, :]
-    feats = nodes[...].astype(F32)
+    ready(1)
+    lines = side_lines(boundary, info[SIDES] > 0)
     for b in range(blocks):
         xcat[b * keys : b * keys + size, :] = packs[0][b * size : (b + 1) * size, :]
         for m in range(MATCHINGS):
@@ -130,7 +168,7 @@
     base = blocks * keys
     places, moves = [], [None, None, None, None]
     for s in range(SIDES):
-        here = (iota((count, rim), 0) == boundary[s : s + 1, :]) & (info[s] > 0)
+        here = (iota((count, rim), 0) == lines[s]) & (info[s] > 0)
         places.append(to_bf(here))
     for s in range(SIDES):
         if merge_y and s >= 2:
@@ -143,6 +181,8 @@
             rows = nn(places[s], rims[s][...])
         xcat[base + s * count : base + (s + 1) * count, :] = rows.astype(BF16)
 
+    for i in (2, 3, 4):
+        ready(i)
     queries = nn(normed, wq[...]).astype(BF16)
     queries_t = flip(queries).astype(BF16)
     wk_t = flip(wk[...]).astype(BF16)
@@ -160,6 +200,8 @@
         rim_keys.append(nn(rows, wk[...]).astype(BF16).astype(F32))
         rim_values.append(nn(rows, wv[...]).astype(BF16).astype(F32))
 
+    ready(5)
+    ready(6)
     bias = []
     eye = iota((size, size), 0) == iota((size, size), 1)
     for b in range(blocks):
@@ -199,24 +241,28 @@
     for b in range(blocks):
         cols = slice(b * size, (b + 1) * size)
         top_rows, inv_rows, att_rows = [], [], []
-        for h in range(HEADS):
-            own = queries_t[:, cols]
-            masked = jnp.where(row_head == h, own, jnp.zeros_like(own))
-            score = nn(key_rows[b], masked) * (scale * log2e) + bias[b]
-            top = jnp.maximum(jnp.max(score, axis=0, keepdims=True), rim_top[h : h + 1, cols])
-            grown = jnp.exp2(score - top)
-            total = jnp.sum(grown, axis=0, keepdims=True)
-            for s in range(SIDES):
-                total = total + jnp.exp2(rim_scores[s][h : h + 1, cols] - top)
-            inverse = 1.0 / total
-            prob = grown * inverse
-            at = slice(h * size, (h + 1) * size)
-            probs[b, :, at] = prob
-            prob_bf = prob.astype(BF16)
-            pbf[b, :, at] = prob_bf
-            att_rows.append(nn(value_cols[b][h * HEAD_DIM : (h + 1) * HEAD_DIM, :], prob_bf))
-            top_rows.append(top)
-            inv_rows.append(inverse)
+        own = queries_t[:, cols]
+        for first in range(0, HEADS, 2):
+            pair = (first, first + 1)
+            masked = [jnp.where(row_head == h, own, jnp.zeros_like(own)) for h in pair]
+            both = nn(key_rows[b], jnp.concatenate(masked, axis=1))
+            for k, h in enumerate(pair):
+                score = both[:, k * size : (k + 1) * size] * (scale * log2e) + bias[b]
+                top = jnp.maximum(jnp.max(score, axis=0, keepdims=True), rim_top[h : h + 1, cols])
+                grown = jnp.exp2(score - top)
+                total = jnp.sum(grown, axis=0, keepdims=True)
+                for s in range(SIDES):
+                    total = total + jnp.exp2(rim_scores[s][h : h + 1, cols] - top)
+                inverse = 1.0 / total
+                prob = grown * inverse
+                at = slice(h * size, (h + 1) * size)
+                probs[b, :, at] = prob
+                pbf[b, :, at] = prob.astype(BF16)
+                top_rows.append(top)
+                inv_rows.append(inverse)
+            rows = slice(first * HEAD_DIM, (first + 2) * HEAD_DIM)
+            wide = nn(value_cols[b][rows, :], pbf[b, :, first * size : (first + 2) * size])
+            att_rows += [wide[0:HEAD_DIM, 0:size], wide[HEAD_DIM:, size:]]
         tops.append(jnp.concatenate(top_rows, axis=0))
         sums.append(jnp.concatenate(inv_rows, axis=0))
         att_blocks.append(jnp.concatenate(att_rows, axis=0))
@@ -234,6 +280,9 @@
     for b in range(blocks):
         limit = jnp.where(slot // size == b, counts[b], limit)
     usable = jnp.where(slot % size < limit, 1.0, 0.0)
+    for i in (0, 7, 8, 9, 10):
+        ready(i)
+    feats = nodes[...].astype(F32)
     hidden = feats + nn(attended, wo[...])
     factor = lax.rsqrt(jnp.mean(hidden * hidden, axis=1, keepdims=True) + EPSILON)
     mid = hidden * factor
@@ -271,21 +320,25 @@
     for b in range(blocks):
         cols = slice(b * size, (b + 1) * size)
         inner_rows, query_rows = [], []
-        for h in range(HEADS):
-            own = grad_att_t[:, cols]
-            masked = jnp.where(row_head == h, own, jnp.zeros_like(own))
-            dots = nn(value_rows[b], masked)
-            at = slice(h * size, (h + 1) * size)
-            prob = probs[b, :, at]
-            inner = jnp.sum(prob * dots, axis=0, keepdims=True) + rim_inner[h : h + 1, cols]
-            graded = (prob * (dots - inner) * scale).astype(BF16)
-            sgrad[b, :, at] = graded
-            query_rows.append(nn(key_cols[b][h * HEAD_DIM : (h + 1) * HEAD_DIM, :], graded))
-            inner_rows.append(inner)
-            mine = queries[cols, :]
-            qstack[at, :] = jnp.where(lane_head == h, mine, jnp.zeros_like(mine))
-            mine = grad_att[cols, :]
-            gstack[at, :] = jnp.where(lane_head == h, mine, jnp.zeros_like(mine))
+        own = grad_att_t[:, cols]
+        for first in range(0, HEADS, 2):
+            pair = (first, first + 1)
+            masked = [jnp.where(row_head == h, own, jnp.zeros_like(own)) for h in pair]
+            both = nn(value_rows[b], jnp.concatenate(masked, axis=1))
+            for k, h in enumerate(pair):
+                dots = both[:, k * size : (k + 1) * size]
+                at = slice(h * size, (h + 1) * size)
+                prob = probs[b, :, at]
+                inner = jnp.sum(prob * dots, axis=0, keepdims=True) + rim_inner[h : h + 1, cols]
+                sgrad[b, :, at] = (prob * (dots - inner) * scale).astype(BF16)
+                inner_rows.append(inner)
+                mine = queries[cols, :]
+                qstack[at, :] = jnp.where(lane_head == h, mine, jnp.zeros_like(mine))
+                mine = grad_att[cols, :]
+                gstack[at, :] = jnp.where(lane_head == h, mine, jnp.zeros_like(mine))
+            rows = slice(first * HEAD_DIM, (first + 2) * HEAD_DIM)
+            wide = nn(key_cols[b][rows, :], sgrad[b, :, first * size : (first + 2) * size])
+            query_rows += [wide[0:HEAD_DIM, 0:size], wide[HEAD_DIM:, size:]]
         inner_blocks.append(jnp.concatenate(inner_rows, axis=0))
         query_blocks.append(jnp.concatenate(query_rows, axis=0))
         span = slice(b * keys, (b + 1) * keys)
@@ -337,16 +390,19 @@
     send[...] = grads[pl.ds(pl.multiple_of((1 - mine) * half_rows, half_rows), half_rows), :].astype(BF16)
 
 
-def nodes_kernel(merge_y, nodes, grad_hidden, grad_normed, boundary, *refs):
-    out = refs[-1]
-    backs, rims = refs[:MATCHINGS], refs[MATCHINGS:-1]
+def nodes_kernel(info, *refs):
+    ready = fetched(refs[:2], refs[-3:-1], refs[-1])
+    grad_hidden, grad_normed = refs[2:4]
+    backs, rims, out = refs[4 : 4 + MATCHINGS], refs[4 + MATCHINGS : -4], refs[-4]
+    nodes, boundary = ready(0), ready(1)
+    lines = side_lines(boundary, info[SIDES] > 0)
     count = nodes.shape[0]
     rim = boundary.shape[1]
     cot = grad_normed[...]
     for back in backs:
         cot = cot + back[...].astype(F32)
     for s, rows in enumerate(rims):
-        place = to_bf(iota((count, rim), 0) == boundary[s : s + 1, :])
+        place = to_bf(iota((count, rim), 0) == lines[s])
         cot = cot + nn(place, rows[...])
     feats = nodes[...].astype(F32)
     factor = lax.rsqrt(jnp.mean(feats * feats, axis=1, keepdims=True) + EPSILON)
@@ -406,9 +462,23 @@
     return sum(1 << bit for k, bit in enumerate(bits) if d >> k & 1)
 
 
-def all_sum(info, keep, arrived, groups, core_mask):
+def all_sum(info, keep, arrived, groups, core_mask, riders):
     width = keep.shape[1]
     kept, pieces = keep, [arrived]
+    riders, rode = list(riders), []
+
+    def exchange(values, masks, several):
+        batch = riders[:several]
+        del riders[:several]
+        if not batch:
+            return [xor_permute(v, m) for v, m in zip(values, masks)]
+        tied = lax.optimization_barrier((tuple(values), tuple(r[0] for r in batch)))
+        moved = [xor_permute(v, m) for v, m in zip(tied[0], masks)]
+        taken = [r[1](v) for r, v in zip(batch, tied[1])]
+        moved, taken = lax.optimization_barrier((tuple(moved), tuple(taken)))
+        rode.extend(taken)
+        return list(moved)
+
     for level, bits in enumerate(groups):
         parts = 2 ** len(bits)
         rows = kept.shape[0] // parts
@@ -421,7 +491,7 @@
             scratch=[pltpu.VMEM(kept.shape, F32)],
         )
         kept = made[0]
-        pieces = [xor_permute(made[d], offset_mask(bits, d)) for d in range(1, parts)]
+        pieces = exchange(made[1:], [offset_mask(bits, d) for d in range(1, parts)], 2)
     whole = call(
         lambda *r, n=len(pieces): reduce_kernel(0, 1, n, *r),
         [(kept.shape, BF16)],
@@ -432,14 +502,15 @@
     for level in reversed(range(len(groups))):
         bits = groups[level]
         parts = 2 ** len(bits)
-        pieces = [whole] + [xor_permute(whole, offset_mask(bits, d)) for d in range(1, parts)]
+        masks = [offset_mask(bits, d) for d in range(1, parts)]
+        pieces = [whole] + exchange([whole] * len(masks), masks, 2 if level else len(riders))
         whole = call(
             lambda *r, level=level: gather_kernel(SIDES + 1 + level, *r),
             [((whole.shape[0] * parts, width), BF16)],
             [info, *pieces],
             smem=1,
         )[0]
-    return whole, xor_permute(whole, core_mask)
+    return whole, xor_permute(whole, core_mask), rode
 
 
 def shards(nodes, grad_out, w_query, w_key, w_value, w_out, w_up, w_down, counts, adjacency, expander, pairing, boundary):
@@ -458,7 +529,7 @@
     ix, iy = lax.axis_index("sx"), lax.axis_index("sy")
     index = ix * size_y + iy
     info = jnp.stack(
-        [ix > 0, ix < size_x - 1, iy > 0, iy < size_y - 1]
+        [ix >= 0, jnp.where(ix % 2 == 0, ix > 0, ix < size_x - 1), iy > 0, iy < size_y - 1]
         + [bit_of([core_bit], index)]
         + [bit_of(bits, index) for bits in groups]
     ).astype(jnp.int32)
@@ -467,12 +538,13 @@
     prepared = call(
         prepare_kernel,
         [((count + EXTRA, width), BF16)] + [((rim, width), BF16)] * rim_count,
-        [counts, feats, boundary],
-        smem=1,
+        [info, counts, feats, boundary],
+        smem=2,
+        hbm=2,
     )
     pack, sent = prepared[0], prepared[1:]
     far = [xor_permute(pack, mask) for mask in partner]
-    arrived = [from_behind(sent[1], "sx", 1), from_behind(sent[0], "sx", -1)]
+    arrived = [pair_permute(sent[0], False), pair_permute(sent[1], True)]
     if not merge_y:
         arrived += [from_behind(sent[3], "sy", 1), from_behind(sent[2], "sy", -1)]
 
@@ -489,8 +561,9 @@
         + [(square, BF16)] * MATCHINGS
         + [((rim, width), BF16)] * rim_count
         + [((total_rows // 2, width), F32), ((total_rows // 2, width), BF16)],
-        [info, counts, pairing, feats, gout, w_query, w_key, w_value, w_out, w_up, w_down, adjacency, expander, boundary, pack, *far, *arrived],
+        [info, counts, pairing, feats, boundary, w_query, w_key, w_value, adjacency, expander, w_out, w_up, w_down, gout, pack, *far, *arrived],
         smem=3,
+        hbm=11,
         scratch=[
             pltpu.VMEM((total_rows, width), F32),
             pltpu.VMEM((all_rows, width), BF16),
@@ -510,15 +583,18 @@
     keep, send = made[-2:]
 
     core_mask = 1 << core_bit
-    own, other = all_sum(info, keep, xor_permute(send, core_mask), groups, core_mask)
-    returned = [xor_permute(back, mask) for back, mask in zip(backs, partner)]
-    rims = [from_behind(rim_back[1], "sx", 1), from_behind(rim_back[0], "sx", -1)]
+    riders = [(back, lambda v, mask=mask: xor_permute(v, mask)) for back, mask in zip(backs, partner)]
+    riders += [(rim_back[0], lambda v: pair_permute(v, False)), (rim_back[1], lambda v: pair_permute(v, True))]
     if not merge_y:
-        rims += [from_behind(rim_back[3], "sy", 1), from_behind(rim_back[2], "sy", -1)]
+        riders += [(rim_back[3], lambda v: from_behind(v, "sy", 1)), (rim_back[2], lambda v: from_behind(v, "sy", -1))]
+    own, other, rode = all_sum(info, keep, xor_permute(send, core_mask), groups, core_mask, riders)
+    returned, rims = rode[:MATCHINGS], rode[MATCHINGS:]
     grad_nodes = call(
-        lambda *r: nodes_kernel(merge_y, *r),
+        nodes_kernel,
         [(square, BF16)],
-        [feats, grad_hidden, grad_normed, boundary, *returned, *rims],
+        [info, feats, boundary, grad_hidden, grad_normed, *returned, *rims],
+        smem=1,
+        hbm=2,
     )[0]
     weights = call(
         lambda *r: final_kernel(SIDES, *r),

time: 103 us -> 85.8 us (0.83)
  local copies, waits for them, and re-layouts: 10.7 us -> 0.84 us
  starting transfers between devices: 35.8 us -> 28.8 us
    unnamed x28 -> x4, local copies, waits for them, and re-layouts: 10.6 us -> 0.66 us
    ppermute x4, starting transfers between devices: 6.25 us -> 1.45 us  [pair_permute(): return lax.ppermute(value, 'sx', pairs + [(b, a) for a, b in pairs])]
    ppermute x20, waiting for transfers between devices: 23.1 us -> 27.4 us  [xor_permute(): return lax.ppermute(value, AXES, [(i, i ^ mask) for i in range(count)])]
    ppermute x4, waiting for transfers between devices: 4.54 us -> 0.36 us  [pair_permute(): return lax.ppermute(value, 'sx', pairs + [(b, a) for a, b in pairs])]
    ppermute x20, starting transfers between devices: 29.5 us -> 27.4 us  [xor_permute(): return lax.ppermute(value, AXES, [(i, i ^ mask) for i in range(count)])]
  transfers between devices with their start and end apart: 24 -> 24, of which waited for: 15 -> 16; matrix products, arithmetic and copies ran while one was open for 0% -> 0% of each run, Pallas kernels for 1% -> 3%
where the time goes in v2:
time: 85.8 us; the launch traced here: 85.6 us
  starting transfers between devices  28.8 us (34%)
  waiting for transfers between devices  27.8 us (32%)
  Pallas kernels  27.4 us (32%)
    ppermute x20, waiting for transfers between devices, xor_permute(): return lax.ppermute(value, AXES, [(i, i ^ mask) for i in range(count)])  27.4 us
    ppermute x20, starting transfers between devices, xor_permute(): return lax.ppermute(value, AXES, [(i, i ^ mask) for i in range(count)])  27.4 us
    pallas_call x9, Pallas kernels, call(): pl.pallas_call(kernel, out_shape=[jax.ShapeDtypeStruct(s, d) for s, d in...  27.4 us
  transfers between devices with their start and end apart: 24, of which 16 were waited for; matrix products, arithmetic and copies ran while one was open for 0% of the time, Pallas kernels for 3%

profile of v2, /device:TPU:0, one launch (start us, length us, event | category | flops | bytes accessed | tf_op | source)
XLA Modules:
  0.0 85.6 jit_solution(8622624113969792227)
XLA Ops:
  0.7 0.1 stack.47.info.r_0_
  0.7 0.0 copy-start
  0.8 0.7 copy-done
  1.4 1.8 %shard_map.188 = (bf16[272,256]{1,0:T(8,128)(2,1)S(1)}, bf16[128,256]{1,0:T(8,128)(2,1)S(1)}, bf16[128,256]{1,0:T(8,128)(2,1)S(1)}) custom-call(s32[7]{0:T(128)S(1)} %stack.47.info.r_0_, s32[2]{0:T(128)S(1)} %bitcast.16, bf16[256,256]{1,0:T(8,128)(2,1)} %bitcast.18, s32[4,128]{1,0:T(4,128)} %bitcast.22), custom_call_target="tpu_custom_call" | custom-call | tf_op jit(solution)/shard_map/pallas_call | solution.py:72
  3.2 3.1 %collective-permute-start.2 = (bf16[272,256]{1,0:T(8,128)(2,1)S(1)}, bf16[272,256]{1,0:T(8,128)(2,1)S(1)}, u32[]{:S(2)}, u32[]{:S(2)}) collective-permute-start(bf16[272,256]{1,0:T(8,128)(2,1)S(1)} %get-tuple-element.63.r_14_), channel_id=1, source_target_pairs={{0,8},{1,9},{2,10},{3,11},{4,12},{5,13},{6,14},{7,15},{8,0},{9,1},... | collective-permute-start | bytes 417800 | tf_op jit(solution)/shard_map/ppermute | solution.py:61
  6.3 1.5 %collective-permute-start.1 = (bf16[272,256]{1,0:T(8,128)(2,1)S(1)}, bf16[272,256]{1,0:T(8,128)(2,1)S(1)}, u32[]{:S(2)}, u32[]{:S(2)}) collective-permute-start(bf16[272,256]{1,0:T(8,128)(2,1)S(1)} %get-tuple-element.63.r_14_), channel_id=1, source_target_pairs={{0,1},{1,0},{2,3},{3,2},{4,5},{5,4},{6,7},{7,6},{8,9},{9,8},{10,11... | collective-permute-start | bytes 417800 | tf_op jit(solution)/shard_map/ppermute | solution.py:61
  7.9 2.6 %collective-permute-start = (bf16[272,256]{1,0:T(8,128)(2,1)S(1)}, bf16[272,256]{1,0:T(8,128)(2,1)S(1)}, u32[]{:S(2)}, u32[]{:S(2)}) collective-permute-start(bf16[272,256]{1,0:T(8,128)(2,1)S(1)} %get-tuple-element.63.r_14_), channel_id=1, source_target_pairs={{0,16},{1,17},{2,18},{3,19},{4,20},{5,21},{6,22},{7,23},{8,24},{9,... | collective-permute-start | bytes 417800 | tf_op jit(solution)/shard_map/ppermute | solution.py:61
  10.4 0.0 collective-permute-start.3
  10.4 0.0 copy-start.1
  10.4 0.8 collective-permute-start.4
  11.2 0.0 copy-done.1
  11.2 0.1 copy.21.r_2_
  11.3 0.4 collective-permute-done.3.r_18_
  11.7 0.0 collective-permute-done.4.r_19_
  11.7 0.0 collective-permute-done.2.r_17_
  11.7 0.0 collective-permute-done.1.r_16_
  11.7 4.9 %collective-permute-done.r_15_ = bf16[272,256]{1,0:T(8,128)(2,1)S(1)} collective-permute-done((bf16[272,256]{1,0:T(8,128)(2,1)S(1)}, bf16[272,256]{1,0:T(8,128)(2,1)S(1)}, u32[]{:S(2)}, u32[]{:S(2)}) %collective-permute-start) | collective-permute-done | bytes 139296 | tf_op jit(solution)/shard_map/ppermute | solution.py:61
  16.6 18.1 %shard_map.189 = (bf16[256,256]{1,0:T(8,128)(2,1)}, f32[256,256]{1,0:T(8,128)S(1)}, f32[256,256]{1,0:T(8,128)S(1)}, bf16[256,256]{1,0:T(8,128)(2,1)S(1)}, bf16[2...) custom-call(s32[7]{0:T(128)S(1)} %stack.47.info.r_0_, ...), custom_call_target="tpu_custom_call" | custom-call | flops 10000000000 | bytes 8388608 | tf_op jit(solution)/shard_map/pallas_call | solution.py:72
  34.7 0.3 collective-permute-start.5
  35.0 1.7 %collective-permute-done.5.r_2_ = bf16[1024,256]{1,0:T(8,128)(2,1)S(1)} collective-permute-done((bf16[1024,256]{1,0:T(8,128)(2,1)S(1)}, bf16[1024,256]{1,0:T(8,128)(2,1)S(1)}, u32[]{:S(2)}, u32[]{:S(2)}) %collective-permute-start.5) | collective-permute-done | bytes 524320 | tf_op jit(solution)/shard_map/ppermute | solution.py:61
  36.7 0.7 shard_map.190
  37.4 0.6 collective-permute-start.6
  38.0 2.1 %collective-permute-start.7 = (bf16[256,256]{1,0:T(8,128)(2,1)S(1)}, bf16[256,256]{1,0:T(8,128)(2,1)S(1)}, u32[]{:S(2)}, u32[]{:S(2)}) collective-permute-start(bf16[256,256]{1,0:T(8,128)(2,1)S(1)} %get-tuple-element.77), channel_id=1, source_target_pairs={{0,4},{1,5},{2,6},{3,7},{4,0},{5,1},{6,2},{7,3},{8,12},{9,13},{10,... | collective-permute-start | bytes 393224 | tf_op jit(solution)/shard_map/ppermute | solution.py:61
  40.2 0.9 %collective-permute-start.8 = (bf16[256,256]{1,0:T(8,128)(2,1)S(1)}, bf16[256,256]{1,0:T(8,128)(2,1)S(1)}, u32[]{:S(2)}, u32[]{:S(2)}) collective-permute-start(bf16[256,256]{1,0:T(8,128)(2,1)S(1)} %get-tuple-element.78), channel_id=1, source_target_pairs={{0,5},{1,4},{2,7},{3,6},{4,1},{5,0},{6,3},{7,2},{8,13},{9,12},{10,... | collective-permute-start | bytes 393224 | tf_op jit(solution)/shard_map/ppermute | solution.py:61
  41.1 2.7 %collective-permute-start.9 = (bf16[256,256]{1,0:T(8,128)(2,1)S(1)}, bf16[256,256]{1,0:T(8,128)(2,1)S(1)}, u32[]{:S(2)}, u32[]{:S(2)}) collective-permute-start(bf16[256,256]{1,0:T(8,128)(2,1)S(1)} %get-tuple-element.79), channel_id=1, source_target_pairs={{0,16},{1,17},{2,18},{3,19},{4,20},{5,21},{6,22},{7,23},{8,24},{9,... | collective-permute-start | bytes 393224 | tf_op jit(solution)/shard_map/ppermute | solution.py:61
  43.9 0.2 collective-permute-start.10
  44.1 0.0 collective-permute-done.6.r_2_
  44.1 0.1 collective-permute-done.7.r_3_
  44.2 3.5 %collective-permute-done.8.r_4_ = bf16[256,256]{1,0:T(8,128)(2,1)S(1)} collective-permute-done((bf16[256,256]{1,0:T(8,128)(2,1)S(1)}, bf16[256,256]{1,0:T(8,128)(2,1)S(1)}, u32[]{:S(2)}, u32[]{:S(2)}) %collective-permute-start.8) | collective-permute-done | bytes 131104 | tf_op jit(solution)/shard_map/ppermute | solution.py:61
  47.8 2.2 %collective-permute-done.9.refs_4_ = bf16[256,256]{1,0:T(8,128)(2,1)S(1)} collective-permute-done((bf16[256,256]{1,0:T(8,128)(2,1)S(1)}, bf16[256,256]{1,0:T(8,128)(2,1)S(1)}, u32[]{:S(2)}, u32[]{:S(2)}) %collective-permute-start.9) | collective-permute-done | bytes 131104 | tf_op jit(solution)/shard_map/ppermute | solution.py:61
  50.0 0.5 collective-permute-done.10.refs_5_
  50.5 0.6 shard_map.191
  51.1 0.4 collective-permute-start.14
  51.5 0.0 collective-permute-start.15
  51.5 1.7 %collective-permute-start.11 = (bf16[64,256]{1,0:T(8,128)(2,1)S(1)}, bf16[64,256]{1,0:T(8,128)(2,1)S(1)}, u32[]{:S(2)}, u32[]{:S(2)}) collective-permute-start(bf16[64,256]{1,0:T(8,128)(2,1)S(1)} %get-tuple-element.92), channel_id=1, source_target_pairs={{0,8},{1,9},{2,10},{3,11},{4,12},{5,13},{6,14},{7,15},{8,0},{9,1},... | collective-permute-start | bytes 98312 | tf_op jit(solution)/shard_map/ppermute | solution.py:61
  53.2 1.2 %collective-permute-start.12 = (bf16[64,256]{1,0:T(8,128)(2,1)S(1)}, bf16[64,256]{1,0:T(8,128)(2,1)S(1)}, u32[]{:S(2)}, u32[]{:S(2)}) collective-permute-start(bf16[64,256]{1,0:T(8,128)(2,1)S(1)} %get-tuple-element.93), channel_id=1, source_target_pairs={{0,16},{1,17},{2,18},{3,19},{4,20},{5,21},{6,22},{7,23},{8,24},{9,... | collective-permute-start | bytes 98312 | tf_op jit(solution)/shard_map/ppermute | solution.py:61
  54.4 1.5 %collective-permute-start.13 = (bf16[64,256]{1,0:T(8,128)(2,1)S(1)}, bf16[64,256]{1,0:T(8,128)(2,1)S(1)}, u32[]{:S(2)}, u32[]{:S(2)}) collective-permute-start(bf16[64,256]{1,0:T(8,128)(2,1)S(1)} %get-tuple-element.94), channel_id=1, source_target_pairs={{0,24},{1,25},{2,26},{3,27},{4,28},{5,29},{6,30},{7,31},{8,16},{9,... | collective-permute-start | bytes 98312 | tf_op jit(solution)/shard_map/ppermute | solution.py:61
  55.9 1.7 %collective-permute-done.11.r_2_ = bf16[64,256]{1,0:T(8,128)(2,1)S(1)} collective-permute-done((bf16[64,256]{1,0:T(8,128)(2,1)S(1)}, bf16[64,256]{1,0:T(8,128)(2,1)S(1)}, u32[]{:S(2)}, u32[]{:S(2)}) %collective-permute-start.11) | collective-permute-done | bytes 32800 | tf_op jit(solution)/shard_map/ppermute | solution.py:61
  57.6 1.1 %collective-permute-done.12.r_3_ = bf16[64,256]{1,0:T(8,128)(2,1)S(1)} collective-permute-done((bf16[64,256]{1,0:T(8,128)(2,1)S(1)}, bf16[64,256]{1,0:T(8,128)(2,1)S(1)}, u32[]{:S(2)}, u32[]{:S(2)}) %collective-permute-start.12) | collective-permute-done | bytes 32800 | tf_op jit(solution)/shard_map/ppermute | solution.py:61
  58.7 1.5 %collective-permute-done.13.r_4_ = bf16[64,256]{1,0:T(8,128)(2,1)S(1)} collective-permute-done((bf16[64,256]{1,0:T(8,128)(2,1)S(1)}, bf16[64,256]{1,0:T(8,128)(2,1)S(1)}, u32[]{:S(2)}, u32[]{:S(2)}) %collective-permute-start.13) | collective-permute-done | bytes 32800 | tf_op jit(solution)/shard_map/ppermute | solution.py:61
  60.1 0.0 collective-permute-done.15.refs_7_
  60.1 0.0 collective-permute-done.14.refs_6_
  60.1 0.6 shard_map.192.r_1_
  60.7 0.7 collective-permute-start.19
  61.4 2.4 %collective-permute-start.16 = (bf16[64,256]{1,0:T(8,128)(2,1)S(1)}, bf16[64,256]{1,0:T(8,128)(2,1)S(1)}, u32[]{:S(2)}, u32[]{:S(2)}) collective-permute-start(bf16[64,256]{1,0:T(8,128)(2,1)S(1)} %shard_map.192.r_1_), channel_id=1, source_target_pairs={{0,8},{1,9},{2,10},{3,11},{4,12},{5,13},{6,14},{7,15},{8,0},{9,1},... | collective-permute-start | bytes 98312 | tf_op jit(solution)/shard_map/ppermute | solution.py:61
  63.7 1.1 %collective-permute-start.17 = (bf16[64,256]{1,0:T(8,128)(2,1)S(1)}, bf16[64,256]{1,0:T(8,128)(2,1)S(1)}, u32[]{:S(2)}, u32[]{:S(2)}) collective-permute-start(bf16[64,256]{1,0:T(8,128)(2,1)S(1)} %shard_map.192.r_1_), channel_id=1, source_target_pairs={{0,16},{1,17},{2,18},{3,19},{4,20},{5,21},{6,22},{7,23},{8,24},{9,... | collective-permute-start | bytes 98312 | tf_op jit(solution)/shard_map/ppermute | solution.py:61
  64.9 1.3 %collective-permute-start.18 = (bf16[64,256]{1,0:T(8,128)(2,1)S(1)}, bf16[64,256]{1,0:T(8,128)(2,1)S(1)}, u32[]{:S(2)}, u32[]{:S(2)}) collective-permute-start(bf16[64,256]{1,0:T(8,128)(2,1)S(1)} %shard_map.192.r_1_), channel_id=1, source_target_pairs={{0,24},{1,25},{2,26},{3,27},{4,28},{5,29},{6,30},{7,31},{8,16},{9,... | collective-permute-start | bytes 98312 | tf_op jit(solution)/shard_map/ppermute | solution.py:61
  66.2 0.1 collective-permute-done.16.r_2_
  66.2 2.5 %collective-permute-done.17.r_3_ = bf16[64,256]{1,0:T(8,128)(2,1)S(1)} collective-permute-done((bf16[64,256]{1,0:T(8,128)(2,1)S(1)}, bf16[64,256]{1,0:T(8,128)(2,1)S(1)}, u32[]{:S(2)}, u32[]{:S(2)}) %collective-permute-start.17) | collective-permute-done | bytes 32800 | tf_op jit(solution)/shard_map/ppermute | solution.py:61
  68.7 2.0 %collective-permute-done.18.r_4_ = bf16[64,256]{1,0:T(8,128)(2,1)S(1)} collective-permute-done((bf16[64,256]{1,0:T(8,128)(2,1)S(1)}, bf16[64,256]{1,0:T(8,128)(2,1)S(1)}, u32[]{:S(2)}, u32[]{:S(2)}) %collective-permute-start.18) | collective-permute-done | bytes 32800 | tf_op jit(solution)/shard_map/ppermute | solution.py:61
  70.7 0.0 collective-permute-done.19.refs_8_
  70.7 0.6 shard_map.194.r_1_
  71.2 1.6 %collective-permute-start.22 = (bf16[256,256]{1,0:T(8,128)(2,1)S(1)}, bf16[256,256]{1,0:T(8,128)(2,1)S(1)}, u32[]{:S(2)}, u32[]{:S(2)}) collective-permute-start(bf16[256,256]{1,0:T(8,128)(2,1)S(1)} %shard_map.194.r_1_), channel_id=1, source_target_pairs={{0,5},{1,4},{2,7},{3,6},{4,1},{5,0},{6,3},{7,2},{8,13},{9,12},{10,... | collective-permute-start | bytes 393224 | tf_op jit(solution)/shard_map/ppermute | solution.py:61
  72.9 0.5 collective-permute-start.21
  73.4 1.4 %collective-permute-start.20 = (bf16[256,256]{1,0:T(8,128)(2,1)S(1)}, bf16[256,256]{1,0:T(8,128)(2,1)S(1)}, u32[]{:S(2)}, u32[]{:S(2)}) collective-permute-start(bf16[256,256]{1,0:T(8,128)(2,1)S(1)} %shard_map.194.r_1_), channel_id=1, source_target_pairs={{0,1},{1,0},{2,3},{3,2},{4,5},{5,4},{6,7},{7,6},{8,9},{9,8},{10,11... | collective-permute-start | bytes 393224 | tf_op jit(solution)/shard_map/ppermute | solution.py:61
  74.8 3.8 %collective-permute-done.22.r_4_ = bf16[256,256]{1,0:T(8,128)(2,1)S(1)} collective-permute-done((bf16[256,256]{1,0:T(8,128)(2,1)S(1)}, bf16[256,256]{1,0:T(8,128)(2,1)S(1)}, u32[]{:S(2)}, u32[]{:S(2)}) %collective-permute-start.22) | collective-permute-done | bytes 131104 | tf_op jit(solution)/shard_map/ppermute | solution.py:61
  78.5 1.2 %collective-permute-done.21.r_3_ = bf16[256,256]{1,0:T(8,128)(2,1)S(1)} collective-permute-done((bf16[256,256]{1,0:T(8,128)(2,1)S(1)}, bf16[256,256]{1,0:T(8,128)(2,1)S(1)}, u32[]{:S(2)}, u32[]{:S(2)}) %collective-permute-start.21) | collective-permute-done | bytes 131104 | tf_op jit(solution)/shard_map/ppermute | solution.py:61
  79.7 0.8 collective-permute-done.20.r_2_
  80.5 0.6 shard_map.195.r_1_
  81.1 0.1 collective-permute-start.23
  81.2 2.4 %shard_map.193 = bf16[256,256]{1,0:T(8,128)(2,1)} custom-call(s32[7]{0:T(128)S(1)} %stack.47.info.r_0_, bf16[256,256]{1,0:T(8,128)(2,1)} %bitcast.20, s32[4,128]{1,0:T(4,128)} %bitcast.24, f32[256,256]{1,0:T(8,128)S(1)} %get-tuple-element.67.refs_2_, f32[256,256]{1,0:T(8,128)S(1)} %get-tuple-element.68.refs_3_, ...), custom_call_target="tpu_custom_call" | custom-call | tf_op jit(solution)/shard_map/pallas_call | solution.py:72
  83.6 0.0 collective-permute-done.23.r_2_
  83.6 1.9 %shard_map.196 = (f32[256,256]{1,0:T(8,128)}, f32[256,256]{1,0:T(8,128)}, f32[256,256]{1,0:T(8,128)}, f32[256,256]{1,0:T(8,128)}, f32[256,512]{1,0:T(8,128)}, /*index=5*/f32[512,256]{1,0:T(8,128)}) custom-call(s32[7]{0:T(128)S(1)} %stack.47.info.r_0_, bf16[1024,256]{1,0:T(8,128)(2,1)S(1)} %shard_map.195.r_1_, bf16[1024,256]{1,0:T(8,128)(2,1)S(1)} %collective-permute-done.23.r_2_), custom_call_target="tpu_custom_call" | custom-call | tf_op jit(solution)/shard_map/pallas_call | solution.py:72
Async XLA Ops:
  0.7 0.7 copy-start
  3.2 8.5 %collective-permute-start.2 = (bf16[272,256]{1,0:T(8,128)(2,1)S(1)}, bf16[272,256]{1,0:T(8,128)(2,1)S(1)}, u32[]{:S(2)}, u32[]{:S(2)}) collective-permute-start(bf16[272,256]{1,0:T(8,128)(2,1)S(1)} %get-tuple-element.63.r_14_), channel_id=1, source_target_pairs={{0,8},{1,9},{2,10},{3,11},{4,12},{5,13},{6,14},{7,15},{8,0},{9,1},... | collective-permute-start | bytes 417800 | tf_op jit(solution)/shard_map/ppermute | solution.py:61
  6.3 5.4 %collective-permute-start.1 = (bf16[272,256]{1,0:T(8,128)(2,1)S(1)}, bf16[272,256]{1,0:T(8,128)(2,1)S(1)}, u32[]{:S(2)}, u32[]{:S(2)}) collective-permute-start(bf16[272,256]{1,0:T(8,128)(2,1)S(1)} %get-tuple-element.63.r_14_), channel_id=1, source_target_pairs={{0,1},{1,0},{2,3},{3,2},{4,5},{5,4},{6,7},{7,6},{8,9},{9,8},{10,11... | collective-permute-start | bytes 417800 | tf_op jit(solution)/shard_map/ppermute | solution.py:61
  7.9 8.7 %collective-permute-start = (bf16[272,256]{1,0:T(8,128)(2,1)S(1)}, bf16[272,256]{1,0:T(8,128)(2,1)S(1)}, u32[]{:S(2)}, u32[]{:S(2)}) collective-permute-start(bf16[272,256]{1,0:T(8,128)(2,1)S(1)} %get-tuple-element.63.r_14_), channel_id=1, source_target_pairs={{0,16},{1,17},{2,18},{3,19},{4,20},{5,21},{6,22},{7,23},{8,24},{9,... | collective-permute-start | bytes 417800 | tf_op jit(solution)/shard_map/ppermute | solution.py:61
  10.4 1.3 %collective-permute-start.3 = (bf16[128,256]{1,0:T(8,128)(2,1)S(1)}, bf16[128,256]{1,0:T(8,128)(2,1)S(1)}, u32[]{:S(2)}, u32[]{:S(2)}) collective-permute-start(bf16[128,256]{1,0:T(8,128)(2,1)S(1)} %get-tuple-element.64), channel_id=1, source_target_pairs={{0,2},{4,6},{8,10},{12,14},{16,18},{20,22},{24,26},{28,30},{2,0},{... | collective-permute-start | bytes 196616 | tf_op jit(solution)/shard_map/ppermute | solution.py:51
  10.4 0.8 copy-start.1
  10.4 1.3 %collective-permute-start.4 = (bf16[128,256]{1,0:T(8,128)(2,1)S(1)}, bf16[128,256]{1,0:T(8,128)(2,1)S(1)}, u32[]{:S(2)}, u32[]{:S(2)}) collective-permute-start(bf16[128,256]{1,0:T(8,128)(2,1)S(1)} %get-tuple-element.65), channel_id=1, source_target_pairs={{2,4},{6,8},{10,12},{14,16},{18,20},{22,24},{26,28},{4,2},{8,6},{1... | collective-permute-start | bytes 196616 | tf_op jit(solution)/shard_map/ppermute | solution.py:51
  34.7 2.0 %collective-permute-start.5 = (bf16[1024,256]{1,0:T(8,128)(2,1)S(1)}, bf16[1024,256]{1,0:T(8,128)(2,1)S(1)}, u32[]{:S(2)}, u32[]{:S(2)}) collective-permute-start(bf16[1024,256]{1,0:T(8,128)(2,1)S(1)} %get-tuple-element.70), channel_id=1, source_target_pairs={{0,2},{1,3},{2,0},{3,1},{4,6},{5,7},{6,4},{7,5},{8,10},{9,11},{10,... | collective-permute-start | bytes 1572872 | tf_op jit(solution)/shard_map/ppermute | solution.py:61
  37.4 6.7 %collective-permute-start.6 = (bf16[256,256]{1,0:T(8,128)(2,1)S(1)}, bf16[256,256]{1,0:T(8,128)(2,1)S(1)}, u32[]{:S(2)}, u32[]{:S(2)}) collective-permute-start(bf16[256,256]{1,0:T(8,128)(2,1)S(1)} %get-tuple-element.76), channel_id=1, source_target_pairs={{0,1},{1,0},{2,3},{3,2},{4,5},{5,4},{6,7},{7,6},{8,9},{9,8},{10,11... | collective-permute-start | bytes 393224 | tf_op jit(solution)/shard_map/ppermute | solution.py:61
  38.0 6.2 %collective-permute-start.7 = (bf16[256,256]{1,0:T(8,128)(2,1)S(1)}, bf16[256,256]{1,0:T(8,128)(2,1)S(1)}, u32[]{:S(2)}, u32[]{:S(2)}) collective-permute-start(bf16[256,256]{1,0:T(8,128)(2,1)S(1)} %get-tuple-element.77), channel_id=1, source_target_pairs={{0,4},{1,5},{2,6},{3,7},{4,0},{5,1},{6,2},{7,3},{8,12},{9,13},{10,... | collective-permute-start | bytes 393224 | tf_op jit(solution)/shard_map/ppermute | solution.py:61
  40.2 7.6 %collective-permute-start.8 = (bf16[256,256]{1,0:T(8,128)(2,1)S(1)}, bf16[256,256]{1,0:T(8,128)(2,1)S(1)}, u32[]{:S(2)}, u32[]{:S(2)}) collective-permute-start(bf16[256,256]{1,0:T(8,128)(2,1)S(1)} %get-tuple-element.78), channel_id=1, source_target_pairs={{0,5},{1,4},{2,7},{3,6},{4,1},{5,0},{6,3},{7,2},{8,13},{9,12},{10,... | collective-permute-start | bytes 393224 | tf_op jit(solution)/shard_map/ppermute | solution.py:61
  41.1 8.9 %collective-permute-start.9 = (bf16[256,256]{1,0:T(8,128)(2,1)S(1)}, bf16[256,256]{1,0:T(8,128)(2,1)S(1)}, u32[]{:S(2)}, u32[]{:S(2)}) collective-permute-start(bf16[256,256]{1,0:T(8,128)(2,1)S(1)} %get-tuple-element.79), channel_id=1, source_target_pairs={{0,16},{1,17},{2,18},{3,19},{4,20},{5,21},{6,22},{7,23},{8,24},{9,... | collective-permute-start | bytes 393224 | tf_op jit(solution)/shard_map/ppermute | solution.py:61
  43.9 6.6 %collective-permute-start.10 = (bf16[256,256]{1,0:T(8,128)(2,1)S(1)}, bf16[256,256]{1,0:T(8,128)(2,1)S(1)}, u32[]{:S(2)}, u32[]{:S(2)}) collective-permute-start(bf16[256,256]{1,0:T(8,128)(2,1)S(1)} %get-tuple-element.80), channel_id=1, source_target_pairs={{0,1},{1,0},{2,3},{3,2},{4,5},{5,4},{6,7},{7,6},{8,9},{9,8},{10,11... | collective-permute-start | bytes 393224 | tf_op jit(solution)/shard_map/ppermute | solution.py:61
  51.1 9.0 %collective-permute-start.14 = (bf16[256,256]{1,0:T(8,128)(2,1)S(1)}, bf16[256,256]{1,0:T(8,128)(2,1)S(1)}, u32[]{:S(2)}, u32[]{:S(2)}) collective-permute-start(bf16[256,256]{1,0:T(8,128)(2,1)S(1)} %get-tuple-element.95), channel_id=1, source_target_pairs={{0,8},{1,9},{2,10},{3,11},{4,12},{5,13},{6,14},{7,15},{8,0},{9,1},... | collective-permute-start | bytes 393224 | tf_op jit(solution)/shard_map/ppermute | solution.py:61
  51.5 8.6 %collective-permute-start.15 = (bf16[128,256]{1,0:T(8,128)(2,1)S(1)}, bf16[128,256]{1,0:T(8,128)(2,1)S(1)}, u32[]{:S(2)}, u32[]{:S(2)}) collective-permute-start(bf16[128,256]{1,0:T(8,128)(2,1)S(1)} %get-tuple-element.96), channel_id=1, source_target_pairs={{0,2},{4,6},{8,10},{12,14},{16,18},{20,22},{24,26},{28,30},{2,0},{... | collective-permute-start | bytes 196616 | tf_op jit(solution)/shard_map/ppermute | solution.py:51
  51.5 6.1 %collective-permute-start.11 = (bf16[64,256]{1,0:T(8,128)(2,1)S(1)}, bf16[64,256]{1,0:T(8,128)(2,1)S(1)}, u32[]{:S(2)}, u32[]{:S(2)}) collective-permute-start(bf16[64,256]{1,0:T(8,128)(2,1)S(1)} %get-tuple-element.92), channel_id=1, source_target_pairs={{0,8},{1,9},{2,10},{3,11},{4,12},{5,13},{6,14},{7,15},{8,0},{9,1},... | collective-permute-start | bytes 98312 | tf_op jit(solution)/shard_map/ppermute | solution.py:61
  53.2 5.5 %collective-permute-start.12 = (bf16[64,256]{1,0:T(8,128)(2,1)S(1)}, bf16[64,256]{1,0:T(8,128)(2,1)S(1)}, u32[]{:S(2)}, u32[]{:S(2)}) collective-permute-start(bf16[64,256]{1,0:T(8,128)(2,1)S(1)} %get-tuple-element.93), channel_id=1, source_target_pairs={{0,16},{1,17},{2,18},{3,19},{4,20},{5,21},{6,22},{7,23},{8,24},{9,... | collective-permute-start | bytes 98312 | tf_op jit(solution)/shard_map/ppermute | solution.py:61
  54.4 5.7 %collective-permute-start.13 = (bf16[64,256]{1,0:T(8,128)(2,1)S(1)}, bf16[64,256]{1,0:T(8,128)(2,1)S(1)}, u32[]{:S(2)}, u32[]{:S(2)}) collective-permute-start(bf16[64,256]{1,0:T(8,128)(2,1)S(1)} %get-tuple-element.94), channel_id=1, source_target_pairs={{0,24},{1,25},{2,26},{3,27},{4,28},{5,29},{6,30},{7,31},{8,16},{9,... | collective-permute-start | bytes 98312 | tf_op jit(solution)/shard_map/ppermute | solution.py:61
  60.7 10.0 %collective-permute-start.19 = (bf16[128,256]{1,0:T(8,128)(2,1)S(1)}, bf16[128,256]{1,0:T(8,128)(2,1)S(1)}, u32[]{:S(2)}, u32[]{:S(2)}) collective-permute-start(bf16[128,256]{1,0:T(8,128)(2,1)S(1)} %get-tuple-element.107), channel_id=1, source_target_pairs={{2,4},{6,8},{10,12},{14,16},{18,20},{22,24},{26,28},{4,2},{8,6},{1... | collective-permute-start | bytes 196616 | tf_op jit(solution)/shard_map/ppermute | solution.py:51
  61.4 4.9 %collective-permute-start.16 = (bf16[64,256]{1,0:T(8,128)(2,1)S(1)}, bf16[64,256]{1,0:T(8,128)(2,1)S(1)}, u32[]{:S(2)}, u32[]{:S(2)}) collective-permute-start(bf16[64,256]{1,0:T(8,128)(2,1)S(1)} %shard_map.192.r_1_), channel_id=1, source_target_pairs={{0,8},{1,9},{2,10},{3,11},{4,12},{5,13},{6,14},{7,15},{8,0},{9,1},... | collective-permute-start | bytes 98312 | tf_op jit(solution)/shard_map/ppermute | solution.py:61
  63.7 5.0 %collective-permute-start.17 = (bf16[64,256]{1,0:T(8,128)(2,1)S(1)}, bf16[64,256]{1,0:T(8,128)(2,1)S(1)}, u32[]{:S(2)}, u32[]{:S(2)}) collective-permute-start(bf16[64,256]{1,0:T(8,128)(2,1)S(1)} %shard_map.192.r_1_), channel_id=1, source_target_pairs={{0,16},{1,17},{2,18},{3,19},{4,20},{5,21},{6,22},{7,23},{8,24},{9,... | collective-permute-start | bytes 98312 | tf_op jit(solution)/shard_map/ppermute | solution.py:61
  64.9 5.8 %collective-permute-start.18 = (bf16[64,256]{1,0:T(8,128)(2,1)S(1)}, bf16[64,256]{1,0:T(8,128)(2,1)S(1)}, u32[]{:S(2)}, u32[]{:S(2)}) collective-permute-start(bf16[64,256]{1,0:T(8,128)(2,1)S(1)} %shard_map.192.r_1_), channel_id=1, source_target_pairs={{0,24},{1,25},{2,26},{3,27},{4,28},{5,29},{6,30},{7,31},{8,16},{9,... | collective-permute-start | bytes 98312 | tf_op jit(solution)/shard_map/ppermute | solution.py:61
  71.2 7.3 %collective-permute-start.22 = (bf16[256,256]{1,0:T(8,128)(2,1)S(1)}, bf16[256,256]{1,0:T(8,128)(2,1)S(1)}, u32[]{:S(2)}, u32[]{:S(2)}) collective-permute-start(bf16[256,256]{1,0:T(8,128)(2,1)S(1)} %shard_map.194.r_1_), channel_id=1, source_target_pairs={{0,5},{1,4},{2,7},{3,6},{4,1},{5,0},{6,3},{7,2},{8,13},{9,12},{10,... | collective-permute-start | bytes 393224 | tf_op jit(solution)/shard_map/ppermute | solution.py:61
  72.9 6.8 %collective-permute-start.21 = (bf16[256,256]{1,0:T(8,128)(2,1)S(1)}, bf16[256,256]{1,0:T(8,128)(2,1)S(1)}, u32[]{:S(2)}, u32[]{:S(2)}) collective-permute-start(bf16[256,256]{1,0:T(8,128)(2,1)S(1)} %shard_map.194.r_1_), channel_id=1, source_target_pairs={{0,4},{1,5},{2,6},{3,7},{4,0},{5,1},{6,2},{7,3},{8,12},{9,13},{10,... | collective-permute-start | bytes 393224 | tf_op jit(solution)/shard_map/ppermute | solution.py:61
  73.4 7.1 %collective-permute-start.20 = (bf16[256,256]{1,0:T(8,128)(2,1)S(1)}, bf16[256,256]{1,0:T(8,128)(2,1)S(1)}, u32[]{:S(2)}, u32[]{:S(2)}) collective-permute-start(bf16[256,256]{1,0:T(8,128)(2,1)S(1)} %shard_map.194.r_1_), channel_id=1, source_target_pairs={{0,1},{1,0},{2,3},{3,2},{4,5},{5,4},{6,7},{7,6},{8,9},{9,8},{10,11... | collective-permute-start | bytes 393224 | tf_op jit(solution)/shard_map/ppermute | solution.py:61
  81.1 2.5 %collective-permute-start.23 = (bf16[1024,256]{1,0:T(8,128)(2,1)S(1)}, bf16[1024,256]{1,0:T(8,128)(2,1)S(1)}, u32[]{:S(2)}, u32[]{:S(2)}) collective-permute-start(bf16[1024,256]{1,0:T(8,128)(2,1)S(1)} %shard_map.195.r_1_), channel_id=1, source_target_pairs={{0,2},{1,3},{2,0},{3,1},{4,6},{5,7},{6,4},{7,5},{8,10},{9,11},{10,... | collective-permute-start | bytes 1572872 | tf_op jit(solution)/shard_map/ppermute | solution.py:61

commit v3 on v2

--- a/solution.py
+++ b/solution.py
@@ -61,14 +61,14 @@
     return lax.ppermute(value, AXES, [(i, i ^ mask) for i in range(count)])
 
 
-def call(kernel, outs, args, smem=0, hbm=0, scratch=(), limit=48, flops=0, nbytes=0):
+def call(kernel, outs, args, smem=0, hbm=0, scratch=(), limit=16, flops=0, nbytes=0):
     specs = [pl.BlockSpec(memory_space=pltpu.SMEM)] * smem
     specs += [pl.BlockSpec(memory_space=pltpu.HBM)] * hbm
     args = [pltpu.with_memory_space_constraint(a, pltpu.HBM) if smem <= i < smem + hbm else a for i, a in enumerate(args)]
     specs += [pl.BlockSpec(memory_space=pltpu.VMEM)] * (len(args) - smem - hbm)
     scratch = list(scratch)
     if hbm:
-        scratch += [pltpu.VMEM(a.shape, a.dtype) for a in args[smem : smem + hbm]] + [pltpu.SemaphoreType.DMA((hbm,))]
+        scratch += [(pltpu.SMEM if a.ndim == 1 else pltpu.VMEM)(a.shape, a.dtype) for a in args[smem : smem + hbm]] + [pltpu.SemaphoreType.DMA((hbm,))]
     return pl.pallas_call(
         kernel,
         out_shape=[jax.ShapeDtypeStruct(s, d) for s, d in outs],
@@ -97,9 +97,10 @@
     return [jnp.where(odd, first, second), jnp.where(odd, second, first), boundary[2:3, :], boundary[3:4, :]]
 
 
-def prepare_kernel(info, counts, *refs):
-    pack, rims = refs[2], refs[3:-3]
-    ready = fetched(refs[:2], refs[-3:-1], refs[-1])
+def prepare_kernel(info, *refs):
+    pack, rims = refs[3], refs[4:-4]
+    ready = fetched(refs[:3], refs[-4:-1], refs[-1])
+    counts = ready(2)
     nodes = ready(0)
     count, width = nodes.shape
     blocks = counts.shape[0]
@@ -128,98 +129,123 @@
         out[...] = tn(place, normed).astype(BF16)
 
 
-def head_rows(width, shape, dim):
+def head_rows(shape, dim):
     return iota(shape, dim) // HEAD_DIM
 
 
+def early_kernel(info, *refs):
+    copied = 6
+    ready = fetched(refs[:copied], refs[-copied - 1 : -1], refs[-1])
+    boundary, wq, wk, wv, adjacency, expander = refs[-copied - 1 : -1]
+    pack = refs[copied]
+    refs = refs[copied + 1 : -copied - 1]
+    squares, places, there = refs
+    count, width = squares.shape[1:]
+    blocks, size = adjacency.shape[0], adjacency.shape[2]
+    rim = places.shape[2]
+    normed = pack[0:count, :]
+    ready(0)
+    lines = side_lines(boundary, info[SIDES] > 0)
+    ones = jnp.ones((HEADS, rim), BF16)
+    for s in range(SIDES):
+        place = to_bf((iota((count, rim), 0) == lines[s]) & (info[s] > 0))
+        places[s] = place
+        there[s] = nt(ones, place)
+    ready(1)
+    queries = nn(normed, wq[...]).astype(BF16)
+    squares[0] = queries
+    squares[9] = flip(queries).astype(BF16)
+    for k, weight in enumerate((wk, wv)):
+        ready(2 + k)
+        squares[1 + k] = weight[...]
+        turned = flip(weight[...]).astype(BF16)
+        squares[3 + k] = turned
+        squares[5 + k] = nn(normed, weight[...]).astype(BF16)
+        squares[7 + k] = nt(turned, normed).astype(BF16)
+    ready(4)
+    ready(5)
+    flags = pack[count : count + EXTRA, :].astype(F32)[0:1, :]
+    eye = iota((size, size), 0) == iota((size, size), 1)
+    for b in range(blocks):
+        real = flags[:, b * size : (b + 1) * size] > 0.5
+        mask = ((adjacency[b] == 1) & real) | eye
+        cols = slice(b * size, (b + 1) * size)
+        squares[10, 0:size, cols] = flip(jnp.where(mask, 0.0, NEG_FILL)).astype(BF16)
+        for m in range(MATCHINGS):
+            lo = (m + 1) * size
+            squares[10 + lo // count, lo % count : lo % count + size, cols] = flip(jnp.where(expander[m, b] == 1, 0.0, NEG_FILL)).astype(BF16)
+
+
 def main_kernel(merge_y, info, counts, pairing, *refs):
-    copied = 11
+    copied = 5
     ready = fetched(refs[:copied], refs[-copied - 1 : -1], refs[-1])
-    nodes, boundary, wq, wk, wv, adjacency, expander, wo, wup, wdown, gout = refs[-copied - 1 : -1]
+    nodes, wo, wup, wdown, gout = refs[-copied - 1 : -1]
     refs = refs[copied : -copied - 1]
+    squares, places, there = refs[:3]
+    refs = refs[3:]
+    weights, weights_t, own_rows, own_cols = (squares.at[i : i + 2] for i in (1, 3, 5, 7))
     packs = refs[: MATCHINGS + 1]
     rims = refs[MATCHINGS + 1 : MATCHINGS + 1 + (2 if merge_y else 4)]
     refs = refs[MATCHINGS + 1 + len(rims) :]
-    layer_out, grad_hidden_out, grad_normed_out = refs[:3]
-    backs = refs[3 : 3 + MATCHINGS]
-    rim_outs = refs[3 + MATCHINGS : 3 + MATCHINGS + len(rims)]
-    refs = refs[3 + MATCHINGS + len(rims) :]
-    keep, send = refs[:2]
-    grads, xcat, kvg, probs, pbf, sgrad, qstack, gstack = refs[2:]
+    keep, send, kvg, moves, query_out, hidden_out, activ_out, grad_hidden_out = refs[:8]
+    grads, xcat, probs, pbf, sgrad, qstack, gstack, real_cols = refs[8:]
 
     count, width = nodes.shape
     hidden_units = wup.shape[1]
     blocks = counts.shape[0]
     size = count // blocks
     keys = (MATCHINGS + 1) * size
-    rim = boundary.shape[1]
+    rim = places.shape[2]
     scale = HEAD_DIM**-0.5
     log2e = math.log2(math.e)
 
     normed = packs[0][0:count, :]
-    ready(1)
-    lines = side_lines(boundary, info[SIDES] > 0)
+    bias = []
+    for m in range(MATCHINGS):
+        real_cols[m] = flip(packs[m + 1][count : count + EXTRA, :])
     for b in range(blocks):
         xcat[b * keys : b * keys + size, :] = packs[0][b * size : (b + 1) * size, :]
         for m in range(MATCHINGS):
             start = pl.multiple_of(pairing[m, b] * size, size)
             lo = b * keys + (m + 1) * size
             xcat[lo : lo + size, :] = packs[m + 1][pl.ds(start, size), :]
+            real = real_cols[m, pl.ds(start, size), :][:, 0:1]
+            at = (m + 1) * size
+            kept = squares[10 + at // count, at % count : at % count + size, b * size : (b + 1) * size]
+            bias.append(kept.astype(F32) + jnp.where(real > 0.5, 0.0, NEG_FILL))
     base = blocks * keys
-    places, moves = [], [None, None, None, None]
-    for s in range(SIDES):
-        here = (iota((count, rim), 0) == lines[s]) & (info[s] > 0)
-        places.append(to_bf(here))
     for s in range(SIDES):
         if merge_y and s >= 2:
             other = 3 if s == 2 else 2
             far_slots = packs[2][count : count + EXTRA, :].astype(F32)[other + 1 : other + 2, 0:rim]
             spots = to_bf(iota((count, rim), 0).astype(F32) == far_slots)
-            moves[s] = nt(places[s], spots).astype(BF16)
-            rows = nn(moves[s], packs[2][0:count, :])
+            move = nt(places[s], spots).astype(BF16)
+            moves[s - 2] = move
+            rows = nn(move, packs[2][0:count, :])
         else:
             rows = nn(places[s], rims[s][...])
         xcat[base + s * count : base + (s + 1) * count, :] = rows.astype(BF16)
 
-    for i in (2, 3, 4):
-        ready(i)
-    queries = nn(normed, wq[...]).astype(BF16)
-    queries_t = flip(queries).astype(BF16)
-    wk_t = flip(wk[...]).astype(BF16)
-    wv_t = flip(wv[...]).astype(BF16)
+    queries = squares[0]
     key_rows, key_cols, value_rows, value_cols = [], [], [], []
     for b in range(blocks):
-        rows = xcat[b * keys : (b + 1) * keys, :]
-        key_rows.append(nn(rows, wk[...]).astype(BF16))
-        value_rows.append(nn(rows, wv[...]).astype(BF16))
-        key_cols.append(nt(wk_t, rows).astype(BF16))
-        value_cols.append(nt(wv_t, rows).astype(BF16))
+        rows = xcat[b * keys + size : (b + 1) * keys, :]
+        own = slice(b * size, (b + 1) * size)
+        key_rows.append(jnp.concatenate([own_rows[0, own, :], nn(rows, weights[0]).astype(BF16)], axis=0))
+        value_rows.append(jnp.concatenate([own_rows[1, own, :], nn(rows, weights[1]).astype(BF16)], axis=0))
+        key_cols.append(jnp.concatenate([own_cols[0, :, own], nt(weights_t[0], rows).astype(BF16)], axis=1))
+        value_cols.append(jnp.concatenate([own_cols[1, :, own], nt(weights_t[1], rows).astype(BF16)], axis=1))
     rim_keys, rim_values = [], []
     for s in range(SIDES):
         rows = xcat[base + s * count : base + (s + 1) * count, :]
-        rim_keys.append(nn(rows, wk[...]).astype(BF16).astype(F32))
-        rim_values.append(nn(rows, wv[...]).astype(BF16).astype(F32))
-
-    ready(5)
-    ready(6)
-    bias = []
-    eye = iota((size, size), 0) == iota((size, size), 1)
-    for b in range(blocks):
-        parts = []
-        for g in range(MATCHINGS + 1):
-            flags = packs[g][count : count + EXTRA, :].astype(F32)[0:1, :]
-            if g == 0:
-                real = flags[:, b * size : (b + 1) * size] > 0.5
-                mask = ((adjacency[b] == 1) & real) | eye
-            else:
-                pick = flags[:, 0:size]
-                for c in range(1, blocks):
-                    pick = jnp.where(pairing[g - 1, b] == c, flags[:, c * size : (c + 1) * size], pick)
-                mask = (expander[g - 1, b] == 1) & (pick > 0.5)
-            parts.append(flip(jnp.where(mask, 0.0, NEG_FILL)))
-        bias.append(jnp.concatenate(parts, axis=0))
-
-    spread = to_bf(head_rows(width, (HEADS, width), 1) == iota((HEADS, width), 0))
+        rim_keys.append(nn(rows, weights[0]).astype(BF16).astype(F32))
+        rim_values.append(nn(rows, weights[1]).astype(BF16).astype(F32))
+    bias = [
+        jnp.concatenate([squares[10, 0:size, b * size : (b + 1) * size].astype(F32)] + bias[b * MATCHINGS : (b + 1) * MATCHINGS], axis=0)
+        for b in range(blocks)
+    ]
+
+    spread = to_bf(head_rows((HEADS, width), 1) == iota((HEADS, width), 0))
 
     def head_sums(product):
         high = product.astype(BF16)
@@ -227,21 +253,19 @@
         return nt(spread, high) + nt(spread, low)
 
     queries_f = queries.astype(F32)
-    ones = jnp.ones((HEADS, rim), BF16)
     rim_scores = []
     for s in range(SIDES):
-        there = nt(ones, places[s]) > 0.5
         score = head_sums(queries_f * rim_keys[s]) * (scale * log2e)
-        rim_scores.append(jnp.where(there, score, NEG_FILL))
+        rim_scores.append(jnp.where(there[s] > 0.5, score, NEG_FILL))
     rim_top = jnp.maximum(jnp.maximum(rim_scores[0], rim_scores[1]), jnp.maximum(rim_scores[2], rim_scores[3]))
 
-    row_head = head_rows(width, (width, size), 0)
+    row_head = head_rows((width, size), 0)
     tops, sums = [], []
     att_blocks = []
     for b in range(blocks):
         cols = slice(b * size, (b + 1) * size)
         top_rows, inv_rows, att_rows = [], [], []
-        own = queries_t[:, cols]
+        own = squares[9, :, cols]
         for first in range(0, HEADS, 2):
             pair = (first, first + 1)
             masked = [jnp.where(row_head == h, own, jnp.zeros_like(own)) for h in pair]
@@ -280,7 +304,7 @@
     for b in range(blocks):
         limit = jnp.where(slot // size == b, counts[b], limit)
     usable = jnp.where(slot % size < limit, 1.0, 0.0)
-    for i in (0, 7, 8, 9, 10):
+    for i in range(copied):
         ready(i)
     feats = nodes[...].astype(F32)
     hidden = feats + nn(attended, wo[...])
@@ -292,7 +316,8 @@
     bent = jnp.tanh(GELU_C * pre * (1.0 + GELU_A * square))
     half = 0.5 * (1.0 + bent)
     activ = (pre * half).astype(BF16)
-    layer_out[...] = ((hidden + nn(activ, wdown[...])) * usable).astype(BF16)
+    hidden_out[...] = hidden
+    activ_out[...] = activ
     upstream = gout[...].astype(F32) * usable
     upstream_bf = upstream.astype(BF16)
     grads[4 * width + hidden_units * 1 : 4 * width + 2 * hidden_units, :] = tn(activ, upstream_bf)
@@ -311,7 +336,7 @@
     grad_att_f = grad_att.astype(F32)
     grad_att_t = flip(grad_att).astype(BF16)
 
-    lane_head = head_rows(width, (size, width), 1)
+    lane_head = head_rows((size, width), 1)
     rim_dots = [head_sums(grad_att_f * rim_values[s]) for s in range(SIDES)]
     rim_inner = rim_probs[0] * rim_dots[0]
     for s in range(1, SIDES):
@@ -320,6 +345,7 @@
     for b in range(blocks):
         cols = slice(b * size, (b + 1) * size)
         inner_rows, query_rows = [], []
+        own = grad_att_t[:, cols]
         own = grad_att_t[:, cols]
         for first in range(0, HEADS, 2):
             pair = (first, first + 1)
@@ -355,18 +381,44 @@
         kvg[span, width : 2 * width] = (rim_wide[s] * grad_att_f).astype(BF16)
     query_total = query_grad.astype(BF16)
 
+    query_out[...] = query_total
+    grads[0:width, :] = tn(normed, query_total)
+    both = tn(xcat[...], kvg[...])
+    grads[width : 2 * width, :] = both[:, 0:width]
+    grads[2 * width : 3 * width, :] = both[:, width : 2 * width]
+
+    half_rows = grads.shape[0] // 2
+    mine = info[SIDES]
+    keep[...] = grads[pl.ds(pl.multiple_of(mine * half_rows, half_rows), half_rows), :]
+    send[...] = grads[pl.ds(pl.multiple_of((1 - mine) * half_rows, half_rows), half_rows), :].astype(BF16)
+
+
+def back_kernel(merge_y, counts, pairing, *refs):
+    copied = 2
+    ready = fetched(refs[:copied], refs[-copied - 1 : -1], refs[-1])
+    wq, wdown = refs[-copied - 1 : -1]
+    refs = refs[copied : -copied - 1]
+    kvg, moves, query_total, hidden, activ, places, squares = refs[:7]
+    layer_out, grad_normed_out, *rest = refs[7:]
+    backs, rim_outs, extra = rest[:MATCHINGS], rest[MATCHINGS:-1], rest[-1]
+    count, width = hidden.shape
+    blocks = counts.shape[0]
+    size = count // blocks
+    keys = (MATCHINGS + 1) * size
+    base = blocks * keys
+    wk_t, wv_t = squares[3], squares[4]
     own_rows = []
     extra_back = None
     for s in range(SIDES):
         span = slice(base + s * count, base + (s + 1) * count)
         back = (nn(kvg[span, 0:width], wk_t) + nn(kvg[span, width : 2 * width], wv_t)).astype(BF16)
         if merge_y and s >= 2:
-            moved = tn(moves[s], back)
+            moved = tn(moves[s - 2], back)
             extra_back = moved if extra_back is None else extra_back + moved
         else:
             rim_outs[s][...] = tn(places[s], back).astype(BF16)
     if merge_y:
-        grads[0:count, :] = extra_back
+        extra[...] = extra_back
     for b in range(blocks):
         span = slice(b * keys, (b + 1) * keys)
         back = nn(kvg[span, 0:width], wk_t) + nn(kvg[span, width : 2 * width], wv_t)
@@ -375,19 +427,17 @@
             start = pl.multiple_of(pairing[m, b] * size, size)
             piece = back[(m + 1) * size : (m + 2) * size]
             if merge_y and m == 1:
-                piece = piece + grads[pl.ds(start, size), :]
+                piece = piece + extra[pl.ds(start, size), :]
             backs[m][pl.ds(start, size), :] = piece.astype(BF16)
-    grad_normed_out[...] = nt(query_total, wq[...]) + jnp.concatenate(own_rows, axis=0)
-
-    grads[0:width, :] = tn(normed, query_total)
-    both = tn(xcat[...], kvg[...])
-    grads[width : 2 * width, :] = both[:, 0:width]
-    grads[2 * width : 3 * width, :] = both[:, width : 2 * width]
-
-    half_rows = grads.shape[0] // 2
-    mine = info[SIDES]
-    keep[...] = grads[pl.ds(pl.multiple_of(mine * half_rows, half_rows), half_rows), :]
-    send[...] = grads[pl.ds(pl.multiple_of((1 - mine) * half_rows, half_rows), half_rows), :].astype(BF16)
+    ready(0)
+    grad_normed_out[...] = nt(query_total[...], wq[...]) + jnp.concatenate(own_rows, axis=0)
+    slot = iota((count, width), 0)
+    limit = jnp.zeros((count, width), jnp.int32)
+    for b in range(blocks):
+        limit = jnp.where(slot // size == b, counts[b], limit)
+    usable = jnp.where(slot % size < limit, 1.0, 0.0)
+    ready(1)
+    layer_out[...] = ((hidden[...] + nn(activ[...], wdown[...])) * usable).astype(BF16)
 
 
 def nodes_kernel(info, *refs):
@@ -400,7 +450,7 @@
     rim = boundary.shape[1]
     cot = grad_normed[...]
     for back in backs:
-        cot = cot + back[...].astype(F32)
+        cot = cot + back[back.shape[0] - count :, :].astype(F32)
     for s, rows in enumerate(rims):
         place = to_bf(iota((count, rim), 0) == lines[s])
         cot = cot + nn(place, rows[...])
@@ -410,31 +460,46 @@
     out[...] = (grad_hidden[...] + factor * (cot - normed * jnp.mean(cot * normed, axis=1, keepdims=True))).astype(BF16)
 
 
-def reduce_kernel(place, parts, kept_rows, *refs):
+def lay_out(outs, values, riders):
+    for out, value, rider in zip(outs, values, riders):
+        out[0 : value.shape[0], :] = value
+        if rider is not None:
+            out[value.shape[0] :, :] = rider[...]
+
+
+def reduce_kernel(place, parts, kept_rows, riding, *refs):
     info, kept = refs[0], refs[1]
     received = refs[2 : 2 + kept_rows]
-    outs = refs[2 + kept_rows : -1]
+    count = sum(riding)
+    riders = iter(refs[2 + kept_rows : 2 + kept_rows + count])
+    riders = [next(riders) if r else None for r in riding]
+    outs = refs[2 + kept_rows + count : -1]
     total_ref = refs[-1]
+    rows = kept.shape[0]
     total = kept[...].astype(F32)
     for piece in received:
-        total = total + piece[...].astype(F32)
+        total = total + piece[0:rows, :].astype(F32)
     if parts == 1:
-        outs[0][...] = total.astype(BF16)
+        lay_out(outs, [total.astype(BF16)] * len(outs), riders)
         return
     total_ref[...] = total
-    rows = total.shape[0] // parts
+    rows = rows // parts
     mine = info[place]
     outs[0][...] = total_ref[pl.ds(pl.multiple_of(mine * rows, rows), rows), :]
-    for d in range(1, parts):
-        outs[d][...] = total_ref[pl.ds(pl.multiple_of((mine ^ d) * rows, rows), rows), :].astype(BF16)
-
-
-def gather_kernel(place, *refs):
-    info, pieces, out = refs[0], refs[1:-1], refs[-1]
+    pieces = [total_ref[pl.ds(pl.multiple_of((mine ^ d) * rows, rows), rows), :].astype(BF16) for d in range(1, parts)]
+    lay_out(outs[1:], pieces, riders)
+
+
+def gather_kernel(place, rows, parts, riding, *refs):
+    info, pieces = refs[0], refs[1 : 1 + parts]
+    count = sum(riding)
+    riders = iter(refs[1 + parts : 1 + parts + count])
+    riders = [next(riders) if r else None for r in riding]
+    outs = refs[1 + parts + count :]
     mine = info[place]
-    rows = pieces[0].shape[0]
     for d, piece in enumerate(pieces):
-        out[pl.ds(pl.multiple_of((mine ^ d) * rows, rows), rows), :] = piece[...]
+        outs[0][pl.ds(pl.multiple_of((mine ^ d) * rows, rows), rows), :] = piece[0:rows, :]
+    lay_out(outs[1:], [outs[0][...]] * (len(outs) - 1), riders[1:])
 
 
 def final_kernel(place, info, own, other, *refs):
@@ -462,55 +527,82 @@
     return sum(1 << bit for k, bit in enumerate(bits) if d >> k & 1)
 
 
-def all_sum(info, keep, arrived, groups, core_mask, riders):
+def all_sum(info, keep, arrived, groups, core_mask, late, riders, loose):
     width = keep.shape[1]
     kept, pieces = keep, [arrived]
-    riders, rode = list(riders), []
-
-    def exchange(values, masks, several):
-        batch = riders[:several]
-        del riders[:several]
-        if not batch:
-            return [xor_permute(v, m) for v, m in zip(values, masks)]
-        tied = lax.optimization_barrier((tuple(values), tuple(r[0] for r in batch)))
-        moved = [xor_permute(v, m) for v, m in zip(tied[0], masks)]
-        taken = [r[1](v) for r, v in zip(batch, tied[1])]
-        moved, taken = lax.optimization_barrier((tuple(moved), tuple(taken)))
-        rode.extend(taken)
+    extras = None
+    moved_riders, moved_loose = {}, []
+    levels = len(groups)
+
+    def carried(stage, masks):
+        found = [next((i for st, m, i in riders if st == stage and m == mask), None) for mask in masks]
+        return found, [extras[i] for i in found if i is not None]
+
+    def exchange(stage, values, masks, found):
+        batch = [(extras[i], route) for i, route in loose.get(stage, [])]
+        if batch:
+            values, arrays = lax.optimization_barrier((tuple(values), tuple(a for a, _ in batch)))
+        moved = [xor_permute(v, m) for v, m in zip(values, masks)]
+        if batch:
+            moved, taken = lax.optimization_barrier((tuple(moved), tuple(r(a) for a, (_, r) in zip(arrays, batch))))
+            moved_loose.extend(taken)
+        for i, piece in zip(found, moved):
+            if i is not None:
+                moved_riders[i] = piece
         return list(moved)
+
+    def message(rows, rider):
+        return ((rows + (0 if rider is None else extras[rider].shape[0]), width), BF16)
 
     for level, bits in enumerate(groups):
         parts = 2 ** len(bits)
         rows = kept.shape[0] // parts
-        outs = [((rows, width), F32)] + [((rows, width), BF16)] * (parts - 1)
+        masks = [offset_mask(bits, d) for d in range(1, parts)]
+        found, cargo = carried(("sum", level), masks)
         made = call(
-            lambda *r, level=level, parts=parts, n=len(pieces): reduce_kernel(SIDES + 1 + level, parts, n, *r),
-            outs,
-            [info, kept, *pieces],
+            lambda *r, level=level, parts=parts, n=len(pieces), riding=[i is not None for i in found]: reduce_kernel(
+                SIDES + 1 + level, parts, n, riding, *r
+            ),
+            [((rows, width), F32)] + [message(rows, i) for i in found],
+            [info, kept, *pieces, *cargo],
             smem=1,
             scratch=[pltpu.VMEM(kept.shape, F32)],
         )
+        if level == 0:
+            made, extras = late(made)
         kept = made[0]
-        pieces = exchange(made[1:], [offset_mask(bits, d) for d in range(1, parts)], 2)
-    whole = call(
-        lambda *r, n=len(pieces): reduce_kernel(0, 1, n, *r),
-        [(kept.shape, BF16)],
-        [info, kept, *pieces],
+        pieces = exchange(("sum", level), made[1:], masks, found)
+    masks = [offset_mask(groups[-1], d) for d in range(1, 2 ** len(groups[-1]))]
+    found, cargo = carried(("spread", levels - 1), masks)
+    riding = [None] + [i for i in found if i is not None]
+    made = call(
+        lambda *r, n=len(pieces), riding=[i is not None for i in riding]: reduce_kernel(0, 1, n, riding, *r),
+        [message(kept.shape[0], i) for i in riding],
+        [info, kept, *pieces, *cargo],
         smem=1,
         scratch=[pltpu.VMEM((8, 128), F32)],
-    )[0]
-    for level in reversed(range(len(groups))):
-        bits = groups[level]
-        parts = 2 ** len(bits)
-        masks = [offset_mask(bits, d) for d in range(1, parts)]
-        pieces = [whole] + exchange([whole] * len(masks), masks, 2 if level else len(riders))
-        whole = call(
-            lambda *r, level=level: gather_kernel(SIDES + 1 + level, *r),
-            [((whole.shape[0] * parts, width), BF16)],
-            [info, *pieces],
+    )
+    for level in reversed(range(levels)):
+        whole, laden = made[0], iter(made[1:])
+        values = [whole if i is None else next(laden) for i in found]
+        pieces = [whole] + exchange(("spread", level), values, masks, found)
+        rows = whole.shape[0]
+        found, cargo = [], []
+        if level:
+            masks_next = [offset_mask(groups[level - 1], d) for d in range(1, 2 ** len(groups[level - 1]))]
+            found, cargo = carried(("spread", level - 1), masks_next)
+        riding = [None] + [i for i in found if i is not None]
+        made = call(
+            lambda *r, level=level, rows=rows, n=len(pieces), riding=[i is not None for i in riding]: gather_kernel(
+                SIDES + 1 + level, rows, n, riding, *r
+            ),
+            [message(rows * len(pieces), i) for i in riding],
+            [info, *pieces, *cargo],
             smem=1,
-        )[0]
-    return whole, xor_permute(whole, core_mask), rode
+        )
+        masks = masks_next if level else None
+    whole = made[0]
+    return whole, xor_permute(whole, core_mask), moved_riders, moved_loose
 
 
 def shards(nodes, grad_out, w_query, w_key, w_value, w_out, w_up, w_down, counts, adjacency, expander, pairing, boundary):
@@ -538,9 +630,9 @@
     prepared = call(
         prepare_kernel,
         [((count + EXTRA, width), BF16)] + [((rim, width), BF16)] * rim_count,
-        [info, counts, feats, boundary],
-        smem=2,
-        hbm=2,
+        [info, feats, boundary, counts],
+        smem=1,
+        hbm=3,
     )
     pack, sent = prepared[0], prepared[1:]
     far = [xor_permute(pack, mask) for mask in partner]
@@ -555,40 +647,84 @@
     total_rows = 4 * width + 2 * units
     all_rows = blocks * keys + SIDES * count
     square = (count, width)
+    heads_wide = HEADS * size
+    early = call(
+        early_kernel,
+        [
+            ((10 + keys // count, *square), BF16),
+            ((SIDES, count, rim), BF16),
+            ((SIDES, HEADS, count), F32),
+        ],
+        [info, boundary, w_query, w_key, w_value, adjacency, expander, pack],
+        smem=1,
+        hbm=6,
+        flops=2 * 10**9,
+        nbytes=4 * 2**20,
+    )
+    places, squares = early[1], early[0]
+    moves_shape = (2, count, count)
     made = call(
         lambda *r: main_kernel(merge_y, *r),
-        [(square, BF16), (square, F32), (square, F32)]
-        + [(square, BF16)] * MATCHINGS
-        + [((rim, width), BF16)] * rim_count
-        + [((total_rows // 2, width), F32), ((total_rows // 2, width), BF16)],
-        [info, counts, pairing, feats, boundary, w_query, w_key, w_value, adjacency, expander, w_out, w_up, w_down, gout, pack, *far, *arrived],
+        [
+            ((total_rows // 2, width), F32),
+            ((total_rows // 2, width), BF16),
+            ((all_rows, 2 * width), BF16),
+            (moves_shape, BF16),
+            (square, BF16),
+            (square, F32),
+            ((count, units), BF16),
+            (square, F32),
+        ],
+        [info, counts, pairing, feats, w_out, w_up, w_down, gout, *early, pack, *far, *arrived],
         smem=3,
-        hbm=11,
+        hbm=5,
         scratch=[
             pltpu.VMEM((total_rows, width), F32),
             pltpu.VMEM((all_rows, width), BF16),
-            pltpu.VMEM((all_rows, 2 * width), BF16),
-            pltpu.VMEM((blocks, keys, HEADS * size), F32),
-            pltpu.VMEM((blocks, keys, HEADS * size), BF16),
-            pltpu.VMEM((blocks, keys, HEADS * size), BF16),
-            pltpu.VMEM((HEADS * size, width), BF16),
-            pltpu.VMEM((HEADS * size, width), BF16),
+            pltpu.VMEM((blocks, keys, heads_wide), F32),
+            pltpu.VMEM((blocks, keys, heads_wide), BF16),
+            pltpu.VMEM((blocks, keys, heads_wide), BF16),
+            pltpu.VMEM((heads_wide, width), BF16),
+            pltpu.VMEM((heads_wide, width), BF16),
+            pltpu.VMEM((MATCHINGS, count, EXTRA), F32),
         ],
+        limit=32,
         flops=10**10,
         nbytes=8 * 2**20,
     )
-    layer_out, grad_hidden, grad_normed = made[:3]
-    backs = made[3 : 3 + MATCHINGS]
-    rim_back = made[3 + MATCHINGS : 3 + MATCHINGS + rim_count]
-    keep, send = made[-2:]
+    keep, send, kvg, moves, query_total, hidden, activ, grad_hidden = made
+    finished = []
+
+    def late(values):
+        values, gradients = lax.optimization_barrier((tuple(values), kvg))
+        results = call(
+            lambda *r: back_kernel(merge_y, *r),
+            [(square, BF16), (square, F32)] + [(square, BF16)] * MATCHINGS + [((rim, width), BF16)] * rim_count,
+            [counts, pairing, w_query, w_down, gradients, moves, query_total, hidden, activ, places, squares],
+            smem=2,
+            hbm=2,
+            scratch=[pltpu.VMEM(square, F32)],
+            flops=2 * 10**9,
+            nbytes=4 * 2**20,
+        )
+        finished.extend(results[:2])
+        return values, results[2:]
 
     core_mask = 1 << core_bit
-    riders = [(back, lambda v, mask=mask: xor_permute(v, mask)) for back, mask in zip(backs, partner)]
-    riders += [(rim_back[0], lambda v: pair_permute(v, False)), (rim_back[1], lambda v: pair_permute(v, True))]
+    level_of = {1 << bit: level for level, bits in enumerate(groups) for bit in bits}
+    riders = [
+        (("sum" if m == 0 else "spread", level_of[mask]), mask, m) for m, mask in enumerate(partner)
+    ]
+    last = ("spread", 0)
+    routes = {("spread", len(groups) - 1): [(MATCHINGS + 1, lambda v: pair_permute(v, True))]}
+    routes.setdefault(last, []).append((MATCHINGS, lambda v: pair_permute(v, False)))
     if not merge_y:
-        riders += [(rim_back[3], lambda v: from_behind(v, "sy", 1)), (rim_back[2], lambda v: from_behind(v, "sy", -1))]
-    own, other, rode = all_sum(info, keep, xor_permute(send, core_mask), groups, core_mask, riders)
-    returned, rims = rode[:MATCHINGS], rode[MATCHINGS:]
+        routes[last].append((MATCHINGS + 3, lambda v: from_behind(v, "sy", 1)))
+        routes[last].append((MATCHINGS + 2, lambda v: from_behind(v, "sy", -1)))
+    own, other, rode, loose = all_sum(info, keep, xor_permute(send, core_mask), groups, core_mask, late, riders, routes)
+    layer_out, grad_normed = finished
+    returned = [rode[m] for m in range(MATCHINGS)]
+    rims = [loose[1], loose[0]] + list(loose[2:])
     grad_nodes = call(
         nodes_kernel,
         [(square, BF16)],

time: 85.8 us -> 84.2 us (0.981)
  Pallas kernels: 27.4 us -> 31.1 us
  waiting for transfers between devices: 27.8 us -> 24.3 us
  starting transfers between devices: 28.8 us -> 27.5 us
    ppermute x20 -> x17, waiting for transfers between devices: 27.4 us -> 23 us  [xor_permute(): return lax.ppermute(value, AXES, [(i, i ^ mask) for i in range(count)])]
    pallas_call x9 -> x11, Pallas kernels: 27.4 us -> 31.1 us  [call(): pl.pallas_call(kernel, out_shape=[jax.ShapeDtypeStruct(s, d) for s, d in...]
    ppermute x20 -> x17, starting transfers between devices: 27.4 us -> 26.2 us  [xor_permute(): return lax.ppermute(value, AXES, [(i, i ^ mask) for i in range(count)])]
    ppermute x4, waiting for transfers between devices: 0.36 us -> 1.26 us  [pair_permute(): return lax.ppermute(value, 'sx', pairs + [(b, a) for a, b in pairs])]
  transfers between devices with their start and end apart: 24 -> 21, of which waited for: 16 -> 12; matrix products, arithmetic and copies ran while one was open for 0% -> 0% of each run, Pallas kernels for 3% -> 10%
where the time goes in v3:
time: 84.2 us; the launch traced here: 83.9 us
  Pallas kernels  31.1 us (37%)
  starting transfers between devices  27.5 us (33%)
  waiting for transfers between devices  24.3 us (29%)
    pallas_call x11, Pallas kernels, call(): pl.pallas_call(kernel, out_shape=[jax.ShapeDtypeStruct(s, d) for s, d in...  31.1 us
    ppermute x17, starting transfers between devices, xor_permute(): return lax.ppermute(value, AXES, [(i, i ^ mask) for i in range(count)])  26.2 us
    ppermute x17, waiting for transfers between devices, xor_permute(): return lax.ppermute(value, AXES, [(i, i ^ mask) for i in range(count)])  23 us
  transfers between devices with their start and end apart: 21, of which 12 were waited for; matrix products, arithmetic and copies ran while one was open for 0% of the time, Pallas kernels for 10%

profile of v3, /device:TPU:0, one launch (start us, length us, event | category | flops | bytes accessed | tf_op | source)
XLA Modules:
  0.0 83.9 jit_solution(16490952843712835718)
XLA Ops:
  0.7 0.1 stack.47.info.r_0_
  0.7 1.8 %shard_map.188 = (bf16[272,256]{1,0:T(8,128)(2,1)S(1)}, bf16[128,256]{1,0:T(8,128)(2,1)S(1)}, bf16[128,256]{1,0:T(8,128)(2,1)S(1)}) custom-call(s32[7]{0:T(128)S(1)} %stack.47.info.r_0_, bf16[256,256]{1,0:T(8,128)(2,1)} %bitcast.19, s32[4,128]{1,0:T(4,128)} %bitcast.23, s32[2]{0:T(128)} %bitcast.16), custom_call_target="tpu_custom_call" | custom-call | tf_op jit(solution)/shard_map/pallas_call | solution.py:72
  2.6 3.1 %collective-permute-start.2 = (bf16[272,256]{1,0:T(8,128)(2,1)S(1)}, bf16[272,256]{1,0:T(8,128)(2,1)S(1)}, u32[]{:S(2)}, u32[]{:S(2)}) collective-permute-start(bf16[272,256]{1,0:T(8,128)(2,1)S(1)} %get-tuple-element.68.refs_6_.r_11_), channel_id=1, source_target_pairs={{0,8},{1,9},{2,10},{3,11},{4,12},{5,13},{6,14},{7,15},{8,0},{9,1},... | collective-permute-start | bytes 417800 | tf_op jit(solution)/shard_map/ppermute | solution.py:61
  5.7 1.5 %collective-permute-start.1 = (bf16[272,256]{1,0:T(8,128)(2,1)S(1)}, bf16[272,256]{1,0:T(8,128)(2,1)S(1)}, u32[]{:S(2)}, u32[]{:S(2)}) collective-permute-start(bf16[272,256]{1,0:T(8,128)(2,1)S(1)} %get-tuple-element.68.refs_6_.r_11_), channel_id=1, source_target_pairs={{0,1},{1,0},{2,3},{3,2},{4,5},{5,4},{6,7},{7,6},{8,9},{9,8},{10,11... | collective-permute-start | bytes 417800 | tf_op jit(solution)/shard_map/ppermute | solution.py:61
  7.2 2.6 %collective-permute-start = (bf16[272,256]{1,0:T(8,128)(2,1)S(1)}, bf16[272,256]{1,0:T(8,128)(2,1)S(1)}, u32[]{:S(2)}, u32[]{:S(2)}) collective-permute-start(bf16[272,256]{1,0:T(8,128)(2,1)S(1)} %get-tuple-element.68.refs_6_.r_11_), channel_id=1, source_target_pairs={{0,16},{1,17},{2,18},{3,19},{4,20},{5,21},{6,22},{7,23},{8,24},{9,... | collective-permute-start | bytes 417800 | tf_op jit(solution)/shard_map/ppermute | solution.py:61
  9.8 0.0 collective-permute-start.3
  9.8 0.7 collective-permute-start.4
  10.5 0.0 copy-start.1
  10.5 0.0 copy-start
  10.5 2.5 %shard_map.189 = (bf16[12,256,256]{2,1,0:T(8,128)(2,1)S(1)}, bf16[4,256,128]{2,1,0:T(8,128)(2,1)S(1)}, f32[4,8,256]{2,1,0:T(8,128)S(1)}) custom-call(s32[7]{0:T(128)S(1)} %stack.47.info.r_0_, s32[4,128]{1,0:T(4,128)} %bitcast.24, bf16[256,256]{1,0:T(8,128)(2,1)} %r_2_.1, bf16[256,256]{1,0:T(8,128)(2,1)} %refs_2_.1, bf16[256,256]{1,0:T(8,128)(2,1)} %refs_3_.1, ...), custom_call_target="tpu_custom_call" | custom-call | flops 2000000000 | bytes 4194304 | tf_op jit(solution)/shard_map/pallas_call | solution.py:72
  13.0 0.0 copy-done.1
  13.0 0.1 copy.22.r_2_.r_1_
  13.1 0.0 collective-permute-done.3.r_15_
  13.1 0.0 collective-permute-done.4.r_16_
  13.1 0.0 collective-permute-done.2.r_14_
  13.1 0.0 collective-permute-done.1.r_13_
  13.1 2.8 %collective-permute-done.r_12_ = bf16[272,256]{1,0:T(8,128)(2,1)S(1)} collective-permute-done((bf16[272,256]{1,0:T(8,128)(2,1)S(1)}, bf16[272,256]{1,0:T(8,128)(2,1)S(1)}, u32[]{:S(2)}, u32[]{:S(2)}) %collective-permute-start) | collective-permute-done | bytes 139296 | tf_op jit(solution)/shard_map/ppermute | solution.py:61
  15.9 0.0 copy-done
  15.9 15.6 %shard_map.190 = (f32[1024,256]{1,0:T(8,128)S(1)}, bf16[1024,256]{1,0:T(8,128)(2,1)S(1)}, bf16[2048,512]{1,0:T(8,128)(2,1)S(1)}, bf16[2,256,256]{2,1,0:T(8,128)(...) custom-call(s32[7]{0:T(128)S(1)} %stack.47.info.r_0_, ...), custom_call_target="tpu_custom_call" | custom-call | flops 10000000000 | bytes 8388608 | tf_op jit(solution)/shard_map/pallas_call | solution.py:72
  31.5 0.2 collective-permute-start.5
  31.7 1.8 %collective-permute-done.5.r_2_ = bf16[1024,256]{1,0:T(8,128)(2,1)S(1)} collective-permute-done((bf16[1024,256]{1,0:T(8,128)(2,1)S(1)}, bf16[1024,256]{1,0:T(8,128)(2,1)S(1)}, u32[]{:S(2)}, u32[]{:S(2)}) %collective-permute-start.5) | collective-permute-done | bytes 524320 | tf_op jit(solution)/shard_map/ppermute | solution.py:61
  33.5 0.9 %shard_map.191 = (f32[256,256]{1,0:T(8,128)S(1)}, bf16[256,256]{1,0:T(8,128)(2,1)S(1)}, bf16[256,256]{1,0:T(8,128)(2,1)S(1)}, bf16[256,256]{1,0:T(8,128)(2,1)S(1)}) custom-call(s32[7]{0:T(128)S(1)} %stack.47.info.r_0_, f32[1024,256]{1,0:T(8,128)S(1)} %get-tuple-element.74.r_1_, bf16[1024,256]{1,0:T(8,128)(2,1)S(1)} %collective-permute-done.5.r_2_), custom_call_target="tpu_custom_call" | custom-call | tf_op jit(solution)/shard_map/pallas_call | solution.py:72
  34.4 0.6 collective-permute-start.6
  35.1 1.9 %collective-permute-start.7 = (bf16[256,256]{1,0:T(8,128)(2,1)S(1)}, bf16[256,256]{1,0:T(8,128)(2,1)S(1)}, u32[]{:S(2)}, u32[]{:S(2)}) collective-permute-start(bf16[256,256]{1,0:T(8,128)(2,1)S(1)} %get-tuple-element.91), channel_id=1, source_target_pairs={{0,4},{1,5},{2,6},{3,7},{4,0},{5,1},{6,2},{7,3},{8,12},{9,13},{10,... | collective-permute-start | bytes 393224 | tf_op jit(solution)/shard_map/ppermute | solution.py:61
  37.0 1.0 %collective-permute-start.8 = (bf16[256,256]{1,0:T(8,128)(2,1)S(1)}, bf16[256,256]{1,0:T(8,128)(2,1)S(1)}, u32[]{:S(2)}, u32[]{:S(2)}) collective-permute-start(bf16[256,256]{1,0:T(8,128)(2,1)S(1)} %get-tuple-element.92), channel_id=1, source_target_pairs={{0,5},{1,4},{2,7},{3,6},{4,1},{5,0},{6,3},{7,2},{8,13},{9,12},{10,... | collective-permute-start | bytes 393224 | tf_op jit(solution)/shard_map/ppermute | solution.py:61
  38.0 3.6 %shard_map.192 = (bf16[256,256]{1,0:T(8,128)(2,1)}, f32[256,256]{1,0:T(8,128)S(1)}, bf16[256,256]{1,0:T(8,128)(2,1)S(1)}, bf16[256,256]{1,0:T(8,128)(2,1)S(1)}, ...) custom-call(s32[2]{0:T(128)S(1)} %bitcast.18, ...), custom_call_target="tpu_custom_call" | custom-call | flops 2000000000 | bytes 4194304 | tf_op jit(solution)/shard_map/pallas_call | solution.py:72
  41.6 0.0 collective-permute-done.6.r_2_
  41.6 0.0 collective-permute-done.7.r_3_
  41.6 2.9 %collective-permute-done.8.r_4_ = bf16[256,256]{1,0:T(8,128)(2,1)S(1)} collective-permute-done((bf16[256,256]{1,0:T(8,128)(2,1)S(1)}, bf16[256,256]{1,0:T(8,128)(2,1)S(1)}, u32[]{:S(2)}, u32[]{:S(2)}) %collective-permute-start.8) | collective-permute-done | bytes 131104 | tf_op jit(solution)/shard_map/ppermute | solution.py:61
  44.5 0.6 shard_map.193
  45.1 2.4 %collective-permute-start.9 = (bf16[320,256]{1,0:T(8,128)(2,1)S(1)}, bf16[320,256]{1,0:T(8,128)(2,1)S(1)}, u32[]{:S(2)}, u32[]{:S(2)}) collective-permute-start(bf16[320,256]{1,0:T(8,128)(2,1)S(1)} %get-tuple-element.94), channel_id=1, source_target_pairs={{0,16},{1,17},{2,18},{3,19},{4,20},{5,21},{6,22},{7,23},{8,24},{9,... | collective-permute-start | bytes 491528 | tf_op jit(solution)/shard_map/ppermute | solution.py:61
  47.6 0.7 collective-permute-start.10
  48.3 1.3 %collective-permute-start.11 = (bf16[64,256]{1,0:T(8,128)(2,1)S(1)}, bf16[64,256]{1,0:T(8,128)(2,1)S(1)}, u32[]{:S(2)}, u32[]{:S(2)}) collective-permute-start(bf16[64,256]{1,0:T(8,128)(2,1)S(1)} %get-tuple-element.97), channel_id=1, source_target_pairs={{0,24},{1,25},{2,26},{3,27},{4,28},{5,29},{6,30},{7,31},{8,16},{9,... | collective-permute-start | bytes 98312 | tf_op jit(solution)/shard_map/ppermute | solution.py:61
  49.6 2.0 %collective-permute-done.10.r_2_ = bf16[64,256]{1,0:T(8,128)(2,1)S(1)} collective-permute-done((bf16[64,256]{1,0:T(8,128)(2,1)S(1)}, bf16[64,256]{1,0:T(8,128)(2,1)S(1)}, u32[]{:S(2)}, u32[]{:S(2)}) %collective-permute-start.10) | collective-permute-done | bytes 32800 | tf_op jit(solution)/shard_map/ppermute | solution.py:61
  51.6 2.5 %collective-permute-done.11.r_4_ = bf16[64,256]{1,0:T(8,128)(2,1)S(1)} collective-permute-done((bf16[64,256]{1,0:T(8,128)(2,1)S(1)}, bf16[64,256]{1,0:T(8,128)(2,1)S(1)}, u32[]{:S(2)}, u32[]{:S(2)}) %collective-permute-start.11) | collective-permute-done | bytes 32800 | tf_op jit(solution)/shard_map/ppermute | solution.py:61
  54.1 1.9 %collective-permute-done.9.r_3_.refs_4_ = bf16[320,256]{1,0:T(8,128)(2,1)S(1)} collective-permute-done((bf16[320,256]{1,0:T(8,128)(2,1)S(1)}, bf16[320,256]{1,0:T(8,128)(2,1)S(1)}, u32[]{:S(2)}, u32[]{:S(2)}) %collective-permute-start.9) | collective-permute-done | bytes 163872 | tf_op jit(solution)/shard_map/ppermute | solution.py:61
  56.0 0.6 shard_map.194
  56.5 1.2 %collective-permute-start.12 = (bf16[320,256]{1,0:T(8,128)(2,1)S(1)}, bf16[320,256]{1,0:T(8,128)(2,1)S(1)}, u32[]{:S(2)}, u32[]{:S(2)}) collective-permute-start(bf16[320,256]{1,0:T(8,128)(2,1)S(1)} %get-tuple-element.102), channel_id=1, source_target_pairs={{0,8},{1,9},{2,10},{3,11},{4,12},{5,13},{6,14},{7,15},{8,0},{9,1},... | collective-permute-start | bytes 491528 | tf_op jit(solution)/shard_map/ppermute | solution.py:61
  57.8 0.7 collective-permute-start.15
  58.5 3.7 %collective-permute-start.13 = (bf16[64,256]{1,0:T(8,128)(2,1)S(1)}, bf16[64,256]{1,0:T(8,128)(2,1)S(1)}, u32[]{:S(2)}, u32[]{:S(2)}) collective-permute-start(bf16[64,256]{1,0:T(8,128)(2,1)S(1)} %get-tuple-element.104.r_1_), channel_id=1, source_target_pairs={{0,16},{1,17},{2,18},{3,19},{4,20},{5,21},{6,22},{7,23},{8,24},{9,... | collective-permute-start | bytes 98312 | tf_op jit(solution)/shard_map/ppermute | solution.py:61
  62.2 2.2 %collective-permute-start.14 = (bf16[64,256]{1,0:T(8,128)(2,1)S(1)}, bf16[64,256]{1,0:T(8,128)(2,1)S(1)}, u32[]{:S(2)}, u32[]{:S(2)}) collective-permute-start(bf16[64,256]{1,0:T(8,128)(2,1)S(1)} %get-tuple-element.104.r_1_), channel_id=1, source_target_pairs={{0,24},{1,25},{2,26},{3,27},{4,28},{5,29},{6,30},{7,31},{8,16},{9,... | collective-permute-start | bytes 98312 | tf_op jit(solution)/shard_map/ppermute | solution.py:61
  64.3 0.3 collective-permute-done.13.r_3_
  64.7 3.2 %collective-permute-done.14.r_4_ = bf16[64,256]{1,0:T(8,128)(2,1)S(1)} collective-permute-done((bf16[64,256]{1,0:T(8,128)(2,1)S(1)}, bf16[64,256]{1,0:T(8,128)(2,1)S(1)}, u32[]{:S(2)}, u32[]{:S(2)}) %collective-permute-start.14) | collective-permute-done | bytes 32800 | tf_op jit(solution)/shard_map/ppermute | solution.py:61
  67.9 0.0 collective-permute-done.15.refs_8_
  67.9 0.0 collective-permute-done.12.r_2_.refs_6_
  67.9 0.6 shard_map.195
  68.5 0.6 collective-permute-start.16
  69.0 0.2 collective-permute-start.17
  69.3 2.7 %collective-permute-start.18 = (bf16[256,256]{1,0:T(8,128)(2,1)S(1)}, bf16[256,256]{1,0:T(8,128)(2,1)S(1)}, u32[]{:S(2)}, u32[]{:S(2)}) collective-permute-start(bf16[256,256]{1,0:T(8,128)(2,1)S(1)} %get-tuple-element.115.r_1_), channel_id=1, source_target_pairs={{0,5},{1,4},{2,7},{3,6},{4,1},{5,0},{6,3},{7,2},{8,13},{9,12},{10,... | collective-permute-start | bytes 393224 | tf_op jit(solution)/shard_map/ppermute | solution.py:61
  72.0 0.0 collective-permute-start.19
  72.0 1.3 %collective-permute-done.19.refs_7_ = bf16[128,256]{1,0:T(8,128)(2,1)S(1)} collective-permute-done((bf16[128,256]{1,0:T(8,128)(2,1)S(1)}, bf16[128,256]{1,0:T(8,128)(2,1)S(1)}, u32[]{:S(2)}, u32[]{:S(2)}) %collective-permute-start.19) | collective-permute-done | bytes 65568 | tf_op jit(solution)/shard_map/ppermute | solution.py:51
  73.3 1.9 %collective-permute-done.17.r_3_ = bf16[256,256]{1,0:T(8,128)(2,1)S(1)} collective-permute-done((bf16[256,256]{1,0:T(8,128)(2,1)S(1)}, bf16[256,256]{1,0:T(8,128)(2,1)S(1)}, u32[]{:S(2)}, u32[]{:S(2)}) %collective-permute-start.17) | collective-permute-done | bytes 131104 | tf_op jit(solution)/shard_map/ppermute | solution.py:61
  75.2 2.1 %collective-permute-done.18.r_4_ = bf16[256,256]{1,0:T(8,128)(2,1)S(1)} collective-permute-done((bf16[256,256]{1,0:T(8,128)(2,1)S(1)}, bf16[256,256]{1,0:T(8,128)(2,1)S(1)}, u32[]{:S(2)}, u32[]{:S(2)}) %collective-permute-start.18) | collective-permute-done | bytes 131104 | tf_op jit(solution)/shard_map/ppermute | solution.py:61
  77.3 1.5 %collective-permute-done.16.refs_5_.r_2_ = bf16[512,256]{1,0:T(8,128)(2,1)S(1)} collective-permute-done((bf16[512,256]{1,0:T(8,128)(2,1)S(1)}, bf16[512,256]{1,0:T(8,128)(2,1)S(1)}, u32[]{:S(2)}, u32[]{:S(2)}) %collective-permute-start.16) | collective-permute-done | bytes 262176 | tf_op jit(solution)/shard_map/ppermute | solution.py:61
  78.8 0.6 shard_map.197.r_1_
  79.4 0.1 collective-permute-start.20
  79.5 2.4 %shard_map.196 = bf16[256,256]{1,0:T(8,128)(2,1)} custom-call(s32[7]{0:T(128)S(1)} %stack.47.info.r_0_, bf16[256,256]{1,0:T(8,128)(2,1)} %bitcast.21, s32[4,128]{1,0:T(4,128)} %bitcast.25, f32[256,256]{1,0:T(8,128)S(1)} %get-tuple-element.87.refs_2_, f32[256,256]{1,0:T(8,128)S(1)} %get-tuple-element.88.refs_3_, ...), custom_call_target="tpu_custom_call" | custom-call | tf_op jit(solution)/shard_map/pallas_call | solution.py:72
  81.9 0.0 collective-permute-done.20.r_2_
  81.9 1.9 %shard_map.198 = (f32[256,256]{1,0:T(8,128)}, f32[256,256]{1,0:T(8,128)}, f32[256,256]{1,0:T(8,128)}, f32[256,256]{1,0:T(8,128)}, f32[256,512]{1,0:T(8,128)}, /*index=5*/f32[512,256]{1,0:T(8,128)}) custom-call(s32[7]{0:T(128)S(1)} %stack.47.info.r_0_, bf16[1024,256]{1,0:T(8,128)(2,1)S(1)} %shard_map.197.r_1_, bf16[1024,256]{1,0:T(8,128)(2,1)S(1)} %collective-permute-done.20.r_2_), custom_call_target="tpu_custom_call" | custom-call | tf_op jit(solution)/shard_map/pallas_call | solution.py:72
Async XLA Ops:
  2.6 10.5 %collective-permute-start.2 = (bf16[272,256]{1,0:T(8,128)(2,1)S(1)}, bf16[272,256]{1,0:T(8,128)(2,1)S(1)}, u32[]{:S(2)}, u32[]{:S(2)}) collective-permute-start(bf16[272,256]{1,0:T(8,128)(2,1)S(1)} %get-tuple-element.68.refs_6_.r_11_), channel_id=1, source_target_pairs={{0,8},{1,9},{2,10},{3,11},{4,12},{5,13},{6,14},{7,15},{8,0},{9,1},... | collective-permute-start | bytes 417800 | tf_op jit(solution)/shard_map/ppermute | solution.py:61
  5.7 7.4 %collective-permute-start.1 = (bf16[272,256]{1,0:T(8,128)(2,1)S(1)}, bf16[272,256]{1,0:T(8,128)(2,1)S(1)}, u32[]{:S(2)}, u32[]{:S(2)}) collective-permute-start(bf16[272,256]{1,0:T(8,128)(2,1)S(1)} %get-tuple-element.68.refs_6_.r_11_), channel_id=1, source_target_pairs={{0,1},{1,0},{2,3},{3,2},{4,5},{5,4},{6,7},{7,6},{8,9},{9,8},{10,11... | collective-permute-start | bytes 417800 | tf_op jit(solution)/shard_map/ppermute | solution.py:61
  7.2 8.7 %collective-permute-start = (bf16[272,256]{1,0:T(8,128)(2,1)S(1)}, bf16[272,256]{1,0:T(8,128)(2,1)S(1)}, u32[]{:S(2)}, u32[]{:S(2)}) collective-permute-start(bf16[272,256]{1,0:T(8,128)(2,1)S(1)} %get-tuple-element.68.refs_6_.r_11_), channel_id=1, source_target_pairs={{0,16},{1,17},{2,18},{3,19},{4,20},{5,21},{6,22},{7,23},{8,24},{9,... | collective-permute-start | bytes 417800 | tf_op jit(solution)/shard_map/ppermute | solution.py:61
  9.8 3.3 %collective-permute-start.3 = (bf16[128,256]{1,0:T(8,128)(2,1)S(1)}, bf16[128,256]{1,0:T(8,128)(2,1)S(1)}, u32[]{:S(2)}, u32[]{:S(2)}) collective-permute-start(bf16[128,256]{1,0:T(8,128)(2,1)S(1)} %get-tuple-element.72), channel_id=1, source_target_pairs={{0,2},{4,6},{8,10},{12,14},{16,18},{20,22},{24,26},{28,30},{2,0},{... | collective-permute-start | bytes 196616 | tf_op jit(solution)/shard_map/ppermute | solution.py:51
  9.8 3.3 %collective-permute-start.4 = (bf16[128,256]{1,0:T(8,128)(2,1)S(1)}, bf16[128,256]{1,0:T(8,128)(2,1)S(1)}, u32[]{:S(2)}, u32[]{:S(2)}) collective-permute-start(bf16[128,256]{1,0:T(8,128)(2,1)S(1)} %get-tuple-element.73), channel_id=1, source_target_pairs={{2,4},{6,8},{10,12},{14,16},{18,20},{22,24},{26,28},{4,2},{8,6},{1... | collective-permute-start | bytes 196616 | tf_op jit(solution)/shard_map/ppermute | solution.py:51
  10.5 2.5 %copy-start.1 = (s32[1,1,3,2]{2,3,1,0:T(2,128)S(1)}, s32[1,1,3,2]{2,3,1,0:T(2,128)}, u32[]{:S(2)}) copy-start(s32[1,1,3,2]{2,3,1,0:T(2,128)} %param.24) | copy-start | bytes 76
  10.5 5.5 %copy-start = (s32[1,1,2]{2,1,0:T(1,128)S(1)}, s32[1,1,2]{2,1,0:T(1,128)}, u32[]{:S(2)}) copy-start(s32[1,1,2]{2,1,0:T(1,128)} %param.21) | copy-start | bytes 28
  31.5 2.0 %collective-permute-start.5 = (bf16[1024,256]{1,0:T(8,128)(2,1)S(1)}, bf16[1024,256]{1,0:T(8,128)(2,1)S(1)}, u32[]{:S(2)}, u32[]{:S(2)}) collective-permute-start(bf16[1024,256]{1,0:T(8,128)(2,1)S(1)} %get-tuple-element.75), channel_id=1, source_target_pairs={{0,2},{1,3},{2,0},{3,1},{4,6},{5,7},{6,4},{7,5},{8,10},{9,11},{10,... | collective-permute-start | bytes 1572872 | tf_op jit(solution)/shard_map/ppermute | solution.py:61
  34.4 7.1 %collective-permute-start.6 = (bf16[256,256]{1,0:T(8,128)(2,1)S(1)}, bf16[256,256]{1,0:T(8,128)(2,1)S(1)}, u32[]{:S(2)}, u32[]{:S(2)}) collective-permute-start(bf16[256,256]{1,0:T(8,128)(2,1)S(1)} %get-tuple-element.90), channel_id=1, source_target_pairs={{0,1},{1,0},{2,3},{3,2},{4,5},{5,4},{6,7},{7,6},{8,9},{9,8},{10,11... | collective-permute-start | bytes 393224 | tf_op jit(solution)/shard_map/ppermute | solution.py:61
  35.1 6.5 %collective-permute-start.7 = (bf16[256,256]{1,0:T(8,128)(2,1)S(1)}, bf16[256,256]{1,0:T(8,128)(2,1)S(1)}, u32[]{:S(2)}, u32[]{:S(2)}) collective-permute-start(bf16[256,256]{1,0:T(8,128)(2,1)S(1)} %get-tuple-element.91), channel_id=1, source_target_pairs={{0,4},{1,5},{2,6},{3,7},{4,0},{5,1},{6,2},{7,3},{8,12},{9,13},{10,... | collective-permute-start | bytes 393224 | tf_op jit(solution)/shard_map/ppermute | solution.py:61
  37.0 7.5 %collective-permute-start.8 = (bf16[256,256]{1,0:T(8,128)(2,1)S(1)}, bf16[256,256]{1,0:T(8,128)(2,1)S(1)}, u32[]{:S(2)}, u32[]{:S(2)}) collective-permute-start(bf16[256,256]{1,0:T(8,128)(2,1)S(1)} %get-tuple-element.92), channel_id=1, source_target_pairs={{0,5},{1,4},{2,7},{3,6},{4,1},{5,0},{6,3},{7,2},{8,13},{9,12},{10,... | collective-permute-start | bytes 393224 | tf_op jit(solution)/shard_map/ppermute | solution.py:61
  45.1 10.8 %collective-permute-start.9 = (bf16[320,256]{1,0:T(8,128)(2,1)S(1)}, bf16[320,256]{1,0:T(8,128)(2,1)S(1)}, u32[]{:S(2)}, u32[]{:S(2)}) collective-permute-start(bf16[320,256]{1,0:T(8,128)(2,1)S(1)} %get-tuple-element.94), channel_id=1, source_target_pairs={{0,16},{1,17},{2,18},{3,19},{4,20},{5,21},{6,22},{7,23},{8,24},{9,... | collective-permute-start | bytes 491528 | tf_op jit(solution)/shard_map/ppermute | solution.py:61
  47.6 4.0 %collective-permute-start.10 = (bf16[64,256]{1,0:T(8,128)(2,1)S(1)}, bf16[64,256]{1,0:T(8,128)(2,1)S(1)}, u32[]{:S(2)}, u32[]{:S(2)}) collective-permute-start(bf16[64,256]{1,0:T(8,128)(2,1)S(1)} %get-tuple-element.96), channel_id=1, source_target_pairs={{0,8},{1,9},{2,10},{3,11},{4,12},{5,13},{6,14},{7,15},{8,0},{9,1},... | collective-permute-start | bytes 98312 | tf_op jit(solution)/shard_map/ppermute | solution.py:61
  48.3 5.8 %collective-permute-start.11 = (bf16[64,256]{1,0:T(8,128)(2,1)S(1)}, bf16[64,256]{1,0:T(8,128)(2,1)S(1)}, u32[]{:S(2)}, u32[]{:S(2)}) collective-permute-start(bf16[64,256]{1,0:T(8,128)(2,1)S(1)} %get-tuple-element.97), channel_id=1, source_target_pairs={{0,24},{1,25},{2,26},{3,27},{4,28},{5,29},{6,30},{7,31},{8,16},{9,... | collective-permute-start | bytes 98312 | tf_op jit(solution)/shard_map/ppermute | solution.py:61
  56.5 11.3 %collective-permute-start.12 = (bf16[320,256]{1,0:T(8,128)(2,1)S(1)}, bf16[320,256]{1,0:T(8,128)(2,1)S(1)}, u32[]{:S(2)}, u32[]{:S(2)}) collective-permute-start(bf16[320,256]{1,0:T(8,128)(2,1)S(1)} %get-tuple-element.102), channel_id=1, source_target_pairs={{0,8},{1,9},{2,10},{3,11},{4,12},{5,13},{6,14},{7,15},{8,0},{9,1},... | collective-permute-start | bytes 491528 | tf_op jit(solution)/shard_map/ppermute | solution.py:61
  57.8 10.1 %collective-permute-start.15 = (bf16[128,256]{1,0:T(8,128)(2,1)S(1)}, bf16[128,256]{1,0:T(8,128)(2,1)S(1)}, u32[]{:S(2)}, u32[]{:S(2)}) collective-permute-start(bf16[128,256]{1,0:T(8,128)(2,1)S(1)} %get-tuple-element.105), channel_id=1, source_target_pairs={{2,4},{6,8},{10,12},{14,16},{18,20},{22,24},{26,28},{4,2},{8,6},{1... | collective-permute-start | bytes 196616 | tf_op jit(solution)/shard_map/ppermute | solution.py:51
  58.5 6.2 %collective-permute-start.13 = (bf16[64,256]{1,0:T(8,128)(2,1)S(1)}, bf16[64,256]{1,0:T(8,128)(2,1)S(1)}, u32[]{:S(2)}, u32[]{:S(2)}) collective-permute-start(bf16[64,256]{1,0:T(8,128)(2,1)S(1)} %get-tuple-element.104.r_1_), channel_id=1, source_target_pairs={{0,16},{1,17},{2,18},{3,19},{4,20},{5,21},{6,22},{7,23},{8,24},{9,... | collective-permute-start | bytes 98312 | tf_op jit(solution)/shard_map/ppermute | solution.py:61
  62.2 5.7 %collective-permute-start.14 = (bf16[64,256]{1,0:T(8,128)(2,1)S(1)}, bf16[64,256]{1,0:T(8,128)(2,1)S(1)}, u32[]{:S(2)}, u32[]{:S(2)}) collective-permute-start(bf16[64,256]{1,0:T(8,128)(2,1)S(1)} %get-tuple-element.104.r_1_), channel_id=1, source_target_pairs={{0,24},{1,25},{2,26},{3,27},{4,28},{5,29},{6,30},{7,31},{8,16},{9,... | collective-permute-start | bytes 98312 | tf_op jit(solution)/shard_map/ppermute | solution.py:61
  68.5 10.4 %collective-permute-start.16 = (bf16[512,256]{1,0:T(8,128)(2,1)S(1)}, bf16[512,256]{1,0:T(8,128)(2,1)S(1)}, u32[]{:S(2)}, u32[]{:S(2)}) collective-permute-start(bf16[512,256]{1,0:T(8,128)(2,1)S(1)} %get-tuple-element.113), channel_id=1, source_target_pairs={{0,1},{1,0},{2,3},{3,2},{4,5},{5,4},{6,7},{7,6},{8,9},{9,8},{10,11... | collective-permute-start | bytes 786440 | tf_op jit(solution)/shard_map/ppermute | solution.py:61
  69.0 6.2 %collective-permute-start.17 = (bf16[256,256]{1,0:T(8,128)(2,1)S(1)}, bf16[256,256]{1,0:T(8,128)(2,1)S(1)}, u32[]{:S(2)}, u32[]{:S(2)}) collective-permute-start(bf16[256,256]{1,0:T(8,128)(2,1)S(1)} %get-tuple-element.115.r_1_), channel_id=1, source_target_pairs={{0,4},{1,5},{2,6},{3,7},{4,0},{5,1},{6,2},{7,3},{8,12},{9,13},{10,... | collective-permute-start | bytes 393224 | tf_op jit(solution)/shard_map/ppermute | solution.py:61
  69.3 8.0 %collective-permute-start.18 = (bf16[256,256]{1,0:T(8,128)(2,1)S(1)}, bf16[256,256]{1,0:T(8,128)(2,1)S(1)}, u32[]{:S(2)}, u32[]{:S(2)}) collective-permute-start(bf16[256,256]{1,0:T(8,128)(2,1)S(1)} %get-tuple-element.115.r_1_), channel_id=1, source_target_pairs={{0,5},{1,4},{2,7},{3,6},{4,1},{5,0},{6,3},{7,2},{8,13},{9,12},{10,... | collective-permute-start | bytes 393224 | tf_op jit(solution)/shard_map/ppermute | solution.py:61
  72.0 1.3 %collective-permute-start.19 = (bf16[128,256]{1,0:T(8,128)(2,1)S(1)}, bf16[128,256]{1,0:T(8,128)(2,1)S(1)}, u32[]{:S(2)}, u32[]{:S(2)}) collective-permute-start(bf16[128,256]{1,0:T(8,128)(2,1)S(1)} %get-tuple-element.116), channel_id=1, source_target_pairs={{0,2},{4,6},{8,10},{12,14},{16,18},{20,22},{24,26},{28,30},{2,0},{... | collective-permute-start | bytes 196616 | tf_op jit(solution)/shard_map/ppermute | solution.py:51
  79.4 2.5 %collective-permute-start.20 = (bf16[1024,256]{1,0:T(8,128)(2,1)S(1)}, bf16[1024,256]{1,0:T(8,128)(2,1)S(1)}, u32[]{:S(2)}, u32[]{:S(2)}) collective-permute-start(bf16[1024,256]{1,0:T(8,128)(2,1)S(1)} %shard_map.197.r_1_), channel_id=1, source_target_pairs={{0,2},{1,3},{2,0},{3,1},{4,6},{5,7},{6,4},{7,5},{8,10},{9,11},{10,... | collective-permute-start | bytes 1572872 | tf_op jit(solution)/shard_map/ppermute | solution.py:61

commit v4 on v3

--- a/solution.py
+++ b/solution.py
@@ -184,7 +184,7 @@
     squares, places, there = refs[:3]
     refs = refs[3:]
     weights, weights_t, own_rows, own_cols = (squares.at[i : i + 2] for i in (1, 3, 5, 7))
-    packs = refs[: MATCHINGS + 1]
+    packs = [refs[0], *refs[MATCHINGS:0:-1]]
     rims = refs[MATCHINGS + 1 : MATCHINGS + 1 + (2 if merge_y else 4)]
     refs = refs[MATCHINGS + 1 + len(rims) :]
     keep, send, kvg, moves, query_out, hidden_out, activ_out, grad_hidden_out = refs[:8]
@@ -393,21 +393,16 @@
     send[...] = grads[pl.ds(pl.multiple_of((1 - mine) * half_rows, half_rows), half_rows), :].astype(BF16)
 
 
-def back_kernel(merge_y, counts, pairing, *refs):
-    copied = 2
-    ready = fetched(refs[:copied], refs[-copied - 1 : -1], refs[-1])
-    wq, wdown = refs[-copied - 1 : -1]
-    refs = refs[copied : -copied - 1]
-    kvg, moves, query_total, hidden, activ, places, squares = refs[:7]
-    layer_out, grad_normed_out, *rest = refs[7:]
+def back_kernel(merge_y, pairing, *refs):
+    kvg, moves, places, squares = refs[:4]
+    own_out, *rest = refs[4:]
     backs, rim_outs, extra = rest[:MATCHINGS], rest[MATCHINGS:-1], rest[-1]
-    count, width = hidden.shape
-    blocks = counts.shape[0]
+    count, width = own_out.shape
+    blocks = pairing.shape[1]
     size = count // blocks
     keys = (MATCHINGS + 1) * size
     base = blocks * keys
     wk_t, wv_t = squares[3], squares[4]
-    own_rows = []
     extra_back = None
     for s in range(SIDES):
         span = slice(base + s * count, base + (s + 1) * count)
@@ -422,35 +417,48 @@
     for b in range(blocks):
         span = slice(b * keys, (b + 1) * keys)
         back = nn(kvg[span, 0:width], wk_t) + nn(kvg[span, width : 2 * width], wv_t)
-        own_rows.append(back[0:size])
+        own_out[b * size : (b + 1) * size, :] = back[0:size]
         for m in range(MATCHINGS):
             start = pl.multiple_of(pairing[m, b] * size, size)
             piece = back[(m + 1) * size : (m + 2) * size]
             if merge_y and m == 1:
                 piece = piece + extra[pl.ds(start, size), :]
             backs[m][pl.ds(start, size), :] = piece.astype(BF16)
-    ready(0)
-    grad_normed_out[...] = nt(query_total[...], wq[...]) + jnp.concatenate(own_rows, axis=0)
+
+
+def output_kernel(counts, *refs):
+    copied = 4
+    ready = fetched(refs[:copied], refs[-copied - 1 : -1], refs[-1])
+    wq, wdown, nodes, boundary = refs[-copied - 1 : -1]
+    own_back, query_total, hidden, activ = refs[copied : copied + 4]
+    layer_out, grad_normed_out, nodes_out, boundary_out = refs[copied + 4 : -copied - 1]
+    count, width = hidden.shape
+    blocks = counts.shape[0]
+    size = count // blocks
     slot = iota((count, width), 0)
     limit = jnp.zeros((count, width), jnp.int32)
     for b in range(blocks):
         limit = jnp.where(slot // size == b, counts[b], limit)
     usable = jnp.where(slot % size < limit, 1.0, 0.0)
+    ready(0)
+    grad_normed_out[...] = nt(query_total[...], wq[...]) + own_back[...]
     ready(1)
     layer_out[...] = ((hidden[...] + nn(activ[...], wdown[...])) * usable).astype(BF16)
+    ready(2)
+    nodes_out[...] = nodes[...]
+    ready(3)
+    boundary_out[...] = boundary[...]
 
 
 def nodes_kernel(info, *refs):
-    ready = fetched(refs[:2], refs[-3:-1], refs[-1])
-    grad_hidden, grad_normed = refs[2:4]
-    backs, rims, out = refs[4 : 4 + MATCHINGS], refs[4 + MATCHINGS : -4], refs[-4]
-    nodes, boundary = ready(0), ready(1)
+    nodes, boundary, grad_hidden, grad_normed = refs[:4]
+    backs, rims, out = refs[4 : 4 + MATCHINGS], refs[4 + MATCHINGS : -1], refs[-1]
     lines = side_lines(boundary, info[SIDES] > 0)
     count = nodes.shape[0]
     rim = boundary.shape[1]
     cot = grad_normed[...]
     for back in backs:
-        cot = cot + back[back.shape[0] - count :, :].astype(F32)
+        cot = cot + back[...].astype(F32)
     for s, rows in enumerate(rims):
         place = to_bf(iota((count, rim), 0) == lines[s])
         cot = cot + nn(place, rows[...])
@@ -460,46 +468,29 @@
     out[...] = (grad_hidden[...] + factor * (cot - normed * jnp.mean(cot * normed, axis=1, keepdims=True))).astype(BF16)
 
 
-def lay_out(outs, values, riders):
-    for out, value, rider in zip(outs, values, riders):
-        out[0 : value.shape[0], :] = value
-        if rider is not None:
-            out[value.shape[0] :, :] = rider[...]
-
-
-def reduce_kernel(place, parts, kept_rows, riding, *refs):
-    info, kept = refs[0], refs[1]
-    received = refs[2 : 2 + kept_rows]
-    count = sum(riding)
-    riders = iter(refs[2 + kept_rows : 2 + kept_rows + count])
-    riders = [next(riders) if r else None for r in riding]
-    outs = refs[2 + kept_rows + count : -1]
-    total_ref = refs[-1]
-    rows = kept.shape[0]
+def reduce_kernel(place, parts, *refs):
+    info, kept, received = refs[0], refs[1], refs[2 : -1 - parts]
+    outs, total_ref = refs[-1 - parts : -1], refs[-1]
     total = kept[...].astype(F32)
     for piece in received:
-        total = total + piece[0:rows, :].astype(F32)
+        total = total + piece[...].astype(F32)
     if parts == 1:
-        lay_out(outs, [total.astype(BF16)] * len(outs), riders)
+        outs[0][...] = total.astype(BF16)
         return
     total_ref[...] = total
-    rows = rows // parts
+    rows = total.shape[0] // parts
     mine = info[place]
     outs[0][...] = total_ref[pl.ds(pl.multiple_of(mine * rows, rows), rows), :]
-    pieces = [total_ref[pl.ds(pl.multiple_of((mine ^ d) * rows, rows), rows), :].astype(BF16) for d in range(1, parts)]
-    lay_out(outs[1:], pieces, riders)
-
-
-def gather_kernel(place, rows, parts, riding, *refs):
-    info, pieces = refs[0], refs[1 : 1 + parts]
-    count = sum(riding)
-    riders = iter(refs[1 + parts : 1 + parts + count])
-    riders = [next(riders) if r else None for r in riding]
-    outs = refs[1 + parts + count :]
+    for d in range(1, parts):
+        outs[d][...] = total_ref[pl.ds(pl.multiple_of((mine ^ d) * rows, rows), rows), :].astype(BF16)
+
+
+def gather_kernel(place, *refs):
+    info, pieces, out = refs[0], [refs[1], *refs[-2:1:-1]], refs[-1]
     mine = info[place]
+    rows = pieces[0].shape[0]
     for d, piece in enumerate(pieces):
-        outs[0][pl.ds(pl.multiple_of((mine ^ d) * rows, rows), rows), :] = piece[0:rows, :]
-    lay_out(outs[1:], [outs[0][...]] * (len(outs) - 1), riders[1:])
+        out[pl.ds(pl.multiple_of((mine ^ d) * rows, rows), rows), :] = piece[...]
 
 
 def final_kernel(place, info, own, other, *refs):
@@ -527,82 +518,51 @@
     return sum(1 << bit for k, bit in enumerate(bits) if d >> k & 1)
 
 
-def all_sum(info, keep, arrived, groups, core_mask, late, riders, loose):
+def all_sum(info, keep, arrived, groups, core_mask, beside, store):
     width = keep.shape[1]
     kept, pieces = keep, [arrived]
-    extras = None
-    moved_riders, moved_loose = {}, []
-    levels = len(groups)
-
-    def carried(stage, masks):
-        found = [next((i for st, m, i in riders if st == stage and m == mask), None) for mask in masks]
-        return found, [extras[i] for i in found if i is not None]
-
-    def exchange(stage, values, masks, found):
-        batch = [(extras[i], route) for i, route in loose.get(stage, [])]
-        if batch:
-            values, arrays = lax.optimization_barrier((tuple(values), tuple(a for a, _ in batch)))
-        moved = [xor_permute(v, m) for v, m in zip(values, masks)]
-        if batch:
-            moved, taken = lax.optimization_barrier((tuple(moved), tuple(r(a) for a, (_, r) in zip(arrays, batch))))
-            moved_loose.extend(taken)
-        for i, piece in zip(found, moved):
-            if i is not None:
-                moved_riders[i] = piece
-        return list(moved)
-
-    def message(rows, rider):
-        return ((rows + (0 if rider is None else extras[rider].shape[0]), width), BF16)
+    stage = 0
+
+    def exchange(values, masks, whole):
+        nonlocal stage
+        work = beside.get(stage)
+        stage += 1
+        if work is None:
+            return whole, [xor_permute(v, m) for v, m in zip(values, masks)]
+        values, waited = work(tuple(values))
+        moved = [xor_permute(v, m) for v, m in zip(values[::-1], masks[::-1])][::-1]
+        moved, done = lax.optimization_barrier((tuple(moved[::-1]), waited()))
+        store.update(done)
+        return whole, list(moved[::-1])
 
     for level, bits in enumerate(groups):
         parts = 2 ** len(bits)
         rows = kept.shape[0] // parts
-        masks = [offset_mask(bits, d) for d in range(1, parts)]
-        found, cargo = carried(("sum", level), masks)
         made = call(
-            lambda *r, level=level, parts=parts, n=len(pieces), riding=[i is not None for i in found]: reduce_kernel(
-                SIDES + 1 + level, parts, n, riding, *r
-            ),
-            [((rows, width), F32)] + [message(rows, i) for i in found],
-            [info, kept, *pieces, *cargo],
+            lambda *r, level=level, parts=parts: reduce_kernel(SIDES + 1 + level, parts, *r),
+            [((rows, width), F32)] + [((rows, width), BF16)] * (parts - 1),
+            [info, kept, *pieces[::-1]],
             smem=1,
             scratch=[pltpu.VMEM(kept.shape, F32)],
         )
-        if level == 0:
-            made, extras = late(made)
-        kept = made[0]
-        pieces = exchange(("sum", level), made[1:], masks, found)
-    masks = [offset_mask(groups[-1], d) for d in range(1, 2 ** len(groups[-1]))]
-    found, cargo = carried(("spread", levels - 1), masks)
-    riding = [None] + [i for i in found if i is not None]
-    made = call(
-        lambda *r, n=len(pieces), riding=[i is not None for i in riding]: reduce_kernel(0, 1, n, riding, *r),
-        [message(kept.shape[0], i) for i in riding],
-        [info, kept, *pieces, *cargo],
+        kept, pieces = exchange(made[1:], [offset_mask(bits, d) for d in range(1, parts)], made[0])
+    whole = call(
+        lambda *r: reduce_kernel(0, 1, *r),
+        [(kept.shape, BF16)],
+        [info, kept, *pieces[::-1]],
         smem=1,
         scratch=[pltpu.VMEM((8, 128), F32)],
-    )
-    for level in reversed(range(levels)):
-        whole, laden = made[0], iter(made[1:])
-        values = [whole if i is None else next(laden) for i in found]
-        pieces = [whole] + exchange(("spread", level), values, masks, found)
-        rows = whole.shape[0]
-        found, cargo = [], []
-        if level:
-            masks_next = [offset_mask(groups[level - 1], d) for d in range(1, 2 ** len(groups[level - 1]))]
-            found, cargo = carried(("spread", level - 1), masks_next)
-        riding = [None] + [i for i in found if i is not None]
-        made = call(
-            lambda *r, level=level, rows=rows, n=len(pieces), riding=[i is not None for i in riding]: gather_kernel(
-                SIDES + 1 + level, rows, n, riding, *r
-            ),
-            [message(rows * len(pieces), i) for i in riding],
-            [info, *pieces, *cargo],
+    )[0]
+    for level in reversed(range(len(groups))):
+        masks = [offset_mask(groups[level], d) for d in range(1, 2 ** len(groups[level]))]
+        whole, pieces = exchange([whole] * len(masks), masks, whole)
+        whole = call(
+            lambda *r, level=level: gather_kernel(SIDES + 1 + level, *r),
+            [((whole.shape[0] * (1 + len(masks)), width), BF16)],
+            [info, whole, *pieces[::-1]],
             smem=1,
-        )
-        masks = masks_next if level else None
-    whole = made[0]
-    return whole, xor_permute(whole, core_mask), moved_riders, moved_loose
+        )[0]
+    return whole, xor_permute(whole, core_mask)
 
 
 def shards(nodes, grad_out, w_query, w_key, w_value, w_out, w_up, w_down, counts, adjacency, expander, pairing, boundary):
@@ -635,10 +595,10 @@
         hbm=3,
     )
     pack, sent = prepared[0], prepared[1:]
-    far = [xor_permute(pack, mask) for mask in partner]
     arrived = [pair_permute(sent[0], False), pair_permute(sent[1], True)]
     if not merge_y:
         arrived += [from_behind(sent[3], "sy", 1), from_behind(sent[2], "sy", -1)]
+    far = [xor_permute(pack, mask) for mask in reversed(partner)][::-1]
 
     blocks = counts.shape[0]
     size = count // blocks
@@ -675,7 +635,7 @@
             ((count, units), BF16),
             (square, F32),
         ],
-        [info, counts, pairing, feats, w_out, w_up, w_down, gout, *early, pack, *far, *arrived],
+        [info, counts, pairing, feats, w_out, w_up, w_down, gout, *early, pack, *far[::-1], *arrived],
         smem=3,
         hbm=5,
         scratch=[
@@ -693,44 +653,73 @@
         nbytes=8 * 2**20,
     )
     keep, send, kvg, moves, query_total, hidden, activ, grad_hidden = made
-    finished = []
-
-    def late(values):
-        values, gradients = lax.optimization_barrier((tuple(values), kvg))
-        results = call(
+    store = {}
+
+    def first_stage(values):
+        values, gradients = lax.optimization_barrier((values, kvg))
+        store["back"] = call(
             lambda *r: back_kernel(merge_y, *r),
-            [(square, BF16), (square, F32)] + [(square, BF16)] * MATCHINGS + [((rim, width), BF16)] * rim_count,
-            [counts, pairing, w_query, w_down, gradients, moves, query_total, hidden, activ, places, squares],
-            smem=2,
-            hbm=2,
+            [(square, F32)] + [(square, BF16)] * MATCHINGS + [((rim, width), BF16)] * rim_count,
+            [pairing, gradients, moves, places, squares],
+            smem=1,
             scratch=[pltpu.VMEM(square, F32)],
             flops=2 * 10**9,
             nbytes=4 * 2**20,
         )
-        finished.extend(results[:2])
-        return values, results[2:]
+
+        def waited():
+            back = store["back"]
+            store["m0"] = xor_permute(back[1], partner[0])
+            store["m2"] = xor_permute(back[3], partner[2])
+            return {}
+
+        return values, waited
+
+    def second_stage(values):
+        back = store["back"]
+        values, own_back = lax.optimization_barrier((values, back[0]))
+        store["out"] = call(
+            output_kernel,
+            [(square, BF16), (square, F32), (square, BF16), (boundary.shape, boundary.dtype)],
+            [counts, w_query, w_down, feats, boundary, own_back, query_total, hidden, activ],
+            smem=1,
+            hbm=4,
+            flops=10**9,
+            nbytes=2 * 2**20,
+        )
+
+        def waited():
+            cargo = [back[2], *back[4:]]
+            grad_normed, cargo = lax.optimization_barrier((store["out"][1], tuple(cargo)))
+            store["grad_normed"] = grad_normed
+            m1, near, beyond, *sides = cargo
+            store["m1"] = xor_permute(m1, partner[1])
+            store["rims"] = [pair_permute(near, False), pair_permute(beyond, True)]
+            if sides:
+                store["rims"] += [from_behind(sides[1], "sy", 1), from_behind(sides[0], "sy", -1)]
+            return {}
+
+        return values, waited
+
+    def third_stage(values):
+        return values, lambda: {"m0": store["m0"], "m2": store["m2"]}
+
+    def fourth_stage(values):
+        return values, lambda: {"m1": store["m1"], "rims": store["rims"]}
 
     core_mask = 1 << core_bit
-    level_of = {1 << bit: level for level, bits in enumerate(groups) for bit in bits}
-    riders = [
-        (("sum" if m == 0 else "spread", level_of[mask]), mask, m) for m, mask in enumerate(partner)
-    ]
-    last = ("spread", 0)
-    routes = {("spread", len(groups) - 1): [(MATCHINGS + 1, lambda v: pair_permute(v, True))]}
-    routes.setdefault(last, []).append((MATCHINGS, lambda v: pair_permute(v, False)))
-    if not merge_y:
-        routes[last].append((MATCHINGS + 3, lambda v: from_behind(v, "sy", 1)))
-        routes[last].append((MATCHINGS + 2, lambda v: from_behind(v, "sy", -1)))
-    own, other, rode, loose = all_sum(info, keep, xor_permute(send, core_mask), groups, core_mask, late, riders, routes)
-    layer_out, grad_normed = finished
-    returned = [rode[m] for m in range(MATCHINGS)]
-    rims = [loose[1], loose[0]] + list(loose[2:])
+    own, other = all_sum(
+        info, keep, xor_permute(send, core_mask), groups, core_mask, {0: first_stage, 1: second_stage, 2: third_stage, 3: fourth_stage}, store
+    )
+    layer_out, _, nodes_near, boundary_near = store["out"]
+    grad_normed = store["grad_normed"]
+    returned = [store["m0"], store["m1"], store["m2"]]
+    rims = store["rims"]
     grad_nodes = call(
         nodes_kernel,
         [(square, BF16)],
-        [info, feats, boundary, grad_hidden, grad_normed, *returned, *rims],
+        [info, nodes_near, boundary_near, grad_hidden, grad_normed, *returned, *rims],
         smem=1,
-        hbm=2,
     )[0]
     weights = call(
         lambda *r: final_kernel(SIDES, *r),

time: 84.2 us -> 76.5 us (0.909)
  waiting for transfers between devices: 24.3 us -> 13.3 us
  starting transfers between devices: 27.5 us -> 30.9 us
    ppermute x17 -> x20, waiting for transfers between devices: 23 us -> 13.3 us  [xor_permute(): return lax.ppermute(value, AXES, [(i, i ^ mask) for i in range(count)])]
    ppermute x17 -> x20, starting transfers between devices: 26.2 us -> 29.5 us  [xor_permute(): return lax.ppermute(value, AXES, [(i, i ^ mask) for i in range(count)])]
    ppermute x4, waiting for transfers between devices: 1.26 us -> 0.01 us  [pair_permute(): return lax.ppermute(value, 'sx', pairs + [(b, a) for a, b in pairs])]
    pallas_call x11 -> x12, Pallas kernels: 31.1 us -> 31.1 us  [call(): pl.pallas_call(kernel, out_shape=[jax.ShapeDtypeStruct(s, d) for s, d in...]
  transfers between devices with their start and end apart: 21 -> 24, of which waited for: 12 -> 8; matrix products, arithmetic and copies ran while one was open for 0% -> 0% of each run, Pallas kernels for 10% -> 13%
where the time goes in v4:
time: 76.5 us; the launch traced here: 76.3 us
  Pallas kernels  31.1 us (41%)
  starting transfers between devices  30.9 us (40%)
  waiting for transfers between devices  13.3 us (17%)
  between operations  0.84 us (1%)
    pallas_call x12, Pallas kernels, call(): pl.pallas_call(kernel, out_shape=[jax.ShapeDtypeStruct(s, d) for s, d in...  31.1 us
    ppermute x20, starting transfers between devices, xor_permute(): return lax.ppermute(value, AXES, [(i, i ^ mask) for i in range(count)])  29.5 us
    ppermute x20, waiting for transfers between devices, xor_permute(): return lax.ppermute(value, AXES, [(i, i ^ mask) for i in range(count)])  13.3 us
  transfers between devices with their start and end apart: 24, of which 8 were waited for; matrix products, arithmetic and copies ran while one was open for 0% of the time, Pallas kernels for 13%

profile of v4, /device:TPU:0, one launch (start us, length us, event | category | flops | bytes accessed | tf_op | source)
XLA Modules:
  0.0 76.3 jit_solution(2468289516106153491)
XLA Ops:
  0.7 0.1 stack.47.info.r_0_
  0.7 1.8 %shard_map.188 = (bf16[272,256]{1,0:T(8,128)(2,1)S(1)}, bf16[128,256]{1,0:T(8,128)(2,1)S(1)}, bf16[128,256]{1,0:T(8,128)(2,1)S(1)}) custom-call(s32[7]{0:T(128)S(1)} %stack.47.info.r_0_, bf16[256,256]{1,0:T(8,128)(2,1)} %bitcast.20, s32[4,128]{1,0:T(4,128)} %bitcast.23, s32[2]{0:T(128)} %bitcast.16), custom_call_target="tpu_custom_call" | custom-call | tf_op jit(solution)/shard_map/pallas_call | solution.py:72
  2.6 4.1 %collective-permute-start.2 = (bf16[272,256]{1,0:T(8,128)(2,1)S(1)}, bf16[272,256]{1,0:T(8,128)(2,1)S(1)}, u32[]{:S(2)}, u32[]{:S(2)}) collective-permute-start(bf16[272,256]{1,0:T(8,128)(2,1)S(1)} %get-tuple-element.75.refs_6_.r_11_), channel_id=1, source_target_pairs={{0,16},{1,17},{2,18},{3,19},{4,20},{5,21},{6,22},{7,23},{8,24},{9,... | collective-permute-start | bytes 417800 | tf_op jit(solution)/shard_map/ppermute | solution.py:61
  6.7 1.5 %collective-permute-start.1 = (bf16[272,256]{1,0:T(8,128)(2,1)S(1)}, bf16[272,256]{1,0:T(8,128)(2,1)S(1)}, u32[]{:S(2)}, u32[]{:S(2)}) collective-permute-start(bf16[272,256]{1,0:T(8,128)(2,1)S(1)} %get-tuple-element.75.refs_6_.r_11_), channel_id=1, source_target_pairs={{0,1},{1,0},{2,3},{3,2},{4,5},{5,4},{6,7},{7,6},{8,9},{9,8},{10,11... | collective-permute-start | bytes 417800 | tf_op jit(solution)/shard_map/ppermute | solution.py:61
  8.2 1.6 %collective-permute-start = (bf16[272,256]{1,0:T(8,128)(2,1)S(1)}, bf16[272,256]{1,0:T(8,128)(2,1)S(1)}, u32[]{:S(2)}, u32[]{:S(2)}) collective-permute-start(bf16[272,256]{1,0:T(8,128)(2,1)S(1)} %get-tuple-element.75.refs_6_.r_11_), channel_id=1, source_target_pairs={{0,8},{1,9},{2,10},{3,11},{4,12},{5,13},{6,14},{7,15},{8,0},{9,1},... | collective-permute-start | bytes 417800 | tf_op jit(solution)/shard_map/ppermute | solution.py:61
  9.8 0.0 collective-permute-start.3
  9.8 0.7 collective-permute-start.4
  10.5 0.0 copy-start.1
  10.5 0.0 copy-start
  10.5 2.5 %shard_map.189 = (bf16[12,256,256]{2,1,0:T(8,128)(2,1)S(1)}, bf16[4,256,128]{2,1,0:T(8,128)(2,1)S(1)}, f32[4,8,256]{2,1,0:T(8,128)S(1)}) custom-call(s32[7]{0:T(128)S(1)} %stack.47.info.r_0_, s32[4,128]{1,0:T(4,128)} %bitcast.24, bf16[256,256]{1,0:T(8,128)(2,1)} %refs_0_.1, bf16[256,256]{1,0:T(8,128)(2,1)} %refs_2_.1, bf16[256,256]{1,0:T(8,128)(2,1)} %refs_3_.1, ...), custom_call_target="tpu_custom_call" | custom-call | flops 2000000000 | bytes 4194304 | tf_op jit(solution)/shard_map/pallas_call | solution.py:72
  13.0 0.1 copy.21.r_2_.r_0_
  13.1 0.0 collective-permute-done.3.r_15_
  13.1 0.0 collective-permute-done.4.r_16_
  13.1 0.4 collective-permute-done.2.r_14_
  13.5 0.0 collective-permute-done.1.r_13_
  13.5 1.4 %collective-permute-done.r_12_ = bf16[272,256]{1,0:T(8,128)(2,1)S(1)} collective-permute-done((bf16[272,256]{1,0:T(8,128)(2,1)S(1)}, bf16[272,256]{1,0:T(8,128)(2,1)S(1)}, u32[]{:S(2)}, u32[]{:S(2)}) %collective-permute-start) | collective-permute-done | bytes 139296 | tf_op jit(solution)/shard_map/ppermute | solution.py:61
  14.9 15.6 %shard_map.190 = (f32[1024,256]{1,0:T(8,128)S(1)}, bf16[1024,256]{1,0:T(8,128)(2,1)S(1)}, bf16[2048,512]{1,0:T(8,128)(2,1)S(1)}, bf16[2,256,256]{2,1,0:T(8,128)(...) custom-call(s32[7]{0:T(128)S(1)} %stack.47.info.r_0_, ...), custom_call_target="tpu_custom_call" | custom-call | flops 10000000000 | bytes 8388608 | tf_op jit(solution)/shard_map/pallas_call | solution.py:72
  30.5 1.2 %collective-permute-start.5 = (bf16[1024,256]{1,0:T(8,128)(2,1)S(1)}, bf16[1024,256]{1,0:T(8,128)(2,1)S(1)}, u32[]{:S(2)}, u32[]{:S(2)}) collective-permute-start(bf16[1024,256]{1,0:T(8,128)(2,1)S(1)} %get-tuple-element.82), channel_id=1, source_target_pairs={{0,2},{1,3},{2,0},{3,1},{4,6},{5,7},{6,4},{7,5},{8,10},{9,11},{10,... | collective-permute-start | bytes 1572872 | tf_op jit(solution)/shard_map/ppermute | solution.py:61
  31.7 1.5 %collective-permute-done.5.r_2_ = bf16[1024,256]{1,0:T(8,128)(2,1)S(1)} collective-permute-done((bf16[1024,256]{1,0:T(8,128)(2,1)S(1)}, bf16[1024,256]{1,0:T(8,128)(2,1)S(1)}, u32[]{:S(2)}, u32[]{:S(2)}) %collective-permute-start.5) | collective-permute-done | bytes 524320 | tf_op jit(solution)/shard_map/ppermute | solution.py:61
  33.2 0.9 %shard_map.191 = (f32[256,256]{1,0:T(8,128)S(1)}, bf16[256,256]{1,0:T(8,128)(2,1)S(1)}, bf16[256,256]{1,0:T(8,128)(2,1)S(1)}, bf16[256,256]{1,0:T(8,128)(2,1)S(1)}) custom-call(s32[7]{0:T(128)S(1)} %stack.47.info.r_0_, f32[1024,256]{1,0:T(8,128)S(1)} %get-tuple-element.81.r_1_, bf16[1024,256]{1,0:T(8,128)(2,1)S(1)} %collective-permute-done.5.r_2_), custom_call_target="tpu_custom_call" | custom-call | tf_op jit(solution)/shard_map/pallas_call | solution.py:72
  34.1 2.3 %collective-permute-start.6 = (bf16[256,256]{1,0:T(8,128)(2,1)S(1)}, bf16[256,256]{1,0:T(8,128)(2,1)S(1)}, u32[]{:S(2)}, u32[]{:S(2)}) collective-permute-start(bf16[256,256]{1,0:T(8,128)(2,1)S(1)} %get-tuple-element.88), channel_id=1, source_target_pairs={{0,5},{1,4},{2,7},{3,6},{4,1},{5,0},{6,3},{7,2},{8,13},{9,12},{10,... | collective-permute-start | bytes 393224 | tf_op jit(solution)/shard_map/ppermute | solution.py:61
  36.4 0.1 collective-permute-start.7
  36.6 1.4 %collective-permute-start.8 = (bf16[256,256]{1,0:T(8,128)(2,1)S(1)}, bf16[256,256]{1,0:T(8,128)(2,1)S(1)}, u32[]{:S(2)}, u32[]{:S(2)}) collective-permute-start(bf16[256,256]{1,0:T(8,128)(2,1)S(1)} %get-tuple-element.90), channel_id=1, source_target_pairs={{0,1},{1,0},{2,3},{3,2},{4,5},{5,4},{6,7},{7,6},{8,9},{9,8},{10,11... | collective-permute-start | bytes 393224 | tf_op jit(solution)/shard_map/ppermute | solution.py:61
  38.0 1.8 %shard_map.193 = (f32[256,256]{1,0:T(8,128)S(1)}, bf16[256,256]{1,0:T(8,128)(2,1)S(1)}, bf16[256,256]{1,0:T(8,128)(2,1)S(1)}, bf16[256,256]{1,0:T(8,128)(2,1)S(1...) custom-call(s32[3,2]{1,0:T(4,128)S(1)} %copy.21.r_2_.r_0_, bf16[2048,512]{1,0:T(8,128)(2,1)S(1)} %get-tuple-element.97.r_1_, ...), custom_call_target="tpu_custom_call" | custom-call | flops 2000000000 | bytes 4194304 | tf_op jit(solution)/shard_map/pallas_call | solution.py:72
  39.8 1.8 %collective-permute-start.15 = (bf16[256,256]{1,0:T(8,128)(2,1)S(1)}, bf16[256,256]{1,0:T(8,128)(2,1)S(1)}, u32[]{:S(2)}, u32[]{:S(2)}) collective-permute-start(bf16[256,256]{1,0:T(8,128)(2,1)S(1)} %get-tuple-element.120), channel_id=1, source_target_pairs={{0,16},{1,17},{2,18},{3,19},{4,20},{5,21},{6,22},{7,23},{8,24},{9,... | collective-permute-start | bytes 393224 | tf_op jit(solution)/shard_map/ppermute | solution.py:61
  41.6 2.0 %collective-permute-start.16 = (bf16[256,256]{1,0:T(8,128)(2,1)S(1)}, bf16[256,256]{1,0:T(8,128)(2,1)S(1)}, u32[]{:S(2)}, u32[]{:S(2)}) collective-permute-start(bf16[256,256]{1,0:T(8,128)(2,1)S(1)} %get-tuple-element.121), channel_id=1, source_target_pairs={{0,8},{1,9},{2,10},{3,11},{4,12},{5,13},{6,14},{7,15},{8,0},{9,1},... | collective-permute-start | bytes 393224 | tf_op jit(solution)/shard_map/ppermute | solution.py:61
  43.7 0.0 collective-permute-done.6.r_2_
  43.7 0.0 collective-permute-done.7.r_3_
  43.7 0.0 collective-permute-done.8.r_4_
  43.7 0.6 shard_map.192
  44.3 3.3 %collective-permute-start.9 = (bf16[64,256]{1,0:T(8,128)(2,1)S(1)}, bf16[64,256]{1,0:T(8,128)(2,1)S(1)}, u32[]{:S(2)}, u32[]{:S(2)}) collective-permute-start(bf16[64,256]{1,0:T(8,128)(2,1)S(1)} %get-tuple-element.114), channel_id=1, source_target_pairs={{0,24},{1,25},{2,26},{3,27},{4,28},{5,29},{6,30},{7,31},{8,16},{9,... | collective-permute-start | bytes 98312 | tf_op jit(solution)/shard_map/ppermute | solution.py:61
  47.7 0.0 collective-permute-start.10
  47.7 1.1 %collective-permute-start.11 = (bf16[64,256]{1,0:T(8,128)(2,1)S(1)}, bf16[64,256]{1,0:T(8,128)(2,1)S(1)}, u32[]{:S(2)}, u32[]{:S(2)}) collective-permute-start(bf16[64,256]{1,0:T(8,128)(2,1)S(1)} %get-tuple-element.116), channel_id=1, source_target_pairs={{0,8},{1,9},{2,10},{3,11},{4,12},{5,13},{6,14},{7,15},{8,0},{9,1},... | collective-permute-start | bytes 98312 | tf_op jit(solution)/shard_map/ppermute | solution.py:61
  48.8 1.7 %collective-permute-done.9.r_2_ = bf16[64,256]{1,0:T(8,128)(2,1)S(1)} collective-permute-done((bf16[64,256]{1,0:T(8,128)(2,1)S(1)}, bf16[64,256]{1,0:T(8,128)(2,1)S(1)}, u32[]{:S(2)}, u32[]{:S(2)}) %collective-permute-start.9) | collective-permute-done | bytes 32800 | tf_op jit(solution)/shard_map/ppermute | solution.py:61
  50.5 2.0 %collective-permute-done.10.r_3_ = bf16[64,256]{1,0:T(8,128)(2,1)S(1)} collective-permute-done((bf16[64,256]{1,0:T(8,128)(2,1)S(1)}, bf16[64,256]{1,0:T(8,128)(2,1)S(1)}, u32[]{:S(2)}, u32[]{:S(2)}) %collective-permute-start.10) | collective-permute-done | bytes 32800 | tf_op jit(solution)/shard_map/ppermute | solution.py:61
  52.5 0.0 collective-permute-done.11.r_4_
  52.5 0.6 shard_map.195.r_1_
  53.0 0.3 collective-permute-start.14
  53.3 1.9 %collective-permute-start.13 = (bf16[64,256]{1,0:T(8,128)(2,1)S(1)}, bf16[64,256]{1,0:T(8,128)(2,1)S(1)}, u32[]{:S(2)}, u32[]{:S(2)}) collective-permute-start(bf16[64,256]{1,0:T(8,128)(2,1)S(1)} %shard_map.195.r_1_), channel_id=1, source_target_pairs={{0,16},{1,17},{2,18},{3,19},{4,20},{5,21},{6,22},{7,23},{8,24},{9,... | collective-permute-start | bytes 98312 | tf_op jit(solution)/shard_map/ppermute | solution.py:61
  55.2 2.3 %collective-permute-start.12 = (bf16[64,256]{1,0:T(8,128)(2,1)S(1)}, bf16[64,256]{1,0:T(8,128)(2,1)S(1)}, u32[]{:S(2)}, u32[]{:S(2)}) collective-permute-start(bf16[64,256]{1,0:T(8,128)(2,1)S(1)} %shard_map.195.r_1_), channel_id=1, source_target_pairs={{0,24},{1,25},{2,26},{3,27},{4,28},{5,29},{6,30},{7,31},{8,16},{9,... | collective-permute-start | bytes 98312 | tf_op jit(solution)/shard_map/ppermute | solution.py:61
  57.5 2.7 %shard_map.194 = (bf16[256,256]{1,0:T(8,128)(2,1)}, f32[256,256]{1,0:T(8,128)S(1)}, bf16[256,256]{1,0:T(8,128)(2,1)S(1)}, s32[4,128]{1,0:T(4,128)S(1)}) custom-call(s32[2]{0:T(128)S(1)} %bitcast.18, bf16[256,256]{1,0:T(8,128)(2,1)} %refs_0_.1, bf16[512,256]{1,0:T(8,128)(2,1)} %refs_1_.3, bf16[256,256]{1,0:T(8,128)(2,1)} %bitcast.22, s32[4,128]{1,0:T(4,128)} %bitcast.25, ...), custom_call_target="tpu_custom_call" | custom-call | flops 1000000000 | bytes 2097152 | tf_op jit(solution)/shard_map/pallas_call | solution.py:72
  60.2 0.0 collective-permute-done.15.refs_4_
  60.2 0.1 collective-permute-start.21
  60.3 0.0 collective-permute-done.16.refs_6_
  60.3 0.7 collective-permute-start.20
  61.0 0.0 collective-permute-done.14.r_4_
  61.0 0.0 collective-permute-done.13.r_3_
  61.0 0.0 collective-permute-done.12.r_2_
  61.0 0.6 shard_map.196.r_1_
  61.6 1.4 %collective-permute-start.19 = (bf16[256,256]{1,0:T(8,128)(2,1)S(1)}, bf16[256,256]{1,0:T(8,128)(2,1)S(1)}, u32[]{:S(2)}, u32[]{:S(2)}) collective-permute-start(bf16[256,256]{1,0:T(8,128)(2,1)S(1)} %shard_map.196.r_1_), channel_id=1, source_target_pairs={{0,1},{1,0},{2,3},{3,2},{4,5},{5,4},{6,7},{7,6},{8,9},{9,8},{10,11... | collective-permute-start | bytes 393224 | tf_op jit(solution)/shard_map/ppermute | solution.py:61
  63.0 0.8 %collective-permute-start.18 = (bf16[256,256]{1,0:T(8,128)(2,1)S(1)}, bf16[256,256]{1,0:T(8,128)(2,1)S(1)}, u32[]{:S(2)}, u32[]{:S(2)}) collective-permute-start(bf16[256,256]{1,0:T(8,128)(2,1)S(1)} %shard_map.196.r_1_), channel_id=1, source_target_pairs={{0,4},{1,5},{2,6},{3,7},{4,0},{5,1},{6,2},{7,3},{8,12},{9,13},{10,... | collective-permute-start | bytes 393224 | tf_op jit(solution)/shard_map/ppermute | solution.py:61
  63.8 1.3 %collective-permute-start.17 = (bf16[256,256]{1,0:T(8,128)(2,1)S(1)}, bf16[256,256]{1,0:T(8,128)(2,1)S(1)}, u32[]{:S(2)}, u32[]{:S(2)}) collective-permute-start(bf16[256,256]{1,0:T(8,128)(2,1)S(1)} %shard_map.196.r_1_), channel_id=1, source_target_pairs={{0,5},{1,4},{2,7},{3,6},{4,1},{5,0},{6,3},{7,2},{8,13},{9,12},{10,... | collective-permute-start | bytes 393224 | tf_op jit(solution)/shard_map/ppermute | solution.py:61
  65.1 0.0 collective-permute-done.21.refs_7_
  65.1 0.7 collective-permute-start.22
  65.8 0.0 collective-permute-done.22.refs_8_
  65.8 0.8 %collective-permute-done.20.refs_5_ = bf16[256,256]{1,0:T(8,128)(2,1)S(1)} collective-permute-done((bf16[256,256]{1,0:T(8,128)(2,1)S(1)}, bf16[256,256]{1,0:T(8,128)(2,1)S(1)}, u32[]{:S(2)}, u32[]{:S(2)}) %collective-permute-start.20) | collective-permute-done | bytes 131104 | tf_op jit(solution)/shard_map/ppermute | solution.py:61
  66.6 5.2 %collective-permute-done.19.r_4_ = bf16[256,256]{1,0:T(8,128)(2,1)S(1)} collective-permute-done((bf16[256,256]{1,0:T(8,128)(2,1)S(1)}, bf16[256,256]{1,0:T(8,128)(2,1)S(1)}, u32[]{:S(2)}, u32[]{:S(2)}) %collective-permute-start.19) | collective-permute-done | bytes 131104 | tf_op jit(solution)/shard_map/ppermute | solution.py:61
  71.8 0.0 collective-permute-done.18.r_3_
  71.8 0.0 collective-permute-done.17.r_2_
  71.8 0.6 shard_map.198.r_1_
  72.4 0.2 collective-permute-start.23
  72.6 1.5 %shard_map.197 = bf16[256,256]{1,0:T(8,128)(2,1)} custom-call(s32[7]{0:T(128)S(1)} %stack.47.info.r_0_, bf16[256,256]{1,0:T(8,128)(2,1)S(1)} %get-tuple-element.105.refs_0_, s32[4,128]{1,0:T(4,128)S(1)} %get-tuple-element.106.refs_1_, f32[256,256]{1,0:T(8,128)S(1)} %get-tuple-element.107.refs_2_, f32[256,256]{1,0:T(8,128)S(1)} %get-tuple-element.112.refs_3_, ...), custom_call_target="tpu_custom_call" | custom-call | tf_op jit(solution)/shard_map/pallas_call | solution.py:72
  74.1 0.3 collective-permute-done.23.r_2_
  74.4 1.9 %shard_map.199 = (f32[256,256]{1,0:T(8,128)}, f32[256,256]{1,0:T(8,128)}, f32[256,256]{1,0:T(8,128)}, f32[256,256]{1,0:T(8,128)}, f32[256,512]{1,0:T(8,128)}, /*index=5*/f32[512,256]{1,0:T(8,128)}) custom-call(s32[7]{0:T(128)S(1)} %stack.47.info.r_0_, bf16[1024,256]{1,0:T(8,128)(2,1)S(1)} %shard_map.198.r_1_, bf16[1024,256]{1,0:T(8,128)(2,1)S(1)} %collective-permute-done.23.r_2_), custom_call_target="tpu_custom_call" | custom-call | tf_op jit(solution)/shard_map/pallas_call | solution.py:72
  (2 shorter events, 0.0 us)
Async XLA Ops:
  2.6 10.9 %collective-permute-start.2 = (bf16[272,256]{1,0:T(8,128)(2,1)S(1)}, bf16[272,256]{1,0:T(8,128)(2,1)S(1)}, u32[]{:S(2)}, u32[]{:S(2)}) collective-permute-start(bf16[272,256]{1,0:T(8,128)(2,1)S(1)} %get-tuple-element.75.refs_6_.r_11_), channel_id=1, source_target_pairs={{0,16},{1,17},{2,18},{3,19},{4,20},{5,21},{6,22},{7,23},{8,24},{9,... | collective-permute-start | bytes 417800 | tf_op jit(solution)/shard_map/ppermute | solution.py:61
  6.7 6.8 %collective-permute-start.1 = (bf16[272,256]{1,0:T(8,128)(2,1)S(1)}, bf16[272,256]{1,0:T(8,128)(2,1)S(1)}, u32[]{:S(2)}, u32[]{:S(2)}) collective-permute-start(bf16[272,256]{1,0:T(8,128)(2,1)S(1)} %get-tuple-element.75.refs_6_.r_11_), channel_id=1, source_target_pairs={{0,1},{1,0},{2,3},{3,2},{4,5},{5,4},{6,7},{7,6},{8,9},{9,8},{10,11... | collective-permute-start | bytes 417800 | tf_op jit(solution)/shard_map/ppermute | solution.py:61
  8.2 6.7 %collective-permute-start = (bf16[272,256]{1,0:T(8,128)(2,1)S(1)}, bf16[272,256]{1,0:T(8,128)(2,1)S(1)}, u32[]{:S(2)}, u32[]{:S(2)}) collective-permute-start(bf16[272,256]{1,0:T(8,128)(2,1)S(1)} %get-tuple-element.75.refs_6_.r_11_), channel_id=1, source_target_pairs={{0,8},{1,9},{2,10},{3,11},{4,12},{5,13},{6,14},{7,15},{8,0},{9,1},... | collective-permute-start | bytes 417800 | tf_op jit(solution)/shard_map/ppermute | solution.py:61
  9.8 3.3 %collective-permute-start.3 = (bf16[128,256]{1,0:T(8,128)(2,1)S(1)}, bf16[128,256]{1,0:T(8,128)(2,1)S(1)}, u32[]{:S(2)}, u32[]{:S(2)}) collective-permute-start(bf16[128,256]{1,0:T(8,128)(2,1)S(1)} %get-tuple-element.79), channel_id=1, source_target_pairs={{0,2},{4,6},{8,10},{12,14},{16,18},{20,22},{24,26},{28,30},{2,0},{... | collective-permute-start | bytes 196616 | tf_op jit(solution)/shard_map/ppermute | solution.py:51
  9.8 3.3 %collective-permute-start.4 = (bf16[128,256]{1,0:T(8,128)(2,1)S(1)}, bf16[128,256]{1,0:T(8,128)(2,1)S(1)}, u32[]{:S(2)}, u32[]{:S(2)}) collective-permute-start(bf16[128,256]{1,0:T(8,128)(2,1)S(1)} %get-tuple-element.80), channel_id=1, source_target_pairs={{2,4},{6,8},{10,12},{14,16},{18,20},{22,24},{26,28},{4,2},{8,6},{1... | collective-permute-start | bytes 196616 | tf_op jit(solution)/shard_map/ppermute | solution.py:51
  10.5 2.5 %copy-start.1 = (s32[1,1,3,2]{2,3,1,0:T(2,128)S(1)}, s32[1,1,3,2]{2,3,1,0:T(2,128)}, u32[]{:S(2)}) copy-start(s32[1,1,3,2]{2,3,1,0:T(2,128)} %param.24) | copy-start | bytes 76
  10.5 4.4 %copy-start = (s32[1,1,2]{2,1,0:T(1,128)S(1)}, s32[1,1,2]{2,1,0:T(1,128)}, u32[]{:S(2)}) copy-start(s32[1,1,2]{2,1,0:T(1,128)} %param.21) | copy-start | bytes 28
  30.5 2.7 %collective-permute-start.5 = (bf16[1024,256]{1,0:T(8,128)(2,1)S(1)}, bf16[1024,256]{1,0:T(8,128)(2,1)S(1)}, u32[]{:S(2)}, u32[]{:S(2)}) collective-permute-start(bf16[1024,256]{1,0:T(8,128)(2,1)S(1)} %get-tuple-element.82), channel_id=1, source_target_pairs={{0,2},{1,3},{2,0},{3,1},{4,6},{5,7},{6,4},{7,5},{8,10},{9,11},{10,... | collective-permute-start | bytes 1572872 | tf_op jit(solution)/shard_map/ppermute | solution.py:61
  34.1 9.6 %collective-permute-start.6 = (bf16[256,256]{1,0:T(8,128)(2,1)S(1)}, bf16[256,256]{1,0:T(8,128)(2,1)S(1)}, u32[]{:S(2)}, u32[]{:S(2)}) collective-permute-start(bf16[256,256]{1,0:T(8,128)(2,1)S(1)} %get-tuple-element.88), channel_id=1, source_target_pairs={{0,5},{1,4},{2,7},{3,6},{4,1},{5,0},{6,3},{7,2},{8,13},{9,12},{10,... | collective-permute-start | bytes 393224 | tf_op jit(solution)/shard_map/ppermute | solution.py:61
  36.4 7.2 %collective-permute-start.7 = (bf16[256,256]{1,0:T(8,128)(2,1)S(1)}, bf16[256,256]{1,0:T(8,128)(2,1)S(1)}, u32[]{:S(2)}, u32[]{:S(2)}) collective-permute-start(bf16[256,256]{1,0:T(8,128)(2,1)S(1)} %get-tuple-element.89), channel_id=1, source_target_pairs={{0,4},{1,5},{2,6},{3,7},{4,0},{5,1},{6,2},{7,3},{8,12},{9,13},{10,... | collective-permute-start | bytes 393224 | tf_op jit(solution)/shard_map/ppermute | solution.py:61
  36.6 7.1 %collective-permute-start.8 = (bf16[256,256]{1,0:T(8,128)(2,1)S(1)}, bf16[256,256]{1,0:T(8,128)(2,1)S(1)}, u32[]{:S(2)}, u32[]{:S(2)}) collective-permute-start(bf16[256,256]{1,0:T(8,128)(2,1)S(1)} %get-tuple-element.90), channel_id=1, source_target_pairs={{0,1},{1,0},{2,3},{3,2},{4,5},{5,4},{6,7},{7,6},{8,9},{9,8},{10,11... | collective-permute-start | bytes 393224 | tf_op jit(solution)/shard_map/ppermute | solution.py:61
  39.8 20.4 %collective-permute-start.15 = (bf16[256,256]{1,0:T(8,128)(2,1)S(1)}, bf16[256,256]{1,0:T(8,128)(2,1)S(1)}, u32[]{:S(2)}, u32[]{:S(2)}) collective-permute-start(bf16[256,256]{1,0:T(8,128)(2,1)S(1)} %get-tuple-element.120), channel_id=1, source_target_pairs={{0,16},{1,17},{2,18},{3,19},{4,20},{5,21},{6,22},{7,23},{8,24},{9,... | collective-permute-start | bytes 393224 | tf_op jit(solution)/shard_map/ppermute | solution.py:61
  41.6 18.6 %collective-permute-start.16 = (bf16[256,256]{1,0:T(8,128)(2,1)S(1)}, bf16[256,256]{1,0:T(8,128)(2,1)S(1)}, u32[]{:S(2)}, u32[]{:S(2)}) collective-permute-start(bf16[256,256]{1,0:T(8,128)(2,1)S(1)} %get-tuple-element.121), channel_id=1, source_target_pairs={{0,8},{1,9},{2,10},{3,11},{4,12},{5,13},{6,14},{7,15},{8,0},{9,1},... | collective-permute-start | bytes 393224 | tf_op jit(solution)/shard_map/ppermute | solution.py:61
  44.3 6.2 %collective-permute-start.9 = (bf16[64,256]{1,0:T(8,128)(2,1)S(1)}, bf16[64,256]{1,0:T(8,128)(2,1)S(1)}, u32[]{:S(2)}, u32[]{:S(2)}) collective-permute-start(bf16[64,256]{1,0:T(8,128)(2,1)S(1)} %get-tuple-element.114), channel_id=1, source_target_pairs={{0,24},{1,25},{2,26},{3,27},{4,28},{5,29},{6,30},{7,31},{8,16},{9,... | collective-permute-start | bytes 98312 | tf_op jit(solution)/shard_map/ppermute | solution.py:61
  47.7 4.8 %collective-permute-start.10 = (bf16[64,256]{1,0:T(8,128)(2,1)S(1)}, bf16[64,256]{1,0:T(8,128)(2,1)S(1)}, u32[]{:S(2)}, u32[]{:S(2)}) collective-permute-start(bf16[64,256]{1,0:T(8,128)(2,1)S(1)} %get-tuple-element.115), channel_id=1, source_target_pairs={{0,16},{1,17},{2,18},{3,19},{4,20},{5,21},{6,22},{7,23},{8,24},{9,... | collective-permute-start | bytes 98312 | tf_op jit(solution)/shard_map/ppermute | solution.py:61
  47.7 4.8 %collective-permute-start.11 = (bf16[64,256]{1,0:T(8,128)(2,1)S(1)}, bf16[64,256]{1,0:T(8,128)(2,1)S(1)}, u32[]{:S(2)}, u32[]{:S(2)}) collective-permute-start(bf16[64,256]{1,0:T(8,128)(2,1)S(1)} %get-tuple-element.116), channel_id=1, source_target_pairs={{0,8},{1,9},{2,10},{3,11},{4,12},{5,13},{6,14},{7,15},{8,0},{9,1},... | collective-permute-start | bytes 98312 | tf_op jit(solution)/shard_map/ppermute | solution.py:61
  53.0 8.0 %collective-permute-start.14 = (bf16[64,256]{1,0:T(8,128)(2,1)S(1)}, bf16[64,256]{1,0:T(8,128)(2,1)S(1)}, u32[]{:S(2)}, u32[]{:S(2)}) collective-permute-start(bf16[64,256]{1,0:T(8,128)(2,1)S(1)} %shard_map.195.r_1_), channel_id=1, source_target_pairs={{0,8},{1,9},{2,10},{3,11},{4,12},{5,13},{6,14},{7,15},{8,0},{9,1},... | collective-permute-start | bytes 98312 | tf_op jit(solution)/shard_map/ppermute | solution.py:61
  53.3 7.7 %collective-permute-start.13 = (bf16[64,256]{1,0:T(8,128)(2,1)S(1)}, bf16[64,256]{1,0:T(8,128)(2,1)S(1)}, u32[]{:S(2)}, u32[]{:S(2)}) collective-permute-start(bf16[64,256]{1,0:T(8,128)(2,1)S(1)} %shard_map.195.r_1_), channel_id=1, source_target_pairs={{0,16},{1,17},{2,18},{3,19},{4,20},{5,21},{6,22},{7,23},{8,24},{9,... | collective-permute-start | bytes 98312 | tf_op jit(solution)/shard_map/ppermute | solution.py:61
  55.2 5.8 %collective-permute-start.12 = (bf16[64,256]{1,0:T(8,128)(2,1)S(1)}, bf16[64,256]{1,0:T(8,128)(2,1)S(1)}, u32[]{:S(2)}, u32[]{:S(2)}) collective-permute-start(bf16[64,256]{1,0:T(8,128)(2,1)S(1)} %shard_map.195.r_1_), channel_id=1, source_target_pairs={{0,24},{1,25},{2,26},{3,27},{4,28},{5,29},{6,30},{7,31},{8,16},{9,... | collective-permute-start | bytes 98312 | tf_op jit(solution)/shard_map/ppermute | solution.py:61
  60.2 4.9 %collective-permute-start.21 = (bf16[128,256]{1,0:T(8,128)(2,1)S(1)}, bf16[128,256]{1,0:T(8,128)(2,1)S(1)}, u32[]{:S(2)}, u32[]{:S(2)}) collective-permute-start(bf16[128,256]{1,0:T(8,128)(2,1)S(1)} %get-tuple-element.127), channel_id=1, source_target_pairs={{0,2},{4,6},{8,10},{12,14},{16,18},{20,22},{24,26},{28,30},{2,0},{... | collective-permute-start | bytes 196616 | tf_op jit(solution)/shard_map/ppermute | solution.py:51
  60.3 6.4 %collective-permute-start.20 = (bf16[256,256]{1,0:T(8,128)(2,1)S(1)}, bf16[256,256]{1,0:T(8,128)(2,1)S(1)}, u32[]{:S(2)}, u32[]{:S(2)}) collective-permute-start(bf16[256,256]{1,0:T(8,128)(2,1)S(1)} %get-tuple-element.126), channel_id=1, source_target_pairs={{0,1},{1,0},{2,3},{3,2},{4,5},{5,4},{6,7},{7,6},{8,9},{9,8},{10,11... | collective-permute-start | bytes 393224 | tf_op jit(solution)/shard_map/ppermute | solution.py:61
  61.6 10.2 %collective-permute-start.19 = (bf16[256,256]{1,0:T(8,128)(2,1)S(1)}, bf16[256,256]{1,0:T(8,128)(2,1)S(1)}, u32[]{:S(2)}, u32[]{:S(2)}) collective-permute-start(bf16[256,256]{1,0:T(8,128)(2,1)S(1)} %shard_map.196.r_1_), channel_id=1, source_target_pairs={{0,1},{1,0},{2,3},{3,2},{4,5},{5,4},{6,7},{7,6},{8,9},{9,8},{10,11... | collective-permute-start | bytes 393224 | tf_op jit(solution)/shard_map/ppermute | solution.py:61
  63.0 8.8 %collective-permute-start.18 = (bf16[256,256]{1,0:T(8,128)(2,1)S(1)}, bf16[256,256]{1,0:T(8,128)(2,1)S(1)}, u32[]{:S(2)}, u32[]{:S(2)}) collective-permute-start(bf16[256,256]{1,0:T(8,128)(2,1)S(1)} %shard_map.196.r_1_), channel_id=1, source_target_pairs={{0,4},{1,5},{2,6},{3,7},{4,0},{5,1},{6,2},{7,3},{8,12},{9,13},{10,... | collective-permute-start | bytes 393224 | tf_op jit(solution)/shard_map/ppermute | solution.py:61
  63.8 8.0 %collective-permute-start.17 = (bf16[256,256]{1,0:T(8,128)(2,1)S(1)}, bf16[256,256]{1,0:T(8,128)(2,1)S(1)}, u32[]{:S(2)}, u32[]{:S(2)}) collective-permute-start(bf16[256,256]{1,0:T(8,128)(2,1)S(1)} %shard_map.196.r_1_), channel_id=1, source_target_pairs={{0,5},{1,4},{2,7},{3,6},{4,1},{5,0},{6,3},{7,2},{8,13},{9,12},{10,... | collective-permute-start | bytes 393224 | tf_op jit(solution)/shard_map/ppermute | solution.py:61
  65.1 0.7 collective-permute-start.22
  72.4 2.0 %collective-permute-start.23 = (bf16[1024,256]{1,0:T(8,128)(2,1)S(1)}, bf16[1024,256]{1,0:T(8,128)(2,1)S(1)}, u32[]{:S(2)}, u32[]{:S(2)}) collective-permute-start(bf16[1024,256]{1,0:T(8,128)(2,1)S(1)} %shard_map.198.r_1_), channel_id=1, source_target_pairs={{0,2},{1,3},{2,0},{3,1},{4,6},{5,7},{6,4},{7,5},{8,10},{9,11},{10,... | collective-permute-start | bytes 1572872 | tf_op jit(solution)/shard_map/ppermute | solution.py:61

commit v5 on v4

--- a/solution.py
+++ b/solution.py
@@ -188,7 +188,7 @@
     rims = refs[MATCHINGS + 1 : MATCHINGS + 1 + (2 if merge_y else 4)]
     refs = refs[MATCHINGS + 1 + len(rims) :]
     keep, send, kvg, moves, query_out, hidden_out, activ_out, grad_hidden_out = refs[:8]
-    grads, xcat, probs, pbf, sgrad, qstack, gstack, real_cols = refs[8:]
+    grads, xcat, probs, dotted, pbf, sgrad, qstack, gstack, across, near_rows, near_cols, real_cols = refs[8:]
 
     count, width = nodes.shape
     hidden_units = wup.shape[1]
@@ -227,21 +227,29 @@
         xcat[base + s * count : base + (s + 1) * count, :] = rows.astype(BF16)
 
     queries = squares[0]
-    key_rows, key_cols, value_rows, value_cols = [], [], [], []
     for b in range(blocks):
         rows = xcat[b * keys + size : (b + 1) * keys, :]
         own = slice(b * size, (b + 1) * size)
-        key_rows.append(jnp.concatenate([own_rows[0, own, :], nn(rows, weights[0]).astype(BF16)], axis=0))
-        value_rows.append(jnp.concatenate([own_rows[1, own, :], nn(rows, weights[1]).astype(BF16)], axis=0))
-        key_cols.append(jnp.concatenate([own_cols[0, :, own], nt(weights_t[0], rows).astype(BF16)], axis=1))
-        value_cols.append(jnp.concatenate([own_cols[1, :, own], nt(weights_t[1], rows).astype(BF16)], axis=1))
+        for k in range(2):
+            near_rows[k, b, 0:size, :] = own_rows[k, own, :]
+            near_rows[k, b, size:keys, :] = nn(rows, weights[k]).astype(BF16)
+            near_cols[k, b, :, 0:size] = own_cols[k, :, own]
+            near_cols[k, b, :, size:keys] = nt(weights_t[k], rows).astype(BF16)
+    row_head = head_rows((width, size), 0)
+    lane_head = head_rows((size, width), 1)
+    for b in range(blocks):
+        own, own_t = queries[b * size : (b + 1) * size, :], squares[9, :, b * size : (b + 1) * size]
+        for h in range(HEADS):
+            at = slice(h * size, (h + 1) * size)
+            across[b, :, at] = jnp.where(row_head == h, own_t, jnp.zeros_like(own_t))
+            qstack[b, at, :] = jnp.where(lane_head == h, own, jnp.zeros_like(own))
     rim_keys, rim_values = [], []
     for s in range(SIDES):
         rows = xcat[base + s * count : base + (s + 1) * count, :]
         rim_keys.append(nn(rows, weights[0]).astype(BF16).astype(F32))
         rim_values.append(nn(rows, weights[1]).astype(BF16).astype(F32))
     bias = [
-        jnp.concatenate([squares[10, 0:size, b * size : (b + 1) * size].astype(F32)] + bias[b * MATCHINGS : (b + 1) * MATCHINGS], axis=0)
+        [squares[10, 0:size, b * size : (b + 1) * size].astype(F32)] + bias[b * MATCHINGS : (b + 1) * MATCHINGS]
         for b in range(blocks)
     ]
 
@@ -259,40 +267,84 @@
         rim_scores.append(jnp.where(there[s] > 0.5, score, NEG_FILL))
     rim_top = jnp.maximum(jnp.maximum(rim_scores[0], rim_scores[1]), jnp.maximum(rim_scores[2], rim_scores[3]))
 
-    row_head = head_rows((width, size), 0)
-    tops, sums = [], []
-    att_blocks = []
-    for b in range(blocks):
+    pairs = [(b, first) for b in range(blocks) for first in range(0, HEADS, 2)]
+    groups = MATCHINGS + 1
+
+    def folded(value, combine):
+        part = value[0:8]
+        for lo in range(8, value.shape[0], 8):
+            part = combine(part, value[lo : lo + 8])
+        return part
+
+    def both_heads(table, b, first):
         cols = slice(b * size, (b + 1) * size)
-        top_rows, inv_rows, att_rows = [], [], []
-        own = squares[9, :, cols]
-        for first in range(0, HEADS, 2):
-            pair = (first, first + 1)
-            masked = [jnp.where(row_head == h, own, jnp.zeros_like(own)) for h in pair]
-            both = nn(key_rows[b], jnp.concatenate(masked, axis=1))
-            for k, h in enumerate(pair):
-                score = both[:, k * size : (k + 1) * size] * (scale * log2e) + bias[b]
-                top = jnp.maximum(jnp.max(score, axis=0, keepdims=True), rim_top[h : h + 1, cols])
-                grown = jnp.exp2(score - top)
-                total = jnp.sum(grown, axis=0, keepdims=True)
-                for s in range(SIDES):
-                    total = total + jnp.exp2(rim_scores[s][h : h + 1, cols] - top)
-                inverse = 1.0 / total
-                prob = grown * inverse
-                at = slice(h * size, (h + 1) * size)
-                probs[b, :, at] = prob
-                pbf[b, :, at] = prob.astype(BF16)
-                top_rows.append(top)
-                inv_rows.append(inverse)
-            rows = slice(first * HEAD_DIM, (first + 2) * HEAD_DIM)
-            wide = nn(value_cols[b][rows, :], pbf[b, :, first * size : (first + 2) * size])
-            att_rows += [wide[0:HEAD_DIM, 0:size], wide[HEAD_DIM:, size:]]
-        tops.append(jnp.concatenate(top_rows, axis=0))
-        sums.append(jnp.concatenate(inv_rows, axis=0))
-        att_blocks.append(jnp.concatenate(att_rows, axis=0))
-    top_all = jnp.concatenate(tops, axis=1)
-    inv_all = jnp.concatenate(sums, axis=1)
-    mixed = flip(jnp.concatenate(att_blocks, axis=1))
+        return jnp.concatenate([table[first : first + 1, cols], table[first + 1 : first + 2, cols]], axis=1)
+
+    tops, sums, inverses, att_parts = {}, {}, {}, {}
+
+    def make_scores(u, c):
+        b, first = pairs[u]
+        at = slice(first * size, (first + 2) * size)
+        rows = slice(c * size, (c + 1) * size)
+        score = nn(near_rows[0, b, rows, :], across[b, :, at]) * (scale * log2e)
+        score = score + jnp.concatenate([bias[b][c], bias[b][c]], axis=1)
+        probs[b, rows, at] = score
+        part = folded(score, jnp.maximum)
+        tops[u] = part if c == 0 else jnp.maximum(tops[u], part)
+        if c == groups - 1:
+            tops[u] = jnp.maximum(jnp.max(tops[u], axis=0, keepdims=True), both_heads(rim_top, b, first))
+
+    def make_exp(u, c):
+        b, first = pairs[u]
+        at = slice(first * size, (first + 2) * size)
+        rows = slice(c * size, (c + 1) * size)
+        grown = jnp.exp2(probs[b, rows, at] - tops[u])
+        probs[b, rows, at] = grown
+        part = folded(grown, jnp.add)
+        sums[u] = part if c == 0 else sums[u] + part
+        if c == groups - 1:
+            total = jnp.sum(sums[u], axis=0, keepdims=True)
+            for s in range(SIDES):
+                total = total + jnp.exp2(both_heads(rim_scores[s], b, first) - tops[u])
+            inverses[u] = 1.0 / total
+
+    def make_probs(u, c):
+        b, first = pairs[u]
+        at = slice(first * size, (first + 2) * size)
+        rows = slice(c * size, (c + 1) * size)
+        prob = probs[b, rows, at] * inverses[u]
+        probs[b, rows, at] = prob
+        pbf[b, rows, at] = prob.astype(BF16)
+
+    def make_mix(u):
+        b, first = pairs[u]
+        rows = slice(first * HEAD_DIM, (first + 2) * HEAD_DIM)
+        wide = nn(near_cols[1, b, rows, :], pbf[b, :, first * size : (first + 2) * size])
+        att_parts[u] = [wide[0:HEAD_DIM, 0:size], wide[HEAD_DIM:, size:]]
+
+    def staggered(stages, last):
+        for t in range(len(pairs) + len(stages)):
+            for c in range(groups):
+                for late, stage in enumerate(stages):
+                    if 0 <= t - late < len(pairs):
+                        stage(t - late, c)
+            if 0 <= t - len(stages) < len(pairs):
+                last(t - len(stages))
+
+    staggered([make_scores, make_exp, make_probs], make_mix)
+
+    def by_block(values):
+        per = HEADS // 2
+        return jnp.concatenate(
+            [jnp.concatenate(sum((values[b * per + i] for i in range(per)), []), axis=0) for b in range(blocks)], axis=1
+        )
+
+    def halves(values):
+        return {u: [v[:, 0:size], v[:, size:]] for u, v in values.items()}
+
+    top_all = by_block(halves(tops))
+    inv_all = by_block(halves(inverses))
+    mixed = flip(by_block(att_parts))
     rim_probs = [jnp.exp2(rim_scores[s] - top_all) * inv_all for s in range(SIDES)]
     rim_wide = [tn(rim_probs[s].astype(BF16), spread) for s in range(SIDES)]
     for s in range(SIDES):
@@ -336,42 +388,48 @@
     grad_att_f = grad_att.astype(F32)
     grad_att_t = flip(grad_att).astype(BF16)
 
-    lane_head = head_rows((size, width), 1)
     rim_dots = [head_sums(grad_att_f * rim_values[s]) for s in range(SIDES)]
     rim_inner = rim_probs[0] * rim_dots[0]
     for s in range(1, SIDES):
         rim_inner = rim_inner + rim_probs[s] * rim_dots[s]
-    inner_blocks, query_blocks = [], []
-    for b in range(blocks):
-        cols = slice(b * size, (b + 1) * size)
-        inner_rows, query_rows = [], []
-        own = grad_att_t[:, cols]
-        own = grad_att_t[:, cols]
-        for first in range(0, HEADS, 2):
-            pair = (first, first + 1)
-            masked = [jnp.where(row_head == h, own, jnp.zeros_like(own)) for h in pair]
-            both = nn(value_rows[b], jnp.concatenate(masked, axis=1))
-            for k, h in enumerate(pair):
-                dots = both[:, k * size : (k + 1) * size]
-                at = slice(h * size, (h + 1) * size)
-                prob = probs[b, :, at]
-                inner = jnp.sum(prob * dots, axis=0, keepdims=True) + rim_inner[h : h + 1, cols]
-                sgrad[b, :, at] = (prob * (dots - inner) * scale).astype(BF16)
-                inner_rows.append(inner)
-                mine = queries[cols, :]
-                qstack[at, :] = jnp.where(lane_head == h, mine, jnp.zeros_like(mine))
-                mine = grad_att[cols, :]
-                gstack[at, :] = jnp.where(lane_head == h, mine, jnp.zeros_like(mine))
-            rows = slice(first * HEAD_DIM, (first + 2) * HEAD_DIM)
-            wide = nn(key_cols[b][rows, :], sgrad[b, :, first * size : (first + 2) * size])
-            query_rows += [wide[0:HEAD_DIM, 0:size], wide[HEAD_DIM:, size:]]
-        inner_blocks.append(jnp.concatenate(inner_rows, axis=0))
-        query_blocks.append(jnp.concatenate(query_rows, axis=0))
+    for b in range(blocks):
+        own, own_t = grad_att[b * size : (b + 1) * size, :], grad_att_t[:, b * size : (b + 1) * size]
+        for h in range(HEADS):
+            at = slice(h * size, (h + 1) * size)
+            across[b, :, at] = jnp.where(row_head == h, own_t, jnp.zeros_like(own_t))
+            gstack[b, at, :] = jnp.where(lane_head == h, own, jnp.zeros_like(own))
+    inners, query_parts = {}, {}
+
+    def make_dots(u, c):
+        b, first = pairs[u]
+        at = slice(first * size, (first + 2) * size)
+        rows = slice(c * size, (c + 1) * size)
+        dots = nn(near_rows[1, b, rows, :], across[b, :, at])
+        dotted[b, rows, at] = dots
+        part = folded(probs[b, rows, at] * dots, jnp.add)
+        inners[u] = part if c == 0 else inners[u] + part
+        if c == groups - 1:
+            inners[u] = jnp.sum(inners[u], axis=0, keepdims=True) + both_heads(rim_inner, b, first)
+
+    def make_grads(u, c):
+        b, first = pairs[u]
+        at = slice(first * size, (first + 2) * size)
+        rows = slice(c * size, (c + 1) * size)
+        sgrad[b, rows, at] = (probs[b, rows, at] * (dotted[b, rows, at] - inners[u]) * scale).astype(BF16)
+
+    def make_query(u):
+        b, first = pairs[u]
+        rows = slice(first * HEAD_DIM, (first + 2) * HEAD_DIM)
+        wide = nn(near_cols[0, b, rows, :], sgrad[b, :, first * size : (first + 2) * size])
+        query_parts[u] = [wide[0:HEAD_DIM, 0:size], wide[HEAD_DIM:, size:]]
+
+    staggered([make_dots, make_grads], make_query)
+    for b in range(blocks):
         span = slice(b * keys, (b + 1) * keys)
-        kvg[span, 0:width] = nn(sgrad[b], qstack[...]).astype(BF16)
-        kvg[span, width : 2 * width] = nn(pbf[b], gstack[...]).astype(BF16)
-    inner_all = jnp.concatenate(inner_blocks, axis=1)
-    query_grad = flip(jnp.concatenate(query_blocks, axis=1))
+        kvg[span, 0:width] = nn(sgrad[b], qstack[b]).astype(BF16)
+        kvg[span, width : 2 * width] = nn(pbf[b], gstack[b]).astype(BF16)
+    inner_all = by_block(halves(inners))
+    query_grad = flip(by_block(query_parts))
     for s in range(SIDES):
         graded = (rim_probs[s] * (rim_dots[s] - inner_all) * scale).astype(BF16)
         wide = tn(graded, spread)
@@ -642,10 +700,14 @@
             pltpu.VMEM((total_rows, width), F32),
             pltpu.VMEM((all_rows, width), BF16),
             pltpu.VMEM((blocks, keys, heads_wide), F32),
+            pltpu.VMEM((blocks, keys, heads_wide), F32),
             pltpu.VMEM((blocks, keys, heads_wide), BF16),
             pltpu.VMEM((blocks, keys, heads_wide), BF16),
-            pltpu.VMEM((heads_wide, width), BF16),
-            pltpu.VMEM((heads_wide, width), BF16),
+            pltpu.VMEM((blocks, heads_wide, width), BF16),
+            pltpu.VMEM((blocks, heads_wide, width), BF16),
+            pltpu.VMEM((blocks, width, heads_wide), BF16),
+            pltpu.VMEM((2, blocks, keys, width), BF16),
+            pltpu.VMEM((2, blocks, width, keys), BF16),
             pltpu.VMEM((MATCHINGS, count, EXTRA), F32),
         ],
         limit=32,

time: 76.5 us -> 70.9 us (0.927)
  Pallas kernels: 31.1 us -> 25.4 us
    pallas_call x12, Pallas kernels: 31.1 us -> 25.4 us  [call(): pl.pallas_call(kernel, out_shape=[jax.ShapeDtypeStruct(s, d) for s, d in...]
  transfers between devices with their start and end apart: 24 -> 24, of which waited for: 8 -> 8; matrix products, arithmetic and copies ran while one was open for 0% -> 0% of each run, Pallas kernels for 13% -> 15%
where the time goes in v5:
time: 70.9 us; the launch traced here: 70.6 us
  starting transfers between devices  30.9 us (44%)
  Pallas kernels  25.4 us (36%)
  waiting for transfers between devices  13.3 us (19%)
  between operations  0.83 us (1%)
    ppermute x20, starting transfers between devices, xor_permute(): return lax.ppermute(value, AXES, [(i, i ^ mask) for i in range(count)])  29.5 us
    pallas_call x12, Pallas kernels, call(): pl.pallas_call(kernel, out_shape=[jax.ShapeDtypeStruct(s, d) for s, d in...  25.4 us
    ppermute x20, waiting for transfers between devices, xor_permute(): return lax.ppermute(value, AXES, [(i, i ^ mask) for i in range(count)])  13.3 us
  transfers between devices with their start and end apart: 24, of which 8 were waited for; matrix products, arithmetic and copies ran while one was open for 0% of the time, Pallas kernels for 15%

profile of v5, /device:TPU:0, one launch (start us, length us, event | category | flops | bytes accessed | tf_op | source)
XLA Modules:
  0.0 70.6 jit_solution(11349717853646389724)
XLA Ops:
  0.7 0.1 stack.47.info.r_0_
  0.7 1.8 %shard_map.188 = (bf16[272,256]{1,0:T(8,128)(2,1)S(1)}, bf16[128,256]{1,0:T(8,128)(2,1)S(1)}, bf16[128,256]{1,0:T(8,128)(2,1)S(1)}) custom-call(s32[7]{0:T(128)S(1)} %stack.47.info.r_0_, bf16[256,256]{1,0:T(8,128)(2,1)} %bitcast.20, s32[4,128]{1,0:T(4,128)} %bitcast.23, s32[2]{0:T(128)} %bitcast.16), custom_call_target="tpu_custom_call" | custom-call | tf_op jit(solution)/shard_map/pallas_call | solution.py:72
  2.6 4.1 %collective-permute-start.2 = (bf16[272,256]{1,0:T(8,128)(2,1)S(1)}, bf16[272,256]{1,0:T(8,128)(2,1)S(1)}, u32[]{:S(2)}, u32[]{:S(2)}) collective-permute-start(bf16[272,256]{1,0:T(8,128)(2,1)S(1)} %get-tuple-element.75.refs_6_.r_11_), channel_id=1, source_target_pairs={{0,16},{1,17},{2,18},{3,19},{4,20},{5,21},{6,22},{7,23},{8,24},{9,... | collective-permute-start | bytes 417800 | tf_op jit(solution)/shard_map/ppermute | solution.py:61
  6.7 1.5 %collective-permute-start.1 = (bf16[272,256]{1,0:T(8,128)(2,1)S(1)}, bf16[272,256]{1,0:T(8,128)(2,1)S(1)}, u32[]{:S(2)}, u32[]{:S(2)}) collective-permute-start(bf16[272,256]{1,0:T(8,128)(2,1)S(1)} %get-tuple-element.75.refs_6_.r_11_), channel_id=1, source_target_pairs={{0,1},{1,0},{2,3},{3,2},{4,5},{5,4},{6,7},{7,6},{8,9},{9,8},{10,11... | collective-permute-start | bytes 417800 | tf_op jit(solution)/shard_map/ppermute | solution.py:61
  8.2 1.6 %collective-permute-start = (bf16[272,256]{1,0:T(8,128)(2,1)S(1)}, bf16[272,256]{1,0:T(8,128)(2,1)S(1)}, u32[]{:S(2)}, u32[]{:S(2)}) collective-permute-start(bf16[272,256]{1,0:T(8,128)(2,1)S(1)} %get-tuple-element.75.refs_6_.r_11_), channel_id=1, source_target_pairs={{0,8},{1,9},{2,10},{3,11},{4,12},{5,13},{6,14},{7,15},{8,0},{9,1},... | collective-permute-start | bytes 417800 | tf_op jit(solution)/shard_map/ppermute | solution.py:61
  9.8 0.0 collective-permute-start.3
  9.8 0.7 collective-permute-start.4
  10.5 0.0 copy-start.1
  10.5 0.0 copy-start
  10.5 2.5 %shard_map.189 = (bf16[12,256,256]{2,1,0:T(8,128)(2,1)S(1)}, bf16[4,256,128]{2,1,0:T(8,128)(2,1)S(1)}, f32[4,8,256]{2,1,0:T(8,128)S(1)}) custom-call(s32[7]{0:T(128)S(1)} %stack.47.info.r_0_, s32[4,128]{1,0:T(4,128)} %bitcast.24, bf16[256,256]{1,0:T(8,128)(2,1)} %refs_0_.1, bf16[256,256]{1,0:T(8,128)(2,1)} %refs_2_.1, bf16[256,256]{1,0:T(8,128)(2,1)} %refs_3_.1, ...), custom_call_target="tpu_custom_call" | custom-call | flops 2000000000 | bytes 4194304 | tf_op jit(solution)/shard_map/pallas_call | solution.py:72
  13.0 0.1 copy.21.r_2_.r_0_
  13.1 0.0 collective-permute-done.3.r_15_
  13.1 0.0 collective-permute-done.4.r_16_
  13.1 0.4 collective-permute-done.2.r_14_
  13.5 0.0 collective-permute-done.1.r_13_
  13.5 1.4 %collective-permute-done.r_12_ = bf16[272,256]{1,0:T(8,128)(2,1)S(1)} collective-permute-done((bf16[272,256]{1,0:T(8,128)(2,1)S(1)}, bf16[272,256]{1,0:T(8,128)(2,1)S(1)}, u32[]{:S(2)}, u32[]{:S(2)}) %collective-permute-start) | collective-permute-done | bytes 139296 | tf_op jit(solution)/shard_map/ppermute | solution.py:61
  14.9 10.1 %shard_map.190 = (f32[1024,256]{1,0:T(8,128)S(1)}, bf16[1024,256]{1,0:T(8,128)(2,1)S(1)}, bf16[2048,512]{1,0:T(8,128)(2,1)S(1)}, bf16[2,256,256]{2,1,0:T(8,128)(...) custom-call(s32[7]{0:T(128)S(1)} %stack.47.info.r_0_, ...), custom_call_target="tpu_custom_call" | custom-call | flops 10000000000 | bytes 8388608 | tf_op jit(solution)/shard_map/pallas_call | solution.py:72
  25.0 1.2 %collective-permute-start.5 = (bf16[1024,256]{1,0:T(8,128)(2,1)S(1)}, bf16[1024,256]{1,0:T(8,128)(2,1)S(1)}, u32[]{:S(2)}, u32[]{:S(2)}) collective-permute-start(bf16[1024,256]{1,0:T(8,128)(2,1)S(1)} %get-tuple-element.82), channel_id=1, source_target_pairs={{0,2},{1,3},{2,0},{3,1},{4,6},{5,7},{6,4},{7,5},{8,10},{9,11},{10,... | collective-permute-start | bytes 1572872 | tf_op jit(solution)/shard_map/ppermute | solution.py:61
  26.2 1.5 %collective-permute-done.5.r_2_ = bf16[1024,256]{1,0:T(8,128)(2,1)S(1)} collective-permute-done((bf16[1024,256]{1,0:T(8,128)(2,1)S(1)}, bf16[1024,256]{1,0:T(8,128)(2,1)S(1)}, u32[]{:S(2)}, u32[]{:S(2)}) %collective-permute-start.5) | collective-permute-done | bytes 524320 | tf_op jit(solution)/shard_map/ppermute | solution.py:61
  27.7 0.7 %shard_map.191 = (f32[256,256]{1,0:T(8,128)S(1)}, bf16[256,256]{1,0:T(8,128)(2,1)S(1)}, bf16[256,256]{1,0:T(8,128)(2,1)S(1)}, bf16[256,256]{1,0:T(8,128)(2,1)S(1)}) custom-call(s32[7]{0:T(128)S(1)} %stack.47.info.r_0_, f32[1024,256]{1,0:T(8,128)S(1)} %get-tuple-element.81.r_1_, bf16[1024,256]{1,0:T(8,128)(2,1)S(1)} %collective-permute-done.5.r_2_), custom_call_target="tpu_custom_call" | custom-call | tf_op jit(solution)/shard_map/pallas_call | solution.py:72
  28.4 2.3 %collective-permute-start.6 = (bf16[256,256]{1,0:T(8,128)(2,1)S(1)}, bf16[256,256]{1,0:T(8,128)(2,1)S(1)}, u32[]{:S(2)}, u32[]{:S(2)}) collective-permute-start(bf16[256,256]{1,0:T(8,128)(2,1)S(1)} %get-tuple-element.88), channel_id=1, source_target_pairs={{0,5},{1,4},{2,7},{3,6},{4,1},{5,0},{6,3},{7,2},{8,13},{9,12},{10,... | collective-permute-start | bytes 393224 | tf_op jit(solution)/shard_map/ppermute | solution.py:61
  30.8 0.1 collective-permute-start.7
  30.9 1.4 %collective-permute-start.8 = (bf16[256,256]{1,0:T(8,128)(2,1)S(1)}, bf16[256,256]{1,0:T(8,128)(2,1)S(1)}, u32[]{:S(2)}, u32[]{:S(2)}) collective-permute-start(bf16[256,256]{1,0:T(8,128)(2,1)S(1)} %get-tuple-element.90), channel_id=1, source_target_pairs={{0,1},{1,0},{2,3},{3,2},{4,5},{5,4},{6,7},{7,6},{8,9},{9,8},{10,11... | collective-permute-start | bytes 393224 | tf_op jit(solution)/shard_map/ppermute | solution.py:61
  32.3 1.8 %shard_map.193 = (f32[256,256]{1,0:T(8,128)S(1)}, bf16[256,256]{1,0:T(8,128)(2,1)S(1)}, bf16[256,256]{1,0:T(8,128)(2,1)S(1)}, bf16[256,256]{1,0:T(8,128)(2,1)S(1...) custom-call(s32[3,2]{1,0:T(4,128)S(1)} %copy.21.r_2_.r_0_, bf16[2048,512]{1,0:T(8,128)(2,1)S(1)} %get-tuple-element.97.r_1_, ...), custom_call_target="tpu_custom_call" | custom-call | flops 2000000000 | bytes 4194304 | tf_op jit(solution)/shard_map/pallas_call | solution.py:72
  34.1 1.8 %collective-permute-start.15 = (bf16[256,256]{1,0:T(8,128)(2,1)S(1)}, bf16[256,256]{1,0:T(8,128)(2,1)S(1)}, u32[]{:S(2)}, u32[]{:S(2)}) collective-permute-start(bf16[256,256]{1,0:T(8,128)(2,1)S(1)} %get-tuple-element.120), channel_id=1, source_target_pairs={{0,16},{1,17},{2,18},{3,19},{4,20},{5,21},{6,22},{7,23},{8,24},{9,... | collective-permute-start | bytes 393224 | tf_op jit(solution)/shard_map/ppermute | solution.py:61
  36.0 2.0 %collective-permute-start.16 = (bf16[256,256]{1,0:T(8,128)(2,1)S(1)}, bf16[256,256]{1,0:T(8,128)(2,1)S(1)}, u32[]{:S(2)}, u32[]{:S(2)}) collective-permute-start(bf16[256,256]{1,0:T(8,128)(2,1)S(1)} %get-tuple-element.121), channel_id=1, source_target_pairs={{0,8},{1,9},{2,10},{3,11},{4,12},{5,13},{6,14},{7,15},{8,0},{9,1},... | collective-permute-start | bytes 393224 | tf_op jit(solution)/shard_map/ppermute | solution.py:61
  38.0 0.0 collective-permute-done.6.r_2_
  38.0 0.0 collective-permute-done.7.r_3_
  38.0 0.0 collective-permute-done.8.r_4_
  38.0 0.6 shard_map.192
  38.6 3.3 %collective-permute-start.9 = (bf16[64,256]{1,0:T(8,128)(2,1)S(1)}, bf16[64,256]{1,0:T(8,128)(2,1)S(1)}, u32[]{:S(2)}, u32[]{:S(2)}) collective-permute-start(bf16[64,256]{1,0:T(8,128)(2,1)S(1)} %get-tuple-element.114), channel_id=1, source_target_pairs={{0,24},{1,25},{2,26},{3,27},{4,28},{5,29},{6,30},{7,31},{8,16},{9,... | collective-permute-start | bytes 98312 | tf_op jit(solution)/shard_map/ppermute | solution.py:61
  42.0 0.0 collective-permute-start.10
  42.0 1.1 %collective-permute-start.11 = (bf16[64,256]{1,0:T(8,128)(2,1)S(1)}, bf16[64,256]{1,0:T(8,128)(2,1)S(1)}, u32[]{:S(2)}, u32[]{:S(2)}) collective-permute-start(bf16[64,256]{1,0:T(8,128)(2,1)S(1)} %get-tuple-element.116), channel_id=1, source_target_pairs={{0,8},{1,9},{2,10},{3,11},{4,12},{5,13},{6,14},{7,15},{8,0},{9,1},... | collective-permute-start | bytes 98312 | tf_op jit(solution)/shard_map/ppermute | solution.py:61
  43.1 1.7 %collective-permute-done.9.r_2_ = bf16[64,256]{1,0:T(8,128)(2,1)S(1)} collective-permute-done((bf16[64,256]{1,0:T(8,128)(2,1)S(1)}, bf16[64,256]{1,0:T(8,128)(2,1)S(1)}, u32[]{:S(2)}, u32[]{:S(2)}) %collective-permute-start.9) | collective-permute-done | bytes 32800 | tf_op jit(solution)/shard_map/ppermute | solution.py:61
  44.8 2.0 %collective-permute-done.10.r_3_ = bf16[64,256]{1,0:T(8,128)(2,1)S(1)} collective-permute-done((bf16[64,256]{1,0:T(8,128)(2,1)S(1)}, bf16[64,256]{1,0:T(8,128)(2,1)S(1)}, u32[]{:S(2)}, u32[]{:S(2)}) %collective-permute-start.10) | collective-permute-done | bytes 32800 | tf_op jit(solution)/shard_map/ppermute | solution.py:61
  46.8 0.0 collective-permute-done.11.r_4_
  46.8 0.6 shard_map.195.r_1_
  47.4 0.3 collective-permute-start.14
  47.6 1.9 %collective-permute-start.13 = (bf16[64,256]{1,0:T(8,128)(2,1)S(1)}, bf16[64,256]{1,0:T(8,128)(2,1)S(1)}, u32[]{:S(2)}, u32[]{:S(2)}) collective-permute-start(bf16[64,256]{1,0:T(8,128)(2,1)S(1)} %shard_map.195.r_1_), channel_id=1, source_target_pairs={{0,16},{1,17},{2,18},{3,19},{4,20},{5,21},{6,22},{7,23},{8,24},{9,... | collective-permute-start | bytes 98312 | tf_op jit(solution)/shard_map/ppermute | solution.py:61
  49.5 2.3 %collective-permute-start.12 = (bf16[64,256]{1,0:T(8,128)(2,1)S(1)}, bf16[64,256]{1,0:T(8,128)(2,1)S(1)}, u32[]{:S(2)}, u32[]{:S(2)}) collective-permute-start(bf16[64,256]{1,0:T(8,128)(2,1)S(1)} %shard_map.195.r_1_), channel_id=1, source_target_pairs={{0,24},{1,25},{2,26},{3,27},{4,28},{5,29},{6,30},{7,31},{8,16},{9,... | collective-permute-start | bytes 98312 | tf_op jit(solution)/shard_map/ppermute | solution.py:61
  51.8 2.7 %shard_map.194 = (bf16[256,256]{1,0:T(8,128)(2,1)}, f32[256,256]{1,0:T(8,128)S(1)}, bf16[256,256]{1,0:T(8,128)(2,1)S(1)}, s32[4,128]{1,0:T(4,128)S(1)}) custom-call(s32[2]{0:T(128)S(1)} %bitcast.18, bf16[256,256]{1,0:T(8,128)(2,1)} %refs_0_.1, bf16[512,256]{1,0:T(8,128)(2,1)} %refs_1_.3, bf16[256,256]{1,0:T(8,128)(2,1)} %bitcast.22, s32[4,128]{1,0:T(4,128)} %bitcast.25, ...), custom_call_target="tpu_custom_call" | custom-call | flops 1000000000 | bytes 2097152 | tf_op jit(solution)/shard_map/pallas_call | solution.py:72
  54.5 0.0 collective-permute-done.15.refs_4_
  54.5 0.1 collective-permute-start.21
  54.6 0.0 collective-permute-done.16.refs_6_
  54.6 0.7 %collective-permute-start.20 = (bf16[256,256]{1,0:T(8,128)(2,1)S(1)}, bf16[256,256]{1,0:T(8,128)(2,1)S(1)}, u32[]{:S(2)}, u32[]{:S(2)}) collective-permute-start(bf16[256,256]{1,0:T(8,128)(2,1)S(1)} %get-tuple-element.126), channel_id=1, source_target_pairs={{0,1},{1,0},{2,3},{3,2},{4,5},{5,4},{6,7},{7,6},{8,9},{9,8},{10,11... | collective-permute-start | bytes 393224 | tf_op jit(solution)/shard_map/ppermute | solution.py:61
  55.3 0.0 collective-permute-done.14.r_4_
  55.3 0.0 collective-permute-done.13.r_3_
  55.3 0.0 collective-permute-done.12.r_2_
  55.3 0.6 shard_map.196.r_1_
  55.9 1.4 %collective-permute-start.19 = (bf16[256,256]{1,0:T(8,128)(2,1)S(1)}, bf16[256,256]{1,0:T(8,128)(2,1)S(1)}, u32[]{:S(2)}, u32[]{:S(2)}) collective-permute-start(bf16[256,256]{1,0:T(8,128)(2,1)S(1)} %shard_map.196.r_1_), channel_id=1, source_target_pairs={{0,1},{1,0},{2,3},{3,2},{4,5},{5,4},{6,7},{7,6},{8,9},{9,8},{10,11... | collective-permute-start | bytes 393224 | tf_op jit(solution)/shard_map/ppermute | solution.py:61
  57.3 0.8 %collective-permute-start.18 = (bf16[256,256]{1,0:T(8,128)(2,1)S(1)}, bf16[256,256]{1,0:T(8,128)(2,1)S(1)}, u32[]{:S(2)}, u32[]{:S(2)}) collective-permute-start(bf16[256,256]{1,0:T(8,128)(2,1)S(1)} %shard_map.196.r_1_), channel_id=1, source_target_pairs={{0,4},{1,5},{2,6},{3,7},{4,0},{5,1},{6,2},{7,3},{8,12},{9,13},{10,... | collective-permute-start | bytes 393224 | tf_op jit(solution)/shard_map/ppermute | solution.py:61
  58.2 1.3 %collective-permute-start.17 = (bf16[256,256]{1,0:T(8,128)(2,1)S(1)}, bf16[256,256]{1,0:T(8,128)(2,1)S(1)}, u32[]{:S(2)}, u32[]{:S(2)}) collective-permute-start(bf16[256,256]{1,0:T(8,128)(2,1)S(1)} %shard_map.196.r_1_), channel_id=1, source_target_pairs={{0,5},{1,4},{2,7},{3,6},{4,1},{5,0},{6,3},{7,2},{8,13},{9,12},{10,... | collective-permute-start | bytes 393224 | tf_op jit(solution)/shard_map/ppermute | solution.py:61
  59.5 0.0 collective-permute-done.21.refs_7_
  59.5 0.7 collective-permute-start.22
  60.1 0.0 collective-permute-done.22.refs_8_
  60.1 0.8 %collective-permute-done.20.refs_5_ = bf16[256,256]{1,0:T(8,128)(2,1)S(1)} collective-permute-done((bf16[256,256]{1,0:T(8,128)(2,1)S(1)}, bf16[256,256]{1,0:T(8,128)(2,1)S(1)}, u32[]{:S(2)}, u32[]{:S(2)}) %collective-permute-start.20) | collective-permute-done | bytes 131104 | tf_op jit(solution)/shard_map/ppermute | solution.py:61
  61.0 5.2 %collective-permute-done.19.r_4_ = bf16[256,256]{1,0:T(8,128)(2,1)S(1)} collective-permute-done((bf16[256,256]{1,0:T(8,128)(2,1)S(1)}, bf16[256,256]{1,0:T(8,128)(2,1)S(1)}, u32[]{:S(2)}, u32[]{:S(2)}) %collective-permute-start.19) | collective-permute-done | bytes 131104 | tf_op jit(solution)/shard_map/ppermute | solution.py:61
  66.1 0.0 collective-permute-done.18.r_3_
  66.1 0.0 collective-permute-done.17.r_2_
  66.1 0.6 shard_map.198.r_1_
  66.7 0.2 collective-permute-start.23
  66.9 1.5 %shard_map.197 = bf16[256,256]{1,0:T(8,128)(2,1)} custom-call(s32[7]{0:T(128)S(1)} %stack.47.info.r_0_, bf16[256,256]{1,0:T(8,128)(2,1)S(1)} %get-tuple-element.105.refs_0_, s32[4,128]{1,0:T(4,128)S(1)} %get-tuple-element.106.refs_1_, f32[256,256]{1,0:T(8,128)S(1)} %get-tuple-element.107.refs_2_, f32[256,256]{1,0:T(8,128)S(1)} %get-tuple-element.112.refs_3_, ...), custom_call_target="tpu_custom_call" | custom-call | tf_op jit(solution)/shard_map/pallas_call | solution.py:72
  68.4 0.3 collective-permute-done.23.r_2_
  68.7 1.9 %shard_map.199 = (f32[256,256]{1,0:T(8,128)}, f32[256,256]{1,0:T(8,128)}, f32[256,256]{1,0:T(8,128)}, f32[256,256]{1,0:T(8,128)}, f32[256,512]{1,0:T(8,128)}, /*index=5*/f32[512,256]{1,0:T(8,128)}) custom-call(s32[7]{0:T(128)S(1)} %stack.47.info.r_0_, bf16[1024,256]{1,0:T(8,128)(2,1)S(1)} %shard_map.198.r_1_, bf16[1024,256]{1,0:T(8,128)(2,1)S(1)} %collective-permute-done.23.r_2_), custom_call_target="tpu_custom_call" | custom-call | tf_op jit(solution)/shard_map/pallas_call | solution.py:72
  (2 shorter events, 0.0 us)
Async XLA Ops:
  2.6 10.9 %collective-permute-start.2 = (bf16[272,256]{1,0:T(8,128)(2,1)S(1)}, bf16[272,256]{1,0:T(8,128)(2,1)S(1)}, u32[]{:S(2)}, u32[]{:S(2)}) collective-permute-start(bf16[272,256]{1,0:T(8,128)(2,1)S(1)} %get-tuple-element.75.refs_6_.r_11_), channel_id=1, source_target_pairs={{0,16},{1,17},{2,18},{3,19},{4,20},{5,21},{6,22},{7,23},{8,24},{9,... | collective-permute-start | bytes 417800 | tf_op jit(solution)/shard_map/ppermute | solution.py:61
  6.7 6.8 %collective-permute-start.1 = (bf16[272,256]{1,0:T(8,128)(2,1)S(1)}, bf16[272,256]{1,0:T(8,128)(2,1)S(1)}, u32[]{:S(2)}, u32[]{:S(2)}) collective-permute-start(bf16[272,256]{1,0:T(8,128)(2,1)S(1)} %get-tuple-element.75.refs_6_.r_11_), channel_id=1, source_target_pairs={{0,1},{1,0},{2,3},{3,2},{4,5},{5,4},{6,7},{7,6},{8,9},{9,8},{10,11... | collective-permute-start | bytes 417800 | tf_op jit(solution)/shard_map/ppermute | solution.py:61
  8.2 6.7 %collective-permute-start = (bf16[272,256]{1,0:T(8,128)(2,1)S(1)}, bf16[272,256]{1,0:T(8,128)(2,1)S(1)}, u32[]{:S(2)}, u32[]{:S(2)}) collective-permute-start(bf16[272,256]{1,0:T(8,128)(2,1)S(1)} %get-tuple-element.75.refs_6_.r_11_), channel_id=1, source_target_pairs={{0,8},{1,9},{2,10},{3,11},{4,12},{5,13},{6,14},{7,15},{8,0},{9,1},... | collective-permute-start | bytes 417800 | tf_op jit(solution)/shard_map/ppermute | solution.py:61
  9.8 3.3 %collective-permute-start.3 = (bf16[128,256]{1,0:T(8,128)(2,1)S(1)}, bf16[128,256]{1,0:T(8,128)(2,1)S(1)}, u32[]{:S(2)}, u32[]{:S(2)}) collective-permute-start(bf16[128,256]{1,0:T(8,128)(2,1)S(1)} %get-tuple-element.79), channel_id=1, source_target_pairs={{0,2},{4,6},{8,10},{12,14},{16,18},{20,22},{24,26},{28,30},{2,0},{... | collective-permute-start | bytes 196616 | tf_op jit(solution)/shard_map/ppermute | solution.py:51
  9.8 3.3 %collective-permute-start.4 = (bf16[128,256]{1,0:T(8,128)(2,1)S(1)}, bf16[128,256]{1,0:T(8,128)(2,1)S(1)}, u32[]{:S(2)}, u32[]{:S(2)}) collective-permute-start(bf16[128,256]{1,0:T(8,128)(2,1)S(1)} %get-tuple-element.80), channel_id=1, source_target_pairs={{2,4},{6,8},{10,12},{14,16},{18,20},{22,24},{26,28},{4,2},{8,6},{1... | collective-permute-start | bytes 196616 | tf_op jit(solution)/shard_map/ppermute | solution.py:51
  10.5 2.5 %copy-start.1 = (s32[1,1,3,2]{2,3,1,0:T(2,128)S(1)}, s32[1,1,3,2]{2,3,1,0:T(2,128)}, u32[]{:S(2)}) copy-start(s32[1,1,3,2]{2,3,1,0:T(2,128)} %param.24) | copy-start | bytes 76
  10.5 4.4 %copy-start = (s32[1,1,2]{2,1,0:T(1,128)S(1)}, s32[1,1,2]{2,1,0:T(1,128)}, u32[]{:S(2)}) copy-start(s32[1,1,2]{2,1,0:T(1,128)} %param.21) | copy-start | bytes 28
  25.0 2.7 %collective-permute-start.5 = (bf16[1024,256]{1,0:T(8,128)(2,1)S(1)}, bf16[1024,256]{1,0:T(8,128)(2,1)S(1)}, u32[]{:S(2)}, u32[]{:S(2)}) collective-permute-start(bf16[1024,256]{1,0:T(8,128)(2,1)S(1)} %get-tuple-element.82), channel_id=1, source_target_pairs={{0,2},{1,3},{2,0},{3,1},{4,6},{5,7},{6,4},{7,5},{8,10},{9,11},{10,... | collective-permute-start | bytes 1572872 | tf_op jit(solution)/shard_map/ppermute | solution.py:61
  28.4 9.6 %collective-permute-start.6 = (bf16[256,256]{1,0:T(8,128)(2,1)S(1)}, bf16[256,256]{1,0:T(8,128)(2,1)S(1)}, u32[]{:S(2)}, u32[]{:S(2)}) collective-permute-start(bf16[256,256]{1,0:T(8,128)(2,1)S(1)} %get-tuple-element.88), channel_id=1, source_target_pairs={{0,5},{1,4},{2,7},{3,6},{4,1},{5,0},{6,3},{7,2},{8,13},{9,12},{10,... | collective-permute-start | bytes 393224 | tf_op jit(solution)/shard_map/ppermute | solution.py:61
  30.8 7.2 %collective-permute-start.7 = (bf16[256,256]{1,0:T(8,128)(2,1)S(1)}, bf16[256,256]{1,0:T(8,128)(2,1)S(1)}, u32[]{:S(2)}, u32[]{:S(2)}) collective-permute-start(bf16[256,256]{1,0:T(8,128)(2,1)S(1)} %get-tuple-element.89), channel_id=1, source_target_pairs={{0,4},{1,5},{2,6},{3,7},{4,0},{5,1},{6,2},{7,3},{8,12},{9,13},{10,... | collective-permute-start | bytes 393224 | tf_op jit(solution)/shard_map/ppermute | solution.py:61
  30.9 7.1 %collective-permute-start.8 = (bf16[256,256]{1,0:T(8,128)(2,1)S(1)}, bf16[256,256]{1,0:T(8,128)(2,1)S(1)}, u32[]{:S(2)}, u32[]{:S(2)}) collective-permute-start(bf16[256,256]{1,0:T(8,128)(2,1)S(1)} %get-tuple-element.90), channel_id=1, source_target_pairs={{0,1},{1,0},{2,3},{3,2},{4,5},{5,4},{6,7},{7,6},{8,9},{9,8},{10,11... | collective-permute-start | bytes 393224 | tf_op jit(solution)/shard_map/ppermute | solution.py:61
  34.1 20.4 %collective-permute-start.15 = (bf16[256,256]{1,0:T(8,128)(2,1)S(1)}, bf16[256,256]{1,0:T(8,128)(2,1)S(1)}, u32[]{:S(2)}, u32[]{:S(2)}) collective-permute-start(bf16[256,256]{1,0:T(8,128)(2,1)S(1)} %get-tuple-element.120), channel_id=1, source_target_pairs={{0,16},{1,17},{2,18},{3,19},{4,20},{5,21},{6,22},{7,23},{8,24},{9,... | collective-permute-start | bytes 393224 | tf_op jit(solution)/shard_map/ppermute | solution.py:61
  36.0 18.6 %collective-permute-start.16 = (bf16[256,256]{1,0:T(8,128)(2,1)S(1)}, bf16[256,256]{1,0:T(8,128)(2,1)S(1)}, u32[]{:S(2)}, u32[]{:S(2)}) collective-permute-start(bf16[256,256]{1,0:T(8,128)(2,1)S(1)} %get-tuple-element.121), channel_id=1, source_target_pairs={{0,8},{1,9},{2,10},{3,11},{4,12},{5,13},{6,14},{7,15},{8,0},{9,1},... | collective-permute-start | bytes 393224 | tf_op jit(solution)/shard_map/ppermute | solution.py:61
  38.6 6.1 %collective-permute-start.9 = (bf16[64,256]{1,0:T(8,128)(2,1)S(1)}, bf16[64,256]{1,0:T(8,128)(2,1)S(1)}, u32[]{:S(2)}, u32[]{:S(2)}) collective-permute-start(bf16[64,256]{1,0:T(8,128)(2,1)S(1)} %get-tuple-element.114), channel_id=1, source_target_pairs={{0,24},{1,25},{2,26},{3,27},{4,28},{5,29},{6,30},{7,31},{8,16},{9,... | collective-permute-start | bytes 98312 | tf_op jit(solution)/shard_map/ppermute | solution.py:61
  42.0 4.8 %collective-permute-start.10 = (bf16[64,256]{1,0:T(8,128)(2,1)S(1)}, bf16[64,256]{1,0:T(8,128)(2,1)S(1)}, u32[]{:S(2)}, u32[]{:S(2)}) collective-permute-start(bf16[64,256]{1,0:T(8,128)(2,1)S(1)} %get-tuple-element.115), channel_id=1, source_target_pairs={{0,16},{1,17},{2,18},{3,19},{4,20},{5,21},{6,22},{7,23},{8,24},{9,... | collective-permute-start | bytes 98312 | tf_op jit(solution)/shard_map/ppermute | solution.py:61
  42.0 4.8 %collective-permute-start.11 = (bf16[64,256]{1,0:T(8,128)(2,1)S(1)}, bf16[64,256]{1,0:T(8,128)(2,1)S(1)}, u32[]{:S(2)}, u32[]{:S(2)}) collective-permute-start(bf16[64,256]{1,0:T(8,128)(2,1)S(1)} %get-tuple-element.116), channel_id=1, source_target_pairs={{0,8},{1,9},{2,10},{3,11},{4,12},{5,13},{6,14},{7,15},{8,0},{9,1},... | collective-permute-start | bytes 98312 | tf_op jit(solution)/shard_map/ppermute | solution.py:61
  47.4 8.0 %collective-permute-start.14 = (bf16[64,256]{1,0:T(8,128)(2,1)S(1)}, bf16[64,256]{1,0:T(8,128)(2,1)S(1)}, u32[]{:S(2)}, u32[]{:S(2)}) collective-permute-start(bf16[64,256]{1,0:T(8,128)(2,1)S(1)} %shard_map.195.r_1_), channel_id=1, source_target_pairs={{0,8},{1,9},{2,10},{3,11},{4,12},{5,13},{6,14},{7,15},{8,0},{9,1},... | collective-permute-start | bytes 98312 | tf_op jit(solution)/shard_map/ppermute | solution.py:61
  47.6 7.7 %collective-permute-start.13 = (bf16[64,256]{1,0:T(8,128)(2,1)S(1)}, bf16[64,256]{1,0:T(8,128)(2,1)S(1)}, u32[]{:S(2)}, u32[]{:S(2)}) collective-permute-start(bf16[64,256]{1,0:T(8,128)(2,1)S(1)} %shard_map.195.r_1_), channel_id=1, source_target_pairs={{0,16},{1,17},{2,18},{3,19},{4,20},{5,21},{6,22},{7,23},{8,24},{9,... | collective-permute-start | bytes 98312 | tf_op jit(solution)/shard_map/ppermute | solution.py:61
  49.5 5.8 %collective-permute-start.12 = (bf16[64,256]{1,0:T(8,128)(2,1)S(1)}, bf16[64,256]{1,0:T(8,128)(2,1)S(1)}, u32[]{:S(2)}, u32[]{:S(2)}) collective-permute-start(bf16[64,256]{1,0:T(8,128)(2,1)S(1)} %shard_map.195.r_1_), channel_id=1, source_target_pairs={{0,24},{1,25},{2,26},{3,27},{4,28},{5,29},{6,30},{7,31},{8,16},{9,... | collective-permute-start | bytes 98312 | tf_op jit(solution)/shard_map/ppermute | solution.py:61
  54.5 4.9 %collective-permute-start.21 = (bf16[128,256]{1,0:T(8,128)(2,1)S(1)}, bf16[128,256]{1,0:T(8,128)(2,1)S(1)}, u32[]{:S(2)}, u32[]{:S(2)}) collective-permute-start(bf16[128,256]{1,0:T(8,128)(2,1)S(1)} %get-tuple-element.127), channel_id=1, source_target_pairs={{0,2},{4,6},{8,10},{12,14},{16,18},{20,22},{24,26},{28,30},{2,0},{... | collective-permute-start | bytes 196616 | tf_op jit(solution)/shard_map/ppermute | solution.py:51
  54.6 6.4 %collective-permute-start.20 = (bf16[256,256]{1,0:T(8,128)(2,1)S(1)}, bf16[256,256]{1,0:T(8,128)(2,1)S(1)}, u32[]{:S(2)}, u32[]{:S(2)}) collective-permute-start(bf16[256,256]{1,0:T(8,128)(2,1)S(1)} %get-tuple-element.126), channel_id=1, source_target_pairs={{0,1},{1,0},{2,3},{3,2},{4,5},{5,4},{6,7},{7,6},{8,9},{9,8},{10,11... | collective-permute-start | bytes 393224 | tf_op jit(solution)/shard_map/ppermute | solution.py:61
  55.9 10.2 %collective-permute-start.19 = (bf16[256,256]{1,0:T(8,128)(2,1)S(1)}, bf16[256,256]{1,0:T(8,128)(2,1)S(1)}, u32[]{:S(2)}, u32[]{:S(2)}) collective-permute-start(bf16[256,256]{1,0:T(8,128)(2,1)S(1)} %shard_map.196.r_1_), channel_id=1, source_target_pairs={{0,1},{1,0},{2,3},{3,2},{4,5},{5,4},{6,7},{7,6},{8,9},{9,8},{10,11... | collective-permute-start | bytes 393224 | tf_op jit(solution)/shard_map/ppermute | solution.py:61
  57.3 8.8 %collective-permute-start.18 = (bf16[256,256]{1,0:T(8,128)(2,1)S(1)}, bf16[256,256]{1,0:T(8,128)(2,1)S(1)}, u32[]{:S(2)}, u32[]{:S(2)}) collective-permute-start(bf16[256,256]{1,0:T(8,128)(2,1)S(1)} %shard_map.196.r_1_), channel_id=1, source_target_pairs={{0,4},{1,5},{2,6},{3,7},{4,0},{5,1},{6,2},{7,3},{8,12},{9,13},{10,... | collective-permute-start | bytes 393224 | tf_op jit(solution)/shard_map/ppermute | solution.py:61
  58.2 8.0 %collective-permute-start.17 = (bf16[256,256]{1,0:T(8,128)(2,1)S(1)}, bf16[256,256]{1,0:T(8,128)(2,1)S(1)}, u32[]{:S(2)}, u32[]{:S(2)}) collective-permute-start(bf16[256,256]{1,0:T(8,128)(2,1)S(1)} %shard_map.196.r_1_), channel_id=1, source_target_pairs={{0,5},{1,4},{2,7},{3,6},{4,1},{5,0},{6,3},{7,2},{8,13},{9,12},{10,... | collective-permute-start | bytes 393224 | tf_op jit(solution)/shard_map/ppermute | solution.py:61
  59.5 0.7 collective-permute-start.22
  66.7 2.0 %collective-permute-start.23 = (bf16[1024,256]{1,0:T(8,128)(2,1)S(1)}, bf16[1024,256]{1,0:T(8,128)(2,1)S(1)}, u32[]{:S(2)}, u32[]{:S(2)}) collective-permute-start(bf16[1024,256]{1,0:T(8,128)(2,1)S(1)} %shard_map.198.r_1_), channel_id=1, source_target_pairs={{0,2},{1,3},{2,0},{3,1},{4,6},{5,7},{6,4},{7,5},{8,10},{9,11},{10,... | collective-permute-start | bytes 1572872 | tf_op jit(solution)/shard_map/ppermute | solution.py:61

commit v6 on v5

--- a/solution.py
+++ b/solution.py
@@ -14,6 +14,7 @@
 AXES = ("sx", "sy")
 EXTRA = 16
 MATCHINGS = 3
+STEPS = 2
 SIDES = 4
 F32 = jnp.float32
 BF16 = jnp.bfloat16
@@ -61,7 +62,7 @@
     return lax.ppermute(value, AXES, [(i, i ^ mask) for i in range(count)])
 
 
-def call(kernel, outs, args, smem=0, hbm=0, scratch=(), limit=16, flops=0, nbytes=0):
+def call(kernel, outs, args, smem=0, hbm=0, scratch=(), limit=16, flops=0, nbytes=0, outside=False):
     specs = [pl.BlockSpec(memory_space=pltpu.SMEM)] * smem
     specs += [pl.BlockSpec(memory_space=pltpu.HBM)] * hbm
     args = [pltpu.with_memory_space_constraint(a, pltpu.HBM) if smem <= i < smem + hbm else a for i, a in enumerate(args)]
@@ -73,7 +74,7 @@
         kernel,
         out_shape=[jax.ShapeDtypeStruct(s, d) for s, d in outs],
         in_specs=specs,
-        out_specs=[pl.BlockSpec(memory_space=pltpu.VMEM)] * len(outs),
+        out_specs=[pl.BlockSpec(memory_space=pltpu.HBM if outside else pltpu.VMEM)] * len(outs),
         scratch_shapes=list(scratch),
         compiler_params=pltpu.CompilerParams(vmem_limit_bytes=limit * 2**20),
         cost_estimate=pl.CostEstimate(flops=flops, bytes_accessed=nbytes, transcendentals=0),
@@ -188,7 +189,7 @@
     rims = refs[MATCHINGS + 1 : MATCHINGS + 1 + (2 if merge_y else 4)]
     refs = refs[MATCHINGS + 1 + len(rims) :]
     keep, send, kvg, moves, query_out, hidden_out, activ_out, grad_hidden_out = refs[:8]
-    grads, xcat, probs, dotted, pbf, sgrad, qstack, gstack, across, near_rows, near_cols, real_cols = refs[8:]
+    grads, xcat, grown, dotted, pbf, sgrad, qstack, gstack, across, near_rows, near_cols, real_cols = refs[8:]
 
     count, width = nodes.shape
     hidden_units = wup.shape[1]
@@ -268,7 +269,8 @@
     rim_top = jnp.maximum(jnp.maximum(rim_scores[0], rim_scores[1]), jnp.maximum(rim_scores[2], rim_scores[3]))
 
     pairs = [(b, first) for b in range(blocks) for first in range(0, HEADS, 2)]
-    groups = MATCHINGS + 1
+    groups = STEPS
+    chunk = keys // groups
 
     def folded(value, combine):
         part = value[0:8]
@@ -285,10 +287,11 @@
     def make_scores(u, c):
         b, first = pairs[u]
         at = slice(first * size, (first + 2) * size)
-        rows = slice(c * size, (c + 1) * size)
+        rows = slice(c * chunk, (c + 1) * chunk)
         score = nn(near_rows[0, b, rows, :], across[b, :, at]) * (scale * log2e)
-        score = score + jnp.concatenate([bias[b][c], bias[b][c]], axis=1)
-        probs[b, rows, at] = score
+        barred = jnp.concatenate(bias[b][c * chunk // size : (c + 1) * chunk // size], axis=0)
+        score = score + jnp.concatenate([barred, barred], axis=1)
+        grown[b, rows, at] = score
         part = folded(score, jnp.maximum)
         tops[u] = part if c == 0 else jnp.maximum(tops[u], part)
         if c == groups - 1:
@@ -297,10 +300,10 @@
     def make_exp(u, c):
         b, first = pairs[u]
         at = slice(first * size, (first + 2) * size)
-        rows = slice(c * size, (c + 1) * size)
-        grown = jnp.exp2(probs[b, rows, at] - tops[u])
-        probs[b, rows, at] = grown
-        part = folded(grown, jnp.add)
+        rows = slice(c * chunk, (c + 1) * chunk)
+        raised = jnp.exp2(grown[b, rows, at] - tops[u])
+        grown[b, rows, at] = raised
+        part = folded(raised, jnp.add)
         sums[u] = part if c == 0 else sums[u] + part
         if c == groups - 1:
             total = jnp.sum(sums[u], axis=0, keepdims=True)
@@ -311,10 +314,8 @@
     def make_probs(u, c):
         b, first = pairs[u]
         at = slice(first * size, (first + 2) * size)
-        rows = slice(c * size, (c + 1) * size)
-        prob = probs[b, rows, at] * inverses[u]
-        probs[b, rows, at] = prob
-        pbf[b, rows, at] = prob.astype(BF16)
+        rows = slice(c * chunk, (c + 1) * chunk)
+        pbf[b, rows, at] = (grown[b, rows, at] * inverses[u]).astype(BF16)
 
     def make_mix(u):
         b, first = pairs[u]
@@ -403,19 +404,20 @@
     def make_dots(u, c):
         b, first = pairs[u]
         at = slice(first * size, (first + 2) * size)
-        rows = slice(c * size, (c + 1) * size)
+        rows = slice(c * chunk, (c + 1) * chunk)
         dots = nn(near_rows[1, b, rows, :], across[b, :, at])
         dotted[b, rows, at] = dots
-        part = folded(probs[b, rows, at] * dots, jnp.add)
+        part = folded(grown[b, rows, at] * dots, jnp.add)
         inners[u] = part if c == 0 else inners[u] + part
         if c == groups - 1:
-            inners[u] = jnp.sum(inners[u], axis=0, keepdims=True) + both_heads(rim_inner, b, first)
+            inners[u] = jnp.sum(inners[u], axis=0, keepdims=True) * inverses[u] + both_heads(rim_inner, b, first)
 
     def make_grads(u, c):
         b, first = pairs[u]
         at = slice(first * size, (first + 2) * size)
-        rows = slice(c * size, (c + 1) * size)
-        sgrad[b, rows, at] = (probs[b, rows, at] * (dotted[b, rows, at] - inners[u]) * scale).astype(BF16)
+        rows = slice(c * chunk, (c + 1) * chunk)
+        graded = grown[b, rows, at] * ((dotted[b, rows, at] - inners[u]) * (inverses[u] * scale))
+        sgrad[b, rows, at] = graded.astype(BF16)
 
     def make_query(u):
         b, first = pairs[u]
@@ -552,17 +554,23 @@
 
 
 def final_kernel(place, info, own, other, *refs):
-    outs, full = refs[:-1], refs[-1]
-    rows = own.shape[0]
+    count = (len(refs) - 1) // 2
+    outs, buffers, semaphores = refs[:count], refs[count:-1], refs[-1]
+    rows, width = own.shape
     mine = info[place]
-    full[pl.ds(pl.multiple_of(mine * rows, rows), rows), :] = own[...]
-    full[pl.ds(pl.multiple_of((1 - mine) * rows, rows), rows), :] = other[...]
-    width = full.shape[1]
     row = 0
-    for out in outs:
-        for part in range(out.shape[1] // width):
-            out[:, part * width : (part + 1) * width] = full[row : row + out.shape[0], :].astype(F32)
-            row += out.shape[0]
+    copies = []
+    for i, (out, buffer) in enumerate(zip(outs, buffers)):
+        for part in range(buffer.shape[1] // width):
+            half, lo = divmod(row, rows)
+            span = slice(lo, lo + buffer.shape[0])
+            value = jnp.where(mine == half, own[span, :].astype(F32), other[span, :].astype(F32))
+            buffer[:, part * width : (part + 1) * width] = value
+            row += buffer.shape[0]
+        copies.append(pltpu.make_async_copy(buffer, out, semaphores.at[i]))
+        copies[-1].start()
+    for copy in copies:
+        copy.wait()
 
 
 def bit_of(mask_bits, index):
@@ -750,20 +758,16 @@
             nbytes=2 * 2**20,
         )
 
-        def waited():
-            cargo = [back[2], *back[4:]]
-            grad_normed, cargo = lax.optimization_barrier((store["out"][1], tuple(cargo)))
-            store["grad_normed"] = grad_normed
-            m1, near, beyond, *sides = cargo
-            store["m1"] = xor_permute(m1, partner[1])
-            store["rims"] = [pair_permute(near, False), pair_permute(beyond, True)]
-            if sides:
-                store["rims"] += [from_behind(sides[1], "sy", 1), from_behind(sides[0], "sy", -1)]
-            return {}
-
-        return values, waited
+        return values, lambda: {"out": tuple(store["out"])}
 
     def third_stage(values):
+        back = store["back"]
+        values, cargo = lax.optimization_barrier((values, (back[2], *back[4:])))
+        m1, near, beyond, *sides = cargo
+        store["m1"] = xor_permute(m1, partner[1])
+        store["rims"] = [pair_permute(near, False), pair_permute(beyond, True)]
+        if sides:
+            store["rims"] += [from_behind(sides[1], "sy", 1), from_behind(sides[0], "sy", -1)]
         return values, lambda: {"m0": store["m0"], "m2": store["m2"]}
 
     def fourth_stage(values):
@@ -774,7 +778,7 @@
         info, keep, xor_permute(send, core_mask), groups, core_mask, {0: first_stage, 1: second_stage, 2: third_stage, 3: fourth_stage}, store
     )
     layer_out, _, nodes_near, boundary_near = store["out"]
-    grad_normed = store["grad_normed"]
+    grad_normed = store["out"][1]
     returned = [store["m0"], store["m1"], store["m2"]]
     rims = store["rims"]
     grad_nodes = call(
@@ -783,12 +787,14 @@
         [info, nodes_near, boundary_near, grad_hidden, grad_normed, *returned, *rims],
         smem=1,
     )[0]
+    shapes = [((width, width), F32)] * 4 + [((width, units), F32), ((units, width), F32)]
     weights = call(
         lambda *r: final_kernel(SIDES, *r),
-        [((width, width), F32)] * 4 + [((width, units), F32), ((units, width), F32)],
+        shapes,
         [info, own, other],
         smem=1,
-        scratch=[pltpu.VMEM((total_rows, width), BF16)],
+        scratch=[pltpu.VMEM(*shape) for shape in shapes] + [pltpu.SemaphoreType.DMA((len(shapes),))],
+        outside=True,
     )
     return (layer_out.reshape(nodes.shape), grad_nodes.reshape(nodes.shape), *weights)
 

time: 70.9 us -> 68.1 us (0.961)
  waiting for transfers between devices: 13.3 us -> 10.6 us
    ppermute x20, waiting for transfers between devices: 13.3 us -> 10.6 us  [xor_permute(): return lax.ppermute(value, AXES, [(i, i ^ mask) for i in range(count)])]
where the time goes in v6:
time: 68.1 us; the launch traced here: 67.7 us
  starting transfers between devices  30.9 us (45%)
  Pallas kernels  25.2 us (37%)
  waiting for transfers between devices  10.6 us (16%)
  between operations  0.83 us (1%)
    ppermute x20, starting transfers between devices, xor_permute(): return lax.ppermute(value, AXES, [(i, i ^ mask) for i in range(count)])  29.6 us
    pallas_call x12, Pallas kernels, call(): pl.pallas_call(kernel, out_shape=[jax.ShapeDtypeStruct(s, d) for s, d in...  25.2 us
    ppermute x20, waiting for transfers between devices, xor_permute(): return lax.ppermute(value, AXES, [(i, i ^ mask) for i in range(count)])  10.6 us
  transfers between devices with their start and end apart: 24, of which 8 were waited for; matrix products, arithmetic and copies ran while one was open for 0% of the time, Pallas kernels for 15%

profile of v6, /device:TPU:0, one launch (start us, length us, event | category | flops | bytes accessed | tf_op | source)
XLA Modules:
  0.0 67.7 jit_solution(4116087056518939617)
XLA Ops:
  0.7 0.1 stack.47.info.r_0_
  0.7 1.8 %shard_map.188 = (bf16[272,256]{1,0:T(8,128)(2,1)S(1)}, bf16[128,256]{1,0:T(8,128)(2,1)S(1)}, bf16[128,256]{1,0:T(8,128)(2,1)S(1)}) custom-call(s32[7]{0:T(128)S(1)} %stack.47.info.r_0_, bf16[256,256]{1,0:T(8,128)(2,1)} %bitcast.20, s32[4,128]{1,0:T(4,128)} %bitcast.23, s32[2]{0:T(128)} %bitcast.16), custom_call_target="tpu_custom_call" | custom-call | tf_op jit(solution)/shard_map/pallas_call | solution.py:73
  2.6 4.1 %collective-permute-start.2 = (bf16[272,256]{1,0:T(8,128)(2,1)S(1)}, bf16[272,256]{1,0:T(8,128)(2,1)S(1)}, u32[]{:S(2)}, u32[]{:S(2)}) collective-permute-start(bf16[272,256]{1,0:T(8,128)(2,1)S(1)} %get-tuple-element.81.refs_6_.r_11_), channel_id=1, source_target_pairs={{0,16},{1,17},{2,18},{3,19},{4,20},{5,21},{6,22},{7,23},{8,24},{9,... | collective-permute-start | bytes 417800 | tf_op jit(solution)/shard_map/ppermute | solution.py:62
  6.7 1.5 %collective-permute-start.1 = (bf16[272,256]{1,0:T(8,128)(2,1)S(1)}, bf16[272,256]{1,0:T(8,128)(2,1)S(1)}, u32[]{:S(2)}, u32[]{:S(2)}) collective-permute-start(bf16[272,256]{1,0:T(8,128)(2,1)S(1)} %get-tuple-element.81.refs_6_.r_11_), channel_id=1, source_target_pairs={{0,1},{1,0},{2,3},{3,2},{4,5},{5,4},{6,7},{7,6},{8,9},{9,8},{10,11... | collective-permute-start | bytes 417800 | tf_op jit(solution)/shard_map/ppermute | solution.py:62
  8.2 1.6 %collective-permute-start = (bf16[272,256]{1,0:T(8,128)(2,1)S(1)}, bf16[272,256]{1,0:T(8,128)(2,1)S(1)}, u32[]{:S(2)}, u32[]{:S(2)}) collective-permute-start(bf16[272,256]{1,0:T(8,128)(2,1)S(1)} %get-tuple-element.81.refs_6_.r_11_), channel_id=1, source_target_pairs={{0,8},{1,9},{2,10},{3,11},{4,12},{5,13},{6,14},{7,15},{8,0},{9,1},... | collective-permute-start | bytes 417800 | tf_op jit(solution)/shard_map/ppermute | solution.py:62
  9.8 0.0 collective-permute-start.3
  9.8 0.7 collective-permute-start.4
  10.5 0.0 copy-start.1
  10.5 0.0 copy-start
  10.5 2.5 %shard_map.189 = (bf16[12,256,256]{2,1,0:T(8,128)(2,1)S(1)}, bf16[4,256,128]{2,1,0:T(8,128)(2,1)S(1)}, f32[4,8,256]{2,1,0:T(8,128)S(1)}) custom-call(s32[7]{0:T(128)S(1)} %stack.47.info.r_0_, s32[4,128]{1,0:T(4,128)} %bitcast.24, bf16[256,256]{1,0:T(8,128)(2,1)} %refs_0_.1, bf16[256,256]{1,0:T(8,128)(2,1)} %refs_2_.1, bf16[256,256]{1,0:T(8,128)(2,1)} %refs_3_.1, ...), custom_call_target="tpu_custom_call" | custom-call | flops 2000000000 | bytes 4194304 | tf_op jit(solution)/shard_map/pallas_call | solution.py:73
  13.0 0.1 copy.21.r_2_.r_0_
  13.1 0.0 collective-permute-done.3.r_15_
  13.1 0.0 collective-permute-done.4.r_16_
  13.1 0.4 collective-permute-done.2.r_14_
  13.5 0.0 collective-permute-done.1.r_13_
  13.5 1.4 %collective-permute-done.r_12_ = bf16[272,256]{1,0:T(8,128)(2,1)S(1)} collective-permute-done((bf16[272,256]{1,0:T(8,128)(2,1)S(1)}, bf16[272,256]{1,0:T(8,128)(2,1)S(1)}, u32[]{:S(2)}, u32[]{:S(2)}) %collective-permute-start) | collective-permute-done | bytes 139296 | tf_op jit(solution)/shard_map/ppermute | solution.py:62
  14.9 9.9 %shard_map.190 = (f32[1024,256]{1,0:T(8,128)S(1)}, bf16[1024,256]{1,0:T(8,128)(2,1)S(1)}, bf16[2048,512]{1,0:T(8,128)(2,1)S(1)}, bf16[2,256,256]{2,1,0:T(8,128)(...) custom-call(s32[7]{0:T(128)S(1)} %stack.47.info.r_0_, ...), custom_call_target="tpu_custom_call" | custom-call | flops 10000000000 | bytes 8388608 | tf_op jit(solution)/shard_map/pallas_call | solution.py:73
  24.8 1.2 %collective-permute-start.5 = (bf16[1024,256]{1,0:T(8,128)(2,1)S(1)}, bf16[1024,256]{1,0:T(8,128)(2,1)S(1)}, u32[]{:S(2)}, u32[]{:S(2)}) collective-permute-start(bf16[1024,256]{1,0:T(8,128)(2,1)S(1)} %get-tuple-element.88), channel_id=1, source_target_pairs={{0,2},{1,3},{2,0},{3,1},{4,6},{5,7},{6,4},{7,5},{8,10},{9,11},{10,... | collective-permute-start | bytes 1572872 | tf_op jit(solution)/shard_map/ppermute | solution.py:62
  26.0 1.5 %collective-permute-done.5.r_2_ = bf16[1024,256]{1,0:T(8,128)(2,1)S(1)} collective-permute-done((bf16[1024,256]{1,0:T(8,128)(2,1)S(1)}, bf16[1024,256]{1,0:T(8,128)(2,1)S(1)}, u32[]{:S(2)}, u32[]{:S(2)}) %collective-permute-start.5) | collective-permute-done | bytes 524320 | tf_op jit(solution)/shard_map/ppermute | solution.py:62
  27.5 0.7 %shard_map.191 = (f32[256,256]{1,0:T(8,128)S(1)}, bf16[256,256]{1,0:T(8,128)(2,1)S(1)}, bf16[256,256]{1,0:T(8,128)(2,1)S(1)}, bf16[256,256]{1,0:T(8,128)(2,1)S(1)}) custom-call(s32[7]{0:T(128)S(1)} %stack.47.info.r_0_, f32[1024,256]{1,0:T(8,128)S(1)} %get-tuple-element.87.r_1_, bf16[1024,256]{1,0:T(8,128)(2,1)S(1)} %collective-permute-done.5.r_2_), custom_call_target="tpu_custom_call" | custom-call | tf_op jit(solution)/shard_map/pallas_call | solution.py:73
  28.2 2.3 %collective-permute-start.6 = (bf16[256,256]{1,0:T(8,128)(2,1)S(1)}, bf16[256,256]{1,0:T(8,128)(2,1)S(1)}, u32[]{:S(2)}, u32[]{:S(2)}) collective-permute-start(bf16[256,256]{1,0:T(8,128)(2,1)S(1)} %get-tuple-element.94), channel_id=1, source_target_pairs={{0,5},{1,4},{2,7},{3,6},{4,1},{5,0},{6,3},{7,2},{8,13},{9,12},{10,... | collective-permute-start | bytes 393224 | tf_op jit(solution)/shard_map/ppermute | solution.py:62
  30.6 0.1 collective-permute-start.7
  30.7 1.4 %collective-permute-start.8 = (bf16[256,256]{1,0:T(8,128)(2,1)S(1)}, bf16[256,256]{1,0:T(8,128)(2,1)S(1)}, u32[]{:S(2)}, u32[]{:S(2)}) collective-permute-start(bf16[256,256]{1,0:T(8,128)(2,1)S(1)} %get-tuple-element.96), channel_id=1, source_target_pairs={{0,1},{1,0},{2,3},{3,2},{4,5},{5,4},{6,7},{7,6},{8,9},{9,8},{10,11... | collective-permute-start | bytes 393224 | tf_op jit(solution)/shard_map/ppermute | solution.py:62
  32.1 1.8 %shard_map.193 = (f32[256,256]{1,0:T(8,128)S(1)}, bf16[256,256]{1,0:T(8,128)(2,1)S(1)}, bf16[256,256]{1,0:T(8,128)(2,1)S(1)}, bf16[256,256]{1,0:T(8,128)(2,1)S(1...) custom-call(s32[3,2]{1,0:T(4,128)S(1)} %copy.21.r_2_.r_0_, bf16[2048,512]{1,0:T(8,128)(2,1)S(1)} %get-tuple-element.103.r_1_, ...), custom_call_target="tpu_custom_call" | custom-call | flops 2000000000 | bytes 4194304 | tf_op jit(solution)/shard_map/pallas_call | solution.py:73
  33.9 1.8 %collective-permute-start.15 = (bf16[256,256]{1,0:T(8,128)(2,1)S(1)}, bf16[256,256]{1,0:T(8,128)(2,1)S(1)}, u32[]{:S(2)}, u32[]{:S(2)}) collective-permute-start(bf16[256,256]{1,0:T(8,128)(2,1)S(1)} %get-tuple-element.132), channel_id=1, source_target_pairs={{0,16},{1,17},{2,18},{3,19},{4,20},{5,21},{6,22},{7,23},{8,24},{9,... | collective-permute-start | bytes 393224 | tf_op jit(solution)/shard_map/ppermute | solution.py:62
  35.8 2.0 %collective-permute-start.16 = (bf16[256,256]{1,0:T(8,128)(2,1)S(1)}, bf16[256,256]{1,0:T(8,128)(2,1)S(1)}, u32[]{:S(2)}, u32[]{:S(2)}) collective-permute-start(bf16[256,256]{1,0:T(8,128)(2,1)S(1)} %get-tuple-element.133), channel_id=1, source_target_pairs={{0,8},{1,9},{2,10},{3,11},{4,12},{5,13},{6,14},{7,15},{8,0},{9,1},... | collective-permute-start | bytes 393224 | tf_op jit(solution)/shard_map/ppermute | solution.py:62
  37.8 0.0 collective-permute-done.6.r_2_
  37.8 0.0 collective-permute-done.7.r_3_
  37.8 0.0 collective-permute-done.8.r_4_
  37.8 0.6 shard_map.192
  38.4 3.3 %collective-permute-start.9 = (bf16[64,256]{1,0:T(8,128)(2,1)S(1)}, bf16[64,256]{1,0:T(8,128)(2,1)S(1)}, u32[]{:S(2)}, u32[]{:S(2)}) collective-permute-start(bf16[64,256]{1,0:T(8,128)(2,1)S(1)} %get-tuple-element.106), channel_id=1, source_target_pairs={{0,24},{1,25},{2,26},{3,27},{4,28},{5,29},{6,30},{7,31},{8,16},{9,... | collective-permute-start | bytes 98312 | tf_op jit(solution)/shard_map/ppermute | solution.py:62
  41.8 0.0 collective-permute-start.10
  41.8 1.1 %collective-permute-start.11 = (bf16[64,256]{1,0:T(8,128)(2,1)S(1)}, bf16[64,256]{1,0:T(8,128)(2,1)S(1)}, u32[]{:S(2)}, u32[]{:S(2)}) collective-permute-start(bf16[64,256]{1,0:T(8,128)(2,1)S(1)} %get-tuple-element.108), channel_id=1, source_target_pairs={{0,8},{1,9},{2,10},{3,11},{4,12},{5,13},{6,14},{7,15},{8,0},{9,1},... | collective-permute-start | bytes 98312 | tf_op jit(solution)/shard_map/ppermute | solution.py:62
  42.9 2.7 %shard_map.194 = (bf16[256,256]{1,0:T(8,128)(2,1)}, f32[256,256]{1,0:T(8,128)S(1)}, bf16[256,256]{1,0:T(8,128)(2,1)S(1)}, s32[4,128]{1,0:T(4,128)S(1)}) custom-call(s32[2]{0:T(128)S(1)} %bitcast.18, bf16[256,256]{1,0:T(8,128)(2,1)} %refs_0_.1, bf16[512,256]{1,0:T(8,128)(2,1)} %refs_1_.3, bf16[256,256]{1,0:T(8,128)(2,1)} %bitcast.22, s32[4,128]{1,0:T(4,128)} %bitcast.25, ...), custom_call_target="tpu_custom_call" | custom-call | flops 1000000000 | bytes 2097152 | tf_op jit(solution)/shard_map/pallas_call | solution.py:73
  45.6 0.0 collective-permute-done.9.r_2_
  45.6 1.0 %collective-permute-done.10.r_3_ = bf16[64,256]{1,0:T(8,128)(2,1)S(1)} collective-permute-done((bf16[64,256]{1,0:T(8,128)(2,1)S(1)}, bf16[64,256]{1,0:T(8,128)(2,1)S(1)}, u32[]{:S(2)}, u32[]{:S(2)}) %collective-permute-start.10) | collective-permute-done | bytes 32800 | tf_op jit(solution)/shard_map/ppermute | solution.py:62
  46.6 0.0 collective-permute-done.11.r_4_
  46.6 0.6 shard_map.195.r_1_
  47.2 2.4 %collective-permute-start.12 = (bf16[64,256]{1,0:T(8,128)(2,1)S(1)}, bf16[64,256]{1,0:T(8,128)(2,1)S(1)}, u32[]{:S(2)}, u32[]{:S(2)}) collective-permute-start(bf16[64,256]{1,0:T(8,128)(2,1)S(1)} %shard_map.195.r_1_), channel_id=1, source_target_pairs={{0,24},{1,25},{2,26},{3,27},{4,28},{5,29},{6,30},{7,31},{8,16},{9,... | collective-permute-start | bytes 98312 | tf_op jit(solution)/shard_map/ppermute | solution.py:62
  49.5 0.0 collective-permute-start.13
  49.5 2.1 %collective-permute-start.14 = (bf16[64,256]{1,0:T(8,128)(2,1)S(1)}, bf16[64,256]{1,0:T(8,128)(2,1)S(1)}, u32[]{:S(2)}, u32[]{:S(2)}) collective-permute-start(bf16[64,256]{1,0:T(8,128)(2,1)S(1)} %shard_map.195.r_1_), channel_id=1, source_target_pairs={{0,8},{1,9},{2,10},{3,11},{4,12},{5,13},{6,14},{7,15},{8,0},{9,1},... | collective-permute-start | bytes 98312 | tf_op jit(solution)/shard_map/ppermute | solution.py:62
  51.6 0.0 collective-permute-done.15.refs_4_
  51.6 0.0 collective-permute-start.21
  51.6 0.0 collective-permute-done.16.refs_6_
  51.6 0.7 %collective-permute-start.20 = (bf16[256,256]{1,0:T(8,128)(2,1)S(1)}, bf16[256,256]{1,0:T(8,128)(2,1)S(1)}, u32[]{:S(2)}, u32[]{:S(2)}) collective-permute-start(bf16[256,256]{1,0:T(8,128)(2,1)S(1)} %get-tuple-element.138), channel_id=1, source_target_pairs={{0,1},{1,0},{2,3},{3,2},{4,5},{5,4},{6,7},{7,6},{8,9},{9,8},{10,11... | collective-permute-start | bytes 393224 | tf_op jit(solution)/shard_map/ppermute | solution.py:62
  52.4 0.6 collective-permute-done.12.r_2_
  52.9 1.5 %collective-permute-done.13.r_3_ = bf16[64,256]{1,0:T(8,128)(2,1)S(1)} collective-permute-done((bf16[64,256]{1,0:T(8,128)(2,1)S(1)}, bf16[64,256]{1,0:T(8,128)(2,1)S(1)}, u32[]{:S(2)}, u32[]{:S(2)}) %collective-permute-start.13) | collective-permute-done | bytes 32800 | tf_op jit(solution)/shard_map/ppermute | solution.py:62
  54.4 0.0 collective-permute-done.14.r_4_
  54.4 0.6 shard_map.196.r_1_
  55.0 0.6 collective-permute-start.19
  55.6 0.9 %collective-permute-start.18 = (bf16[256,256]{1,0:T(8,128)(2,1)S(1)}, bf16[256,256]{1,0:T(8,128)(2,1)S(1)}, u32[]{:S(2)}, u32[]{:S(2)}) collective-permute-start(bf16[256,256]{1,0:T(8,128)(2,1)S(1)} %shard_map.196.r_1_), channel_id=1, source_target_pairs={{0,4},{1,5},{2,6},{3,7},{4,0},{5,1},{6,2},{7,3},{8,12},{9,13},{10,... | collective-permute-start | bytes 393224 | tf_op jit(solution)/shard_map/ppermute | solution.py:62
  56.5 2.0 %collective-permute-start.17 = (bf16[256,256]{1,0:T(8,128)(2,1)S(1)}, bf16[256,256]{1,0:T(8,128)(2,1)S(1)}, u32[]{:S(2)}, u32[]{:S(2)}) collective-permute-start(bf16[256,256]{1,0:T(8,128)(2,1)S(1)} %shard_map.196.r_1_), channel_id=1, source_target_pairs={{0,5},{1,4},{2,7},{3,6},{4,1},{5,0},{6,3},{7,2},{8,13},{9,12},{10,... | collective-permute-start | bytes 393224 | tf_op jit(solution)/shard_map/ppermute | solution.py:62
  58.5 0.0 collective-permute-done.21.refs_7_
  58.5 0.7 collective-permute-start.22
  59.2 0.0 collective-permute-done.22.refs_8_
  59.2 0.0 collective-permute-done.20.refs_5_
  59.2 3.9 %collective-permute-done.19.r_4_ = bf16[256,256]{1,0:T(8,128)(2,1)S(1)} collective-permute-done((bf16[256,256]{1,0:T(8,128)(2,1)S(1)}, bf16[256,256]{1,0:T(8,128)(2,1)S(1)}, u32[]{:S(2)}, u32[]{:S(2)}) %collective-permute-start.19) | collective-permute-done | bytes 131104 | tf_op jit(solution)/shard_map/ppermute | solution.py:62
  63.2 0.0 collective-permute-done.18.r_3_
  63.2 0.0 collective-permute-done.17.r_2_
  63.2 0.6 shard_map.198.r_1_
  63.8 0.3 collective-permute-start.23
  64.0 1.5 %shard_map.197 = bf16[256,256]{1,0:T(8,128)(2,1)} custom-call(s32[7]{0:T(128)S(1)} %stack.47.info.r_0_, bf16[256,256]{1,0:T(8,128)(2,1)S(1)} %get-tuple-element.118.refs_0_, s32[4,128]{1,0:T(4,128)S(1)} %get-tuple-element.119.refs_1_, f32[256,256]{1,0:T(8,128)S(1)} %get-tuple-element.120.refs_2_, f32[256,256]{1,0:T(8,128)S(1)} %get-tuple-element.121.refs_3_, ...), custom_call_target="tpu_custom_call" | custom-call | tf_op jit(solution)/shard_map/pallas_call | solution.py:73
  65.5 0.2 collective-permute-done.23.r_2_
  65.7 1.9 %shard_map.199 = (f32[256,256]{1,0:T(8,128)}, f32[256,256]{1,0:T(8,128)}, f32[256,256]{1,0:T(8,128)}, f32[256,256]{1,0:T(8,128)}, f32[256,512]{1,0:T(8,128)}, /*index=5*/f32[512,256]{1,0:T(8,128)}) custom-call(s32[7]{0:T(128)S(1)} %stack.47.info.r_0_, bf16[1024,256]{1,0:T(8,128)(2,1)S(1)} %shard_map.198.r_1_, bf16[1024,256]{1,0:T(8,128)(2,1)S(1)} %collective-permute-done.23.r_2_), custom_call_target="tpu_custom_call" | custom-call | tf_op jit(solution)/shard_map/pallas_call | solution.py:73
  (2 shorter events, 0.0 us)
Async XLA Ops:
  2.6 10.9 %collective-permute-start.2 = (bf16[272,256]{1,0:T(8,128)(2,1)S(1)}, bf16[272,256]{1,0:T(8,128)(2,1)S(1)}, u32[]{:S(2)}, u32[]{:S(2)}) collective-permute-start(bf16[272,256]{1,0:T(8,128)(2,1)S(1)} %get-tuple-element.81.refs_6_.r_11_), channel_id=1, source_target_pairs={{0,16},{1,17},{2,18},{3,19},{4,20},{5,21},{6,22},{7,23},{8,24},{9,... | collective-permute-start | bytes 417800 | tf_op jit(solution)/shard_map/ppermute | solution.py:62
  6.7 6.8 %collective-permute-start.1 = (bf16[272,256]{1,0:T(8,128)(2,1)S(1)}, bf16[272,256]{1,0:T(8,128)(2,1)S(1)}, u32[]{:S(2)}, u32[]{:S(2)}) collective-permute-start(bf16[272,256]{1,0:T(8,128)(2,1)S(1)} %get-tuple-element.81.refs_6_.r_11_), channel_id=1, source_target_pairs={{0,1},{1,0},{2,3},{3,2},{4,5},{5,4},{6,7},{7,6},{8,9},{9,8},{10,11... | collective-permute-start | bytes 417800 | tf_op jit(solution)/shard_map/ppermute | solution.py:62
  8.2 6.7 %collective-permute-start = (bf16[272,256]{1,0:T(8,128)(2,1)S(1)}, bf16[272,256]{1,0:T(8,128)(2,1)S(1)}, u32[]{:S(2)}, u32[]{:S(2)}) collective-permute-start(bf16[272,256]{1,0:T(8,128)(2,1)S(1)} %get-tuple-element.81.refs_6_.r_11_), channel_id=1, source_target_pairs={{0,8},{1,9},{2,10},{3,11},{4,12},{5,13},{6,14},{7,15},{8,0},{9,1},... | collective-permute-start | bytes 417800 | tf_op jit(solution)/shard_map/ppermute | solution.py:62
  9.8 3.3 %collective-permute-start.3 = (bf16[128,256]{1,0:T(8,128)(2,1)S(1)}, bf16[128,256]{1,0:T(8,128)(2,1)S(1)}, u32[]{:S(2)}, u32[]{:S(2)}) collective-permute-start(bf16[128,256]{1,0:T(8,128)(2,1)S(1)} %get-tuple-element.85), channel_id=1, source_target_pairs={{0,2},{4,6},{8,10},{12,14},{16,18},{20,22},{24,26},{28,30},{2,0},{... | collective-permute-start | bytes 196616 | tf_op jit(solution)/shard_map/ppermute | solution.py:52
  9.8 3.3 %collective-permute-start.4 = (bf16[128,256]{1,0:T(8,128)(2,1)S(1)}, bf16[128,256]{1,0:T(8,128)(2,1)S(1)}, u32[]{:S(2)}, u32[]{:S(2)}) collective-permute-start(bf16[128,256]{1,0:T(8,128)(2,1)S(1)} %get-tuple-element.86), channel_id=1, source_target_pairs={{2,4},{6,8},{10,12},{14,16},{18,20},{22,24},{26,28},{4,2},{8,6},{1... | collective-permute-start | bytes 196616 | tf_op jit(solution)/shard_map/ppermute | solution.py:52
  10.5 2.5 %copy-start.1 = (s32[1,1,3,2]{2,3,1,0:T(2,128)S(1)}, s32[1,1,3,2]{2,3,1,0:T(2,128)}, u32[]{:S(2)}) copy-start(s32[1,1,3,2]{2,3,1,0:T(2,128)} %param.24) | copy-start | bytes 76
  10.5 4.4 %copy-start = (s32[1,1,2]{2,1,0:T(1,128)S(1)}, s32[1,1,2]{2,1,0:T(1,128)}, u32[]{:S(2)}) copy-start(s32[1,1,2]{2,1,0:T(1,128)} %param.21) | copy-start | bytes 28
  24.8 2.7 %collective-permute-start.5 = (bf16[1024,256]{1,0:T(8,128)(2,1)S(1)}, bf16[1024,256]{1,0:T(8,128)(2,1)S(1)}, u32[]{:S(2)}, u32[]{:S(2)}) collective-permute-start(bf16[1024,256]{1,0:T(8,128)(2,1)S(1)} %get-tuple-element.88), channel_id=1, source_target_pairs={{0,2},{1,3},{2,0},{3,1},{4,6},{5,7},{6,4},{7,5},{8,10},{9,11},{10,... | collective-permute-start | bytes 1572872 | tf_op jit(solution)/shard_map/ppermute | solution.py:62
  28.2 9.6 %collective-permute-start.6 = (bf16[256,256]{1,0:T(8,128)(2,1)S(1)}, bf16[256,256]{1,0:T(8,128)(2,1)S(1)}, u32[]{:S(2)}, u32[]{:S(2)}) collective-permute-start(bf16[256,256]{1,0:T(8,128)(2,1)S(1)} %get-tuple-element.94), channel_id=1, source_target_pairs={{0,5},{1,4},{2,7},{3,6},{4,1},{5,0},{6,3},{7,2},{8,13},{9,12},{10,... | collective-permute-start | bytes 393224 | tf_op jit(solution)/shard_map/ppermute | solution.py:62
  30.6 7.2 %collective-permute-start.7 = (bf16[256,256]{1,0:T(8,128)(2,1)S(1)}, bf16[256,256]{1,0:T(8,128)(2,1)S(1)}, u32[]{:S(2)}, u32[]{:S(2)}) collective-permute-start(bf16[256,256]{1,0:T(8,128)(2,1)S(1)} %get-tuple-element.95), channel_id=1, source_target_pairs={{0,4},{1,5},{2,6},{3,7},{4,0},{5,1},{6,2},{7,3},{8,12},{9,13},{10,... | collective-permute-start | bytes 393224 | tf_op jit(solution)/shard_map/ppermute | solution.py:62
  30.7 7.1 %collective-permute-start.8 = (bf16[256,256]{1,0:T(8,128)(2,1)S(1)}, bf16[256,256]{1,0:T(8,128)(2,1)S(1)}, u32[]{:S(2)}, u32[]{:S(2)}) collective-permute-start(bf16[256,256]{1,0:T(8,128)(2,1)S(1)} %get-tuple-element.96), channel_id=1, source_target_pairs={{0,1},{1,0},{2,3},{3,2},{4,5},{5,4},{6,7},{7,6},{8,9},{9,8},{10,11... | collective-permute-start | bytes 393224 | tf_op jit(solution)/shard_map/ppermute | solution.py:62
  33.9 17.7 %collective-permute-start.15 = (bf16[256,256]{1,0:T(8,128)(2,1)S(1)}, bf16[256,256]{1,0:T(8,128)(2,1)S(1)}, u32[]{:S(2)}, u32[]{:S(2)}) collective-permute-start(bf16[256,256]{1,0:T(8,128)(2,1)S(1)} %get-tuple-element.132), channel_id=1, source_target_pairs={{0,16},{1,17},{2,18},{3,19},{4,20},{5,21},{6,22},{7,23},{8,24},{9,... | collective-permute-start | bytes 393224 | tf_op jit(solution)/shard_map/ppermute | solution.py:62
  35.8 15.9 %collective-permute-start.16 = (bf16[256,256]{1,0:T(8,128)(2,1)S(1)}, bf16[256,256]{1,0:T(8,128)(2,1)S(1)}, u32[]{:S(2)}, u32[]{:S(2)}) collective-permute-start(bf16[256,256]{1,0:T(8,128)(2,1)S(1)} %get-tuple-element.133), channel_id=1, source_target_pairs={{0,8},{1,9},{2,10},{3,11},{4,12},{5,13},{6,14},{7,15},{8,0},{9,1},... | collective-permute-start | bytes 393224 | tf_op jit(solution)/shard_map/ppermute | solution.py:62
  38.4 7.1 %collective-permute-start.9 = (bf16[64,256]{1,0:T(8,128)(2,1)S(1)}, bf16[64,256]{1,0:T(8,128)(2,1)S(1)}, u32[]{:S(2)}, u32[]{:S(2)}) collective-permute-start(bf16[64,256]{1,0:T(8,128)(2,1)S(1)} %get-tuple-element.106), channel_id=1, source_target_pairs={{0,24},{1,25},{2,26},{3,27},{4,28},{5,29},{6,30},{7,31},{8,16},{9,... | collective-permute-start | bytes 98312 | tf_op jit(solution)/shard_map/ppermute | solution.py:62
  41.8 4.8 %collective-permute-start.10 = (bf16[64,256]{1,0:T(8,128)(2,1)S(1)}, bf16[64,256]{1,0:T(8,128)(2,1)S(1)}, u32[]{:S(2)}, u32[]{:S(2)}) collective-permute-start(bf16[64,256]{1,0:T(8,128)(2,1)S(1)} %get-tuple-element.107), channel_id=1, source_target_pairs={{0,16},{1,17},{2,18},{3,19},{4,20},{5,21},{6,22},{7,23},{8,24},{9,... | collective-permute-start | bytes 98312 | tf_op jit(solution)/shard_map/ppermute | solution.py:62
  41.8 4.8 %collective-permute-start.11 = (bf16[64,256]{1,0:T(8,128)(2,1)S(1)}, bf16[64,256]{1,0:T(8,128)(2,1)S(1)}, u32[]{:S(2)}, u32[]{:S(2)}) collective-permute-start(bf16[64,256]{1,0:T(8,128)(2,1)S(1)} %get-tuple-element.108), channel_id=1, source_target_pairs={{0,8},{1,9},{2,10},{3,11},{4,12},{5,13},{6,14},{7,15},{8,0},{9,1},... | collective-permute-start | bytes 98312 | tf_op jit(solution)/shard_map/ppermute | solution.py:62
  47.2 5.8 %collective-permute-start.12 = (bf16[64,256]{1,0:T(8,128)(2,1)S(1)}, bf16[64,256]{1,0:T(8,128)(2,1)S(1)}, u32[]{:S(2)}, u32[]{:S(2)}) collective-permute-start(bf16[64,256]{1,0:T(8,128)(2,1)S(1)} %shard_map.195.r_1_), channel_id=1, source_target_pairs={{0,24},{1,25},{2,26},{3,27},{4,28},{5,29},{6,30},{7,31},{8,16},{9,... | collective-permute-start | bytes 98312 | tf_op jit(solution)/shard_map/ppermute | solution.py:62
  49.5 4.9 %collective-permute-start.13 = (bf16[64,256]{1,0:T(8,128)(2,1)S(1)}, bf16[64,256]{1,0:T(8,128)(2,1)S(1)}, u32[]{:S(2)}, u32[]{:S(2)}) collective-permute-start(bf16[64,256]{1,0:T(8,128)(2,1)S(1)} %shard_map.195.r_1_), channel_id=1, source_target_pairs={{0,16},{1,17},{2,18},{3,19},{4,20},{5,21},{6,22},{7,23},{8,24},{9,... | collective-permute-start | bytes 98312 | tf_op jit(solution)/shard_map/ppermute | solution.py:62
  49.5 4.9 %collective-permute-start.14 = (bf16[64,256]{1,0:T(8,128)(2,1)S(1)}, bf16[64,256]{1,0:T(8,128)(2,1)S(1)}, u32[]{:S(2)}, u32[]{:S(2)}) collective-permute-start(bf16[64,256]{1,0:T(8,128)(2,1)S(1)} %shard_map.195.r_1_), channel_id=1, source_target_pairs={{0,8},{1,9},{2,10},{3,11},{4,12},{5,13},{6,14},{7,15},{8,0},{9,1},... | collective-permute-start | bytes 98312 | tf_op jit(solution)/shard_map/ppermute | solution.py:62
  51.6 6.9 %collective-permute-start.21 = (bf16[128,256]{1,0:T(8,128)(2,1)S(1)}, bf16[128,256]{1,0:T(8,128)(2,1)S(1)}, u32[]{:S(2)}, u32[]{:S(2)}) collective-permute-start(bf16[128,256]{1,0:T(8,128)(2,1)S(1)} %get-tuple-element.139), channel_id=1, source_target_pairs={{0,2},{4,6},{8,10},{12,14},{16,18},{20,22},{24,26},{28,30},{2,0},{... | collective-permute-start | bytes 196616 | tf_op jit(solution)/shard_map/ppermute | solution.py:52
  51.6 7.6 %collective-permute-start.20 = (bf16[256,256]{1,0:T(8,128)(2,1)S(1)}, bf16[256,256]{1,0:T(8,128)(2,1)S(1)}, u32[]{:S(2)}, u32[]{:S(2)}) collective-permute-start(bf16[256,256]{1,0:T(8,128)(2,1)S(1)} %get-tuple-element.138), channel_id=1, source_target_pairs={{0,1},{1,0},{2,3},{3,2},{4,5},{5,4},{6,7},{7,6},{8,9},{9,8},{10,11... | collective-permute-start | bytes 393224 | tf_op jit(solution)/shard_map/ppermute | solution.py:62
  55.0 8.2 %collective-permute-start.19 = (bf16[256,256]{1,0:T(8,128)(2,1)S(1)}, bf16[256,256]{1,0:T(8,128)(2,1)S(1)}, u32[]{:S(2)}, u32[]{:S(2)}) collective-permute-start(bf16[256,256]{1,0:T(8,128)(2,1)S(1)} %shard_map.196.r_1_), channel_id=1, source_target_pairs={{0,1},{1,0},{2,3},{3,2},{4,5},{5,4},{6,7},{7,6},{8,9},{9,8},{10,11... | collective-permute-start | bytes 393224 | tf_op jit(solution)/shard_map/ppermute | solution.py:62
  55.6 7.5 %collective-permute-start.18 = (bf16[256,256]{1,0:T(8,128)(2,1)S(1)}, bf16[256,256]{1,0:T(8,128)(2,1)S(1)}, u32[]{:S(2)}, u32[]{:S(2)}) collective-permute-start(bf16[256,256]{1,0:T(8,128)(2,1)S(1)} %shard_map.196.r_1_), channel_id=1, source_target_pairs={{0,4},{1,5},{2,6},{3,7},{4,0},{5,1},{6,2},{7,3},{8,12},{9,13},{10,... | collective-permute-start | bytes 393224 | tf_op jit(solution)/shard_map/ppermute | solution.py:62
  56.5 6.7 %collective-permute-start.17 = (bf16[256,256]{1,0:T(8,128)(2,1)S(1)}, bf16[256,256]{1,0:T(8,128)(2,1)S(1)}, u32[]{:S(2)}, u32[]{:S(2)}) collective-permute-start(bf16[256,256]{1,0:T(8,128)(2,1)S(1)} %shard_map.196.r_1_), channel_id=1, source_target_pairs={{0,5},{1,4},{2,7},{3,6},{4,1},{5,0},{6,3},{7,2},{8,13},{9,12},{10,... | collective-permute-start | bytes 393224 | tf_op jit(solution)/shard_map/ppermute | solution.py:62
  58.5 0.7 collective-permute-start.22
  63.8 2.0 %collective-permute-start.23 = (bf16[1024,256]{1,0:T(8,128)(2,1)S(1)}, bf16[1024,256]{1,0:T(8,128)(2,1)S(1)}, u32[]{:S(2)}, u32[]{:S(2)}) collective-permute-start(bf16[1024,256]{1,0:T(8,128)(2,1)S(1)} %shard_map.198.r_1_), channel_id=1, source_target_pairs={{0,2},{1,3},{2,0},{3,1},{4,6},{5,7},{6,4},{7,5},{8,10},{9,11},{10,... | collective-permute-start | bytes 1572872 | tf_op jit(solution)/shard_map/ppermute | solution.py:62

commit v7 on v6

--- a/solution.py
+++ b/solution.py
@@ -450,7 +450,7 @@
     half_rows = grads.shape[0] // 2
     mine = info[SIDES]
     keep[...] = grads[pl.ds(pl.multiple_of(mine * half_rows, half_rows), half_rows), :]
-    send[...] = grads[pl.ds(pl.multiple_of((1 - mine) * half_rows, half_rows), half_rows), :].astype(BF16)
+    send[...] = grads[pl.ds(pl.multiple_of((1 - mine) * half_rows, half_rows), half_rows), :]
 
 
 def back_kernel(merge_y, pairing, *refs):
@@ -542,11 +542,11 @@
     mine = info[place]
     outs[0][...] = total_ref[pl.ds(pl.multiple_of(mine * rows, rows), rows), :]
     for d in range(1, parts):
-        outs[d][...] = total_ref[pl.ds(pl.multiple_of((mine ^ d) * rows, rows), rows), :].astype(BF16)
-
-
-def gather_kernel(place, *refs):
-    info, pieces, out = refs[0], [refs[1], *refs[-2:1:-1]], refs[-1]
+        outs[d][...] = total_ref[pl.ds(pl.multiple_of((mine ^ d) * rows, rows), rows), :].astype(outs[d].dtype)
+
+
+def gather_kernel(place, turn, *refs):
+    info, pieces, out = refs[0], [refs[1], *refs[2:-1][::turn]], refs[-1]
     mine = info[place]
     rows = pieces[0].shape[0]
     for d, piece in enumerate(pieces):
@@ -596,17 +596,18 @@
         if work is None:
             return whole, [xor_permute(v, m) for v, m in zip(values, masks)]
         values, waited = work(tuple(values))
-        moved = [xor_permute(v, m) for v, m in zip(values[::-1], masks[::-1])][::-1]
-        moved, done = lax.optimization_barrier((tuple(moved[::-1]), waited()))
+        turn = 1 if stage == 2 * len(groups) else -1
+        moved = [xor_permute(v, m) for v, m in zip(values[::turn], masks[::turn])]
+        moved, done = lax.optimization_barrier((tuple(moved), waited()))
         store.update(done)
-        return whole, list(moved[::-1])
+        return whole, list(moved[::turn])
 
     for level, bits in enumerate(groups):
         parts = 2 ** len(bits)
         rows = kept.shape[0] // parts
         made = call(
             lambda *r, level=level, parts=parts: reduce_kernel(SIDES + 1 + level, parts, *r),
-            [((rows, width), F32)] + [((rows, width), BF16)] * (parts - 1),
+            [((rows, width), F32)] + [((rows, width), F32 if level else BF16)] * (parts - 1),
             [info, kept, *pieces[::-1]],
             smem=1,
             scratch=[pltpu.VMEM(kept.shape, F32)],
@@ -623,9 +624,9 @@
         masks = [offset_mask(groups[level], d) for d in range(1, 2 ** len(groups[level]))]
         whole, pieces = exchange([whole] * len(masks), masks, whole)
         whole = call(
-            lambda *r, level=level: gather_kernel(SIDES + 1 + level, *r),
+            lambda *r, level=level, turn=-1 if level else 1: gather_kernel(SIDES + 1 + level, turn, *r),
             [((whole.shape[0] * (1 + len(masks)), width), BF16)],
-            [info, whole, *pieces[::-1]],
+            [info, whole, *pieces[:: -1 if level else 1]],
             smem=1,
         )[0]
     return whole, xor_permute(whole, core_mask)
@@ -693,7 +694,7 @@
         lambda *r: main_kernel(merge_y, *r),
         [
             ((total_rows // 2, width), F32),
-            ((total_rows // 2, width), BF16),
+            ((total_rows // 2, width), F32),
             ((all_rows, 2 * width), BF16),
             (moves_shape, BF16),
             (square, BF16),

time: 68.1 us -> 70.8 us (1.040)
  waiting for transfers between devices: 10.6 us -> 13.1 us
    ppermute x20, waiting for transfers between devices: 10.6 us -> 13.1 us  [xor_permute(): return lax.ppermute(value, AXES, [(i, i ^ mask) for i in range(count)])]
  transfers between devices with their start and end apart: 24 -> 24, of which waited for: 8 -> 10; matrix products, arithmetic and copies ran while one was open for 0% -> 0% of each run, Pallas kernels for 15% -> 15%
where the time goes in v7:
time: 70.8 us; the launch traced here: 70.3 us
  starting transfers between devices  31 us (44%)
  Pallas kernels  25.2 us (36%)
  waiting for transfers between devices  13.1 us (19%)
  between operations  0.82 us (1%)
    ppermute x20, starting transfers between devices, xor_permute(): return lax.ppermute(value, AXES, [(i, i ^ mask) for i in range(count)])  29.7 us
    pallas_call x12, Pallas kernels, call(): pl.pallas_call(kernel, out_shape=[jax.ShapeDtypeStruct(s, d) for s, d in...  25.2 us
    ppermute x20, waiting for transfers between devices, xor_permute(): return lax.ppermute(value, AXES, [(i, i ^ mask) for i in range(count)])  13.1 us
  transfers between devices with their start and end apart: 24, of which 10 were waited for; matrix products, arithmetic and copies ran while one was open for 0% of the time, Pallas kernels for 15%

profile of v7, /device:TPU:0, one launch (start us, length us, event | category | flops | bytes accessed | tf_op | source)
XLA Modules:
  0.0 70.3 jit_solution(5577723807410550028)
XLA Ops:
  0.7 0.1 stack.47.info.r_0_
  0.7 1.8 %shard_map.188 = (bf16[272,256]{1,0:T(8,128)(2,1)S(1)}, bf16[128,256]{1,0:T(8,128)(2,1)S(1)}, bf16[128,256]{1,0:T(8,128)(2,1)S(1)}) custom-call(s32[7]{0:T(128)S(1)} %stack.47.info.r_0_, bf16[256,256]{1,0:T(8,128)(2,1)} %bitcast.20, s32[4,128]{1,0:T(4,128)} %bitcast.23, s32[2]{0:T(128)} %bitcast.16), custom_call_target="tpu_custom_call" | custom-call | tf_op jit(solution)/shard_map/pallas_call | solution.py:73
  2.6 4.1 %collective-permute-start.2 = (bf16[272,256]{1,0:T(8,128)(2,1)S(1)}, bf16[272,256]{1,0:T(8,128)(2,1)S(1)}, u32[]{:S(2)}, u32[]{:S(2)}) collective-permute-start(bf16[272,256]{1,0:T(8,128)(2,1)S(1)} %get-tuple-element.81.refs_6_.r_11_), channel_id=1, source_target_pairs={{0,16},{1,17},{2,18},{3,19},{4,20},{5,21},{6,22},{7,23},{8,24},{9,... | collective-permute-start | bytes 417800 | tf_op jit(solution)/shard_map/ppermute | solution.py:62
  6.7 1.5 %collective-permute-start.1 = (bf16[272,256]{1,0:T(8,128)(2,1)S(1)}, bf16[272,256]{1,0:T(8,128)(2,1)S(1)}, u32[]{:S(2)}, u32[]{:S(2)}) collective-permute-start(bf16[272,256]{1,0:T(8,128)(2,1)S(1)} %get-tuple-element.81.refs_6_.r_11_), channel_id=1, source_target_pairs={{0,1},{1,0},{2,3},{3,2},{4,5},{5,4},{6,7},{7,6},{8,9},{9,8},{10,11... | collective-permute-start | bytes 417800 | tf_op jit(solution)/shard_map/ppermute | solution.py:62
  8.2 1.6 %collective-permute-start = (bf16[272,256]{1,0:T(8,128)(2,1)S(1)}, bf16[272,256]{1,0:T(8,128)(2,1)S(1)}, u32[]{:S(2)}, u32[]{:S(2)}) collective-permute-start(bf16[272,256]{1,0:T(8,128)(2,1)S(1)} %get-tuple-element.81.refs_6_.r_11_), channel_id=1, source_target_pairs={{0,8},{1,9},{2,10},{3,11},{4,12},{5,13},{6,14},{7,15},{8,0},{9,1},... | collective-permute-start | bytes 417800 | tf_op jit(solution)/shard_map/ppermute | solution.py:62
  9.8 0.0 collective-permute-start.3
  9.8 0.7 collective-permute-start.4
  10.5 0.0 copy-start.1
  10.5 0.0 copy-start
  10.5 2.5 %shard_map.189 = (bf16[12,256,256]{2,1,0:T(8,128)(2,1)S(1)}, bf16[4,256,128]{2,1,0:T(8,128)(2,1)S(1)}, f32[4,8,256]{2,1,0:T(8,128)S(1)}) custom-call(s32[7]{0:T(128)S(1)} %stack.47.info.r_0_, s32[4,128]{1,0:T(4,128)} %bitcast.24, bf16[256,256]{1,0:T(8,128)(2,1)} %refs_0_.1, bf16[256,256]{1,0:T(8,128)(2,1)} %refs_2_.1, bf16[256,256]{1,0:T(8,128)(2,1)} %refs_3_.1, ...), custom_call_target="tpu_custom_call" | custom-call | flops 2000000000 | bytes 4194304 | tf_op jit(solution)/shard_map/pallas_call | solution.py:73
  13.0 0.1 copy.21.r_2_.r_0_
  13.1 0.0 collective-permute-done.3.r_15_
  13.1 0.0 collective-permute-done.4.r_16_
  13.1 0.4 collective-permute-done.2.r_14_
  13.5 0.0 collective-permute-done.1.r_13_
  13.5 1.4 %collective-permute-done.r_12_ = bf16[272,256]{1,0:T(8,128)(2,1)S(1)} collective-permute-done((bf16[272,256]{1,0:T(8,128)(2,1)S(1)}, bf16[272,256]{1,0:T(8,128)(2,1)S(1)}, u32[]{:S(2)}, u32[]{:S(2)}) %collective-permute-start) | collective-permute-done | bytes 139296 | tf_op jit(solution)/shard_map/ppermute | solution.py:62
  14.9 9.9 %shard_map.190 = (f32[1024,256]{1,0:T(8,128)S(1)}, f32[1024,256]{1,0:T(8,128)S(1)}, bf16[2048,512]{1,0:T(8,128)(2,1)S(1)}, bf16[2,256,256]{2,1,0:T(8,128)(2,1)S(...) custom-call(s32[7]{0:T(128)S(1)} %stack.47.info.r_0_, ...), custom_call_target="tpu_custom_call" | custom-call | flops 10000000000 | bytes 8388608 | tf_op jit(solution)/shard_map/pallas_call | solution.py:73
  24.8 1.2 %collective-permute-start.5 = (f32[1024,256]{1,0:T(8,128)S(1)}, f32[1024,256]{1,0:T(8,128)S(1)}, u32[]{:S(2)}, u32[]{:S(2)}) collective-permute-start(f32[1024,256]{1,0:T(8,128)S(1)} %get-tuple-element.88), channel_id=1, source_target_pairs={{0,2},{1,3},{2,0},{3,1},{4,6},{5,7},{6,4},{7,5},{8,10},{9,11},{10,... | collective-permute-start | bytes 3145736 | tf_op jit(solution)/shard_map/ppermute | solution.py:62
  26.0 2.3 %collective-permute-done.5.r_2_ = f32[1024,256]{1,0:T(8,128)S(1)} collective-permute-done((f32[1024,256]{1,0:T(8,128)S(1)}, f32[1024,256]{1,0:T(8,128)S(1)}, u32[]{:S(2)}, u32[]{:S(2)}) %collective-permute-start.5) | collective-permute-done | bytes 1048608 | tf_op jit(solution)/shard_map/ppermute | solution.py:62
  28.3 0.7 %shard_map.191 = (f32[256,256]{1,0:T(8,128)S(1)}, bf16[256,256]{1,0:T(8,128)(2,1)S(1)}, bf16[256,256]{1,0:T(8,128)(2,1)S(1)}, bf16[256,256]{1,0:T(8,128)(2,1)S(1)}) custom-call(s32[7]{0:T(128)S(1)} %stack.47.info.r_0_, f32[1024,256]{1,0:T(8,128)S(1)} %get-tuple-element.87.r_1_, f32[1024,256]{1,0:T(8,128)S(1)} %collective-permute-done.5.r_2_), custom_call_target="tpu_custom_call" | custom-call | tf_op jit(solution)/shard_map/pallas_call | solution.py:73
  29.0 2.3 %collective-permute-start.6 = (bf16[256,256]{1,0:T(8,128)(2,1)S(1)}, bf16[256,256]{1,0:T(8,128)(2,1)S(1)}, u32[]{:S(2)}, u32[]{:S(2)}) collective-permute-start(bf16[256,256]{1,0:T(8,128)(2,1)S(1)} %get-tuple-element.94), channel_id=1, source_target_pairs={{0,5},{1,4},{2,7},{3,6},{4,1},{5,0},{6,3},{7,2},{8,13},{9,12},{10,... | collective-permute-start | bytes 393224 | tf_op jit(solution)/shard_map/ppermute | solution.py:62
  31.3 0.1 collective-permute-start.7
  31.5 1.4 %collective-permute-start.8 = (bf16[256,256]{1,0:T(8,128)(2,1)S(1)}, bf16[256,256]{1,0:T(8,128)(2,1)S(1)}, u32[]{:S(2)}, u32[]{:S(2)}) collective-permute-start(bf16[256,256]{1,0:T(8,128)(2,1)S(1)} %get-tuple-element.96), channel_id=1, source_target_pairs={{0,1},{1,0},{2,3},{3,2},{4,5},{5,4},{6,7},{7,6},{8,9},{9,8},{10,11... | collective-permute-start | bytes 393224 | tf_op jit(solution)/shard_map/ppermute | solution.py:62
  32.8 1.8 %shard_map.193 = (f32[256,256]{1,0:T(8,128)S(1)}, bf16[256,256]{1,0:T(8,128)(2,1)S(1)}, bf16[256,256]{1,0:T(8,128)(2,1)S(1)}, bf16[256,256]{1,0:T(8,128)(2,1)S(1...) custom-call(s32[3,2]{1,0:T(4,128)S(1)} %copy.21.r_2_.r_0_, bf16[2048,512]{1,0:T(8,128)(2,1)S(1)} %get-tuple-element.103.r_1_, ...), custom_call_target="tpu_custom_call" | custom-call | flops 2000000000 | bytes 4194304 | tf_op jit(solution)/shard_map/pallas_call | solution.py:73
  34.7 1.8 %collective-permute-start.15 = (bf16[256,256]{1,0:T(8,128)(2,1)S(1)}, bf16[256,256]{1,0:T(8,128)(2,1)S(1)}, u32[]{:S(2)}, u32[]{:S(2)}) collective-permute-start(bf16[256,256]{1,0:T(8,128)(2,1)S(1)} %get-tuple-element.132), channel_id=1, source_target_pairs={{0,16},{1,17},{2,18},{3,19},{4,20},{5,21},{6,22},{7,23},{8,24},{9,... | collective-permute-start | bytes 393224 | tf_op jit(solution)/shard_map/ppermute | solution.py:62
  36.5 2.0 %collective-permute-start.16 = (bf16[256,256]{1,0:T(8,128)(2,1)S(1)}, bf16[256,256]{1,0:T(8,128)(2,1)S(1)}, u32[]{:S(2)}, u32[]{:S(2)}) collective-permute-start(bf16[256,256]{1,0:T(8,128)(2,1)S(1)} %get-tuple-element.133), channel_id=1, source_target_pairs={{0,8},{1,9},{2,10},{3,11},{4,12},{5,13},{6,14},{7,15},{8,0},{9,1},... | collective-permute-start | bytes 393224 | tf_op jit(solution)/shard_map/ppermute | solution.py:62
  38.6 0.0 collective-permute-done.6.r_2_
  38.6 0.0 collective-permute-done.7.r_3_
  38.6 0.0 collective-permute-done.8.r_4_
  38.6 0.6 shard_map.192
  39.2 3.3 %collective-permute-start.9 = (f32[64,256]{1,0:T(8,128)S(1)}, f32[64,256]{1,0:T(8,128)S(1)}, u32[]{:S(2)}, u32[]{:S(2)}) collective-permute-start(f32[64,256]{1,0:T(8,128)S(1)} %get-tuple-element.106), channel_id=1, source_target_pairs={{0,24},{1,25},{2,26},{3,27},{4,28},{5,29},{6,30},{7,31},{8,16},{9,... | collective-permute-start | bytes 196616 | tf_op jit(solution)/shard_map/ppermute | solution.py:62
  42.6 0.0 collective-permute-start.10
  42.6 1.1 %collective-permute-start.11 = (f32[64,256]{1,0:T(8,128)S(1)}, f32[64,256]{1,0:T(8,128)S(1)}, u32[]{:S(2)}, u32[]{:S(2)}) collective-permute-start(f32[64,256]{1,0:T(8,128)S(1)} %get-tuple-element.108), channel_id=1, source_target_pairs={{0,8},{1,9},{2,10},{3,11},{4,12},{5,13},{6,14},{7,15},{8,0},{9,1},... | collective-permute-start | bytes 196616 | tf_op jit(solution)/shard_map/ppermute | solution.py:62
  43.7 2.7 %shard_map.194 = (bf16[256,256]{1,0:T(8,128)(2,1)}, f32[256,256]{1,0:T(8,128)S(1)}, bf16[256,256]{1,0:T(8,128)(2,1)S(1)}, s32[4,128]{1,0:T(4,128)S(1)}) custom-call(s32[2]{0:T(128)S(1)} %bitcast.18, bf16[256,256]{1,0:T(8,128)(2,1)} %refs_0_.1, bf16[512,256]{1,0:T(8,128)(2,1)} %refs_1_.3, bf16[256,256]{1,0:T(8,128)(2,1)} %bitcast.22, s32[4,128]{1,0:T(4,128)} %bitcast.25, ...), custom_call_target="tpu_custom_call" | custom-call | flops 1000000000 | bytes 2097152 | tf_op jit(solution)/shard_map/pallas_call | solution.py:73
  46.3 0.0 collective-permute-done.9.r_2_
  46.4 2.9 %collective-permute-done.10.r_3_ = f32[64,256]{1,0:T(8,128)S(1)} collective-permute-done((f32[64,256]{1,0:T(8,128)S(1)}, f32[64,256]{1,0:T(8,128)S(1)}, u32[]{:S(2)}, u32[]{:S(2)}) %collective-permute-start.10) | collective-permute-done | bytes 65568 | tf_op jit(solution)/shard_map/ppermute | solution.py:62
  49.3 0.0 collective-permute-done.11.r_4_
  49.3 0.6 shard_map.195.r_1_
  49.8 2.2 %collective-permute-start.12 = (bf16[64,256]{1,0:T(8,128)(2,1)S(1)}, bf16[64,256]{1,0:T(8,128)(2,1)S(1)}, u32[]{:S(2)}, u32[]{:S(2)}) collective-permute-start(bf16[64,256]{1,0:T(8,128)(2,1)S(1)} %shard_map.195.r_1_), channel_id=1, source_target_pairs={{0,24},{1,25},{2,26},{3,27},{4,28},{5,29},{6,30},{7,31},{8,16},{9,... | collective-permute-start | bytes 98312 | tf_op jit(solution)/shard_map/ppermute | solution.py:62
  52.1 0.0 collective-permute-start.13
  52.1 2.2 %collective-permute-start.14 = (bf16[64,256]{1,0:T(8,128)(2,1)S(1)}, bf16[64,256]{1,0:T(8,128)(2,1)S(1)}, u32[]{:S(2)}, u32[]{:S(2)}) collective-permute-start(bf16[64,256]{1,0:T(8,128)(2,1)S(1)} %shard_map.195.r_1_), channel_id=1, source_target_pairs={{0,8},{1,9},{2,10},{3,11},{4,12},{5,13},{6,14},{7,15},{8,0},{9,1},... | collective-permute-start | bytes 98312 | tf_op jit(solution)/shard_map/ppermute | solution.py:62
  54.3 0.0 collective-permute-done.15.refs_4_
  54.3 0.0 collective-permute-start.21
  54.3 0.0 collective-permute-done.16.refs_6_
  54.3 0.7 %collective-permute-start.20 = (bf16[256,256]{1,0:T(8,128)(2,1)S(1)}, bf16[256,256]{1,0:T(8,128)(2,1)S(1)}, u32[]{:S(2)}, u32[]{:S(2)}) collective-permute-start(bf16[256,256]{1,0:T(8,128)(2,1)S(1)} %get-tuple-element.138), channel_id=1, source_target_pairs={{0,1},{1,0},{2,3},{3,2},{4,5},{5,4},{6,7},{7,6},{8,9},{9,8},{10,11... | collective-permute-start | bytes 393224 | tf_op jit(solution)/shard_map/ppermute | solution.py:62
  55.0 0.6 collective-permute-done.12.r_2_
  55.6 1.3 %collective-permute-done.13.r_3_ = bf16[64,256]{1,0:T(8,128)(2,1)S(1)} collective-permute-done((bf16[64,256]{1,0:T(8,128)(2,1)S(1)}, bf16[64,256]{1,0:T(8,128)(2,1)S(1)}, u32[]{:S(2)}, u32[]{:S(2)}) %collective-permute-start.13) | collective-permute-done | bytes 32800 | tf_op jit(solution)/shard_map/ppermute | solution.py:62
  56.9 0.0 collective-permute-done.14.r_4_
  56.9 0.6 shard_map.196.r_1_
  57.5 1.3 %collective-permute-start.19 = (bf16[256,256]{1,0:T(8,128)(2,1)S(1)}, bf16[256,256]{1,0:T(8,128)(2,1)S(1)}, u32[]{:S(2)}, u32[]{:S(2)}) collective-permute-start(bf16[256,256]{1,0:T(8,128)(2,1)S(1)} %shard_map.196.r_1_), channel_id=1, source_target_pairs={{0,5},{1,4},{2,7},{3,6},{4,1},{5,0},{6,3},{7,2},{8,13},{9,12},{10,... | collective-permute-start | bytes 393224 | tf_op jit(solution)/shard_map/ppermute | solution.py:62
  58.7 1.3 %collective-permute-start.18 = (bf16[256,256]{1,0:T(8,128)(2,1)S(1)}, bf16[256,256]{1,0:T(8,128)(2,1)S(1)}, u32[]{:S(2)}, u32[]{:S(2)}) collective-permute-start(bf16[256,256]{1,0:T(8,128)(2,1)S(1)} %shard_map.196.r_1_), channel_id=1, source_target_pairs={{0,4},{1,5},{2,6},{3,7},{4,0},{5,1},{6,2},{7,3},{8,12},{9,13},{10,... | collective-permute-start | bytes 393224 | tf_op jit(solution)/shard_map/ppermute | solution.py:62
  60.1 0.9 %collective-permute-start.17 = (bf16[256,256]{1,0:T(8,128)(2,1)S(1)}, bf16[256,256]{1,0:T(8,128)(2,1)S(1)}, u32[]{:S(2)}, u32[]{:S(2)}) collective-permute-start(bf16[256,256]{1,0:T(8,128)(2,1)S(1)} %shard_map.196.r_1_), channel_id=1, source_target_pairs={{0,1},{1,0},{2,3},{3,2},{4,5},{5,4},{6,7},{7,6},{8,9},{9,8},{10,11... | collective-permute-start | bytes 393224 | tf_op jit(solution)/shard_map/ppermute | solution.py:62
  61.0 0.0 collective-permute-done.21.refs_7_
  61.0 0.7 collective-permute-start.22
  61.7 0.0 collective-permute-done.22.refs_8_
  61.7 0.4 collective-permute-done.20.refs_5_
  62.1 2.0 %collective-permute-done.19.r_4_ = bf16[256,256]{1,0:T(8,128)(2,1)S(1)} collective-permute-done((bf16[256,256]{1,0:T(8,128)(2,1)S(1)}, bf16[256,256]{1,0:T(8,128)(2,1)S(1)}, u32[]{:S(2)}, u32[]{:S(2)}) %collective-permute-start.19) | collective-permute-done | bytes 131104 | tf_op jit(solution)/shard_map/ppermute | solution.py:62
  64.1 0.9 %collective-permute-done.18.r_3_ = bf16[256,256]{1,0:T(8,128)(2,1)S(1)} collective-permute-done((bf16[256,256]{1,0:T(8,128)(2,1)S(1)}, bf16[256,256]{1,0:T(8,128)(2,1)S(1)}, u32[]{:S(2)}, u32[]{:S(2)}) %collective-permute-start.18) | collective-permute-done | bytes 131104 | tf_op jit(solution)/shard_map/ppermute | solution.py:62
  65.0 0.8 %collective-permute-done.17.r_2_ = bf16[256,256]{1,0:T(8,128)(2,1)S(1)} collective-permute-done((bf16[256,256]{1,0:T(8,128)(2,1)S(1)}, bf16[256,256]{1,0:T(8,128)(2,1)S(1)}, u32[]{:S(2)}, u32[]{:S(2)}) %collective-permute-start.17) | collective-permute-done | bytes 131104 | tf_op jit(solution)/shard_map/ppermute | solution.py:62
  65.8 0.6 shard_map.198.r_1_
  66.4 0.4 collective-permute-start.23
  66.9 1.5 %shard_map.197 = bf16[256,256]{1,0:T(8,128)(2,1)} custom-call(s32[7]{0:T(128)S(1)} %stack.47.info.r_0_, bf16[256,256]{1,0:T(8,128)(2,1)S(1)} %get-tuple-element.118.refs_0_, s32[4,128]{1,0:T(4,128)S(1)} %get-tuple-element.119.refs_1_, f32[256,256]{1,0:T(8,128)S(1)} %get-tuple-element.120.refs_2_, f32[256,256]{1,0:T(8,128)S(1)} %get-tuple-element.121.refs_3_, ...), custom_call_target="tpu_custom_call" | custom-call | tf_op jit(solution)/shard_map/pallas_call | solution.py:73
  68.4 0.0 collective-permute-done.23.r_2_
  68.4 1.9 %shard_map.199 = (f32[256,256]{1,0:T(8,128)}, f32[256,256]{1,0:T(8,128)}, f32[256,256]{1,0:T(8,128)}, f32[256,256]{1,0:T(8,128)}, f32[256,512]{1,0:T(8,128)}, /*index=5*/f32[512,256]{1,0:T(8,128)}) custom-call(s32[7]{0:T(128)S(1)} %stack.47.info.r_0_, bf16[1024,256]{1,0:T(8,128)(2,1)S(1)} %shard_map.198.r_1_, bf16[1024,256]{1,0:T(8,128)(2,1)S(1)} %collective-permute-done.23.r_2_), custom_call_target="tpu_custom_call" | custom-call | tf_op jit(solution)/shard_map/pallas_call | solution.py:73
  (2 shorter events, 0.0 us)
Async XLA Ops:
  2.6 10.9 %collective-permute-start.2 = (bf16[272,256]{1,0:T(8,128)(2,1)S(1)}, bf16[272,256]{1,0:T(8,128)(2,1)S(1)}, u32[]{:S(2)}, u32[]{:S(2)}) collective-permute-start(bf16[272,256]{1,0:T(8,128)(2,1)S(1)} %get-tuple-element.81.refs_6_.r_11_), channel_id=1, source_target_pairs={{0,16},{1,17},{2,18},{3,19},{4,20},{5,21},{6,22},{7,23},{8,24},{9,... | collective-permute-start | bytes 417800 | tf_op jit(solution)/shard_map/ppermute | solution.py:62
  6.7 6.8 %collective-permute-start.1 = (bf16[272,256]{1,0:T(8,128)(2,1)S(1)}, bf16[272,256]{1,0:T(8,128)(2,1)S(1)}, u32[]{:S(2)}, u32[]{:S(2)}) collective-permute-start(bf16[272,256]{1,0:T(8,128)(2,1)S(1)} %get-tuple-element.81.refs_6_.r_11_), channel_id=1, source_target_pairs={{0,1},{1,0},{2,3},{3,2},{4,5},{5,4},{6,7},{7,6},{8,9},{9,8},{10,11... | collective-permute-start | bytes 417800 | tf_op jit(solution)/shard_map/ppermute | solution.py:62
  8.2 6.7 %collective-permute-start = (bf16[272,256]{1,0:T(8,128)(2,1)S(1)}, bf16[272,256]{1,0:T(8,128)(2,1)S(1)}, u32[]{:S(2)}, u32[]{:S(2)}) collective-permute-start(bf16[272,256]{1,0:T(8,128)(2,1)S(1)} %get-tuple-element.81.refs_6_.r_11_), channel_id=1, source_target_pairs={{0,8},{1,9},{2,10},{3,11},{4,12},{5,13},{6,14},{7,15},{8,0},{9,1},... | collective-permute-start | bytes 417800 | tf_op jit(solution)/shard_map/ppermute | solution.py:62
  9.8 3.3 %collective-permute-start.3 = (bf16[128,256]{1,0:T(8,128)(2,1)S(1)}, bf16[128,256]{1,0:T(8,128)(2,1)S(1)}, u32[]{:S(2)}, u32[]{:S(2)}) collective-permute-start(bf16[128,256]{1,0:T(8,128)(2,1)S(1)} %get-tuple-element.85), channel_id=1, source_target_pairs={{0,2},{4,6},{8,10},{12,14},{16,18},{20,22},{24,26},{28,30},{2,0},{... | collective-permute-start | bytes 196616 | tf_op jit(solution)/shard_map/ppermute | solution.py:52
  9.8 3.3 %collective-permute-start.4 = (bf16[128,256]{1,0:T(8,128)(2,1)S(1)}, bf16[128,256]{1,0:T(8,128)(2,1)S(1)}, u32[]{:S(2)}, u32[]{:S(2)}) collective-permute-start(bf16[128,256]{1,0:T(8,128)(2,1)S(1)} %get-tuple-element.86), channel_id=1, source_target_pairs={{2,4},{6,8},{10,12},{14,16},{18,20},{22,24},{26,28},{4,2},{8,6},{1... | collective-permute-start | bytes 196616 | tf_op jit(solution)/shard_map/ppermute | solution.py:52
  10.5 2.5 %copy-start.1 = (s32[1,1,3,2]{2,3,1,0:T(2,128)S(1)}, s32[1,1,3,2]{2,3,1,0:T(2,128)}, u32[]{:S(2)}) copy-start(s32[1,1,3,2]{2,3,1,0:T(2,128)} %param.24) | copy-start | bytes 76
  10.5 4.4 %copy-start = (s32[1,1,2]{2,1,0:T(1,128)S(1)}, s32[1,1,2]{2,1,0:T(1,128)}, u32[]{:S(2)}) copy-start(s32[1,1,2]{2,1,0:T(1,128)} %param.21) | copy-start | bytes 28
  24.8 3.5 %collective-permute-start.5 = (f32[1024,256]{1,0:T(8,128)S(1)}, f32[1024,256]{1,0:T(8,128)S(1)}, u32[]{:S(2)}, u32[]{:S(2)}) collective-permute-start(f32[1024,256]{1,0:T(8,128)S(1)} %get-tuple-element.88), channel_id=1, source_target_pairs={{0,2},{1,3},{2,0},{3,1},{4,6},{5,7},{6,4},{7,5},{8,10},{9,11},{10,... | collective-permute-start | bytes 3145736 | tf_op jit(solution)/shard_map/ppermute | solution.py:62
  29.0 9.6 %collective-permute-start.6 = (bf16[256,256]{1,0:T(8,128)(2,1)S(1)}, bf16[256,256]{1,0:T(8,128)(2,1)S(1)}, u32[]{:S(2)}, u32[]{:S(2)}) collective-permute-start(bf16[256,256]{1,0:T(8,128)(2,1)S(1)} %get-tuple-element.94), channel_id=1, source_target_pairs={{0,5},{1,4},{2,7},{3,6},{4,1},{5,0},{6,3},{7,2},{8,13},{9,12},{10,... | collective-permute-start | bytes 393224 | tf_op jit(solution)/shard_map/ppermute | solution.py:62
  31.3 7.2 %collective-permute-start.7 = (bf16[256,256]{1,0:T(8,128)(2,1)S(1)}, bf16[256,256]{1,0:T(8,128)(2,1)S(1)}, u32[]{:S(2)}, u32[]{:S(2)}) collective-permute-start(bf16[256,256]{1,0:T(8,128)(2,1)S(1)} %get-tuple-element.95), channel_id=1, source_target_pairs={{0,4},{1,5},{2,6},{3,7},{4,0},{5,1},{6,2},{7,3},{8,12},{9,13},{10,... | collective-permute-start | bytes 393224 | tf_op jit(solution)/shard_map/ppermute | solution.py:62
  31.5 7.1 %collective-permute-start.8 = (bf16[256,256]{1,0:T(8,128)(2,1)S(1)}, bf16[256,256]{1,0:T(8,128)(2,1)S(1)}, u32[]{:S(2)}, u32[]{:S(2)}) collective-permute-start(bf16[256,256]{1,0:T(8,128)(2,1)S(1)} %get-tuple-element.96), channel_id=1, source_target_pairs={{0,1},{1,0},{2,3},{3,2},{4,5},{5,4},{6,7},{7,6},{8,9},{9,8},{10,11... | collective-permute-start | bytes 393224 | tf_op jit(solution)/shard_map/ppermute | solution.py:62
  34.7 19.6 %collective-permute-start.15 = (bf16[256,256]{1,0:T(8,128)(2,1)S(1)}, bf16[256,256]{1,0:T(8,128)(2,1)S(1)}, u32[]{:S(2)}, u32[]{:S(2)}) collective-permute-start(bf16[256,256]{1,0:T(8,128)(2,1)S(1)} %get-tuple-element.132), channel_id=1, source_target_pairs={{0,16},{1,17},{2,18},{3,19},{4,20},{5,21},{6,22},{7,23},{8,24},{9,... | collective-permute-start | bytes 393224 | tf_op jit(solution)/shard_map/ppermute | solution.py:62
  36.5 17.8 %collective-permute-start.16 = (bf16[256,256]{1,0:T(8,128)(2,1)S(1)}, bf16[256,256]{1,0:T(8,128)(2,1)S(1)}, u32[]{:S(2)}, u32[]{:S(2)}) collective-permute-start(bf16[256,256]{1,0:T(8,128)(2,1)S(1)} %get-tuple-element.133), channel_id=1, source_target_pairs={{0,8},{1,9},{2,10},{3,11},{4,12},{5,13},{6,14},{7,15},{8,0},{9,1},... | collective-permute-start | bytes 393224 | tf_op jit(solution)/shard_map/ppermute | solution.py:62
  39.2 7.1 %collective-permute-start.9 = (f32[64,256]{1,0:T(8,128)S(1)}, f32[64,256]{1,0:T(8,128)S(1)}, u32[]{:S(2)}, u32[]{:S(2)}) collective-permute-start(f32[64,256]{1,0:T(8,128)S(1)} %get-tuple-element.106), channel_id=1, source_target_pairs={{0,24},{1,25},{2,26},{3,27},{4,28},{5,29},{6,30},{7,31},{8,16},{9,... | collective-permute-start | bytes 196616 | tf_op jit(solution)/shard_map/ppermute | solution.py:62
  42.6 6.7 %collective-permute-start.10 = (f32[64,256]{1,0:T(8,128)S(1)}, f32[64,256]{1,0:T(8,128)S(1)}, u32[]{:S(2)}, u32[]{:S(2)}) collective-permute-start(f32[64,256]{1,0:T(8,128)S(1)} %get-tuple-element.107), channel_id=1, source_target_pairs={{0,16},{1,17},{2,18},{3,19},{4,20},{5,21},{6,22},{7,23},{8,24},{9,... | collective-permute-start | bytes 196616 | tf_op jit(solution)/shard_map/ppermute | solution.py:62
  42.6 6.7 %collective-permute-start.11 = (f32[64,256]{1,0:T(8,128)S(1)}, f32[64,256]{1,0:T(8,128)S(1)}, u32[]{:S(2)}, u32[]{:S(2)}) collective-permute-start(f32[64,256]{1,0:T(8,128)S(1)} %get-tuple-element.108), channel_id=1, source_target_pairs={{0,8},{1,9},{2,10},{3,11},{4,12},{5,13},{6,14},{7,15},{8,0},{9,1},... | collective-permute-start | bytes 196616 | tf_op jit(solution)/shard_map/ppermute | solution.py:62
  49.8 5.8 %collective-permute-start.12 = (bf16[64,256]{1,0:T(8,128)(2,1)S(1)}, bf16[64,256]{1,0:T(8,128)(2,1)S(1)}, u32[]{:S(2)}, u32[]{:S(2)}) collective-permute-start(bf16[64,256]{1,0:T(8,128)(2,1)S(1)} %shard_map.195.r_1_), channel_id=1, source_target_pairs={{0,24},{1,25},{2,26},{3,27},{4,28},{5,29},{6,30},{7,31},{8,16},{9,... | collective-permute-start | bytes 98312 | tf_op jit(solution)/shard_map/ppermute | solution.py:62
  52.1 4.8 %collective-permute-start.13 = (bf16[64,256]{1,0:T(8,128)(2,1)S(1)}, bf16[64,256]{1,0:T(8,128)(2,1)S(1)}, u32[]{:S(2)}, u32[]{:S(2)}) collective-permute-start(bf16[64,256]{1,0:T(8,128)(2,1)S(1)} %shard_map.195.r_1_), channel_id=1, source_target_pairs={{0,16},{1,17},{2,18},{3,19},{4,20},{5,21},{6,22},{7,23},{8,24},{9,... | collective-permute-start | bytes 98312 | tf_op jit(solution)/shard_map/ppermute | solution.py:62
  52.1 4.8 %collective-permute-start.14 = (bf16[64,256]{1,0:T(8,128)(2,1)S(1)}, bf16[64,256]{1,0:T(8,128)(2,1)S(1)}, u32[]{:S(2)}, u32[]{:S(2)}) collective-permute-start(bf16[64,256]{1,0:T(8,128)(2,1)S(1)} %shard_map.195.r_1_), channel_id=1, source_target_pairs={{0,8},{1,9},{2,10},{3,11},{4,12},{5,13},{6,14},{7,15},{8,0},{9,1},... | collective-permute-start | bytes 98312 | tf_op jit(solution)/shard_map/ppermute | solution.py:62
  54.3 6.7 %collective-permute-start.21 = (bf16[128,256]{1,0:T(8,128)(2,1)S(1)}, bf16[128,256]{1,0:T(8,128)(2,1)S(1)}, u32[]{:S(2)}, u32[]{:S(2)}) collective-permute-start(bf16[128,256]{1,0:T(8,128)(2,1)S(1)} %get-tuple-element.139), channel_id=1, source_target_pairs={{0,2},{4,6},{8,10},{12,14},{16,18},{20,22},{24,26},{28,30},{2,0},{... | collective-permute-start | bytes 196616 | tf_op jit(solution)/shard_map/ppermute | solution.py:52
  54.3 7.8 %collective-permute-start.20 = (bf16[256,256]{1,0:T(8,128)(2,1)S(1)}, bf16[256,256]{1,0:T(8,128)(2,1)S(1)}, u32[]{:S(2)}, u32[]{:S(2)}) collective-permute-start(bf16[256,256]{1,0:T(8,128)(2,1)S(1)} %get-tuple-element.138), channel_id=1, source_target_pairs={{0,1},{1,0},{2,3},{3,2},{4,5},{5,4},{6,7},{7,6},{8,9},{9,8},{10,11... | collective-permute-start | bytes 393224 | tf_op jit(solution)/shard_map/ppermute | solution.py:62
  57.5 6.7 %collective-permute-start.19 = (bf16[256,256]{1,0:T(8,128)(2,1)S(1)}, bf16[256,256]{1,0:T(8,128)(2,1)S(1)}, u32[]{:S(2)}, u32[]{:S(2)}) collective-permute-start(bf16[256,256]{1,0:T(8,128)(2,1)S(1)} %shard_map.196.r_1_), channel_id=1, source_target_pairs={{0,5},{1,4},{2,7},{3,6},{4,1},{5,0},{6,3},{7,2},{8,13},{9,12},{10,... | collective-permute-start | bytes 393224 | tf_op jit(solution)/shard_map/ppermute | solution.py:62
  58.7 6.3 %collective-permute-start.18 = (bf16[256,256]{1,0:T(8,128)(2,1)S(1)}, bf16[256,256]{1,0:T(8,128)(2,1)S(1)}, u32[]{:S(2)}, u32[]{:S(2)}) collective-permute-start(bf16[256,256]{1,0:T(8,128)(2,1)S(1)} %shard_map.196.r_1_), channel_id=1, source_target_pairs={{0,4},{1,5},{2,6},{3,7},{4,0},{5,1},{6,2},{7,3},{8,12},{9,13},{10,... | collective-permute-start | bytes 393224 | tf_op jit(solution)/shard_map/ppermute | solution.py:62
  60.1 5.8 %collective-permute-start.17 = (bf16[256,256]{1,0:T(8,128)(2,1)S(1)}, bf16[256,256]{1,0:T(8,128)(2,1)S(1)}, u32[]{:S(2)}, u32[]{:S(2)}) collective-permute-start(bf16[256,256]{1,0:T(8,128)(2,1)S(1)} %shard_map.196.r_1_), channel_id=1, source_target_pairs={{0,1},{1,0},{2,3},{3,2},{4,5},{5,4},{6,7},{7,6},{8,9},{9,8},{10,11... | collective-permute-start | bytes 393224 | tf_op jit(solution)/shard_map/ppermute | solution.py:62
  61.0 0.7 collective-permute-start.22
  66.4 2.0 %collective-permute-start.23 = (bf16[1024,256]{1,0:T(8,128)(2,1)S(1)}, bf16[1024,256]{1,0:T(8,128)(2,1)S(1)}, u32[]{:S(2)}, u32[]{:S(2)}) collective-permute-start(bf16[1024,256]{1,0:T(8,128)(2,1)S(1)} %shard_map.198.r_1_), channel_id=1, source_target_pairs={{0,2},{1,3},{2,0},{3,1},{4,6},{5,7},{6,4},{7,5},{8,10},{9,11},{10,... | collective-permute-start | bytes 1572872 | tf_op jit(solution)/shard_map/ppermute | solution.py:62

commit v8 on v7

--- a/solution.py
+++ b/solution.py
@@ -450,7 +450,7 @@
     half_rows = grads.shape[0] // 2
     mine = info[SIDES]
     keep[...] = grads[pl.ds(pl.multiple_of(mine * half_rows, half_rows), half_rows), :]
-    send[...] = grads[pl.ds(pl.multiple_of((1 - mine) * half_rows, half_rows), half_rows), :]
+    send[...] = grads[pl.ds(pl.multiple_of((1 - mine) * half_rows, half_rows), half_rows), :].astype(BF16)
 
 
 def back_kernel(merge_y, pairing, *refs):
@@ -694,7 +694,7 @@
         lambda *r: main_kernel(merge_y, *r),
         [
             ((total_rows // 2, width), F32),
-            ((total_rows // 2, width), F32),
+            ((total_rows // 2, width), BF16),
             ((all_rows, 2 * width), BF16),
             (moves_shape, BF16),
             (square, BF16),

time: 70.8 us -> 70 us (0.989)
  waiting for transfers between devices: 13.1 us -> 12.3 us
    ppermute x20, waiting for transfers between devices: 13.1 us -> 12.3 us  [xor_permute(): return lax.ppermute(value, AXES, [(i, i ^ mask) for i in range(count)])]
where the time goes in v8:
time: 70 us; the launch traced here: 69.6 us
  starting transfers between devices  31 us (44%)
  Pallas kernels  25.2 us (36%)
  waiting for transfers between devices  12.3 us (18%)
  between operations  0.82 us (1%)
    ppermute x20, starting transfers between devices, xor_permute(): return lax.ppermute(value, AXES, [(i, i ^ mask) for i in range(count)])  29.7 us
    pallas_call x12, Pallas kernels, call(): pl.pallas_call(kernel, out_shape=[jax.ShapeDtypeStruct(s, d) for s, d in...  25.2 us
    ppermute x20, waiting for transfers between devices, xor_permute(): return lax.ppermute(value, AXES, [(i, i ^ mask) for i in range(count)])  12.3 us
  transfers between devices with their start and end apart: 24, of which 10 were waited for; matrix products, arithmetic and copies ran while one was open for 0% of the time, Pallas kernels for 15%

profile of v8, /device:TPU:0, one launch (start us, length us, event | category | flops | bytes accessed | tf_op | source)
XLA Modules:
  0.0 69.6 jit_solution(15577495497195672664)
XLA Ops:
  0.7 0.1 stack.47.info.r_0_
  0.7 1.8 %shard_map.188 = (bf16[272,256]{1,0:T(8,128)(2,1)S(1)}, bf16[128,256]{1,0:T(8,128)(2,1)S(1)}, bf16[128,256]{1,0:T(8,128)(2,1)S(1)}) custom-call(s32[7]{0:T(128)S(1)} %stack.47.info.r_0_, bf16[256,256]{1,0:T(8,128)(2,1)} %bitcast.20, s32[4,128]{1,0:T(4,128)} %bitcast.23, s32[2]{0:T(128)} %bitcast.16), custom_call_target="tpu_custom_call" | custom-call | tf_op jit(solution)/shard_map/pallas_call | solution.py:73
  2.6 4.1 %collective-permute-start.2 = (bf16[272,256]{1,0:T(8,128)(2,1)S(1)}, bf16[272,256]{1,0:T(8,128)(2,1)S(1)}, u32[]{:S(2)}, u32[]{:S(2)}) collective-permute-start(bf16[272,256]{1,0:T(8,128)(2,1)S(1)} %get-tuple-element.81.refs_6_.r_11_), channel_id=1, source_target_pairs={{0,16},{1,17},{2,18},{3,19},{4,20},{5,21},{6,22},{7,23},{8,24},{9,... | collective-permute-start | bytes 417800 | tf_op jit(solution)/shard_map/ppermute | solution.py:62
  6.7 1.5 %collective-permute-start.1 = (bf16[272,256]{1,0:T(8,128)(2,1)S(1)}, bf16[272,256]{1,0:T(8,128)(2,1)S(1)}, u32[]{:S(2)}, u32[]{:S(2)}) collective-permute-start(bf16[272,256]{1,0:T(8,128)(2,1)S(1)} %get-tuple-element.81.refs_6_.r_11_), channel_id=1, source_target_pairs={{0,1},{1,0},{2,3},{3,2},{4,5},{5,4},{6,7},{7,6},{8,9},{9,8},{10,11... | collective-permute-start | bytes 417800 | tf_op jit(solution)/shard_map/ppermute | solution.py:62
  8.2 1.6 %collective-permute-start = (bf16[272,256]{1,0:T(8,128)(2,1)S(1)}, bf16[272,256]{1,0:T(8,128)(2,1)S(1)}, u32[]{:S(2)}, u32[]{:S(2)}) collective-permute-start(bf16[272,256]{1,0:T(8,128)(2,1)S(1)} %get-tuple-element.81.refs_6_.r_11_), channel_id=1, source_target_pairs={{0,8},{1,9},{2,10},{3,11},{4,12},{5,13},{6,14},{7,15},{8,0},{9,1},... | collective-permute-start | bytes 417800 | tf_op jit(solution)/shard_map/ppermute | solution.py:62
  9.8 0.0 collective-permute-start.3
  9.8 0.7 collective-permute-start.4
  10.5 0.0 copy-start.1
  10.5 0.0 copy-start
  10.5 2.5 %shard_map.189 = (bf16[12,256,256]{2,1,0:T(8,128)(2,1)S(1)}, bf16[4,256,128]{2,1,0:T(8,128)(2,1)S(1)}, f32[4,8,256]{2,1,0:T(8,128)S(1)}) custom-call(s32[7]{0:T(128)S(1)} %stack.47.info.r_0_, s32[4,128]{1,0:T(4,128)} %bitcast.24, bf16[256,256]{1,0:T(8,128)(2,1)} %refs_0_.1, bf16[256,256]{1,0:T(8,128)(2,1)} %refs_2_.1, bf16[256,256]{1,0:T(8,128)(2,1)} %refs_3_.1, ...), custom_call_target="tpu_custom_call" | custom-call | flops 2000000000 | bytes 4194304 | tf_op jit(solution)/shard_map/pallas_call | solution.py:73
  13.0 0.1 copy.21.r_2_.r_0_
  13.1 0.0 collective-permute-done.3.r_15_
  13.1 0.0 collective-permute-done.4.r_16_
  13.1 0.4 collective-permute-done.2.r_14_
  13.5 0.0 collective-permute-done.1.r_13_
  13.5 1.4 %collective-permute-done.r_12_ = bf16[272,256]{1,0:T(8,128)(2,1)S(1)} collective-permute-done((bf16[272,256]{1,0:T(8,128)(2,1)S(1)}, bf16[272,256]{1,0:T(8,128)(2,1)S(1)}, u32[]{:S(2)}, u32[]{:S(2)}) %collective-permute-start) | collective-permute-done | bytes 139296 | tf_op jit(solution)/shard_map/ppermute | solution.py:62
  14.9 9.9 %shard_map.190 = (f32[1024,256]{1,0:T(8,128)S(1)}, bf16[1024,256]{1,0:T(8,128)(2,1)S(1)}, bf16[2048,512]{1,0:T(8,128)(2,1)S(1)}, bf16[2,256,256]{2,1,0:T(8,128)(...) custom-call(s32[7]{0:T(128)S(1)} %stack.47.info.r_0_, ...), custom_call_target="tpu_custom_call" | custom-call | flops 10000000000 | bytes 8388608 | tf_op jit(solution)/shard_map/pallas_call | solution.py:73
  24.8 1.2 %collective-permute-start.5 = (bf16[1024,256]{1,0:T(8,128)(2,1)S(1)}, bf16[1024,256]{1,0:T(8,128)(2,1)S(1)}, u32[]{:S(2)}, u32[]{:S(2)}) collective-permute-start(bf16[1024,256]{1,0:T(8,128)(2,1)S(1)} %get-tuple-element.88), channel_id=1, source_target_pairs={{0,2},{1,3},{2,0},{3,1},{4,6},{5,7},{6,4},{7,5},{8,10},{9,11},{10,... | collective-permute-start | bytes 1572872 | tf_op jit(solution)/shard_map/ppermute | solution.py:62
  26.0 1.5 %collective-permute-done.5.r_2_ = bf16[1024,256]{1,0:T(8,128)(2,1)S(1)} collective-permute-done((bf16[1024,256]{1,0:T(8,128)(2,1)S(1)}, bf16[1024,256]{1,0:T(8,128)(2,1)S(1)}, u32[]{:S(2)}, u32[]{:S(2)}) %collective-permute-start.5) | collective-permute-done | bytes 524320 | tf_op jit(solution)/shard_map/ppermute | solution.py:62
  27.5 0.7 %shard_map.191 = (f32[256,256]{1,0:T(8,128)S(1)}, bf16[256,256]{1,0:T(8,128)(2,1)S(1)}, bf16[256,256]{1,0:T(8,128)(2,1)S(1)}, bf16[256,256]{1,0:T(8,128)(2,1)S(1)}) custom-call(s32[7]{0:T(128)S(1)} %stack.47.info.r_0_, f32[1024,256]{1,0:T(8,128)S(1)} %get-tuple-element.87.r_1_, bf16[1024,256]{1,0:T(8,128)(2,1)S(1)} %collective-permute-done.5.r_2_), custom_call_target="tpu_custom_call" | custom-call | tf_op jit(solution)/shard_map/pallas_call | solution.py:73
  28.2 2.3 %collective-permute-start.6 = (bf16[256,256]{1,0:T(8,128)(2,1)S(1)}, bf16[256,256]{1,0:T(8,128)(2,1)S(1)}, u32[]{:S(2)}, u32[]{:S(2)}) collective-permute-start(bf16[256,256]{1,0:T(8,128)(2,1)S(1)} %get-tuple-element.94), channel_id=1, source_target_pairs={{0,5},{1,4},{2,7},{3,6},{4,1},{5,0},{6,3},{7,2},{8,13},{9,12},{10,... | collective-permute-start | bytes 393224 | tf_op jit(solution)/shard_map/ppermute | solution.py:62
  30.6 0.1 collective-permute-start.7
  30.7 1.4 %collective-permute-start.8 = (bf16[256,256]{1,0:T(8,128)(2,1)S(1)}, bf16[256,256]{1,0:T(8,128)(2,1)S(1)}, u32[]{:S(2)}, u32[]{:S(2)}) collective-permute-start(bf16[256,256]{1,0:T(8,128)(2,1)S(1)} %get-tuple-element.96), channel_id=1, source_target_pairs={{0,1},{1,0},{2,3},{3,2},{4,5},{5,4},{6,7},{7,6},{8,9},{9,8},{10,11... | collective-permute-start | bytes 393224 | tf_op jit(solution)/shard_map/ppermute | solution.py:62
  32.1 1.8 %shard_map.193 = (f32[256,256]{1,0:T(8,128)S(1)}, bf16[256,256]{1,0:T(8,128)(2,1)S(1)}, bf16[256,256]{1,0:T(8,128)(2,1)S(1)}, bf16[256,256]{1,0:T(8,128)(2,1)S(1...) custom-call(s32[3,2]{1,0:T(4,128)S(1)} %copy.21.r_2_.r_0_, bf16[2048,512]{1,0:T(8,128)(2,1)S(1)} %get-tuple-element.103.r_1_, ...), custom_call_target="tpu_custom_call" | custom-call | flops 2000000000 | bytes 4194304 | tf_op jit(solution)/shard_map/pallas_call | solution.py:73
  33.9 1.8 %collective-permute-start.15 = (bf16[256,256]{1,0:T(8,128)(2,1)S(1)}, bf16[256,256]{1,0:T(8,128)(2,1)S(1)}, u32[]{:S(2)}, u32[]{:S(2)}) collective-permute-start(bf16[256,256]{1,0:T(8,128)(2,1)S(1)} %get-tuple-element.132), channel_id=1, source_target_pairs={{0,16},{1,17},{2,18},{3,19},{4,20},{5,21},{6,22},{7,23},{8,24},{9,... | collective-permute-start | bytes 393224 | tf_op jit(solution)/shard_map/ppermute | solution.py:62
  35.8 2.0 %collective-permute-start.16 = (bf16[256,256]{1,0:T(8,128)(2,1)S(1)}, bf16[256,256]{1,0:T(8,128)(2,1)S(1)}, u32[]{:S(2)}, u32[]{:S(2)}) collective-permute-start(bf16[256,256]{1,0:T(8,128)(2,1)S(1)} %get-tuple-element.133), channel_id=1, source_target_pairs={{0,8},{1,9},{2,10},{3,11},{4,12},{5,13},{6,14},{7,15},{8,0},{9,1},... | collective-permute-start | bytes 393224 | tf_op jit(solution)/shard_map/ppermute | solution.py:62
  37.8 0.0 collective-permute-done.6.r_2_
  37.8 0.0 collective-permute-done.7.r_3_
  37.8 0.0 collective-permute-done.8.r_4_
  37.8 0.6 shard_map.192
  38.4 3.3 %collective-permute-start.9 = (f32[64,256]{1,0:T(8,128)S(1)}, f32[64,256]{1,0:T(8,128)S(1)}, u32[]{:S(2)}, u32[]{:S(2)}) collective-permute-start(f32[64,256]{1,0:T(8,128)S(1)} %get-tuple-element.106), channel_id=1, source_target_pairs={{0,24},{1,25},{2,26},{3,27},{4,28},{5,29},{6,30},{7,31},{8,16},{9,... | collective-permute-start | bytes 196616 | tf_op jit(solution)/shard_map/ppermute | solution.py:62
  41.8 0.0 collective-permute-start.10
  41.8 1.1 %collective-permute-start.11 = (f32[64,256]{1,0:T(8,128)S(1)}, f32[64,256]{1,0:T(8,128)S(1)}, u32[]{:S(2)}, u32[]{:S(2)}) collective-permute-start(f32[64,256]{1,0:T(8,128)S(1)} %get-tuple-element.108), channel_id=1, source_target_pairs={{0,8},{1,9},{2,10},{3,11},{4,12},{5,13},{6,14},{7,15},{8,0},{9,1},... | collective-permute-start | bytes 196616 | tf_op jit(solution)/shard_map/ppermute | solution.py:62
  42.9 2.7 %shard_map.194 = (bf16[256,256]{1,0:T(8,128)(2,1)}, f32[256,256]{1,0:T(8,128)S(1)}, bf16[256,256]{1,0:T(8,128)(2,1)S(1)}, s32[4,128]{1,0:T(4,128)S(1)}) custom-call(s32[2]{0:T(128)S(1)} %bitcast.18, bf16[256,256]{1,0:T(8,128)(2,1)} %refs_0_.1, bf16[512,256]{1,0:T(8,128)(2,1)} %refs_1_.3, bf16[256,256]{1,0:T(8,128)(2,1)} %bitcast.22, s32[4,128]{1,0:T(4,128)} %bitcast.25, ...), custom_call_target="tpu_custom_call" | custom-call | flops 1000000000 | bytes 2097152 | tf_op jit(solution)/shard_map/pallas_call | solution.py:73
  45.6 0.0 collective-permute-done.9.r_2_
  45.6 2.9 %collective-permute-done.10.r_3_ = f32[64,256]{1,0:T(8,128)S(1)} collective-permute-done((f32[64,256]{1,0:T(8,128)S(1)}, f32[64,256]{1,0:T(8,128)S(1)}, u32[]{:S(2)}, u32[]{:S(2)}) %collective-permute-start.10) | collective-permute-done | bytes 65568 | tf_op jit(solution)/shard_map/ppermute | solution.py:62
  48.5 0.0 collective-permute-done.11.r_4_
  48.5 0.6 shard_map.195.r_1_
  49.1 2.2 %collective-permute-start.12 = (bf16[64,256]{1,0:T(8,128)(2,1)S(1)}, bf16[64,256]{1,0:T(8,128)(2,1)S(1)}, u32[]{:S(2)}, u32[]{:S(2)}) collective-permute-start(bf16[64,256]{1,0:T(8,128)(2,1)S(1)} %shard_map.195.r_1_), channel_id=1, source_target_pairs={{0,24},{1,25},{2,26},{3,27},{4,28},{5,29},{6,30},{7,31},{8,16},{9,... | collective-permute-start | bytes 98312 | tf_op jit(solution)/shard_map/ppermute | solution.py:62
  51.3 0.0 collective-permute-start.13
  51.3 2.2 %collective-permute-start.14 = (bf16[64,256]{1,0:T(8,128)(2,1)S(1)}, bf16[64,256]{1,0:T(8,128)(2,1)S(1)}, u32[]{:S(2)}, u32[]{:S(2)}) collective-permute-start(bf16[64,256]{1,0:T(8,128)(2,1)S(1)} %shard_map.195.r_1_), channel_id=1, source_target_pairs={{0,8},{1,9},{2,10},{3,11},{4,12},{5,13},{6,14},{7,15},{8,0},{9,1},... | collective-permute-start | bytes 98312 | tf_op jit(solution)/shard_map/ppermute | solution.py:62
  53.5 0.0 collective-permute-done.15.refs_4_
  53.5 0.0 collective-permute-start.21
  53.5 0.0 collective-permute-done.16.refs_6_
  53.5 0.7 %collective-permute-start.20 = (bf16[256,256]{1,0:T(8,128)(2,1)S(1)}, bf16[256,256]{1,0:T(8,128)(2,1)S(1)}, u32[]{:S(2)}, u32[]{:S(2)}) collective-permute-start(bf16[256,256]{1,0:T(8,128)(2,1)S(1)} %get-tuple-element.138), channel_id=1, source_target_pairs={{0,1},{1,0},{2,3},{3,2},{4,5},{5,4},{6,7},{7,6},{8,9},{9,8},{10,11... | collective-permute-start | bytes 393224 | tf_op jit(solution)/shard_map/ppermute | solution.py:62
  54.2 0.6 collective-permute-done.12.r_2_
  54.9 1.3 %collective-permute-done.13.r_3_ = bf16[64,256]{1,0:T(8,128)(2,1)S(1)} collective-permute-done((bf16[64,256]{1,0:T(8,128)(2,1)S(1)}, bf16[64,256]{1,0:T(8,128)(2,1)S(1)}, u32[]{:S(2)}, u32[]{:S(2)}) %collective-permute-start.13) | collective-permute-done | bytes 32800 | tf_op jit(solution)/shard_map/ppermute | solution.py:62
  56.1 0.0 collective-permute-done.14.r_4_
  56.1 0.6 shard_map.196.r_1_
  56.7 1.3 %collective-permute-start.19 = (bf16[256,256]{1,0:T(8,128)(2,1)S(1)}, bf16[256,256]{1,0:T(8,128)(2,1)S(1)}, u32[]{:S(2)}, u32[]{:S(2)}) collective-permute-start(bf16[256,256]{1,0:T(8,128)(2,1)S(1)} %shard_map.196.r_1_), channel_id=1, source_target_pairs={{0,5},{1,4},{2,7},{3,6},{4,1},{5,0},{6,3},{7,2},{8,13},{9,12},{10,... | collective-permute-start | bytes 393224 | tf_op jit(solution)/shard_map/ppermute | solution.py:62
  58.0 1.3 %collective-permute-start.18 = (bf16[256,256]{1,0:T(8,128)(2,1)S(1)}, bf16[256,256]{1,0:T(8,128)(2,1)S(1)}, u32[]{:S(2)}, u32[]{:S(2)}) collective-permute-start(bf16[256,256]{1,0:T(8,128)(2,1)S(1)} %shard_map.196.r_1_), channel_id=1, source_target_pairs={{0,4},{1,5},{2,6},{3,7},{4,0},{5,1},{6,2},{7,3},{8,12},{9,13},{10,... | collective-permute-start | bytes 393224 | tf_op jit(solution)/shard_map/ppermute | solution.py:62
  59.3 0.9 %collective-permute-start.17 = (bf16[256,256]{1,0:T(8,128)(2,1)S(1)}, bf16[256,256]{1,0:T(8,128)(2,1)S(1)}, u32[]{:S(2)}, u32[]{:S(2)}) collective-permute-start(bf16[256,256]{1,0:T(8,128)(2,1)S(1)} %shard_map.196.r_1_), channel_id=1, source_target_pairs={{0,1},{1,0},{2,3},{3,2},{4,5},{5,4},{6,7},{7,6},{8,9},{9,8},{10,11... | collective-permute-start | bytes 393224 | tf_op jit(solution)/shard_map/ppermute | solution.py:62
  60.2 0.0 collective-permute-done.21.refs_7_
  60.2 0.7 collective-permute-start.22
  60.9 0.0 collective-permute-done.22.refs_8_
  60.9 0.4 collective-permute-done.20.refs_5_
  61.3 2.0 %collective-permute-done.19.r_4_ = bf16[256,256]{1,0:T(8,128)(2,1)S(1)} collective-permute-done((bf16[256,256]{1,0:T(8,128)(2,1)S(1)}, bf16[256,256]{1,0:T(8,128)(2,1)S(1)}, u32[]{:S(2)}, u32[]{:S(2)}) %collective-permute-start.19) | collective-permute-done | bytes 131104 | tf_op jit(solution)/shard_map/ppermute | solution.py:62
  63.3 0.9 %collective-permute-done.18.r_3_ = bf16[256,256]{1,0:T(8,128)(2,1)S(1)} collective-permute-done((bf16[256,256]{1,0:T(8,128)(2,1)S(1)}, bf16[256,256]{1,0:T(8,128)(2,1)S(1)}, u32[]{:S(2)}, u32[]{:S(2)}) %collective-permute-start.18) | collective-permute-done | bytes 131104 | tf_op jit(solution)/shard_map/ppermute | solution.py:62
  64.3 0.8 %collective-permute-done.17.r_2_ = bf16[256,256]{1,0:T(8,128)(2,1)S(1)} collective-permute-done((bf16[256,256]{1,0:T(8,128)(2,1)S(1)}, bf16[256,256]{1,0:T(8,128)(2,1)S(1)}, u32[]{:S(2)}, u32[]{:S(2)}) %collective-permute-start.17) | collective-permute-done | bytes 131104 | tf_op jit(solution)/shard_map/ppermute | solution.py:62
  65.1 0.6 shard_map.198.r_1_
  65.7 0.4 collective-permute-start.23
  66.1 1.5 %shard_map.197 = bf16[256,256]{1,0:T(8,128)(2,1)} custom-call(s32[7]{0:T(128)S(1)} %stack.47.info.r_0_, bf16[256,256]{1,0:T(8,128)(2,1)S(1)} %get-tuple-element.118.refs_0_, s32[4,128]{1,0:T(4,128)S(1)} %get-tuple-element.119.refs_1_, f32[256,256]{1,0:T(8,128)S(1)} %get-tuple-element.120.refs_2_, f32[256,256]{1,0:T(8,128)S(1)} %get-tuple-element.121.refs_3_, ...), custom_call_target="tpu_custom_call" | custom-call | tf_op jit(solution)/shard_map/pallas_call | solution.py:73
  67.6 0.0 collective-permute-done.23.r_2_
  67.6 1.9 %shard_map.199 = (f32[256,256]{1,0:T(8,128)}, f32[256,256]{1,0:T(8,128)}, f32[256,256]{1,0:T(8,128)}, f32[256,256]{1,0:T(8,128)}, f32[256,512]{1,0:T(8,128)}, /*index=5*/f32[512,256]{1,0:T(8,128)}) custom-call(s32[7]{0:T(128)S(1)} %stack.47.info.r_0_, bf16[1024,256]{1,0:T(8,128)(2,1)S(1)} %shard_map.198.r_1_, bf16[1024,256]{1,0:T(8,128)(2,1)S(1)} %collective-permute-done.23.r_2_), custom_call_target="tpu_custom_call" | custom-call | tf_op jit(solution)/shard_map/pallas_call | solution.py:73
  (2 shorter events, 0.0 us)
Async XLA Ops:
  2.6 10.9 %collective-permute-start.2 = (bf16[272,256]{1,0:T(8,128)(2,1)S(1)}, bf16[272,256]{1,0:T(8,128)(2,1)S(1)}, u32[]{:S(2)}, u32[]{:S(2)}) collective-permute-start(bf16[272,256]{1,0:T(8,128)(2,1)S(1)} %get-tuple-element.81.refs_6_.r_11_), channel_id=1, source_target_pairs={{0,16},{1,17},{2,18},{3,19},{4,20},{5,21},{6,22},{7,23},{8,24},{9,... | collective-permute-start | bytes 417800 | tf_op jit(solution)/shard_map/ppermute | solution.py:62
  6.7 6.8 %collective-permute-start.1 = (bf16[272,256]{1,0:T(8,128)(2,1)S(1)}, bf16[272,256]{1,0:T(8,128)(2,1)S(1)}, u32[]{:S(2)}, u32[]{:S(2)}) collective-permute-start(bf16[272,256]{1,0:T(8,128)(2,1)S(1)} %get-tuple-element.81.refs_6_.r_11_), channel_id=1, source_target_pairs={{0,1},{1,0},{2,3},{3,2},{4,5},{5,4},{6,7},{7,6},{8,9},{9,8},{10,11... | collective-permute-start | bytes 417800 | tf_op jit(solution)/shard_map/ppermute | solution.py:62
  8.2 6.7 %collective-permute-start = (bf16[272,256]{1,0:T(8,128)(2,1)S(1)}, bf16[272,256]{1,0:T(8,128)(2,1)S(1)}, u32[]{:S(2)}, u32[]{:S(2)}) collective-permute-start(bf16[272,256]{1,0:T(8,128)(2,1)S(1)} %get-tuple-element.81.refs_6_.r_11_), channel_id=1, source_target_pairs={{0,8},{1,9},{2,10},{3,11},{4,12},{5,13},{6,14},{7,15},{8,0},{9,1},... | collective-permute-start | bytes 417800 | tf_op jit(solution)/shard_map/ppermute | solution.py:62
  9.8 3.3 %collective-permute-start.3 = (bf16[128,256]{1,0:T(8,128)(2,1)S(1)}, bf16[128,256]{1,0:T(8,128)(2,1)S(1)}, u32[]{:S(2)}, u32[]{:S(2)}) collective-permute-start(bf16[128,256]{1,0:T(8,128)(2,1)S(1)} %get-tuple-element.85), channel_id=1, source_target_pairs={{0,2},{4,6},{8,10},{12,14},{16,18},{20,22},{24,26},{28,30},{2,0},{... | collective-permute-start | bytes 196616 | tf_op jit(solution)/shard_map/ppermute | solution.py:52
  9.8 3.3 %collective-permute-start.4 = (bf16[128,256]{1,0:T(8,128)(2,1)S(1)}, bf16[128,256]{1,0:T(8,128)(2,1)S(1)}, u32[]{:S(2)}, u32[]{:S(2)}) collective-permute-start(bf16[128,256]{1,0:T(8,128)(2,1)S(1)} %get-tuple-element.86), channel_id=1, source_target_pairs={{2,4},{6,8},{10,12},{14,16},{18,20},{22,24},{26,28},{4,2},{8,6},{1... | collective-permute-start | bytes 196616 | tf_op jit(solution)/shard_map/ppermute | solution.py:52
  10.5 2.5 %copy-start.1 = (s32[1,1,3,2]{2,3,1,0:T(2,128)S(1)}, s32[1,1,3,2]{2,3,1,0:T(2,128)}, u32[]{:S(2)}) copy-start(s32[1,1,3,2]{2,3,1,0:T(2,128)} %param.24) | copy-start | bytes 76
  10.5 4.4 %copy-start = (s32[1,1,2]{2,1,0:T(1,128)S(1)}, s32[1,1,2]{2,1,0:T(1,128)}, u32[]{:S(2)}) copy-start(s32[1,1,2]{2,1,0:T(1,128)} %param.21) | copy-start | bytes 28
  24.8 2.7 %collective-permute-start.5 = (bf16[1024,256]{1,0:T(8,128)(2,1)S(1)}, bf16[1024,256]{1,0:T(8,128)(2,1)S(1)}, u32[]{:S(2)}, u32[]{:S(2)}) collective-permute-start(bf16[1024,256]{1,0:T(8,128)(2,1)S(1)} %get-tuple-element.88), channel_id=1, source_target_pairs={{0,2},{1,3},{2,0},{3,1},{4,6},{5,7},{6,4},{7,5},{8,10},{9,11},{10,... | collective-permute-start | bytes 1572872 | tf_op jit(solution)/shard_map/ppermute | solution.py:62
  28.2 9.6 %collective-permute-start.6 = (bf16[256,256]{1,0:T(8,128)(2,1)S(1)}, bf16[256,256]{1,0:T(8,128)(2,1)S(1)}, u32[]{:S(2)}, u32[]{:S(2)}) collective-permute-start(bf16[256,256]{1,0:T(8,128)(2,1)S(1)} %get-tuple-element.94), channel_id=1, source_target_pairs={{0,5},{1,4},{2,7},{3,6},{4,1},{5,0},{6,3},{7,2},{8,13},{9,12},{10,... | collective-permute-start | bytes 393224 | tf_op jit(solution)/shard_map/ppermute | solution.py:62
  30.6 7.2 %collective-permute-start.7 = (bf16[256,256]{1,0:T(8,128)(2,1)S(1)}, bf16[256,256]{1,0:T(8,128)(2,1)S(1)}, u32[]{:S(2)}, u32[]{:S(2)}) collective-permute-start(bf16[256,256]{1,0:T(8,128)(2,1)S(1)} %get-tuple-element.95), channel_id=1, source_target_pairs={{0,4},{1,5},{2,6},{3,7},{4,0},{5,1},{6,2},{7,3},{8,12},{9,13},{10,... | collective-permute-start | bytes 393224 | tf_op jit(solution)/shard_map/ppermute | solution.py:62
  30.7 7.1 %collective-permute-start.8 = (bf16[256,256]{1,0:T(8,128)(2,1)S(1)}, bf16[256,256]{1,0:T(8,128)(2,1)S(1)}, u32[]{:S(2)}, u32[]{:S(2)}) collective-permute-start(bf16[256,256]{1,0:T(8,128)(2,1)S(1)} %get-tuple-element.96), channel_id=1, source_target_pairs={{0,1},{1,0},{2,3},{3,2},{4,5},{5,4},{6,7},{7,6},{8,9},{9,8},{10,11... | collective-permute-start | bytes 393224 | tf_op jit(solution)/shard_map/ppermute | solution.py:62
  33.9 19.6 %collective-permute-start.15 = (bf16[256,256]{1,0:T(8,128)(2,1)S(1)}, bf16[256,256]{1,0:T(8,128)(2,1)S(1)}, u32[]{:S(2)}, u32[]{:S(2)}) collective-permute-start(bf16[256,256]{1,0:T(8,128)(2,1)S(1)} %get-tuple-element.132), channel_id=1, source_target_pairs={{0,16},{1,17},{2,18},{3,19},{4,20},{5,21},{6,22},{7,23},{8,24},{9,... | collective-permute-start | bytes 393224 | tf_op jit(solution)/shard_map/ppermute | solution.py:62
  35.8 17.8 %collective-permute-start.16 = (bf16[256,256]{1,0:T(8,128)(2,1)S(1)}, bf16[256,256]{1,0:T(8,128)(2,1)S(1)}, u32[]{:S(2)}, u32[]{:S(2)}) collective-permute-start(bf16[256,256]{1,0:T(8,128)(2,1)S(1)} %get-tuple-element.133), channel_id=1, source_target_pairs={{0,8},{1,9},{2,10},{3,11},{4,12},{5,13},{6,14},{7,15},{8,0},{9,1},... | collective-permute-start | bytes 393224 | tf_op jit(solution)/shard_map/ppermute | solution.py:62
  38.4 7.1 %collective-permute-start.9 = (f32[64,256]{1,0:T(8,128)S(1)}, f32[64,256]{1,0:T(8,128)S(1)}, u32[]{:S(2)}, u32[]{:S(2)}) collective-permute-start(f32[64,256]{1,0:T(8,128)S(1)} %get-tuple-element.106), channel_id=1, source_target_pairs={{0,24},{1,25},{2,26},{3,27},{4,28},{5,29},{6,30},{7,31},{8,16},{9,... | collective-permute-start | bytes 196616 | tf_op jit(solution)/shard_map/ppermute | solution.py:62
  41.8 6.7 %collective-permute-start.10 = (f32[64,256]{1,0:T(8,128)S(1)}, f32[64,256]{1,0:T(8,128)S(1)}, u32[]{:S(2)}, u32[]{:S(2)}) collective-permute-start(f32[64,256]{1,0:T(8,128)S(1)} %get-tuple-element.107), channel_id=1, source_target_pairs={{0,16},{1,17},{2,18},{3,19},{4,20},{5,21},{6,22},{7,23},{8,24},{9,... | collective-permute-start | bytes 196616 | tf_op jit(solution)/shard_map/ppermute | solution.py:62
  41.8 6.7 %collective-permute-start.11 = (f32[64,256]{1,0:T(8,128)S(1)}, f32[64,256]{1,0:T(8,128)S(1)}, u32[]{:S(2)}, u32[]{:S(2)}) collective-permute-start(f32[64,256]{1,0:T(8,128)S(1)} %get-tuple-element.108), channel_id=1, source_target_pairs={{0,8},{1,9},{2,10},{3,11},{4,12},{5,13},{6,14},{7,15},{8,0},{9,1},... | collective-permute-start | bytes 196616 | tf_op jit(solution)/shard_map/ppermute | solution.py:62
  49.1 5.8 %collective-permute-start.12 = (bf16[64,256]{1,0:T(8,128)(2,1)S(1)}, bf16[64,256]{1,0:T(8,128)(2,1)S(1)}, u32[]{:S(2)}, u32[]{:S(2)}) collective-permute-start(bf16[64,256]{1,0:T(8,128)(2,1)S(1)} %shard_map.195.r_1_), channel_id=1, source_target_pairs={{0,24},{1,25},{2,26},{3,27},{4,28},{5,29},{6,30},{7,31},{8,16},{9,... | collective-permute-start | bytes 98312 | tf_op jit(solution)/shard_map/ppermute | solution.py:62
  51.3 4.8 %collective-permute-start.13 = (bf16[64,256]{1,0:T(8,128)(2,1)S(1)}, bf16[64,256]{1,0:T(8,128)(2,1)S(1)}, u32[]{:S(2)}, u32[]{:S(2)}) collective-permute-start(bf16[64,256]{1,0:T(8,128)(2,1)S(1)} %shard_map.195.r_1_), channel_id=1, source_target_pairs={{0,16},{1,17},{2,18},{3,19},{4,20},{5,21},{6,22},{7,23},{8,24},{9,... | collective-permute-start | bytes 98312 | tf_op jit(solution)/shard_map/ppermute | solution.py:62
  51.3 4.8 %collective-permute-start.14 = (bf16[64,256]{1,0:T(8,128)(2,1)S(1)}, bf16[64,256]{1,0:T(8,128)(2,1)S(1)}, u32[]{:S(2)}, u32[]{:S(2)}) collective-permute-start(bf16[64,256]{1,0:T(8,128)(2,1)S(1)} %shard_map.195.r_1_), channel_id=1, source_target_pairs={{0,8},{1,9},{2,10},{3,11},{4,12},{5,13},{6,14},{7,15},{8,0},{9,1},... | collective-permute-start | bytes 98312 | tf_op jit(solution)/shard_map/ppermute | solution.py:62
  53.5 6.7 %collective-permute-start.21 = (bf16[128,256]{1,0:T(8,128)(2,1)S(1)}, bf16[128,256]{1,0:T(8,128)(2,1)S(1)}, u32[]{:S(2)}, u32[]{:S(2)}) collective-permute-start(bf16[128,256]{1,0:T(8,128)(2,1)S(1)} %get-tuple-element.139), channel_id=1, source_target_pairs={{0,2},{4,6},{8,10},{12,14},{16,18},{20,22},{24,26},{28,30},{2,0},{... | collective-permute-start | bytes 196616 | tf_op jit(solution)/shard_map/ppermute | solution.py:52
  53.5 7.8 %collective-permute-start.20 = (bf16[256,256]{1,0:T(8,128)(2,1)S(1)}, bf16[256,256]{1,0:T(8,128)(2,1)S(1)}, u32[]{:S(2)}, u32[]{:S(2)}) collective-permute-start(bf16[256,256]{1,0:T(8,128)(2,1)S(1)} %get-tuple-element.138), channel_id=1, source_target_pairs={{0,1},{1,0},{2,3},{3,2},{4,5},{5,4},{6,7},{7,6},{8,9},{9,8},{10,11... | collective-permute-start | bytes 393224 | tf_op jit(solution)/shard_map/ppermute | solution.py:62
  56.7 6.7 %collective-permute-start.19 = (bf16[256,256]{1,0:T(8,128)(2,1)S(1)}, bf16[256,256]{1,0:T(8,128)(2,1)S(1)}, u32[]{:S(2)}, u32[]{:S(2)}) collective-permute-start(bf16[256,256]{1,0:T(8,128)(2,1)S(1)} %shard_map.196.r_1_), channel_id=1, source_target_pairs={{0,5},{1,4},{2,7},{3,6},{4,1},{5,0},{6,3},{7,2},{8,13},{9,12},{10,... | collective-permute-start | bytes 393224 | tf_op jit(solution)/shard_map/ppermute | solution.py:62
  58.0 6.3 %collective-permute-start.18 = (bf16[256,256]{1,0:T(8,128)(2,1)S(1)}, bf16[256,256]{1,0:T(8,128)(2,1)S(1)}, u32[]{:S(2)}, u32[]{:S(2)}) collective-permute-start(bf16[256,256]{1,0:T(8,128)(2,1)S(1)} %shard_map.196.r_1_), channel_id=1, source_target_pairs={{0,4},{1,5},{2,6},{3,7},{4,0},{5,1},{6,2},{7,3},{8,12},{9,13},{10,... | collective-permute-start | bytes 393224 | tf_op jit(solution)/shard_map/ppermute | solution.py:62
  59.3 5.8 %collective-permute-start.17 = (bf16[256,256]{1,0:T(8,128)(2,1)S(1)}, bf16[256,256]{1,0:T(8,128)(2,1)S(1)}, u32[]{:S(2)}, u32[]{:S(2)}) collective-permute-start(bf16[256,256]{1,0:T(8,128)(2,1)S(1)} %shard_map.196.r_1_), channel_id=1, source_target_pairs={{0,1},{1,0},{2,3},{3,2},{4,5},{5,4},{6,7},{7,6},{8,9},{9,8},{10,11... | collective-permute-start | bytes 393224 | tf_op jit(solution)/shard_map/ppermute | solution.py:62
  60.2 0.7 collective-permute-start.22
  65.7 2.0 %collective-permute-start.23 = (bf16[1024,256]{1,0:T(8,128)(2,1)S(1)}, bf16[1024,256]{1,0:T(8,128)(2,1)S(1)}, u32[]{:S(2)}, u32[]{:S(2)}) collective-permute-start(bf16[1024,256]{1,0:T(8,128)(2,1)S(1)} %shard_map.198.r_1_), channel_id=1, source_target_pairs={{0,2},{1,3},{2,0},{3,1},{4,6},{5,7},{6,4},{7,5},{8,10},{9,11},{10,... | collective-permute-start | bytes 1572872 | tf_op jit(solution)/shard_map/ppermute | solution.py:62
